TPU v7x, 256 devices: a whole 4x4x8 slice. The times are simulated.
256 devices in a mesh: grp: 16 (over x, z_lo), kin: 16 (over z_hi, y, core).
Axes of the slice: x: 4, y: 4, z: 8 (z_hi: 2, z_lo: 4; z = z_hi * 4 + z_lo), core: 2. Of those that a mesh axis runs over, the one named last changes fastest.
Arguments:
- waves: bfloat16 [256, 2, 8, 1024], P(('grp', 'kin')), may hold values from -6 to 6
- vector: float32 [256, 2, 16], P(('grp', 'kin')), may hold values from -6 to 6
- energies: float32 [256, 16], P(('grp', 'kin')), may hold values from 0.5 to 1.5
- basis: bfloat16 [2, 1024, 1536], replicated, may hold values from -0.1875 to 0.1875
- screening: float32 [256, 1536], replicated, may hold values from 0.05 to 1
- coulomb: float32 [1536], replicated, may hold values from 0.01 to 0.2
- qmap: int32 [256, 256], P(('grp', 'kin')), may hold values from 0 to 255, as said below
Outputs:
- applied: float32 [256, 2, 16], P(('grp', 'kin'))
Inputs may be any that keep to these rules, and one draw needn't show every extreme that they name: qmap[s, s2] is the index, on the periodic 16 x 16 k-grid, of the difference of the grid points of the stored k-points s and s2 (grid point x * 16 + y); the stored k-points are a permutation of the grid points, so each row holds every value once.
All inputs are finite; a program needn't handle non-finite values.
Results may differ from a plain program's by a relative error of at most 0.0057.
Values may be sent and summed in bfloat16 or wider, within the bound.
No kernel may reach another device: no remote copies, remote signals or barrier semaphores. Data moves between devices by JAX's collectives and lax.ppermute only.
A program may use at most 64 MiB of HBM per device.

v0:
```python
import jax
import jax.numpy as jnp
from jax import lax
from jax.sharding import PartitionSpec as P

NV = 4
NC = 4
NT = 16


def shifted(value, axis, steps):
    count = lax.axis_size(axis)
    pairs = [(source, (source + steps) % count) for source in range(count)]
    return lax.ppermute(value, axis, pairs)


def conj_products(left, right):
    left_re = left[:, 0].astype(jnp.float32)[:, None, :, None, :]
    left_im = left[:, 1].astype(jnp.float32)[:, None, :, None, :]
    right_re = right[:, 0].astype(jnp.float32)[None, :, None, :, :]
    right_im = right[:, 1].astype(jnp.float32)[None, :, None, :, :]
    real_part = (left_re * right_re + left_im * right_im).astype(jnp.bfloat16)
    imag_part = (left_re * right_im - left_im * right_re).astype(jnp.bfloat16)
    return (real_part, imag_part)


def densities(pair_re, pair_im, basis):
    rows = pair_re.shape[0]
    stacked = jnp.concatenate([pair_re, pair_im], 0)
    first = jnp.dot(stacked, basis[0], preferred_element_type=jnp.float32)
    second = jnp.dot(stacked, basis[1], preferred_element_type=jnp.float32)
    real_part = (first[:rows] - second[rows:]).astype(jnp.bfloat16)
    imag_part = (second[:rows] + first[rows:]).astype(jnp.bfloat16)
    return (real_part, imag_part)


def block_terms(own_waves, own_vector, part_waves, part_vector, weights, basis):
    highest = lax.Precision.HIGHEST
    owners = own_waves.shape[0]
    partners = part_waves.shape[0]
    points = own_waves.shape[3]
    cond_re, cond_im = conj_products(own_waves[:, :, NV:], part_waves[:, :, NV:])
    val_re, val_im = conj_products(own_waves[:, :, :NV], part_waves[:, :, :NV])
    pair_re = jnp.concatenate(
        [
            cond_re.reshape(owners, partners, NC * NC, points),
            val_re.reshape(owners, partners, NV * NV, points),
        ],
        2,
    ).reshape(-1, points)
    pair_im = jnp.concatenate(
        [
            cond_im.reshape(owners, partners, NC * NC, points),
            val_im.reshape(owners, partners, NV * NV, points),
        ],
        2,
    ).reshape(-1, points)
    dens_re, dens_im = densities(pair_re, pair_im, basis)
    dens_re = dens_re.reshape(owners, partners, NC * NC + NV * NV, -1)
    dens_im = dens_im.reshape(owners, partners, NC * NC + NV * NV, -1)
    wcond_re = dens_re[:, :, : NC * NC].astype(jnp.float32) * weights[:, :, None, :]
    wcond_im = dens_im[:, :, : NC * NC].astype(jnp.float32) * weights[:, :, None, :]
    val_dre = dens_re[:, :, NC * NC :].astype(jnp.float32)
    val_dim = dens_im[:, :, NC * NC :].astype(jnp.float32)
    kern_re = jnp.einsum("abpg,abqg->abpq", wcond_re, val_dre, precision=highest) + jnp.einsum(
        "abpg,abqg->abpq", wcond_im, val_dim, precision=highest
    )
    kern_im = jnp.einsum("abpg,abqg->abpq", wcond_re, val_dim, precision=highest) - jnp.einsum(
        "abpg,abqg->abpq", wcond_im, val_dre, precision=highest
    )
    kern_re = kern_re.reshape(owners, partners, NC, NC, NV, NV)
    kern_im = kern_im.reshape(owners, partners, NC, NC, NV, NV)
    own_x = own_vector.astype(jnp.float32).reshape(owners, 2, NV, NC)
    part_x = part_vector.astype(jnp.float32).reshape(partners, 2, NV, NC)
    form_d = "abcdvw,bwd->avc"
    direct_re = jnp.einsum(form_d, kern_re, part_x[:, 0], precision=highest) - jnp.einsum(
        form_d, kern_im, part_x[:, 1], precision=highest
    )
    direct_im = jnp.einsum(form_d, kern_re, part_x[:, 1], precision=highest) + jnp.einsum(
        form_d, kern_im, part_x[:, 0], precision=highest
    )
    form_h = "abcdvw,avc->bwd"
    herm_re = jnp.einsum(form_h, kern_re, own_x[:, 0], precision=highest) + jnp.einsum(
        form_h, kern_im, own_x[:, 1], precision=highest
    )
    herm_im = jnp.einsum(form_h, kern_re, own_x[:, 1], precision=highest) - jnp.einsum(
        form_h, kern_im, own_x[:, 0], precision=highest
    )
    direct = jnp.stack([direct_re.reshape(owners, NT), direct_im.reshape(owners, NT)], 1)
    hermitian = jnp.stack([herm_re.reshape(partners, NT), herm_im.reshape(partners, NT)], 1)
    return (direct, hermitian)


def own_densities(waves, basis):
    count = waves.shape[0]
    points = waves.shape[3]
    val_re = waves[:, 0, :NV].astype(jnp.float32)[:, :, None, :]
    val_im = waves[:, 1, :NV].astype(jnp.float32)[:, :, None, :]
    con_re = waves[:, 0, NV:].astype(jnp.float32)[:, None, :, :]
    con_im = waves[:, 1, NV:].astype(jnp.float32)[:, None, :, :]
    pair_re = (val_re * con_re + val_im * con_im).astype(jnp.bfloat16).reshape(-1, points)
    pair_im = (val_re * con_im - val_im * con_re).astype(jnp.bfloat16).reshape(-1, points)
    dens_re, dens_im = densities(pair_re, pair_im, basis)
    return (dens_re.reshape(count, NT, -1), dens_im.reshape(count, NT, -1))


def on_device(waves, vector, energies, basis, screening, coulomb, qmap):
    highest = lax.Precision.HIGHEST
    groups = lax.axis_size("grp")
    members = lax.axis_size("kin")
    offset = groups // 4
    own_count = waves.shape[0]
    block = own_count * members
    total = block * groups
    coarse = vector.astype(jnp.bfloat16)
    group_waves, group_vector = (
        lax.all_gather(waves, "kin", axis=0, tiled=True),
        lax.all_gather(coarse, "kin", axis=0, tiled=True),
    )
    partner_waves, partner_vector = shifted((group_waves, group_vector), "grp", offset)
    partner_group = (lax.axis_index("grp") - offset) % groups
    qrows = lax.dynamic_slice_in_dim(qmap, partner_group * block, block, 1)
    weights = jnp.take(screening, qrows.reshape(-1), axis=0).reshape(own_count, block, -1)
    direct, hermitian = block_terms(waves, coarse, partner_waves, partner_vector, weights, basis)
    ex_re, ex_im = own_densities(waves, basis)
    ex_re = ex_re.astype(jnp.float32)
    ex_im = ex_im.astype(jnp.float32)
    coarse_x = coarse.astype(jnp.float32)
    part_re = jnp.einsum("atg,at->g", ex_re, coarse_x[:, 0], precision=highest) - jnp.einsum(
        "atg,at->g", ex_im, coarse_x[:, 1], precision=highest
    )
    part_im = jnp.einsum("atg,at->g", ex_re, coarse_x[:, 1], precision=highest) + jnp.einsum(
        "atg,at->g", ex_im, coarse_x[:, 0], precision=highest
    )
    sum_re, sum_im = lax.psum((part_re, part_im), ("grp", "kin"))
    pot_re = coulomb * sum_re
    pot_im = coulomb * sum_im
    exch_re = jnp.einsum("atg,g->at", ex_re, pot_re, precision=highest) + jnp.einsum(
        "atg,g->at", ex_im, pot_im, precision=highest
    )
    exch_im = jnp.einsum("atg,g->at", ex_re, pot_im, precision=highest) - jnp.einsum(
        "atg,g->at", ex_im, pot_re, precision=highest
    )
    exchange = jnp.stack([exch_re, exch_im], 1)
    summed = lax.psum_scatter(hermitian, "kin", scatter_dimension=0, tiled=True)
    returned = shifted(summed, "grp", -offset)
    scale = jnp.float32(1.0 / total)
    return energies[:, None, :] * vector + 2.0 * scale * exchange - scale * (direct + returned)


def solution(mesh):
    return jax.shard_map(
        on_device,
        mesh=mesh,
        in_specs=(
            P(("grp", "kin"), None, None, None),
            P(("grp", "kin"), None, None),
            P(("grp", "kin"), None),
            P(),
            P(),
            P(),
            P(("grp", "kin"), None),
        ),
        out_specs=P(("grp", "kin"), None, None),
        check_vma=False,
    )
```

profile of v0, /device:TPU:6, one launch (start us, length us, event | category | flops | bytes accessed | tf_op | source)
XLA Modules:
  0.0 279.5 jit_solution(1810780097922811389)
XLA Ops:
  0.0 35.3 %all_gather.6 = bf16[16,2,8,1024]{3,2,1,0:T(8,128)(2,1)S(1)} all-gather(bf16[1,2,8,1024]{3,2,1,0:T(8,128)(2,1)} %param.7), channel_id=1, replica_groups=mesh['grp'=16,'kin'=16] {'kin'}, dimensions={0}, use_global_device_ids=true | all-gather | bytes 557056 | tf_op jit(solution)/shard_map/all_gather | solution.py:117
  35.3 0.5 collective-permute-start
  35.7 0.7 convert_element_type.197
  36.4 23.7 %all_gather.7 = bf16[16,2,16]{2,1,0:T(2,128)(2,1)S(1)} all-gather(bf16[1,2,16]{2,1,0:T(2,128)(2,1)S(1)} %convert_element_type.197), channel_id=1, replica_groups=mesh['grp'=16,'kin'=16] {'kin'}, dimensions={0}, use_global_device_ids=true | all-gather | bytes 1088 | tf_op jit(solution)/shard_map/all_gather | solution.py:118
  60.2 1.5 collective-permute-start.1
  61.7 0.8 bitcast_convert_fusion.2
  62.7 2.5 fusion.4
  65.3 2.5 fusion.8
  68.1 0.1 convolution_reduce_fusion.2
  68.7 73.7 %all-reduce.1 = (f32[1536]{0:T(1024)S(1)}, f32[1536]{0:T(1024)S(1)}) all-reduce(f32[1536]{0:T(1024)S(1)} %sub.70, f32[1536]{0:T(1024)S(1)} %add.99), channel_id=1, replica_groups=mesh['grp'=16,'kin'=16] {'grp','kin'}, use_global_device_ids=true, to_apply=%region_0.1 | all-reduce | flops 3072 | bytes 24576 | tf_op jit(solution)/shard_map/psum | solution.py:135
  142.6 0.1 convolution_bitcast_fusion.2
  142.7 0.7 fusion.31
  143.5 0.6 gather_fusion
  144.1 0.7 broadcast_select_fusion
  144.8 0.7 fusion.29
  145.5 0.6 mul.331
  146.1 0.6 mul.325
  147.0 0.6 dynamic-slice
  147.6 0.3 fusion.42
  147.9 1.2 mul.341
  149.1 1.6 mul.342
  150.7 1.3 mul.337
  151.9 2.6 mul.338
  154.5 1.3 mul.333
  155.8 2.6 mul.334
  158.3 1.2 mul.327
  159.6 2.6 mul.328
  162.2 1.7 add_convert_fusion
  163.9 0.2 copy-done.2
  164.0 0.3 add_convert_fusion.1
  164.4 0.2 pad_maximum_fusion.3
  164.6 5.4 %fusion.6 = f32[1024,1536]{1,0:T(8,128)S(1)} fusion(bf16[2,1024,1536]{2,1,0:T(8,128)(2,1)} %param.10, bf16[512,1024]{1,0:T(8,128)(2,1)S(1)} %bitcast.193, bf16[512,1024]{1,0:T(8,128)(2,1)S(1)} %bitcast.191), kind=kOutput, calls=%fused_computation.9 | convolution fusion | flops 3225419776 | bytes 11534336 | tf_op jit(solution)/shard_map/dot_general | solution.py:30
  170.0 3.4 %fusion.2 = f32[1024,1536]{1,0:T(8,128)S(1)} fusion(bf16[2,1024,1536]{2,1,0:T(8,128)(2,1)S(1)} %bitcast.210, bf16[512,1024]{1,0:T(8,128)(2,1)S(1)} %bitcast.194, bf16[512,1024]{1,0:T(8,128)(2,1)S(1)} %bitcast.192), kind=kOutput, calls=%fused_computation.5 | convolution fusion | flops 3225419776 | bytes 11534336 | tf_op jit(solution)/shard_map/dot_general | solution.py:31
  173.5 1.7 fusion
  175.2 1.8 fusion.16
  177.1 1.2 fusion.14
  178.3 1.2 fusion.25
  179.7 2.2 fusion.22
  182.0 1.0 fusion.48
  182.9 1.0 fusion.50
  183.9 1.0 fusion.44
  184.9 1.0 fusion.46
  185.9 0.2 multiply_reduce_fusion.2
  186.2 87.1 %all-reduce = f32[16,2,16]{2,1,0:T(2,128)S(1)} all-reduce(f32[16,2,16]{2,1,0:T(2,128)S(1)} %copy.29), channel_id=2, replica_groups=mesh['grp'=16,'kin'=16] {'kin'}, use_global_device_ids=true, to_apply=%region_2.3.clone | all-reduce | flops 512 | bytes 4096
  273.4 0.6 constant_dynamic-slice_fusion
  274.0 0.7 collective-permute-start.2
  275.1 3.8 %collective-permute-done.2 = f32[1,2,16]{2,1,0:T(2,128)S(1)} collective-permute-done((f32[1,2,16]{2,1,0:T(2,128)S(1)}, f32[1,2,16]{2,1,0:T(2,128)S(1)}, u32[]{:S(2)}, u32[]{:S(2)}) %collective-permute-start.2) | collective-permute-done | bytes 160 | tf_op jit(solution)/shard_map/ppermute | solution.py:14
  278.9 0.6 fusion.61
  (74 shorter events, 2.1 us)
Async XLA Ops:
  0.0 143.5 %copy-start = (f32[256,1536]{1,0:T(8,128)S(1)}, f32[256,1536]{1,0:T(8,128)}, u32[]{:S(2)}) copy-start(f32[256,1536]{1,0:T(8,128)} %param.11) | copy-start | bytes 4718596
  35.3 112.3 %collective-permute-start = (bf16[16,2,8,1024]{3,2,1,0:T(8,128)(2,1)S(1)}, bf16[16,2,8,1024]{3,2,1,0:T(8,128)(2,1)S(1)}, u32[]{:S(2)}, u32[]{:S(2)}) collective-permute-start(bf16[16,2,8,1024]{3,2,1,0:T(8,128)(2,1)S(1)} %all_gather.6), channel_id=1, source_target_pairs={{0,64},{16,80},{32,96},{48,112},{64,128},{80,144},{96,160},{112,17... | collective-permute-start | bytes 1572872 | tf_op jit(solution)/shard_map/ppermute | solution.py:14
  60.2 87.4 %collective-permute-start.1 = (bf16[16,2,16]{0,2,1:T(8,128)(2,1)S(1)}, bf16[16,2,16]{0,2,1:T(8,128)(2,1)S(1)}, u32[]{:S(2)}, u32[]{:S(2)}) collective-permute-start(bf16[16,2,16]{0,2,1:T(8,128)(2,1)S(1)} %copy.25), channel_id=1, source_target_pairs={{0,64},{16,80},{32,96},{48,112},{64,128},{80,144},{96,160},{112,17... | collective-permute-start | bytes 3080 | tf_op jit(solution)/shard_map/ppermute | solution.py:14
  65.3 3.2 %copy-start.11 = (s32[1,256]{1,0:T(1,128)S(1)}, s32[1,256]{1,0:T(1,128)}, u32[]{:S(2)}) copy-start(s32[1,256]{1,0:T(1,128)} %param.13) | copy-start | bytes 3076
  65.3 77.2 %copy-start.6 = (f32[1536]{0:T(1024)S(1)}, f32[1536]{0:T(1024)}, u32[]{:S(2)}) copy-start(f32[1536]{0:T(1024)} %param.12) | copy-start | bytes 18436
  67.8 79.1 %copy-start.12 = (u32[256]{0:T(256)S(1)}, u32[256]{0:T(256)}, u32[]{:S(2)}) copy-start(u32[256]{0:T(256)} %constant.52) | copy-start | bytes 3076
  162.2 1.7 copy-start.1
  162.2 1.9 copy-start.2
  162.2 1.9 copy-start.3
  162.2 1.9 copy-start.4
  164.4 5.7 %slice-start = ((s8[6291456]{0:T(1024)(128)(4,1)}), s8[4194304]{0:T(1024)(128)(4,1)S(1)}, s32[]{:S(2)}) async-start(s8[6291456]{0:T(1024)(128)(4,1)} %bitcast.209), calls=%async_computation | async-start | bytes 8388608
  164.6 5.5 %slice-start.1 = ((s8[6291456]{0:T(1024)(128)(4,1)}), s8[2097152]{0:T(1024)(128)(4,1)S(1)}, s32[]{:S(2)}) async-start(s8[6291456]{0:T(1024)(128)(4,1)} %bitcast.209), calls=%async_computation.1 | async-start | bytes 4194304
  173.5 1.8 copy-start.5
  179.6 99.3 %copy-start.7 = (f32[1,2,16]{2,1,0:T(2,128)S(1)}, f32[1,2,16]{2,1,0:T(2,128)}, u32[]{:S(2)}) copy-start(f32[1,2,16]{2,1,0:T(2,128)} %param.8) | copy-start | bytes 388
  179.6 99.3 %copy-start.8 = (f32[1,16]{1,0:T(1,128)S(1)}, f32[1,16]{1,0:T(1,128)}, u32[]{:S(2)}) copy-start(f32[1,16]{1,0:T(1,128)} %param.9) | copy-start | bytes 196
  179.6 99.3 %copy-start.9 = (f32[1,1,16]{2,1,0:T(1,128)S(1)}, f32[1,1,16]{2,1,0:T(1,128)}, u32[]{:S(2)}) copy-start(f32[1,1,16]{2,1,0:T(1,128)} %fusion.31) | copy-start | bytes 196
  179.6 99.3 %copy-start.10 = (f32[1,1,16]{2,1,0:T(1,128)S(1)}, f32[1,1,16]{2,1,0:T(1,128)}, u32[]{:S(2)}) copy-start(f32[1,1,16]{2,1,0:T(1,128)} %fusion.29) | copy-start | bytes 196
  274.0 4.9 %collective-permute-start.2 = (f32[1,2,16]{2,1,0:T(2,128)S(1)}, f32[1,2,16]{2,1,0:T(2,128)S(1)}, u32[]{:S(2)}, u32[]{:S(2)}) collective-permute-start(f32[1,2,16]{2,1,0:T(2,128)S(1)} %constant_dynamic-slice_fusion), channel_id=1, source_target_pairs={{0,192},{16,208},{32,224},{48,240},{64,0},{80,16},{96,32},{112,48}... | collective-permute-start | bytes 392 | tf_op jit(solution)/shard_map/ppermute | solution.py:14
where the time goes:
time: 280 us; the launch traced here: 279 us
  blocking collectives  220 us (79%)
  matrix products  26.5 us (9%)
  local copies, waits for them, and re-layouts  18.8 us (7%)
  other arithmetic  7.43 us (3%)
  waiting for transfers between devices  3.8 us (1%)
    unnamed x1, blocking collectives  87.1 us
    psum x1, blocking collectives, on_device(): sum_re, sum_im = lax.psum((part_re, part_im), ('grp', 'kin'))  73.7 us
    all_gather x1, blocking collectives, on_device(): lax.all_gather(waves, 'kin', axis=0, tiled=True)  35.3 us
    all_gather x1, blocking collectives, on_device(): lax.all_gather(coarse, 'kin', axis=0, tiled=True)  23.7 us
    mul x12, local copies, waits for them, and re-layouts, conj_products(): real_part = (left_re * right_re + left_im * right_im).astype(jnp.bfloat16)  15.6 us
    dot_general x2, matrix products, densities(): first = jnp.dot(stacked, basis[0], preferred_element_type=jnp.float32)  7.99 us
    dot_general x2, matrix products, densities(): second = jnp.dot(stacked, basis[1], preferred_element_type=jnp.float32)  5.95 us
  transfers between devices with their start and end apart: 3, of which 1 were waited for; matrix products, arithmetic and copies ran while one was open for 5% of the time, Pallas kernels for 0%

commit v1 on v0

v1 whole, which is shorter than its diff:
```python
import jax
import jax.numpy as jnp
from jax import lax
from jax.experimental import pallas as pl
from jax.experimental.pallas import tpu as pltpu
from jax.sharding import PartitionSpec as P

NV = 4
NC = 4
NT = 16
NMU = 1024
NG = 1536
WIDTH = NMU + 128
CHUNK = 256
PAIRS = 16
HALF = 2 * PAIRS * NT + NT
F32 = jnp.float32
BF16 = jnp.bfloat16


def move(value, rule):
    pairs = []
    for x in range(4):
        for z in range(4):
            for far in range(2):
                for y in range(4):
                    for core in range(2):
                        nx, nz, nfar, ny, ncore = rule(x, z, far, y, core)
                        source = (x * 4 + z) * 16 + far * 8 + y * 2 + core
                        target = (nx % 4 * 4 + nz) * 16 + nfar * 8 + ny * 2 + ncore
                        pairs.append((source, target))
    return lax.ppermute(value, ("grp", "kin"), pairs)


def flip(x=0, z=0, far=0, y=0, core=0, step=0):
    return lambda a, b, c, d, e: ((a + step) ^ x, b ^ z, c ^ far, d ^ y, e ^ core)


def iota(shape, dim):
    return lax.broadcasted_iota(jnp.int32, shape, dim)


def dot(left, right):
    return jnp.dot(left, right, preferred_element_type=F32)


def dot_t(left, right):
    return lax.dot_general(left, right, (((1,), (1,)), ((), ())), preferred_element_type=F32)


def split(value):
    high = value.astype(BF16)
    return high, (value - high.astype(F32)).astype(BF16)


def dot_split(left, right):
    high, low = split(left)
    return dot(high, right) + dot(low, right)


def onehot(condition):
    return jnp.where(condition, 1.0, 0.0).astype(BF16)


def spread(repeat):
    row = iota((64, 16), 0)
    col = iota((64, 16), 1)
    band = (row >> 2) & 3 if repeat else row & 3
    base = jnp.where(row < 32, 4, 0) + jnp.where((row >> 4) & 1 == 1, 8, 0)
    return onehot(col == band + base)


def transitions_kernel(b0, b1, b2, y_ref):
    total_re = jnp.zeros((1, NMU), F32)
    total_im = jnp.zeros((1, NMU), F32)
    for pay in (b0[...], b1[...], b2[0:16], b2[16:32]):
        waves = pay[:, :NMU]
        mixed = dot(pay[:, NMU : NMU + 16], waves)
        waves = waves.astype(F32)
        val_re, val_im = waves[0:4], waves[8:12]
        mix_re, mix_im = mixed[0:4], mixed[4:8]
        total_re += jnp.sum(val_re * mix_re + val_im * mix_im, 0, keepdims=True)
        total_im += jnp.sum(val_re * mix_im - val_im * mix_re, 0, keepdims=True)
    y_ref[...] = jnp.concatenate([total_re, total_im], 0)


def main_kernel(a0, a1, a2, a3, b0, b1, b2, w_ref, z_ref, out_ref, rx_ref, lhs, xa, xb, kre, kim, ca, cb, cc):
    step = pl.program_id(0)

    def put(row, left_re, left_im, right_re, right_im):
        real = left_re * right_re + left_im * right_im
        imag = left_re * right_im - left_im * right_re
        imag_bf = imag.astype(BF16)
        real_bf = real.astype(BF16)
        lhs[row : row + 16, 0:NMU] = real_bf
        lhs[row : row + 16, NMU : 2 * NMU] = -imag_bf
        lhs[HALF + row : HALF + row + 16, 0:NMU] = imag_bf
        lhs[HALF + row : HALF + row + 16, NMU : 2 * NMU] = real_bf

    @pl.when(step == 0)
    def _():
        rep = spread(True)
        til = spread(False)
        for m, pay in enumerate((a0, a1, a2, a3)):
            xa[m] = dot(rep, pay[:, 0:NMU])
        for n, pay in enumerate((b0[:, 0:NMU], b1[:, 0:NMU], b2[0:16, 0:NMU], b2[16:32, 0:NMU])):
            xb[n] = dot(til, pay)
        own = dot(til, a0[:, 0:NMU])
        for m in range(4):
            for n in range(4):
                row = (m * 4 + n) * 16
                put(row, xa[m, 0:16], xa[m, 16:32], xb[n, 0:16], xb[n, 16:32])
                put(256 + row, xa[m, 32:48], xa[m, 48:64], xb[n, 32:48], xb[n, 48:64])
        put(512, xa[0, 32:48], xa[0, 48:64], own[0:16], own[16:32])
        kre[...] = jnp.zeros_like(kre)
        kim[...] = jnp.zeros_like(kim)

    z = z_ref[...]
    weight = w_ref[...]
    con_re = dot(lhs[0:256], z)
    for p in range(PAIRS):
        ca[p * 16 : p * 16 + 16, 0:CHUNK] = (con_re[p * 16 : p * 16 + 16] * weight[p : p + 1]).astype(BF16)
    con_im = dot(lhs[HALF : HALF + 256], z)
    for p in range(PAIRS):
        ca[p * 16 : p * 16 + 16, CHUNK : 2 * CHUNK] = (con_im[p * 16 : p * 16 + 16] * weight[p : p + 1]).astype(BF16)
    val_re = dot(lhs[256:512], z).astype(BF16)
    cb[:, 0:CHUNK] = val_re
    cc[:, CHUNK : 2 * CHUNK] = -val_re
    val_im = dot(lhs[HALF + 256 : HALF + 512], z).astype(BF16)
    cb[:, CHUNK : 2 * CHUNK] = val_im
    cc[:, 0:CHUNK] = val_im
    rx_ref[0:16] = dot(lhs[512:528], z)
    rx_ref[16:32] = dot(lhs[HALF + 512 : HALF + 528], z)
    kre[...] += dot_t(ca[...], cb[...])
    kim[...] += dot_t(ca[...], cc[...])

    @pl.when(step == pl.num_programs(0) - 1)
    def _():
        pick_row = iota((8, 16), 0)
        pick_col = iota((8, 16), 1)
        xv_a = jnp.zeros((8, 128), F32)
        xv_b = jnp.zeros((8, 128), F32)
        for m, pay in enumerate((a0, a1, a2, a3)):
            xv_a += dot(onehot((pick_row == m) & (pick_col == 8)), pay[:, NMU:WIDTH])
        for n, pay in enumerate((b0[:, NMU:WIDTH], b1[:, NMU:WIDTH], b2[0:16, NMU:WIDTH], b2[16:32, NMU:WIDTH])):
            xv_b += dot(onehot((pick_row == n) & (pick_col == 8)), pay)
        row = iota((256, 8), 0)
        col = iota((256, 8), 1)
        of_a = onehot(row >> 6 == col)
        of_b = onehot((row >> 4) & 3 == col)
        row = iota((256, 128), 0)
        lane = iota((256, 128), 1)
        same_c = (lane & 3) == ((row >> 2) & 3)
        same_d = (lane & 3) == (row & 3)
        spread_a = jnp.where(same_c, dot(of_a, xv_a.astype(BF16)), 0.0).astype(BF16)
        spread_b = jnp.where(same_d, dot(of_b, xv_b.astype(BF16)), 0.0).astype(BF16)
        lane = iota((128, 256), 0)
        col = iota((128, 256), 1)
        by_w = (lane >> 2) & 3 == col & 3
        by_v = (lane >> 2) & 3 == (col >> 2) & 3
        first = lane < 16
        second = (lane >= 16) & (lane < 32)
        pair = (iota((256, 256), 0) >> 4) == (iota((256, 256), 1) >> 4)
        k_re = jnp.where(pair, kre[...], 0.0)
        k_im = jnp.where(pair, kim[...], 0.0)
        xd_re = dot(spread_b, onehot(by_w & first))
        xd_im = dot(spread_b, onehot(by_w & second))
        xh_re = dot(spread_a, onehot(by_v & first))
        xh_im = dot(spread_a, onehot(by_v & second))
        lane = iota((256, 128), 1)
        col = iota((256, 128), 0)
        by_w = (lane >> 2) & 3 == col & 3
        by_v = (lane >> 2) & 3 == (col >> 2) & 3
        first = lane < 16
        second = (lane >= 16) & (lane < 32)
        sum_d = dot_split(k_re * xd_re - k_im * xd_im, onehot(by_v & first)) + dot_split(
            k_re * xd_im + k_im * xd_re, onehot(by_v & second)
        )
        sum_h = dot_split(k_re * xh_re + k_im * xh_im, onehot(by_w & first)) + dot_split(
            k_re * xh_im - k_im * xh_re, onehot(by_w & second)
        )
        sum_d = jnp.where(same_c, sum_d, 0.0)
        sum_h = jnp.where(same_d, sum_h, 0.0)
        row = iota((8, 256), 0)
        col = iota((8, 256), 1)
        to_a = onehot(row == col >> 6)
        to_b = onehot(row == 4 + ((col >> 4) & 3))
        high_d, low_d = split(sum_d)
        high_h, low_h = split(sum_h)
        out_ref[...] = dot(to_a, high_d) + dot(to_a, low_d) + dot(to_b, high_h) + dot(to_b, low_h)


def exchange_kernel(y0, y1, y2, y3, c_ref, rx_ref, z_ref, out_ref, lhs, acc_re, acc_im):
    step = pl.program_id(0)

    @pl.when(step == 0)
    def _():
        total = y0[...] + y1[...] + y2[...] + y3[...]
        swap = jnp.concatenate([-total[1:2], total[0:1]], 0)
        high, low = split(jnp.concatenate([total, swap], 1))
        pad = jnp.zeros((12, 2 * NMU), F32)
        lhs[...] = jnp.concatenate([high.astype(F32), low.astype(F32), pad], 0).astype(BF16)
        acc_re[...] = jnp.zeros_like(acc_re)
        acc_im[...] = jnp.zeros_like(acc_im)

    total = dot(lhs[...], z_ref[...])
    pot_re = (total[0:1] + total[2:3]) * c_ref[...]
    pot_im = (total[1:2] + total[3:4]) * c_ref[...]
    rx_re = rx_ref[0:16]
    rx_im = rx_ref[16:32]
    real = rx_re * pot_re + rx_im * pot_im
    imag = rx_re * pot_im - rx_im * pot_re
    for at in range(0, CHUNK, 128):
        acc_re[...] += real[:, at : at + 128]
        acc_im[...] += imag[:, at : at + 128]

    @pl.when(step == pl.num_programs(0) - 1)
    def _():
        ones = jnp.ones((8, 128), BF16)
        out = []
        for acc in (acc_re[...], acc_im[...]):
            high, low = split(acc)
            out.append((dot_t(ones, high) + dot_t(ones, low))[0:1])
        out_ref[...] = jnp.concatenate(out, 0)


def whole(shape):
    return pl.BlockSpec(shape, lambda i: tuple(0 for _ in shape))


def pack(waves, vector):
    block = waves.reshape(16, NMU)
    coarse = vector.astype(BF16).reshape(2, NT)
    real = coarse[0].reshape(NV, NC)
    imag = coarse[1].reshape(NV, NC)
    gap = jnp.zeros((NV, NC), BF16)
    mixer = jnp.concatenate(
        [
            jnp.concatenate([gap, real, gap, -imag], 1),
            jnp.concatenate([gap, imag, gap, real], 1),
        ],
        0,
    )
    mixer = jnp.pad(mixer, ((0, 0), (0, 112)))
    line = jnp.pad(coarse.reshape(1, 32), ((0, 7), (0, 96)))
    return jnp.concatenate([block, jnp.concatenate([mixer, line], 0)], 1)


def pair_rows(qmap):
    own = lax.axis_index("grp")
    member = lax.axis_index("kin")
    partner = (own - 4) % 16
    row = qmap[0]
    from_a = jnp.stack([row[own * 16 + (member ^ (m << 1))] for m in range(4)])
    from_b = jnp.stack([row[partner * 16 + (member ^ n)] for n in (0, 8, 1, 9)])
    step_x = ((from_b >> 4)[None, :] - (from_a >> 4)[:, None]) & 15
    step_y = (from_b[None, :] - from_a[:, None]) & 15
    return (step_x * 16 + step_y).reshape(-1)


def on_device(waves, vector, energies, basis, screening, coulomb, qmap):
    pay = pack(waves, vector)
    b1 = move(pay, flip(step=1, far=1))
    b0 = move(pay, flip(step=1))
    b2 = move(jnp.concatenate([b0, b1], 0), flip(core=1))
    a2 = move(pay, flip(y=2))
    a1 = move(pay, flip(y=1))
    a3 = move(pay, flip(y=3))
    weights = jnp.take(screening, pair_rows(qmap), axis=0)
    stacked = basis.reshape(2 * NMU, NG)
    steps = NG // CHUNK

    y = pl.pallas_call(
        transitions_kernel,
        out_shape=jax.ShapeDtypeStruct((2, NMU), F32),
    )(b0, b1, b2)
    out, rx = pl.pallas_call(
        main_kernel,
        grid=(steps,),
        in_specs=[whole((16, WIDTH))] * 6
        + [
            whole((32, WIDTH)),
            pl.BlockSpec((PAIRS, CHUNK), lambda i: (0, i)),
            pl.BlockSpec((2 * NMU, CHUNK), lambda i: (0, i)),
        ],
        out_specs=[whole((8, 128)), pl.BlockSpec((32, CHUNK), lambda i: (0, i))],
        out_shape=[
            jax.ShapeDtypeStruct((8, 128), F32),
            jax.ShapeDtypeStruct((32, NG), F32),
        ],
        scratch_shapes=[
            pltpu.VMEM((2 * HALF, 2 * NMU), BF16),
            pltpu.VMEM((4, 64, NMU), F32),
            pltpu.VMEM((4, 64, NMU), F32),
            pltpu.VMEM((256, 256), F32),
            pltpu.VMEM((256, 256), F32),
            pltpu.VMEM((256, 2 * CHUNK), BF16),
            pltpu.VMEM((256, 2 * CHUNK), BF16),
            pltpu.VMEM((256, 2 * CHUNK), BF16),
        ],
        compiler_params=pltpu.CompilerParams(vmem_limit_bytes=32 * 1024 * 1024),
        cost_estimate=pl.CostEstimate(
            flops=2 * 2 * HALF * 2 * NMU * NG, bytes_accessed=4 * NMU * NG, transcendentals=0
        ),
    )(a0_of(pay), a1, a2, a3, b0, b1, b2, weights, stacked)

    for rules in (
        [flip(y=n) for n in (2, 1, 3)],
        [flip(x=n) for n in (2, 1, 3)],
    ):
        y = y + move(y, rules[0]) + move(y, rules[1]) + move(y, rules[2])
    others = [move(y, flip(z=n)) for n in (2, 1, 3)]
    exchange = pl.pallas_call(
        exchange_kernel,
        grid=(steps,),
        in_specs=[whole((2, NMU))] * 4
        + [
            pl.BlockSpec((1, CHUNK), lambda i: (0, i)),
            pl.BlockSpec((32, CHUNK), lambda i: (0, i)),
            pl.BlockSpec((2 * NMU, CHUNK), lambda i: (0, i)),
        ],
        out_specs=whole((2, 16)),
        out_shape=jax.ShapeDtypeStruct((2, 16), F32),
        scratch_shapes=[
            pltpu.VMEM((16, 2 * NMU), BF16),
            pltpu.VMEM((16, 128), F32),
            pltpu.VMEM((16, 128), F32),
        ],
        compiler_params=pltpu.CompilerParams(vmem_limit_bytes=32 * 1024 * 1024),
        cost_estimate=pl.CostEstimate(
            flops=2 * 16 * 2 * NMU * NG, bytes_accessed=4 * NMU * NG, transcendentals=0
        ),
    )(y, *others, coulomb.reshape(1, NG), rx, stacked)

    herm = out[4:6] + move(out[6:8], flip(core=1))
    terms = (
        out[0:1]
        + move(out[1:2], flip(y=1))
        + move(out[2:3], flip(y=2))
        + move(out[3:4], flip(y=3))
        + move(herm[0:1], flip(step=3))
        + move(herm[1:2], flip(step=3, far=1))
    )
    terms = terms[:, 0:32].reshape(1, 2, NT)
    scale = jnp.float32(1.0 / 256)
    return energies[:, None, :] * vector + 2.0 * scale * exchange[None] - scale * terms


def a0_of(pay):
    return pay


def solution(mesh):
    return jax.shard_map(
        on_device,
        mesh=mesh,
        in_specs=(
            P(("grp", "kin"), None, None, None),
            P(("grp", "kin"), None, None),
            P(("grp", "kin"), None),
            P(),
            P(),
            P(),
            P(("grp", "kin"), None),
        ),
        out_specs=P(("grp", "kin"), None, None),
        check_vma=False,
    )
```

time: 280 us -> 77.5 us (0.28)
  blocking collectives: 220 us -> 0 us
  starting transfers between devices: 2.66 us -> 33.7 us
  matrix products: 26.5 us -> 0 us
  Pallas kernels: 0 us -> 17.1 us
  local copies, waits for them, and re-layouts: 18.8 us -> 9.1 us
  waiting for transfers between devices: 3.8 us -> 7.97 us
    unnamed x1 -> x0, blocking collectives: 87.1 us -> none
    psum x1 -> x0, blocking collectives: 73.7 us -> none  [on_device(): sum_re, sum_im = lax.psum((part_re, part_im), ('grp', 'kin'))]
    all_gather x2 -> x0, blocking collectives: 58.9 us -> none  [the longest x1 35.3 us: on_device(): lax.all_gather(waves, 'kin', axis=0, tiled=True)]
    ppermute x3 -> x21, starting transfers between devices: 2.66 us -> 33.7 us  [move(): return lax.ppermute(value, ('grp', 'kin'), pairs)]
    dot_general x20 -> x0, matrix products: 26.5 us -> none  [the longest x2 7.99 us: densities(): first = jnp.dot(stacked, basis[0], preferred_element_type=jnp.float32)]
    pallas_call x0 -> x3, Pallas kernels: none -> 17.1 us  [the longest x1 13.1 us: on_device(): pl.pallas_call(main_kernel, grid=(steps,), in_specs=[whole((16, WIDTH))]...]
    mul x22 -> x1, local copies, waits for them, and re-layouts: 15.8 us -> 0.08 us  [on_device(): scale * terms]
    shift_right_arithmetic x0 -> x1, other arithmetic: none -> 5.15 us  [pair_rows(): step_x = (from_b >> 4)[None, :] - (from_a >> 4)[:, None] & 15]
  transfers between devices with their start and end apart: 3 -> 21, of which waited for: 1 -> 6; matrix products, arithmetic and copies ran while one was open for 5% -> 12% of each run, Pallas kernels for 0% -> 2%
where the time goes in v1:
time: 77.5 us; the launch traced here: 76.4 us
  starting transfers between devices  33.7 us (43%)
  Pallas kernels  17.1 us (22%)
  local copies, waits for them, and re-layouts  9.1 us (12%)
  other arithmetic  8.31 us (11%)
  waiting for transfers between devices  7.97 us (10%)
    ppermute x21, starting transfers between devices, move(): return lax.ppermute(value, ('grp', 'kin'), pairs)  33.7 us
    pallas_call x1, Pallas kernels, on_device(): pl.pallas_call(main_kernel, grid=(steps,), in_specs=[whole((16, WIDTH))]...  13.1 us
    ppermute x21, waiting for transfers between devices, move(): return lax.ppermute(value, ('grp', 'kin'), pairs)  7.97 us
    unnamed x16, local copies, waits for them, and re-layouts  5.62 us
    shift_right_arithmetic x1, other arithmetic, pair_rows(): step_x = (from_b >> 4)[None, :] - (from_a >> 4)[:, None] & 15  5.15 us
    pallas_call x1, Pallas kernels, on_device(): pl.pallas_call(exchange_kernel, grid=(steps,), in_specs=[whole((2, NMU))]...  2.23 us
    pallas_call x1, Pallas kernels, on_device(): pl.pallas_call(transitions_kernel, out_shape=jax.ShapeDtypeStruct((2, NMU...  1.76 us
    dynamic_slice x1, local copies, waits for them, and re-layouts, pair_rows(): from_b = jnp.stack([row[partner * 16 + (member ^ n)] for n in (0, 8, 1, 9)])  1.64 us
  transfers between devices with their start and end apart: 21, of which 6 were waited for; matrix products, arithmetic and copies ran while one was open for 12% of the time, Pallas kernels for 2%

profile of v1, /device:TPU:6, one launch (start us, length us, event | category | flops | bytes accessed | tf_op | source)
XLA Modules:
  0.0 76.4 jit_solution(13436419361009831259)
XLA Ops:
  0.0 0.8 %convert_element_type.7 = bf16[1,2,16]{2,1,0:T(2,128)(2,1)S(1)} convert(f32[1,2,16]{2,1,0:T(2,128)} %param.8) | non-fusion elementwise | flops 32 | bytes 192 | tf_op jit(solution)/shard_map/convert_element_type | solution.py:233
  0.8 0.1 reshape_reshape.3
  0.9 0.1 reshape_squeeze.6
  1.0 0.1 reshape_squeeze.7
  1.1 0.1 fusion.16
  1.2 0.8 %fusion.4.a0 = bf16[16,1152]{1,0:T(8,128)(2,1)S(1)} fusion(bf16[1,32]{1,0:T(2,128)(2,1)S(1)} %reshape_reshape.3, bf16[8,128]{1,0:T(8,128)(2,1)S(1)} %fusion.16, bf16[16,1024]{1,0:T(8,128)(2,1)} %bitcast.19), kind=kLoop, calls=%fused_computation.9 | loop fusion | flops 202752 | bytes 71744 | tf_op jit(solution)/shard_map/concatenate | solution.py:246
  2.0 1.6 %collective-permute-start.12 = (bf16[16,1152]{1,0:T(8,128)(2,1)S(1)}, bf16[16,1152]{1,0:T(8,128)(2,1)S(1)}, u32[]{:S(2)}, u32[]{:S(2)}) collective-permute-start(bf16[16,1152]{1,0:T(8,128)(2,1)S(1)} %fusion.4.a0), channel_id=1, source_target_pairs={{0,2},{1,3},{2,0},{3,1},{4,6},{5,7},{6,4},{7,5},{8,10},{9,11},{10,... | collective-permute-start | bytes 110600 | tf_op jit(solution)/shard_map/ppermute | solution.py:32
  3.5 2.9 %collective-permute-start.13 = (bf16[16,1152]{1,0:T(8,128)(2,1)S(1)}, bf16[16,1152]{1,0:T(8,128)(2,1)S(1)}, u32[]{:S(2)}, u32[]{:S(2)}) collective-permute-start(bf16[16,1152]{1,0:T(8,128)(2,1)S(1)} %fusion.4.a0), channel_id=1, source_target_pairs={{0,4},{1,5},{2,6},{3,7},{4,0},{5,1},{6,2},{7,3},{8,12},{9,13},{10,... | collective-permute-start | bytes 110600 | tf_op jit(solution)/shard_map/ppermute | solution.py:32
  6.4 0.2 collective-permute-start.14
  6.7 2.2 %collective-permute-start = (bf16[16,1152]{1,0:T(8,128)(2,1)S(1)}, bf16[16,1152]{1,0:T(8,128)(2,1)S(1)}, u32[]{:S(2)}, u32[]{:S(2)}) collective-permute-start(bf16[16,1152]{1,0:T(8,128)(2,1)S(1)} %fusion.4.a0), channel_id=1, source_target_pairs={{0,64},{1,65},{2,66},{3,67},{4,68},{5,69},{6,70},{7,71},{8,72},{9,... | collective-permute-start | bytes 110600 | tf_op jit(solution)/shard_map/ppermute | solution.py:32
  8.9 6.4 %collective-permute-start.1 = (bf16[16,1152]{1,0:T(8,128)(2,1)S(1)}, bf16[16,1152]{1,0:T(8,128)(2,1)S(1)}, u32[]{:S(2)}, u32[]{:S(2)}) collective-permute-start(bf16[16,1152]{1,0:T(8,128)(2,1)S(1)} %fusion.4.a0), channel_id=1, source_target_pairs={{0,72},{1,73},{2,74},{3,75},{4,76},{5,77},{6,78},{7,79},{8,64},{9,... | collective-permute-start | bytes 110600 | tf_op jit(solution)/shard_map/ppermute | solution.py:32
  15.2 1.6 %constant_dynamic-slice_fusion.7 = (s32[1,1]{1,0:T(1,128)}, s32[1,1]{1,0:T(1,128)}, s32[1,1]{1,0:T(1,128)}, s32[1,1]{1,0:T(1,128)}, s32[1,1]{1,0:T(1,128)}, /*in...) fusion(s32[1,256]{1,0:T(1,128)} %param.13, s32[]{:T(128)S(6)} %select_n.52, s32[]{:T(128)S(6)} %select_n.57, ...), kind=kLoop, calls=%fused_computation.39 | loop fusion | bytes 96 | tf_op jit(solution)/shard_map/dynamic_slice | solution.py:255
  16.9 5.1 %broadcast_shift-right-arithmetic_fusion = (s32[4]{0:T(128)S(1)}, s32[4]{0:T(128)S(1)}, s32[4]{0:T(128)S(1)}, s32[4]{0:T(128)S(1)}) fusion(s32[1]{0:T(128)} %bitcast.9, s32[1]{0:T(128)} %bitcast.8, s32[1]{0:T(128)} %bitcast.7, s32[1]{0:T(128)} %bitcast.6, s32[1]{0:T(128)} %bitcast.5, s32[1]{0:T(128)} %bitcast.4, s32[1]{0:T(128)} %bitcast.3, s32[1]{0:T(128)} %bitcast.2), kind=kLoop, calls=%fused_computation.51 | loop fusion | flops 32 | bytes 96 | tf_op jit(solution)/shard_map/shift_right_arithmetic | solution.py:256
  22.0 0.1 and_add_fusion
  22.1 0.1 add.156
  22.2 0.1 add.154
  22.3 0.6 gather_fusion
  22.9 0.0 collective-permute-done.1.b1
  23.0 0.1 collective-permute-start.2
  23.1 0.1 broadcast_select_fusion.w_ref
  23.2 0.7 reshape.192.c_ref
  23.9 0.5 collective-permute-done.2.b2
  24.3 2.8 %copy-done.1 = bf16[2,1024,1536]{2,1,0:T(8,128)(2,1)S(1)} copy-done((bf16[2,1024,1536]{2,1,0:T(8,128)(2,1)S(1)}, bf16[2,1024,1536]{2,1,0:T(8,128)(2,1)}, u32[]{:S(2)}) %copy-start.1) | copy-done | bytes 6291480
  27.1 13.1 %shard_map.74 = (f32[8,128]{1,0:T(8,128)S(1)}, f32[32,1536]{1,0:T(8,128)S(1)}) custom-call(bf16[16,1152]{1,0:T(8,128)(2,1)S(1)} %fusion.4.a0, bf16[16,1152]{1,0:T(8,128)(2,1)S(1)} %collective-permute-done.12.a1, bf16[16,1152]{1,0:T(8,128)(2,1)S(1)} %collective-permute-done.13.a2, bf16[16,1152]{1,0:T(8,128)(2,1)S(1)} %collective-permute-done.14.a3, ...), custom_call_target="tpu_custom_call" | custom-call | flops 6643777536 | bytes 6291456 | tf_op jit(solution)/shard_map/pallas_call | solution.py:277
  40.3 0.0 copy-done.3
  40.3 0.2 collective-permute-start.18
  40.5 1.8 %shard_map.73 = f32[2,1024]{1,0:T(2,128)} custom-call(bf16[16,1152]{1,0:T(8,128)(2,1)} %copy-done.3, bf16[16,1152]{1,0:T(8,128)(2,1)} %copy-done.4, bf16[32,1152]{1,0:T(8,128)(2,1)} %copy-done.5), custom_call_target="tpu_custom_call" | custom-call | tf_op jit(solution)/shard_map/pallas_call | solution.py:273
  42.3 3.0 %collective-permute-start.5 = (f32[2,1024]{1,0:T(2,128)}, f32[2,1024]{1,0:T(2,128)S(1)}, u32[]{:S(2)}, u32[]{:S(2)}) collective-permute-start(f32[2,1024]{1,0:T(2,128)} %shard_map.73), channel_id=1, source_target_pairs={{0,6},{1,7},{2,4},{3,5},{4,2},{5,3},{6,0},{7,1},{8,14},{9,15},{10,... | collective-permute-start | bytes 24584 | tf_op jit(solution)/shard_map/ppermute | solution.py:32
  45.3 1.7 %collective-permute-start.3 = (f32[2,1024]{1,0:T(2,128)}, f32[2,1024]{1,0:T(2,128)S(1)}, u32[]{:S(2)}, u32[]{:S(2)}) collective-permute-start(f32[2,1024]{1,0:T(2,128)} %shard_map.73), channel_id=1, source_target_pairs={{0,4},{1,5},{2,6},{3,7},{4,0},{5,1},{6,2},{7,3},{8,12},{9,13},{10,... | collective-permute-start | bytes 24584 | tf_op jit(solution)/shard_map/ppermute | solution.py:32
  47.0 3.0 %collective-permute-start.17 = (f32[1,128]{1,0:T(1,128)S(1)}, f32[1,128]{1,0:T(1,128)S(1)}, u32[]{:S(2)}, u32[]{:S(2)}) collective-permute-start(f32[1,128]{1,0:T(1,128)S(1)} %get-tuple-element.16), channel_id=1, source_target_pairs={{0,6},{1,7},{2,4},{3,5},{4,2},{5,3},{6,0},{7,1},{8,14},{9,15},{10,... | collective-permute-start | bytes 1544 | tf_op jit(solution)/shard_map/ppermute | solution.py:32
  50.1 1.1 %collective-permute-start.15 = (f32[1,128]{1,0:T(1,128)S(1)}, f32[1,128]{1,0:T(1,128)S(1)}, u32[]{:S(2)}, u32[]{:S(2)}) collective-permute-start(f32[1,128]{1,0:T(1,128)S(1)} %get-tuple-element.15), channel_id=1, source_target_pairs={{0,2},{1,3},{2,0},{3,1},{4,6},{5,7},{6,4},{7,5},{8,10},{9,11},{10,... | collective-permute-start | bytes 1544 | tf_op jit(solution)/shard_map/ppermute | solution.py:32
  51.2 1.1 %collective-permute-start.20 = (f32[1,128]{1,0:T(1,128)S(1)}, f32[1,128]{1,0:T(1,128)S(1)}, u32[]{:S(2)}, u32[]{:S(2)}) collective-permute-start(f32[1,128]{1,0:T(1,128)S(1)} %get-tuple-element.19), channel_id=1, source_target_pairs={{0,200},{1,201},{2,202},{3,203},{4,204},{5,205},{6,206},{7,207},{8... | collective-permute-start | bytes 1544 | tf_op jit(solution)/shard_map/ppermute | solution.py:32
  52.3 0.8 %collective-permute-start.19 = (f32[1,128]{1,0:T(1,128)S(1)}, f32[1,128]{1,0:T(1,128)S(1)}, u32[]{:S(2)}, u32[]{:S(2)}) collective-permute-start(f32[1,128]{1,0:T(1,128)S(1)} %get-tuple-element.18), channel_id=1, source_target_pairs={{0,192},{1,193},{2,194},{3,195},{4,196},{5,197},{6,198},{7,199},{8... | collective-permute-start | bytes 1544 | tf_op jit(solution)/shard_map/ppermute | solution.py:32
  53.1 0.7 add_add_fusion.1
  53.9 2.5 %collective-permute-start.8 = (f32[2,1024]{1,0:T(2,128)S(1)}, f32[2,1024]{1,0:T(2,128)S(1)}, u32[]{:S(2)}, u32[]{:S(2)}) collective-permute-start(f32[2,1024]{1,0:T(2,128)S(1)} %add_add_fusion.1), channel_id=1, source_target_pairs={{0,192},{1,193},{2,194},{3,195},{4,196},{5,197},{6,198},{7,199},{8... | collective-permute-start | bytes 24584 | tf_op jit(solution)/shard_map/ppermute | solution.py:32
  56.4 2.3 %collective-permute-start.6 = (f32[2,1024]{1,0:T(2,128)S(1)}, f32[2,1024]{1,0:T(2,128)S(1)}, u32[]{:S(2)}, u32[]{:S(2)}) collective-permute-start(f32[2,1024]{1,0:T(2,128)S(1)} %add_add_fusion.1), channel_id=1, source_target_pairs={{0,128},{1,129},{2,130},{3,131},{4,132},{5,133},{6,134},{7,135},{8... | collective-permute-start | bytes 24584 | tf_op jit(solution)/shard_map/ppermute | solution.py:32
  58.7 2.1 %collective-permute-done.20 = f32[1,128]{1,0:T(1,128)S(1)} collective-permute-done((f32[1,128]{1,0:T(1,128)S(1)}, f32[1,128]{1,0:T(1,128)S(1)}, u32[]{:S(2)}, u32[]{:S(2)}) %collective-permute-start.20) | collective-permute-done | bytes 544 | tf_op jit(solution)/shard_map/ppermute | solution.py:32
  60.8 0.8 %collective-permute-done.6 = f32[2,1024]{1,0:T(2,128)S(1)} collective-permute-done((f32[2,1024]{1,0:T(2,128)S(1)}, f32[2,1024]{1,0:T(2,128)S(1)}, u32[]{:S(2)}, u32[]{:S(2)}) %collective-permute-start.6) | collective-permute-done | bytes 8224 | tf_op jit(solution)/shard_map/ppermute | solution.py:32
  61.6 1.8 %collective-permute-start.9 = (f32[2,1024]{1,0:T(2,128)S(1)}, f32[2,1024]{1,0:T(2,128)S(1)}, u32[]{:S(2)}, u32[]{:S(2)}) collective-permute-start(f32[2,1024]{1,0:T(2,128)S(1)} %add_add_fusion.y0), channel_id=1, source_target_pairs={{0,32},{1,33},{2,34},{3,35},{4,36},{5,37},{6,38},{7,39},{8,40},{9,... | collective-permute-start | bytes 24584 | tf_op jit(solution)/shard_map/ppermute | solution.py:32
  63.4 1.9 %collective-permute-start.10 = (f32[2,1024]{1,0:T(2,128)S(1)}, f32[2,1024]{1,0:T(2,128)S(1)}, u32[]{:S(2)}, u32[]{:S(2)}) collective-permute-start(f32[2,1024]{1,0:T(2,128)S(1)} %add_add_fusion.y0), channel_id=1, source_target_pairs={{0,16},{1,17},{2,18},{3,19},{4,20},{5,21},{6,22},{7,23},{8,24},{9,... | collective-permute-start | bytes 24584 | tf_op jit(solution)/shard_map/ppermute | solution.py:32
  65.3 0.8 %collective-permute-start.11 = (f32[2,1024]{1,0:T(2,128)S(1)}, f32[2,1024]{1,0:T(2,128)S(1)}, u32[]{:S(2)}, u32[]{:S(2)}) collective-permute-start(f32[2,1024]{1,0:T(2,128)S(1)} %add_add_fusion.y0), channel_id=1, source_target_pairs={{0,48},{1,49},{2,50},{3,51},{4,52},{5,53},{6,54},{7,55},{8,56},{9,... | collective-permute-start | bytes 24584 | tf_op jit(solution)/shard_map/ppermute | solution.py:32
  66.1 0.1 mul.74
  66.2 0.1 collective-permute-done.9.y1
  66.3 0.8 %collective-permute-done.10.y2 = f32[2,1024]{1,0:T(2,128)S(1)} collective-permute-done((f32[2,1024]{1,0:T(2,128)S(1)}, f32[2,1024]{1,0:T(2,128)S(1)}, u32[]{:S(2)}, u32[]{:S(2)}) %collective-permute-start.10) | collective-permute-done | bytes 8224 | tf_op jit(solution)/shard_map/ppermute | solution.py:32
  67.1 3.7 %collective-permute-done.11.y3 = f32[2,1024]{1,0:T(2,128)S(1)} collective-permute-done((f32[2,1024]{1,0:T(2,128)S(1)}, f32[2,1024]{1,0:T(2,128)S(1)}, u32[]{:S(2)}, u32[]{:S(2)}) %collective-permute-start.11) | collective-permute-done | bytes 8224 | tf_op jit(solution)/shard_map/ppermute | solution.py:32
  70.8 2.8 %copy-done.2 = bf16[2,1024,1536]{2,1,0:T(8,128)(2,1)S(1)} copy-done((bf16[2,1024,1536]{2,1,0:T(8,128)(2,1)S(1)}, bf16[2,1024,1536]{2,1,0:T(8,128)(2,1)}, u32[]{:S(2)}) %copy-start.2) | copy-done | bytes 6291480
  73.6 2.2 %shard_map.75 = f32[2,16]{1,0:T(2,128)S(1)} custom-call(f32[2,1024]{1,0:T(2,128)S(1)} %add_add_fusion.y0, f32[2,1024]{1,0:T(2,128)S(1)} %collective-permute-done.9.y1, f32[2,1024]{1,0:T(2,128)S(1)} %collective-permute-done.10.y2, f32[2,1024]{1,0:T(2,128)S(1)} %collective-permute-done.11.y3, f32[1,1536]{1,0:T(1,128)S(1)} %reshape.192.c_ref, ...), custom_call_target="tpu_custom_call" | custom-call | flops 100663296 | bytes 6291456 | tf_op jit(solution)/shard_map/pallas_call | solution.py:313
  75.8 0.6 fusion.20
  (44 shorter events, 0.2 us)
Async XLA Ops:
  0.0 22.3 %copy-start = (f32[256,1536]{1,0:T(8,128)S(1)}, f32[256,1536]{1,0:T(8,128)}, u32[]{:S(2)}) copy-start(f32[256,1536]{1,0:T(8,128)} %param.11) | copy-start | bytes 4718596
  2.0 21.9 %collective-permute-start.12 = (bf16[16,1152]{1,0:T(8,128)(2,1)S(1)}, bf16[16,1152]{1,0:T(8,128)(2,1)S(1)}, u32[]{:S(2)}, u32[]{:S(2)}) collective-permute-start(bf16[16,1152]{1,0:T(8,128)(2,1)S(1)} %fusion.4.a0), channel_id=1, source_target_pairs={{0,2},{1,3},{2,0},{3,1},{4,6},{5,7},{6,4},{7,5},{8,10},{9,11},{10,... | collective-permute-start | bytes 110600 | tf_op jit(solution)/shard_map/ppermute | solution.py:32
  3.5 20.3 %collective-permute-start.13 = (bf16[16,1152]{1,0:T(8,128)(2,1)S(1)}, bf16[16,1152]{1,0:T(8,128)(2,1)S(1)}, u32[]{:S(2)}, u32[]{:S(2)}) collective-permute-start(bf16[16,1152]{1,0:T(8,128)(2,1)S(1)} %fusion.4.a0), channel_id=1, source_target_pairs={{0,4},{1,5},{2,6},{3,7},{4,0},{5,1},{6,2},{7,3},{8,12},{9,13},{10,... | collective-permute-start | bytes 110600 | tf_op jit(solution)/shard_map/ppermute | solution.py:32
  6.4 17.4 %collective-permute-start.14 = (bf16[16,1152]{1,0:T(8,128)(2,1)S(1)}, bf16[16,1152]{1,0:T(8,128)(2,1)S(1)}, u32[]{:S(2)}, u32[]{:S(2)}) collective-permute-start(bf16[16,1152]{1,0:T(8,128)(2,1)S(1)} %fusion.4.a0), channel_id=1, source_target_pairs={{0,6},{1,7},{2,4},{3,5},{4,2},{5,3},{6,0},{7,1},{8,14},{9,15},{10,... | collective-permute-start | bytes 110600 | tf_op jit(solution)/shard_map/ppermute | solution.py:32
  6.7 16.3 %collective-permute-start = (bf16[16,1152]{1,0:T(8,128)(2,1)S(1)}, bf16[16,1152]{1,0:T(8,128)(2,1)S(1)}, u32[]{:S(2)}, u32[]{:S(2)}) collective-permute-start(bf16[16,1152]{1,0:T(8,128)(2,1)S(1)} %fusion.4.a0), channel_id=1, source_target_pairs={{0,64},{1,65},{2,66},{3,67},{4,68},{5,69},{6,70},{7,71},{8,72},{9,... | collective-permute-start | bytes 110600 | tf_op jit(solution)/shard_map/ppermute | solution.py:32
  8.9 14.1 %collective-permute-start.1 = (bf16[16,1152]{1,0:T(8,128)(2,1)S(1)}, bf16[16,1152]{1,0:T(8,128)(2,1)S(1)}, u32[]{:S(2)}, u32[]{:S(2)}) collective-permute-start(bf16[16,1152]{1,0:T(8,128)(2,1)S(1)} %fusion.4.a0), channel_id=1, source_target_pairs={{0,72},{1,73},{2,74},{3,75},{4,76},{5,77},{6,78},{7,79},{8,64},{9,... | collective-permute-start | bytes 110600 | tf_op jit(solution)/shard_map/ppermute | solution.py:32
  22.9 17.3 %copy-start.3 = (bf16[16,1152]{1,0:T(8,128)(2,1)}, bf16[16,1152]{1,0:T(8,128)(2,1)S(1)}, u32[]{:S(2)}) copy-start(bf16[16,1152]{1,0:T(8,128)(2,1)S(1)} %collective-permute-done.b0) | copy-start | bytes 110596
  22.9 17.3 %copy-start.4 = (bf16[16,1152]{1,0:T(8,128)(2,1)}, bf16[16,1152]{1,0:T(8,128)(2,1)S(1)}, u32[]{:S(2)}) copy-start(bf16[16,1152]{1,0:T(8,128)(2,1)S(1)} %collective-permute-done.1.b1) | copy-start | bytes 110596
  23.0 1.4 %collective-permute-start.2 = (bf16[32,1152]{1,0:T(8,128)(2,1)S(1)}, bf16[32,1152]{1,0:T(8,128)(2,1)S(1)}, u32[]{:S(2)}, u32[]{:S(2)}) collective-permute-start(bf16[32,1152]{1,0:T(8,128)(2,1)S(1)} %pad_maximum_fusion), channel_id=1, source_target_pairs={{0,1},{1,0},{2,3},{3,2},{4,5},{5,4},{6,7},{7,6},{8,9},{9,8},{10,11... | collective-permute-start | bytes 221192 | tf_op jit(solution)/shard_map/ppermute | solution.py:32
  24.3 16.0 %copy-start.5 = (bf16[32,1152]{1,0:T(8,128)(2,1)}, bf16[32,1152]{1,0:T(8,128)(2,1)S(1)}, u32[]{:S(2)}) copy-start(bf16[32,1152]{1,0:T(8,128)(2,1)S(1)} %collective-permute-done.2.b2) | copy-start | bytes 221188
  24.3 2.8 %copy-start.1 = (bf16[2,1024,1536]{2,1,0:T(8,128)(2,1)S(1)}, bf16[2,1024,1536]{2,1,0:T(8,128)(2,1)}, u32[]{:S(2)}) copy-start(bf16[2,1024,1536]{2,1,0:T(8,128)(2,1)} %param.10) | copy-start | bytes 18874372
  40.3 9.7 %collective-permute-start.18 = (f32[2,128]{1,0:T(2,128)S(1)}, f32[2,128]{1,0:T(2,128)S(1)}, u32[]{:S(2)}, u32[]{:S(2)}) collective-permute-start(f32[2,128]{1,0:T(2,128)S(1)} %slice.42), channel_id=1, source_target_pairs={{0,1},{1,0},{2,3},{3,2},{4,5},{5,4},{6,7},{7,6},{8,9},{9,8},{10,11... | collective-permute-start | bytes 3080 | tf_op jit(solution)/shard_map/ppermute | solution.py:32
  42.3 7.7 %collective-permute-start.5 = (f32[2,1024]{1,0:T(2,128)}, f32[2,1024]{1,0:T(2,128)S(1)}, u32[]{:S(2)}, u32[]{:S(2)}) collective-permute-start(f32[2,1024]{1,0:T(2,128)} %shard_map.73), channel_id=1, source_target_pairs={{0,6},{1,7},{2,4},{3,5},{4,2},{5,3},{6,0},{7,1},{8,14},{9,15},{10,... | collective-permute-start | bytes 24584 | tf_op jit(solution)/shard_map/ppermute | solution.py:32
  45.3 5.9 %collective-permute-start.4 = (f32[2,1024]{1,0:T(2,128)}, f32[2,1024]{1,0:T(2,128)S(1)}, u32[]{:S(2)}, u32[]{:S(2)}) collective-permute-start(f32[2,1024]{1,0:T(2,128)} %shard_map.73), channel_id=1, source_target_pairs={{0,2},{1,3},{2,0},{3,1},{4,6},{5,7},{6,4},{7,5},{8,10},{9,11},{10,... | collective-permute-start | bytes 24584 | tf_op jit(solution)/shard_map/ppermute | solution.py:32
  45.3 7.0 %collective-permute-start.3 = (f32[2,1024]{1,0:T(2,128)}, f32[2,1024]{1,0:T(2,128)S(1)}, u32[]{:S(2)}, u32[]{:S(2)}) collective-permute-start(f32[2,1024]{1,0:T(2,128)} %shard_map.73), channel_id=1, source_target_pairs={{0,4},{1,5},{2,6},{3,7},{4,0},{5,1},{6,2},{7,3},{8,12},{9,13},{10,... | collective-permute-start | bytes 24584 | tf_op jit(solution)/shard_map/ppermute | solution.py:32
  47.0 6.8 %collective-permute-start.17 = (f32[1,128]{1,0:T(1,128)S(1)}, f32[1,128]{1,0:T(1,128)S(1)}, u32[]{:S(2)}, u32[]{:S(2)}) collective-permute-start(f32[1,128]{1,0:T(1,128)S(1)} %get-tuple-element.16), channel_id=1, source_target_pairs={{0,6},{1,7},{2,4},{3,5},{4,2},{5,3},{6,0},{7,1},{8,14},{9,15},{10,... | collective-permute-start | bytes 1544 | tf_op jit(solution)/shard_map/ppermute | solution.py:32
  50.0 6.3 %collective-permute-start.16 = (f32[1,128]{1,0:T(1,128)S(1)}, f32[1,128]{1,0:T(1,128)S(1)}, u32[]{:S(2)}, u32[]{:S(2)}) collective-permute-start(f32[1,128]{1,0:T(1,128)S(1)} %get-tuple-element.17), channel_id=1, source_target_pairs={{0,4},{1,5},{2,6},{3,7},{4,0},{5,1},{6,2},{7,3},{8,12},{9,13},{10,... | collective-permute-start | bytes 1544 | tf_op jit(solution)/shard_map/ppermute | solution.py:32
  50.1 6.3 %collective-permute-start.15 = (f32[1,128]{1,0:T(1,128)S(1)}, f32[1,128]{1,0:T(1,128)S(1)}, u32[]{:S(2)}, u32[]{:S(2)}) collective-permute-start(f32[1,128]{1,0:T(1,128)S(1)} %get-tuple-element.15), channel_id=1, source_target_pairs={{0,2},{1,3},{2,0},{3,1},{4,6},{5,7},{6,4},{7,5},{8,10},{9,11},{10,... | collective-permute-start | bytes 1544 | tf_op jit(solution)/shard_map/ppermute | solution.py:32
  51.2 9.6 %collective-permute-start.20 = (f32[1,128]{1,0:T(1,128)S(1)}, f32[1,128]{1,0:T(1,128)S(1)}, u32[]{:S(2)}, u32[]{:S(2)}) collective-permute-start(f32[1,128]{1,0:T(1,128)S(1)} %get-tuple-element.19), channel_id=1, source_target_pairs={{0,200},{1,201},{2,202},{3,203},{4,204},{5,205},{6,206},{7,207},{8... | collective-permute-start | bytes 1544 | tf_op jit(solution)/shard_map/ppermute | solution.py:32
  52.3 8.4 %collective-permute-start.19 = (f32[1,128]{1,0:T(1,128)S(1)}, f32[1,128]{1,0:T(1,128)S(1)}, u32[]{:S(2)}, u32[]{:S(2)}) collective-permute-start(f32[1,128]{1,0:T(1,128)S(1)} %get-tuple-element.18), channel_id=1, source_target_pairs={{0,192},{1,193},{2,194},{3,195},{4,196},{5,197},{6,198},{7,199},{8... | collective-permute-start | bytes 1544 | tf_op jit(solution)/shard_map/ppermute | solution.py:32
  53.9 6.9 %collective-permute-start.8 = (f32[2,1024]{1,0:T(2,128)S(1)}, f32[2,1024]{1,0:T(2,128)S(1)}, u32[]{:S(2)}, u32[]{:S(2)}) collective-permute-start(f32[2,1024]{1,0:T(2,128)S(1)} %add_add_fusion.1), channel_id=1, source_target_pairs={{0,192},{1,193},{2,194},{3,195},{4,196},{5,197},{6,198},{7,199},{8... | collective-permute-start | bytes 24584 | tf_op jit(solution)/shard_map/ppermute | solution.py:32
  56.4 4.4 %collective-permute-start.7 = (f32[2,1024]{1,0:T(2,128)S(1)}, f32[2,1024]{1,0:T(2,128)S(1)}, u32[]{:S(2)}, u32[]{:S(2)}) collective-permute-start(f32[2,1024]{1,0:T(2,128)S(1)} %add_add_fusion.1), channel_id=1, source_target_pairs={{0,64},{1,65},{2,66},{3,67},{4,68},{5,69},{6,70},{7,71},{8,72},{9,... | collective-permute-start | bytes 24584 | tf_op jit(solution)/shard_map/ppermute | solution.py:32
  56.4 5.2 %collective-permute-start.6 = (f32[2,1024]{1,0:T(2,128)S(1)}, f32[2,1024]{1,0:T(2,128)S(1)}, u32[]{:S(2)}, u32[]{:S(2)}) collective-permute-start(f32[2,1024]{1,0:T(2,128)S(1)} %add_add_fusion.1), channel_id=1, source_target_pairs={{0,128},{1,129},{2,130},{3,131},{4,132},{5,133},{6,134},{7,135},{8... | collective-permute-start | bytes 24584 | tf_op jit(solution)/shard_map/ppermute | solution.py:32
  61.6 4.6 %collective-permute-start.9 = (f32[2,1024]{1,0:T(2,128)S(1)}, f32[2,1024]{1,0:T(2,128)S(1)}, u32[]{:S(2)}, u32[]{:S(2)}) collective-permute-start(f32[2,1024]{1,0:T(2,128)S(1)} %add_add_fusion.y0), channel_id=1, source_target_pairs={{0,32},{1,33},{2,34},{3,35},{4,36},{5,37},{6,38},{7,39},{8,40},{9,... | collective-permute-start | bytes 24584 | tf_op jit(solution)/shard_map/ppermute | solution.py:32
  63.4 3.7 %collective-permute-start.10 = (f32[2,1024]{1,0:T(2,128)S(1)}, f32[2,1024]{1,0:T(2,128)S(1)}, u32[]{:S(2)}, u32[]{:S(2)}) collective-permute-start(f32[2,1024]{1,0:T(2,128)S(1)} %add_add_fusion.y0), channel_id=1, source_target_pairs={{0,16},{1,17},{2,18},{3,19},{4,20},{5,21},{6,22},{7,23},{8,24},{9,... | collective-permute-start | bytes 24584 | tf_op jit(solution)/shard_map/ppermute | solution.py:32
  65.3 5.4 %collective-permute-start.11 = (f32[2,1024]{1,0:T(2,128)S(1)}, f32[2,1024]{1,0:T(2,128)S(1)}, u32[]{:S(2)}, u32[]{:S(2)}) collective-permute-start(f32[2,1024]{1,0:T(2,128)S(1)} %add_add_fusion.y0), channel_id=1, source_target_pairs={{0,48},{1,49},{2,50},{3,51},{4,52},{5,53},{6,54},{7,55},{8,56},{9,... | collective-permute-start | bytes 24584 | tf_op jit(solution)/shard_map/ppermute | solution.py:32
  70.8 2.8 %copy-start.2 = (bf16[2,1024,1536]{2,1,0:T(8,128)(2,1)S(1)}, bf16[2,1024,1536]{2,1,0:T(8,128)(2,1)}, u32[]{:S(2)}) copy-start(bf16[2,1024,1536]{2,1,0:T(8,128)(2,1)} %param.10) | copy-start | bytes 18874372
  73.5 2.2 %copy-start.6 = (f32[1,2,16]{2,1,0:T(2,128)S(1)}, f32[1,2,16]{2,1,0:T(2,128)}, u32[]{:S(2)}) copy-start(f32[1,2,16]{2,1,0:T(2,128)} %param.8) | copy-start | bytes 388
  73.6 2.2 %copy-start.7 = (f32[1,16]{1,0:T(1,128)S(1)}, f32[1,16]{1,0:T(1,128)}, u32[]{:S(2)}) copy-start(f32[1,16]{1,0:T(1,128)} %param.9) | copy-start | bytes 196

commit v2 on v0

v2 whole, which is shorter than its diff:
```python
import functools

import jax
import jax.numpy as jnp
from jax import lax
from jax.experimental import pallas as pl
from jax.experimental.pallas import tpu as pltpu
from jax.sharding import PartitionSpec as P

NT = 16
NMU = 1024
NG = 1536
WIDTH = NMU + 128
CHUNK = 512
ROWS = 128
F32 = jnp.float32
BF16 = jnp.bfloat16
VMEM = pl.BlockSpec(memory_space=pltpu.VMEM)
SMEM = pl.BlockSpec(memory_space=pltpu.SMEM)
ANY = pl.BlockSpec(memory_space=pl.ANY)


def move(value, x=0, z=0, far=0, y=0, core=0, step=0):
    pairs = []
    for a in range(4):
        for b in range(4):
            for c in range(2):
                for d in range(4):
                    for e in range(2):
                        source = (a * 4 + b) * 16 + c * 8 + d * 2 + e
                        group = (((a + step) % 4) ^ x) * 4 + (b ^ z)
                        member = (c ^ far) * 8 + (d ^ y) * 2 + (e ^ core)
                        pairs.append((source, group * 16 + member))
    return lax.ppermute(value, ("grp", "kin"), pairs)


def iota(shape, dim):
    return lax.broadcasted_iota(jnp.int32, shape, dim)


def dot(left, right):
    return jnp.dot(left, right, preferred_element_type=F32)


def dot_t(left, right):
    return lax.dot_general(left, right, (((1,), (1,)), ((), ())), preferred_element_type=F32)


def split(value):
    high = value.astype(BF16)
    return high, (value - high.astype(F32)).astype(BF16)


def dot_split(left, right):
    high, low = split(left)
    return dot(high, right) + dot(low, right)


def onehot(condition):
    return jnp.where(condition, 1.0, 0.0).astype(BF16)


def spread(repeat):
    row = iota((64, 16), 0)
    col = iota((64, 16), 1)
    band = (row >> 2) & 3 if repeat else row & 3
    base = jnp.where(row < 32, 4, 0) + jnp.where((row >> 4) & 1 == 1, 8, 0)
    return onehot(col == band + base)


def conj_product(left_re, left_im, right_re, right_im):
    real = (left_re * right_re + left_im * right_im).astype(BF16)
    imag = (left_re * right_im - left_im * right_re).astype(BF16)
    return real, imag


def pack_kernel(waves_ref, vector_ref, pay_ref):
    coarse = vector_ref[...].astype(BF16).astype(F32)
    real = jnp.broadcast_to(coarse[0:1], (16, 16))
    imag = jnp.broadcast_to(coarse[1:2], (16, 16))
    row = iota((16, 16), 0)
    lane = iota((16, 16), 1)
    of_v = lane >> 2 == row & 3
    by_c = onehot(row & 3 == lane & 3)
    real_v = dot(jnp.where(of_v, real, 0.0).astype(BF16), by_c)
    imag_v = dot(jnp.where(of_v, imag, 0.0).astype(BF16), by_c)
    upper = row < 8
    first = jnp.where(upper, real_v, imag_v)
    second = jnp.where(upper, -imag_v, real_v)
    mixer = jnp.where(lane & 8 == 0, first, second)
    mixer = jnp.where((row & 4 == 0) & (lane & 4 == 4), mixer, 0.0).astype(BF16)
    line_re = jnp.where(row == 12, real, 0.0).astype(BF16)
    line_im = jnp.where(row == 12, imag, 0.0).astype(BF16)
    row = iota((16, 128), 0)
    lane = iota((16, 128), 1)
    block = dot(mixer, onehot(lane == row)) + dot(line_re, onehot(lane == row + 16)) + dot(line_im, onehot(lane == row + 32))
    pay_ref[:, 0:NMU] = waves_ref[...]
    pay_ref[:, NMU:WIDTH] = block.astype(BF16)


def own_kernel(where_ref, qmap_ref, pay_ref, z_ref, screening, rx_ref, first_ref, second_ref, lhs, sems):
    own = where_ref[0]
    member = where_ref[1]
    partner = (own + 12) & 15
    steps = []
    for m, flip in enumerate((8, 9, 0, 1)):
        from_a = qmap_ref[0, own * 16 + (member ^ flip)]
        for n in range(4):
            from_b = qmap_ref[0, partner * 16 + (member ^ (2 * n))]
            index = (((from_b >> 4) - (from_a >> 4)) & 15) * 16 + ((from_b - from_a) & 15)
            target = first_ref if m < 2 else second_ref
            at = (m & 1) * 4 + n
            copy = pltpu.make_async_copy(
                screening.at[pl.ds(index, 1)], target.at[pl.ds(at, 1)], sems.at[m * 4 + n]
            )
            copy.start()
            steps.append(copy)
    waves = pay_ref[:, 0:NMU]
    left = dot(spread(True), waves)
    right = dot(spread(False), waves)
    real, imag = conj_product(left[32:48], left[48:64], right[0:16], right[16:32])
    lhs[0:16, 0:NMU] = real
    lhs[0:16, NMU : 2 * NMU] = -imag
    lhs[16:32, 0:NMU] = imag
    lhs[16:32, NMU : 2 * NMU] = real
    rx_ref[...] = dot(lhs[...], z_ref[...])
    for copy in steps:
        copy.wait()


def transitions_kernel(a0, a1, a2, y_ref):
    total_re = jnp.zeros((8, NMU), F32)
    total_im = jnp.zeros((8, NMU), F32)
    for pay in (a0[...], a1[...], a2[0:16], a2[16:32]):
        waves = pay[:, :NMU]
        mixed = dot(pay[:, NMU : NMU + 16], waves)
        waves = waves.astype(F32)
        val_re, val_im = waves[0:8], waves[8:16]
        mix_re, mix_im = mixed[0:8], mixed[8:16]
        total_re += val_re * mix_re + val_im * mix_im
        total_im += val_re * mix_im - val_im * mix_re
    total_re = jnp.sum(total_re, 0, keepdims=True)
    total_im = jnp.sum(total_im, 0, keepdims=True)
    y_ref[...] = jnp.concatenate([total_re, total_im], 0)


def pair_kernel(from_core, *refs):
    a_near, a_pair, b0, b1, b2, b3, w_ref, z_ref, _, out_ref, lhs, xa, xb, acc, ca, cb = refs
    a_pays = (a_near[...], a_pair[from_core : from_core + 16])
    b_pays = (b0[...], b1[...], b2[...], b3[...])
    half = 2 * ROWS

    def put(row, left, right, at):
        real, imag = conj_product(left[at : at + 16], left[at + 16 : at + 32], right[at : at + 16], right[at + 16 : at + 32])
        lhs[row : row + 16, 0:NMU] = real
        lhs[row : row + 16, NMU : 2 * NMU] = -imag
        lhs[half + row : half + row + 16, 0:NMU] = imag
        lhs[half + row : half + row + 16, NMU : 2 * NMU] = real

    rep = spread(True)
    til = spread(False)
    for m in range(2):
        xa[m] = dot(rep, a_pays[m][:, 0:NMU])
    for n in range(4):
        xb[n] = dot(til, b_pays[n][:, 0:NMU])
    for m in range(2):
        for n in range(4):
            row = (m * 4 + n) * 16
            put(row, xa[m], xb[n], 0)
            put(ROWS + row, xa[m], xb[n], 32)
    acc[...] = jnp.zeros_like(acc)
    for at in range(0, NG, CHUNK):
        z = z_ref[:, at : at + CHUNK]
        con_re = dot(lhs[0:ROWS], z)
        for p in range(8):
            weight = w_ref[p : p + 1, at : at + CHUNK]
            ca[p * 16 : p * 16 + 16, 0:CHUNK] = (con_re[p * 16 : p * 16 + 16] * weight).astype(BF16)
        con_im = dot(lhs[half : half + ROWS], z)
        for p in range(8):
            weight = w_ref[p : p + 1, at : at + CHUNK]
            ca[p * 16 : p * 16 + 16, CHUNK : 2 * CHUNK] = (con_im[p * 16 : p * 16 + 16] * weight).astype(BF16)
        val_re = dot(lhs[ROWS:half], z).astype(BF16)
        cb[0:ROWS, 0:CHUNK] = val_re
        cb[ROWS:half, CHUNK : 2 * CHUNK] = -val_re
        val_im = dot(lhs[half + ROWS : 2 * half], z).astype(BF16)
        cb[0:ROWS, CHUNK : 2 * CHUNK] = val_im
        cb[ROWS:half, 0:CHUNK] = val_im
        acc[...] += dot_t(ca[...], cb[...])

    pick_row = iota((8, 16), 0)
    pick_col = iota((8, 16), 1)
    xv_a = jnp.zeros((8, 128), F32)
    xv_b = jnp.zeros((8, 128), F32)
    for m in range(2):
        xv_a += dot(onehot((pick_row == m) & (pick_col == 12)), a_pays[m][:, NMU:WIDTH])
    for n in range(4):
        xv_b += dot(onehot((pick_row == n) & (pick_col == 12)), b_pays[n][:, NMU:WIDTH])
    row = iota((ROWS, 8), 0)
    col = iota((ROWS, 8), 1)
    of_a = onehot(row >> 6 == col)
    of_b = onehot((row >> 4) & 3 == col)
    row = iota((ROWS, 128), 0)
    lane = iota((ROWS, 128), 1)
    same_c = lane & 3 == (row >> 2) & 3
    same_d = lane & 3 == row & 3
    spread_a = jnp.where(same_c, dot(of_a, xv_a.astype(BF16)), 0.0).astype(BF16)
    spread_b = jnp.where(same_d, dot(of_b, xv_b.astype(BF16)), 0.0).astype(BF16)
    lane = iota((128, ROWS), 0)
    col = iota((128, ROWS), 1)
    by_w = (lane >> 2) & 3 == col & 3
    by_v = (lane >> 2) & 3 == (col >> 2) & 3
    first = lane >> 4 == 1
    second = lane >> 4 == 2
    pair = iota((ROWS, ROWS), 0) >> 4 == iota((ROWS, ROWS), 1) >> 4
    k_re = jnp.where(pair, acc[:, 0:ROWS], 0.0)
    k_im = jnp.where(pair, acc[:, ROWS:half], 0.0)
    xd_re = dot(spread_b, onehot(by_w & first))
    xd_im = dot(spread_b, onehot(by_w & second))
    xh_re = dot(spread_a, onehot(by_v & first))
    xh_im = dot(spread_a, onehot(by_v & second))
    lane = iota((ROWS, 128), 1)
    col = iota((ROWS, 128), 0)
    by_w = (lane >> 2) & 3 == col & 3
    by_v = (lane >> 2) & 3 == (col >> 2) & 3
    first = lane >> 4 == 0
    second = lane >> 4 == 1
    sum_d = dot_split(k_re * xd_re - k_im * xd_im, onehot(by_v & first)) + dot_split(
        k_re * xd_im + k_im * xd_re, onehot(by_v & second)
    )
    sum_h = dot_split(k_re * xh_re + k_im * xh_im, onehot(by_w & first)) + dot_split(
        k_re * xh_im - k_im * xh_re, onehot(by_w & second)
    )
    sum_d = jnp.where(same_c, sum_d, 0.0)
    sum_h = jnp.where(same_d, sum_h, 0.0)
    row = iota((8, ROWS), 0)
    col = iota((8, ROWS), 1)
    to_a = onehot(row == col >> 6)
    to_b = onehot(row == 4 + ((col >> 4) & 3))
    high_d, low_d = split(sum_d)
    high_h, low_h = split(sum_h)
    out_ref[...] = dot(to_a, high_d) + dot(to_a, low_d) + dot(to_b, high_h) + dot(to_b, low_h)


def exchange_kernel(y0, y1, y2, y3, c_ref, rx_ref, z_ref, out_ref, lhs):
    total = y0[...] + y1[...] + y2[...] + y3[...]
    swap = jnp.concatenate([-total[1:2], total[0:1]], 0)
    high, low = split(jnp.concatenate([total, swap], 1))
    pad = jnp.zeros((12, 2 * NMU), F32)
    lhs[...] = jnp.concatenate([high.astype(F32), low.astype(F32), pad], 0).astype(BF16)
    acc_re = jnp.zeros((16, 128), F32)
    acc_im = jnp.zeros((16, 128), F32)
    for start in range(0, NG, CHUNK):
        part = pl.ds(start, CHUNK)
        total = dot(lhs[...], z_ref[:, part])
        pot_re = (total[0:1] + total[2:3]) * c_ref[:, part]
        pot_im = (total[1:2] + total[3:4]) * c_ref[:, part]
        rx_re = rx_ref[0:16, part]
        rx_im = rx_ref[16:32, part]
        real = rx_re * pot_re + rx_im * pot_im
        imag = rx_re * pot_im - rx_im * pot_re
        for at in range(0, CHUNK, 128):
            acc_re += real[:, at : at + 128]
            acc_im += imag[:, at : at + 128]
    ones = jnp.ones((8, 128), BF16)
    out = []
    for acc in (acc_re, acc_im):
        high, low = split(acc)
        out.append((dot_t(ones, high) + dot_t(ones, low))[0:1])
    out_ref[...] = jnp.concatenate(out, 0)


def params(mib):
    return pltpu.CompilerParams(vmem_limit_bytes=mib * 1024 * 1024)


def cost(rows):
    return pl.CostEstimate(flops=2 * rows * 2 * NMU * NG, bytes_accessed=4 * NMU * NG, transcendentals=0)


def pair_call(from_core, a_near, a_pair, b_pays, weights, basis, after):
    return pl.pallas_call(
        functools.partial(pair_kernel, from_core),
        in_specs=[VMEM] * 8 + [ANY],
        out_specs=VMEM,
        out_shape=jax.ShapeDtypeStruct((8, 128), F32),
        scratch_shapes=[
            pltpu.VMEM((4 * ROWS, 2 * NMU), BF16),
            pltpu.VMEM((2, 64, NMU), F32),
            pltpu.VMEM((4, 64, NMU), F32),
            pltpu.VMEM((ROWS, 2 * ROWS), F32),
            pltpu.VMEM((ROWS, 2 * CHUNK), BF16),
            pltpu.VMEM((2 * ROWS, 2 * CHUNK), BF16),
        ],
        compiler_params=params(24),
        cost_estimate=cost(4 * ROWS),
    )(a_near, a_pair, *b_pays, weights, basis, after)


def on_device(waves, vector, energies, basis, screening, coulomb, qmap):
    basis = basis.reshape(2 * NMU, NG)
    pay = pl.pallas_call(
        pack_kernel,
        in_specs=[VMEM] * 2,
        out_specs=VMEM,
        out_shape=jax.ShapeDtypeStruct((16, WIDTH), BF16),
    )(waves.reshape(16, NMU), vector.reshape(2, NT))
    b0 = move(pay, step=1)
    a1 = move(pay, far=1)
    where = jnp.stack([lax.axis_index("grp"), lax.axis_index("kin")]).astype(jnp.int32)
    rx, far_weights, near_weights = pl.pallas_call(
        own_kernel,
        in_specs=[SMEM, SMEM, VMEM, VMEM, ANY],
        out_specs=[VMEM] * 3,
        out_shape=[
            jax.ShapeDtypeStruct((32, NG), F32),
            jax.ShapeDtypeStruct((8, NG), F32),
            jax.ShapeDtypeStruct((8, NG), F32),
        ],
        scratch_shapes=[pltpu.VMEM((32, 2 * NMU), BF16), pltpu.SemaphoreType.DMA((16,))],
        compiler_params=params(24),
        cost_estimate=cost(128),
    )(where, qmap, pay, basis, screening)
    b2 = move(b0, y=2)
    b1 = move(b0, y=1)
    b3 = move(b0, y=3)
    a23 = move(jnp.concatenate([pay, a1], 0), core=1)
    y = pl.pallas_call(
        transitions_kernel,
        in_specs=[VMEM] * 3,
        out_specs=VMEM,
        out_shape=jax.ShapeDtypeStruct((2, NMU), F32),
    )(pay, a1, a23)
    b_pays = (b0, b1, b2, b3)
    far_out = pair_call(16, a1, a23, b_pays, far_weights, basis, y)
    y = y + move(y, y=2) + move(y, y=1) + move(y, y=3)
    near_out = pair_call(0, pay, a23, b_pays, near_weights, basis, y)
    y = y + move(y, x=2) + move(y, x=1) + move(y, x=3)
    others = [move(y, z=n) for n in (2, 1, 3)]
    exchange = pl.pallas_call(
        exchange_kernel,
        in_specs=[VMEM] * 7,
        out_specs=VMEM,
        out_shape=jax.ShapeDtypeStruct((2, NT), F32),
        scratch_shapes=[pltpu.VMEM((16, 2 * NMU), BF16)],
        compiler_params=params(24),
        cost_estimate=cost(128),
    )(y, *others, coulomb.reshape(1, NG), rx, basis)

    far_sum = far_out[0:1] + move(far_out[1:2], core=1)
    herm = far_out[4:8] + near_out[4:8]
    herm = herm[0:1] + move(herm[2:3], y=2) + move(herm[1:2], y=1) + move(herm[3:4], y=3)
    terms = near_out[0:1] + move(near_out[1:2], core=1) + move(far_sum, far=1) + move(herm, step=3)
    terms = terms[:, 0:32].reshape(1, 2, NT)
    scale = jnp.float32(1.0 / 256)
    return energies[:, None, :] * vector + 2.0 * scale * exchange[None] - scale * terms


def solution(mesh):
    return jax.shard_map(
        on_device,
        mesh=mesh,
        in_specs=(
            P(("grp", "kin"), None, None, None),
            P(("grp", "kin"), None, None),
            P(("grp", "kin"), None),
            P(),
            P(),
            P(),
            P(("grp", "kin"), None),
        ),
        out_specs=P(("grp", "kin"), None, None),
        check_vma=False,
    )
```

time: 280 us -> 78.1 us (0.28)
  blocking collectives: 220 us -> 0 us
  starting transfers between devices: 2.66 us -> 35.3 us
  matrix products: 26.5 us -> 0 us
  Pallas kernels: 0 us -> 16.9 us
  other arithmetic: 7.43 us -> 1.51 us
  waiting for transfers between devices: 3.8 us -> 8.85 us
  local copies, waits for them, and re-layouts: 18.8 us -> 14.3 us
    unnamed x1 -> x0, blocking collectives: 87.1 us -> none
    psum x1 -> x0, blocking collectives: 73.7 us -> none  [on_device(): sum_re, sum_im = lax.psum((part_re, part_im), ('grp', 'kin'))]
    all_gather x2 -> x0, blocking collectives: 58.9 us -> none  [the longest x1 35.3 us: on_device(): lax.all_gather(waves, 'kin', axis=0, tiled=True)]
    ppermute x3 -> x22, starting transfers between devices: 2.66 us -> 35.3 us  [move(): return lax.ppermute(value, ('grp', 'kin'), pairs)]
    dot_general x20 -> x0, matrix products: 26.5 us -> none  [the longest x2 7.99 us: densities(): first = jnp.dot(stacked, basis[0], preferred_element_type=jnp.float32)]
    pallas_call x0 -> x6, Pallas kernels: none -> 16.9 us  [the longest x2 10.2 us: pair_call(): pl.pallas_call(functools.partial(pair_kernel, from_core), in_specs=[VMEM]...]
    mul x22 -> x1, local copies, waits for them, and re-layouts: 15.8 us -> 0.08 us  [on_device(): scale * terms]
    unnamed x34 -> x36, local copies, waits for them, and re-layouts: 1.64 us -> 14.2 us
  transfers between devices with their start and end apart: 3 -> 22, of which waited for: 1 -> 7; matrix products, arithmetic and copies ran while one was open for 5% -> 1% of each run, Pallas kernels for 0% -> 18%
where the time goes in v2:
time: 78.1 us; the launch traced here: 77.1 us
  starting transfers between devices  35.3 us (45%)
  Pallas kernels  16.9 us (22%)
  local copies, waits for them, and re-layouts  14.3 us (18%)
  waiting for transfers between devices  8.85 us (11%)
  other arithmetic  1.51 us (2%)
    ppermute x22, starting transfers between devices, move(): return lax.ppermute(value, ('grp', 'kin'), pairs)  35.3 us
    unnamed x36, local copies, waits for them, and re-layouts  14.2 us
    pallas_call x2, Pallas kernels, pair_call(): pl.pallas_call(functools.partial(pair_kernel, from_core), in_specs=[VMEM]...  10.2 us
    ppermute x22, waiting for transfers between devices, move(): return lax.ppermute(value, ('grp', 'kin'), pairs)  8.85 us
    pallas_call x1, Pallas kernels, on_device(): pl.pallas_call(own_kernel, in_specs=[SMEM, SMEM, VMEM, VMEM, ANY], out_sp...  2.3 us
    pallas_call x1, Pallas kernels, on_device(): pl.pallas_call(transitions_kernel, in_specs=[VMEM] * 3, out_specs=VMEM, o...  1.71 us
    pallas_call x1, Pallas kernels, on_device(): pl.pallas_call(pack_kernel, in_specs=[VMEM] * 2, out_specs=VMEM, out_shap...  1.61 us
  transfers between devices with their start and end apart: 22, of which 7 were waited for; matrix products, arithmetic and copies ran while one was open for 1% of the time, Pallas kernels for 18%

profile of v2, /device:TPU:6, one launch (start us, length us, event | category | flops | bytes accessed | tf_op | source)
XLA Modules:
  0.0 77.1 jit_solution(8191505634053957151)
XLA Ops:
  0.0 1.6 %shard_map.73.a0.pay_ref.refs_0_ = bf16[16,1152]{1,0:T(8,128)(2,1)} custom-call(bf16[16,1024]{1,0:T(8,128)(2,1)} %bitcast.16, f32[2,16]{1,0:T(2,128)} %bitcast.17), custom_call_target="tpu_custom_call" | custom-call | tf_op jit(solution)/shard_map/pallas_call | solution.py:301
  1.6 7.2 %collective-permute-start = (bf16[16,1152]{1,0:T(8,128)(2,1)}, bf16[16,1152]{1,0:T(8,128)(2,1)S(1)}, u32[]{:S(2)}, u32[]{:S(2)}) collective-permute-start(bf16[16,1152]{1,0:T(8,128)(2,1)} %shard_map.73.a0.pay_ref.refs_0_), channel_id=1, source_target_pairs={{0,8},{1,9},{2,10},{3,11},{4,12},{5,13},{6,14},{7,15},{8,0},{9,1},... | collective-permute-start | bytes 110600 | tf_op jit(solution)/shard_map/ppermute | solution.py:34
  8.8 0.5 collective-permute-start.11
  9.3 0.1 pad_add_fusion.where_ref
  9.4 1.6 %collective-permute-done.a1.refs_0_ = bf16[16,1152]{1,0:T(8,128)(2,1)S(1)} collective-permute-done((bf16[16,1152]{1,0:T(8,128)(2,1)}, bf16[16,1152]{1,0:T(8,128)(2,1)S(1)}, u32[]{:S(2)}, u32[]{:S(2)}) %collective-permute-start) | collective-permute-done | bytes 36896 | tf_op jit(solution)/shard_map/ppermute | solution.py:34
  11.0 0.8 %pad_maximum_fusion = bf16[32,1152]{1,0:T(8,128)(2,1)S(1)} fusion(bf16[16,1152]{1,0:T(8,128)(2,1)S(1)} %collective-permute-done.a1.refs_0_, bf16[16,1152]{1,0:T(8,128)(2,1)} %shard_map.73.a0.pay_ref.refs_0_), kind=kLoop, calls=%fused_computation | loop fusion | flops 147456 | bytes 147456 | tf_op jit(solution)/shard_map/concatenate | solution.py:326
  11.8 1.2 %collective-permute-done.11.refs_2_ = bf16[16,1152]{1,0:T(8,128)(2,1)S(1)} collective-permute-done((bf16[16,1152]{1,0:T(8,128)(2,1)}, bf16[16,1152]{1,0:T(8,128)(2,1)S(1)}, u32[]{:S(2)}, u32[]{:S(2)}) %collective-permute-start.11) | collective-permute-done | bytes 36896 | tf_op jit(solution)/shard_map/ppermute | solution.py:34
  13.0 1.6 %collective-permute-start.12 = (bf16[16,1152]{1,0:T(8,128)(2,1)S(1)}, bf16[16,1152]{1,0:T(8,128)(2,1)S(1)}, u32[]{:S(2)}, u32[]{:S(2)}) collective-permute-start(bf16[16,1152]{1,0:T(8,128)(2,1)S(1)} %collective-permute-done.11.refs_2_), channel_id=1, source_target_pairs={{0,2},{1,3},{2,0},{3,1},{4,6},{5,7},{6,4},{7,5},{8,10},{9,11},{10,... | collective-permute-start | bytes 110600 | tf_op jit(solution)/shard_map/ppermute | solution.py:34
  14.6 2.9 %collective-permute-start.13 = (bf16[16,1152]{1,0:T(8,128)(2,1)S(1)}, bf16[16,1152]{1,0:T(8,128)(2,1)S(1)}, u32[]{:S(2)}, u32[]{:S(2)}) collective-permute-start(bf16[16,1152]{1,0:T(8,128)(2,1)S(1)} %collective-permute-done.11.refs_2_), channel_id=1, source_target_pairs={{0,4},{1,5},{2,6},{3,7},{4,0},{5,1},{6,2},{7,3},{8,12},{9,13},{10,... | collective-permute-start | bytes 110600 | tf_op jit(solution)/shard_map/ppermute | solution.py:34
  17.5 0.2 collective-permute-start.14
  17.7 2.8 %copy-done = bf16[2,1024,1536]{2,1,0:T(8,128)(2,1)S(1)} copy-done((bf16[2,1024,1536]{2,1,0:T(8,128)(2,1)S(1)}, bf16[2,1024,1536]{2,1,0:T(8,128)(2,1)}, u32[]{:S(2)}) %copy-start) | copy-done | bytes 6291480
  20.5 1.4 %copy-done.3 = f32[256,1536]{1,0:T(8,128)S(1)} copy-done((f32[256,1536]{1,0:T(8,128)S(1)}, f32[256,1536]{1,0:T(8,128)}, u32[]{:S(2)}) %copy-start.3) | copy-done | bytes 1572888
  21.9 0.8 copy-done.4
  22.6 0.7 copy-done.12
  23.3 2.3 %shard_map.75 = (f32[32,1536]{1,0:T(8,128)S(1)}, f32[8,1536]{1,0:T(8,128)S(1)}, f32[8,1536]{1,0:T(8,128)S(1)}) custom-call(s32[2]{0:T(128)S(1)} %pad_add_fusion.where_ref, s32[1,256]{1,0:T(1,128)S(1)} %copy-done.12, bf16[16,1152]{1,0:T(8,128)(2,1)S(1)} %copy-done.4, bf16[2048,1536]{1,0:T(8,128)(2,1)S(1)} %bitcast.10, f32[256,1536]{1,0:T(8,128)S(1)} %copy-done.3), custom_call_target="tpu_custom_call" | custom-call | flops 805306368 | bytes 6291456 | tf_op jit(solution)/shard_map/pallas_call | solution.py:310
  25.7 0.6 copy-done.8
  26.3 1.7 %shard_map.74.refs_8_ = f32[2,1024]{1,0:T(2,128)} custom-call(bf16[16,1152]{1,0:T(8,128)(2,1)} %shard_map.73.a0.pay_ref.refs_0_, bf16[16,1152]{1,0:T(8,128)(2,1)} %copy-done.6, bf16[32,1152]{1,0:T(8,128)(2,1)} %copy-done.8), custom_call_target="tpu_custom_call" | custom-call | tf_op jit(solution)/shard_map/pallas_call | solution.py:327
  28.0 2.0 %collective-permute-start.2 = (f32[2,1024]{1,0:T(2,128)}, f32[2,1024]{1,0:T(2,128)S(1)}, u32[]{:S(2)}, u32[]{:S(2)}) collective-permute-start(f32[2,1024]{1,0:T(2,128)} %shard_map.74.refs_8_), channel_id=1, source_target_pairs={{0,4},{1,5},{2,6},{3,7},{4,0},{5,1},{6,2},{7,3},{8,12},{9,13},{10,... | collective-permute-start | bytes 24584 | tf_op jit(solution)/shard_map/ppermute | solution.py:34
  30.0 1.9 %collective-permute-start.3 = (f32[2,1024]{1,0:T(2,128)}, f32[2,1024]{1,0:T(2,128)S(1)}, u32[]{:S(2)}, u32[]{:S(2)}) collective-permute-start(f32[2,1024]{1,0:T(2,128)} %shard_map.74.refs_8_), channel_id=1, source_target_pairs={{0,2},{1,3},{2,0},{3,1},{4,6},{5,7},{6,4},{7,5},{8,10},{9,11},{10,... | collective-permute-start | bytes 24584 | tf_op jit(solution)/shard_map/ppermute | solution.py:34
  31.9 0.2 collective-permute-start.4
  32.1 2.8 %copy-done.1 = bf16[2,1024,1536]{2,1,0:T(8,128)(2,1)S(1)} copy-done((bf16[2,1024,1536]{2,1,0:T(8,128)(2,1)S(1)}, bf16[2,1024,1536]{2,1,0:T(8,128)(2,1)}, u32[]{:S(2)}) %copy-start.1) | copy-done | bytes 6291480
  34.9 0.8 copy-done.7
  35.7 0.9 %copy-done.9 = bf16[32,1152]{1,0:T(8,128)(2,1)S(1)} copy-done((bf16[32,1152]{1,0:T(8,128)(2,1)S(1)}, bf16[32,1152]{1,0:T(8,128)(2,1)}, u32[]{:S(2)}) %copy-start.9) | copy-done | bytes 73752
  36.5 0.7 copy-done.10
  37.2 4.9 %shard_map.78 = f32[8,128]{1,0:T(8,128)S(1)} custom-call(bf16[16,1152]{1,0:T(8,128)(2,1)S(1)} %copy-done.7, bf16[32,1152]{1,0:T(8,128)(2,1)S(1)} %copy-done.9, bf16[16,1152]{1,0:T(8,128)(2,1)S(1)} %collective-permute-done.11.refs_2_, bf16[16,1152]{1,0:T(8,128)(2,1)S(1)} %collective-permute-done.12.refs_3_, ...), custom_call_target="tpu_custom_call" | custom-call | flops 3221225472 | bytes 6291456 | tf_op jit(solution)/shard_map/pallas_call | solution.py:281
  42.1 0.3 collective-permute-start.16
  42.5 0.0 copy-start.14
  42.5 5.3 %shard_map.77 = f32[8,128]{1,0:T(8,128)S(1)} custom-call(bf16[16,1152]{1,0:T(8,128)(2,1)S(1)} %copy-done.5, bf16[32,1152]{1,0:T(8,128)(2,1)S(1)} %copy-done.9, bf16[16,1152]{1,0:T(8,128)(2,1)S(1)} %collective-permute-done.11.refs_2_, bf16[16,1152]{1,0:T(8,128)(2,1)S(1)} %collective-permute-done.12.refs_3_, ...), custom_call_target="tpu_custom_call" | custom-call | flops 3221225472 | bytes 6291456 | tf_op jit(solution)/shard_map/pallas_call | solution.py:281
  47.9 2.1 %collective-permute-start.18 = (f32[1,128]{1,0:T(1,128)S(1)}, f32[1,128]{1,0:T(1,128)S(1)}, u32[]{:S(2)}, u32[]{:S(2)}) collective-permute-start(f32[1,128]{1,0:T(1,128)S(1)} %get-tuple-element.11), channel_id=1, source_target_pairs={{0,4},{1,5},{2,6},{3,7},{4,0},{5,1},{6,2},{7,3},{8,12},{9,13},{10,... | collective-permute-start | bytes 1544 | tf_op jit(solution)/shard_map/ppermute | solution.py:34
  50.0 1.9 %collective-permute-start.19 = (f32[1,128]{1,0:T(1,128)S(1)}, f32[1,128]{1,0:T(1,128)S(1)}, u32[]{:S(2)}, u32[]{:S(2)}) collective-permute-start(f32[1,128]{1,0:T(1,128)S(1)} %get-tuple-element.13), channel_id=1, source_target_pairs={{0,2},{1,3},{2,0},{3,1},{4,6},{5,7},{6,4},{7,5},{8,10},{9,11},{10,... | collective-permute-start | bytes 1544 | tf_op jit(solution)/shard_map/ppermute | solution.py:34
  51.9 0.2 collective-permute-start.20
  52.1 4.8 %collective-permute-start.17 = (f32[1,128]{1,0:T(1,128)S(1)}, f32[1,128]{1,0:T(1,128)S(1)}, u32[]{:S(2)}, u32[]{:S(2)}) collective-permute-start(f32[1,128]{1,0:T(1,128)S(1)} %slice_add_fusion.1), channel_id=1, source_target_pairs={{0,8},{1,9},{2,10},{3,11},{4,12},{5,13},{6,14},{7,15},{8,0},{9,1},... | collective-permute-start | bytes 1544 | tf_op jit(solution)/shard_map/ppermute | solution.py:34
  57.0 0.9 %collective-permute-start.21 = (f32[1,128]{1,0:T(1,128)S(1)}, f32[1,128]{1,0:T(1,128)S(1)}, u32[]{:S(2)}, u32[]{:S(2)}) collective-permute-start(f32[1,128]{1,0:T(1,128)S(1)} %add_add_fusion.2), channel_id=1, source_target_pairs={{0,192},{1,193},{2,194},{3,195},{4,196},{5,197},{6,198},{7,199},{8... | collective-permute-start | bytes 1544 | tf_op jit(solution)/shard_map/ppermute | solution.py:34
  57.9 2.0 %collective-permute-start.5 = (f32[2,1024]{1,0:T(2,128)S(1)}, f32[2,1024]{1,0:T(2,128)S(1)}, u32[]{:S(2)}, u32[]{:S(2)}) collective-permute-start(f32[2,1024]{1,0:T(2,128)S(1)} %add_add_fusion.1.refs_8_), channel_id=1, source_target_pairs={{0,128},{1,129},{2,130},{3,131},{4,132},{5,133},{6,134},{7,135},{8... | collective-permute-start | bytes 24584 | tf_op jit(solution)/shard_map/ppermute | solution.py:34
  59.9 1.3 %collective-permute-start.6 = (f32[2,1024]{1,0:T(2,128)S(1)}, f32[2,1024]{1,0:T(2,128)S(1)}, u32[]{:S(2)}, u32[]{:S(2)}) collective-permute-start(f32[2,1024]{1,0:T(2,128)S(1)} %add_add_fusion.1.refs_8_), channel_id=1, source_target_pairs={{0,64},{1,65},{2,66},{3,67},{4,68},{5,69},{6,70},{7,71},{8,72},{9,... | collective-permute-start | bytes 24584 | tf_op jit(solution)/shard_map/ppermute | solution.py:34
  61.2 0.8 %collective-permute-start.7 = (f32[2,1024]{1,0:T(2,128)S(1)}, f32[2,1024]{1,0:T(2,128)S(1)}, u32[]{:S(2)}, u32[]{:S(2)}) collective-permute-start(f32[2,1024]{1,0:T(2,128)S(1)} %add_add_fusion.1.refs_8_), channel_id=1, source_target_pairs={{0,192},{1,193},{2,194},{3,195},{4,196},{5,197},{6,198},{7,199},{8... | collective-permute-start | bytes 24584 | tf_op jit(solution)/shard_map/ppermute | solution.py:34
  62.1 1.0 %collective-permute-done.5 = f32[2,1024]{1,0:T(2,128)S(1)} collective-permute-done((f32[2,1024]{1,0:T(2,128)S(1)}, f32[2,1024]{1,0:T(2,128)S(1)}, u32[]{:S(2)}, u32[]{:S(2)}) %collective-permute-start.5) | collective-permute-done | bytes 8224 | tf_op jit(solution)/shard_map/ppermute | solution.py:34
  63.1 0.4 collective-permute-done.6
  63.5 2.6 %collective-permute-done.7 = f32[2,1024]{1,0:T(2,128)S(1)} collective-permute-done((f32[2,1024]{1,0:T(2,128)S(1)}, f32[2,1024]{1,0:T(2,128)S(1)}, u32[]{:S(2)}, u32[]{:S(2)}) %collective-permute-start.7) | collective-permute-done | bytes 8224 | tf_op jit(solution)/shard_map/ppermute | solution.py:34
  66.1 2.0 %collective-permute-start.10 = (f32[2,1024]{1,0:T(2,128)S(1)}, f32[2,1024]{1,0:T(2,128)S(1)}, u32[]{:S(2)}, u32[]{:S(2)}) collective-permute-start(f32[2,1024]{1,0:T(2,128)S(1)} %add_add_fusion.y0), channel_id=1, source_target_pairs={{0,48},{1,49},{2,50},{3,51},{4,52},{5,53},{6,54},{7,55},{8,56},{9,... | collective-permute-start | bytes 24584 | tf_op jit(solution)/shard_map/ppermute | solution.py:34
  68.1 0.8 %collective-permute-start.8 = (f32[2,1024]{1,0:T(2,128)S(1)}, f32[2,1024]{1,0:T(2,128)S(1)}, u32[]{:S(2)}, u32[]{:S(2)}) collective-permute-start(f32[2,1024]{1,0:T(2,128)S(1)} %add_add_fusion.y0), channel_id=1, source_target_pairs={{0,32},{1,33},{2,34},{3,35},{4,36},{5,37},{6,38},{7,39},{8,40},{9,... | collective-permute-start | bytes 24584 | tf_op jit(solution)/shard_map/ppermute | solution.py:34
  68.9 1.7 %collective-permute-start.9 = (f32[2,1024]{1,0:T(2,128)S(1)}, f32[2,1024]{1,0:T(2,128)S(1)}, u32[]{:S(2)}, u32[]{:S(2)}) collective-permute-start(f32[2,1024]{1,0:T(2,128)S(1)} %add_add_fusion.y0), channel_id=1, source_target_pairs={{0,16},{1,17},{2,18},{3,19},{4,20},{5,21},{6,22},{7,23},{8,24},{9,... | collective-permute-start | bytes 24584 | tf_op jit(solution)/shard_map/ppermute | solution.py:34
  70.6 0.1 mul.44
  70.7 1.0 %collective-permute-done.10.y3 = f32[2,1024]{1,0:T(2,128)S(1)} collective-permute-done((f32[2,1024]{1,0:T(2,128)S(1)}, f32[2,1024]{1,0:T(2,128)S(1)}, u32[]{:S(2)}, u32[]{:S(2)}) %collective-permute-start.10) | collective-permute-done | bytes 8224 | tf_op jit(solution)/shard_map/ppermute | solution.py:34
  71.6 1.0 %collective-permute-done.8.y1 = f32[2,1024]{1,0:T(2,128)S(1)} collective-permute-done((f32[2,1024]{1,0:T(2,128)S(1)}, f32[2,1024]{1,0:T(2,128)S(1)}, u32[]{:S(2)}, u32[]{:S(2)}) %collective-permute-start.8) | collective-permute-done | bytes 8224 | tf_op jit(solution)/shard_map/ppermute | solution.py:34
  72.7 2.8 %copy-done.2 = bf16[2,1024,1536]{2,1,0:T(8,128)(2,1)S(1)} copy-done((bf16[2,1024,1536]{2,1,0:T(8,128)(2,1)S(1)}, bf16[2,1024,1536]{2,1,0:T(8,128)(2,1)}, u32[]{:S(2)}) %copy-start.2) | copy-done | bytes 6291480
  75.5 1.1 %shard_map.76 = f32[2,16]{1,0:T(2,128)S(1)} custom-call(f32[2,1024]{1,0:T(2,128)S(1)} %add_add_fusion.y0, f32[2,1024]{1,0:T(2,128)S(1)} %collective-permute-done.8.y1, f32[2,1024]{1,0:T(2,128)S(1)} %collective-permute-done.9.y2, f32[2,1024]{1,0:T(2,128)S(1)} %collective-permute-done.10.y3, f32[1,1536]{1,0:T(1,128)S(1)} %reshape.33.c_ref, ...), custom_call_target="tpu_custom_call" | custom-call | flops 805306368 | bytes 6291456 | tf_op jit(solution)/shard_map/pallas_call | solution.py:339
  76.5 0.6 fusion
  (54 shorter events, 0.2 us)
Async XLA Ops:
  1.6 9.4 %collective-permute-start = (bf16[16,1152]{1,0:T(8,128)(2,1)}, bf16[16,1152]{1,0:T(8,128)(2,1)S(1)}, u32[]{:S(2)}, u32[]{:S(2)}) collective-permute-start(bf16[16,1152]{1,0:T(8,128)(2,1)} %shard_map.73.a0.pay_ref.refs_0_), channel_id=1, source_target_pairs={{0,8},{1,9},{2,10},{3,11},{4,12},{5,13},{6,14},{7,15},{8,0},{9,1},... | collective-permute-start | bytes 110600 | tf_op jit(solution)/shard_map/ppermute | solution.py:34
  8.8 4.2 %collective-permute-start.11 = (bf16[16,1152]{1,0:T(8,128)(2,1)}, bf16[16,1152]{1,0:T(8,128)(2,1)S(1)}, u32[]{:S(2)}, u32[]{:S(2)}) collective-permute-start(bf16[16,1152]{1,0:T(8,128)(2,1)} %shard_map.73.a0.pay_ref.refs_0_), channel_id=1, source_target_pairs={{0,64},{1,65},{2,66},{3,67},{4,68},{5,69},{6,70},{7,71},{8,72},{9,... | collective-permute-start | bytes 110600 | tf_op jit(solution)/shard_map/ppermute | solution.py:34
  11.0 14.6 %copy-start.6 = (bf16[16,1152]{1,0:T(8,128)(2,1)}, bf16[16,1152]{1,0:T(8,128)(2,1)S(1)}, u32[]{:S(2)}) copy-start(bf16[16,1152]{1,0:T(8,128)(2,1)S(1)} %collective-permute-done.a1.refs_0_) | copy-start | bytes 110596
  11.8 13.8 %collective-permute-start.1 = (bf16[32,1152]{1,0:T(8,128)(2,1)S(1)}, bf16[32,1152]{1,0:T(8,128)(2,1)S(1)}, u32[]{:S(2)}, u32[]{:S(2)}) collective-permute-start(bf16[32,1152]{1,0:T(8,128)(2,1)S(1)} %pad_maximum_fusion), channel_id=1, source_target_pairs={{0,1},{1,0},{2,3},{3,2},{4,5},{5,4},{6,7},{7,6},{8,9},{9,8},{10,11... | collective-permute-start | bytes 221192 | tf_op jit(solution)/shard_map/ppermute | solution.py:34
  13.0 18.9 %collective-permute-start.12 = (bf16[16,1152]{1,0:T(8,128)(2,1)S(1)}, bf16[16,1152]{1,0:T(8,128)(2,1)S(1)}, u32[]{:S(2)}, u32[]{:S(2)}) collective-permute-start(bf16[16,1152]{1,0:T(8,128)(2,1)S(1)} %collective-permute-done.11.refs_2_), channel_id=1, source_target_pairs={{0,2},{1,3},{2,0},{3,1},{4,6},{5,7},{6,4},{7,5},{8,10},{9,11},{10,... | collective-permute-start | bytes 110600 | tf_op jit(solution)/shard_map/ppermute | solution.py:34
  14.6 17.5 %collective-permute-start.13 = (bf16[16,1152]{1,0:T(8,128)(2,1)S(1)}, bf16[16,1152]{1,0:T(8,128)(2,1)S(1)}, u32[]{:S(2)}, u32[]{:S(2)}) collective-permute-start(bf16[16,1152]{1,0:T(8,128)(2,1)S(1)} %collective-permute-done.11.refs_2_), channel_id=1, source_target_pairs={{0,4},{1,5},{2,6},{3,7},{4,0},{5,1},{6,2},{7,3},{8,12},{9,13},{10,... | collective-permute-start | bytes 110600 | tf_op jit(solution)/shard_map/ppermute | solution.py:34
  17.5 14.6 %collective-permute-start.14 = (bf16[16,1152]{1,0:T(8,128)(2,1)S(1)}, bf16[16,1152]{1,0:T(8,128)(2,1)S(1)}, u32[]{:S(2)}, u32[]{:S(2)}) collective-permute-start(bf16[16,1152]{1,0:T(8,128)(2,1)S(1)} %collective-permute-done.11.refs_2_), channel_id=1, source_target_pairs={{0,6},{1,7},{2,4},{3,5},{4,2},{5,3},{6,0},{7,1},{8,14},{9,15},{10,... | collective-permute-start | bytes 110600 | tf_op jit(solution)/shard_map/ppermute | solution.py:34
  17.7 2.8 %copy-start = (bf16[2,1024,1536]{2,1,0:T(8,128)(2,1)S(1)}, bf16[2,1024,1536]{2,1,0:T(8,128)(2,1)}, u32[]{:S(2)}) copy-start(bf16[2,1024,1536]{2,1,0:T(8,128)(2,1)} %param.10) | copy-start | bytes 18874372
  20.5 1.4 %copy-start.3 = (f32[256,1536]{1,0:T(8,128)S(1)}, f32[256,1536]{1,0:T(8,128)}, u32[]{:S(2)}) copy-start(f32[256,1536]{1,0:T(8,128)} %screening.1) | copy-start | bytes 4718596
  21.9 0.8 copy-start.4
  22.6 0.7 copy-start.12
  23.3 19.1 %slice-start = ((s8[6291456]{0:T(1024)(128)(4,1)}), s8[2097152]{0:T(1024)(128)(4,1)S(1)}, s32[]{:S(2)}) async-start(s8[6291456]{0:T(1024)(128)(4,1)} %bitcast.12), calls=%async_computation | async-start | bytes 4194304
  25.6 16.9 %copy-start.5 = (bf16[16,1152]{1,0:T(8,128)(2,1)S(1)}, bf16[16,1152]{1,0:T(8,128)(2,1)}, u32[]{:S(2)}) copy-start(bf16[16,1152]{1,0:T(8,128)(2,1)} %shard_map.73.a0.pay_ref.refs_0_) | copy-start | bytes 110596
  25.7 0.6 copy-start.8
  28.0 14.4 %collective-permute-start.2 = (f32[2,1024]{1,0:T(2,128)}, f32[2,1024]{1,0:T(2,128)S(1)}, u32[]{:S(2)}, u32[]{:S(2)}) collective-permute-start(f32[2,1024]{1,0:T(2,128)} %shard_map.74.refs_8_), channel_id=1, source_target_pairs={{0,4},{1,5},{2,6},{3,7},{4,0},{5,1},{6,2},{7,3},{8,12},{9,13},{10,... | collective-permute-start | bytes 24584 | tf_op jit(solution)/shard_map/ppermute | solution.py:34
  30.0 12.4 %collective-permute-start.3 = (f32[2,1024]{1,0:T(2,128)}, f32[2,1024]{1,0:T(2,128)S(1)}, u32[]{:S(2)}, u32[]{:S(2)}) collective-permute-start(f32[2,1024]{1,0:T(2,128)} %shard_map.74.refs_8_), channel_id=1, source_target_pairs={{0,2},{1,3},{2,0},{3,1},{4,6},{5,7},{6,4},{7,5},{8,10},{9,11},{10,... | collective-permute-start | bytes 24584 | tf_op jit(solution)/shard_map/ppermute | solution.py:34
  31.9 10.6 %collective-permute-start.4 = (f32[2,1024]{1,0:T(2,128)}, f32[2,1024]{1,0:T(2,128)S(1)}, u32[]{:S(2)}, u32[]{:S(2)}) collective-permute-start(f32[2,1024]{1,0:T(2,128)} %shard_map.74.refs_8_), channel_id=1, source_target_pairs={{0,6},{1,7},{2,4},{3,5},{4,2},{5,3},{6,0},{7,1},{8,14},{9,15},{10,... | collective-permute-start | bytes 24584 | tf_op jit(solution)/shard_map/ppermute | solution.py:34
  32.1 2.8 %copy-start.1 = (bf16[2,1024,1536]{2,1,0:T(8,128)(2,1)S(1)}, bf16[2,1024,1536]{2,1,0:T(8,128)(2,1)}, u32[]{:S(2)}) copy-start(bf16[2,1024,1536]{2,1,0:T(8,128)(2,1)} %param.10) | copy-start | bytes 18874372
  34.9 0.8 copy-start.7
  35.7 0.9 %copy-start.9 = (bf16[32,1152]{1,0:T(8,128)(2,1)S(1)}, bf16[32,1152]{1,0:T(8,128)(2,1)}, u32[]{:S(2)}) copy-start(bf16[32,1152]{1,0:T(8,128)(2,1)} %copy-done.8) | copy-start | bytes 221188
  36.5 0.7 copy-start.10
  37.2 5.2 %copy-start.11 = (f32[2,1024]{1,0:T(2,128)S(1)}, f32[2,1024]{1,0:T(2,128)}, u32[]{:S(2)}) copy-start(f32[2,1024]{1,0:T(2,128)} %shard_map.74.refs_8_) | copy-start | bytes 24580
  37.2 5.2 %slice-start.1 = ((s8[6291456]{0:T(1024)(128)(4,1)}), s8[4194304]{0:T(1024)(128)(4,1)S(1)}, s32[]{:S(2)}) async-start(s8[6291456]{0:T(1024)(128)(4,1)} %bitcast.12), calls=%async_computation.1 | async-start | bytes 8388608
  42.1 15.7 %copy-start.13 = (f32[1536]{0:T(1024)S(1)}, f32[1536]{0:T(1024)}, u32[]{:S(2)}) copy-start(f32[1536]{0:T(1024)} %param.12) | copy-start | bytes 18436
  42.1 10.0 %collective-permute-start.16 = (f32[1,128]{1,0:T(1,128)S(1)}, f32[1,128]{1,0:T(1,128)S(1)}, u32[]{:S(2)}, u32[]{:S(2)}) collective-permute-start(f32[1,128]{1,0:T(1,128)S(1)} %slice.36), channel_id=1, source_target_pairs={{0,1},{1,0},{2,3},{3,2},{4,5},{5,4},{6,7},{7,6},{8,9},{9,8},{10,11... | collective-permute-start | bytes 1544 | tf_op jit(solution)/shard_map/ppermute | solution.py:34
  42.5 34.0 %copy-start.14 = (f32[1,2,16]{2,1,0:T(2,128)S(1)}, f32[1,2,16]{2,1,0:T(2,128)}, u32[]{:S(2)}) copy-start(f32[1,2,16]{2,1,0:T(2,128)} %param.8) | copy-start | bytes 388
  42.5 34.0 %copy-start.15 = (f32[1,16]{1,0:T(1,128)S(1)}, f32[1,16]{1,0:T(1,128)}, u32[]{:S(2)}) copy-start(f32[1,16]{1,0:T(1,128)} %param.9) | copy-start | bytes 196
  47.9 9.0 %collective-permute-start.18 = (f32[1,128]{1,0:T(1,128)S(1)}, f32[1,128]{1,0:T(1,128)S(1)}, u32[]{:S(2)}, u32[]{:S(2)}) collective-permute-start(f32[1,128]{1,0:T(1,128)S(1)} %get-tuple-element.11), channel_id=1, source_target_pairs={{0,4},{1,5},{2,6},{3,7},{4,0},{5,1},{6,2},{7,3},{8,12},{9,13},{10,... | collective-permute-start | bytes 1544 | tf_op jit(solution)/shard_map/ppermute | solution.py:34
  50.0 6.9 %collective-permute-start.19 = (f32[1,128]{1,0:T(1,128)S(1)}, f32[1,128]{1,0:T(1,128)S(1)}, u32[]{:S(2)}, u32[]{:S(2)}) collective-permute-start(f32[1,128]{1,0:T(1,128)S(1)} %get-tuple-element.13), channel_id=1, source_target_pairs={{0,2},{1,3},{2,0},{3,1},{4,6},{5,7},{6,4},{7,5},{8,10},{9,11},{10,... | collective-permute-start | bytes 1544 | tf_op jit(solution)/shard_map/ppermute | solution.py:34
  51.9 5.1 %collective-permute-start.20 = (f32[1,128]{1,0:T(1,128)S(1)}, f32[1,128]{1,0:T(1,128)S(1)}, u32[]{:S(2)}, u32[]{:S(2)}) collective-permute-start(f32[1,128]{1,0:T(1,128)S(1)} %get-tuple-element.12), channel_id=1, source_target_pairs={{0,6},{1,7},{2,4},{3,5},{4,2},{5,3},{6,0},{7,1},{8,14},{9,15},{10,... | collective-permute-start | bytes 1544 | tf_op jit(solution)/shard_map/ppermute | solution.py:34
  52.1 9.1 %collective-permute-start.17 = (f32[1,128]{1,0:T(1,128)S(1)}, f32[1,128]{1,0:T(1,128)S(1)}, u32[]{:S(2)}, u32[]{:S(2)}) collective-permute-start(f32[1,128]{1,0:T(1,128)S(1)} %slice_add_fusion.1), channel_id=1, source_target_pairs={{0,8},{1,9},{2,10},{3,11},{4,12},{5,13},{6,14},{7,15},{8,0},{9,1},... | collective-permute-start | bytes 1544 | tf_op jit(solution)/shard_map/ppermute | solution.py:34
  56.9 5.2 %collective-permute-start.15 = (f32[1,128]{1,0:T(1,128)S(1)}, f32[1,128]{1,0:T(1,128)S(1)}, u32[]{:S(2)}, u32[]{:S(2)}) collective-permute-start(f32[1,128]{1,0:T(1,128)S(1)} %slice.34), channel_id=1, source_target_pairs={{0,1},{1,0},{2,3},{3,2},{4,5},{5,4},{6,7},{7,6},{8,9},{9,8},{10,11... | collective-permute-start | bytes 1544 | tf_op jit(solution)/shard_map/ppermute | solution.py:34
  57.0 5.1 %collective-permute-start.21 = (f32[1,128]{1,0:T(1,128)S(1)}, f32[1,128]{1,0:T(1,128)S(1)}, u32[]{:S(2)}, u32[]{:S(2)}) collective-permute-start(f32[1,128]{1,0:T(1,128)S(1)} %add_add_fusion.2), channel_id=1, source_target_pairs={{0,192},{1,193},{2,194},{3,195},{4,196},{5,197},{6,198},{7,199},{8... | collective-permute-start | bytes 1544 | tf_op jit(solution)/shard_map/ppermute | solution.py:34
  57.9 5.2 %collective-permute-start.5 = (f32[2,1024]{1,0:T(2,128)S(1)}, f32[2,1024]{1,0:T(2,128)S(1)}, u32[]{:S(2)}, u32[]{:S(2)}) collective-permute-start(f32[2,1024]{1,0:T(2,128)S(1)} %add_add_fusion.1.refs_8_), channel_id=1, source_target_pairs={{0,128},{1,129},{2,130},{3,131},{4,132},{5,133},{6,134},{7,135},{8... | collective-permute-start | bytes 24584 | tf_op jit(solution)/shard_map/ppermute | solution.py:34
  59.9 3.7 %collective-permute-start.6 = (f32[2,1024]{1,0:T(2,128)S(1)}, f32[2,1024]{1,0:T(2,128)S(1)}, u32[]{:S(2)}, u32[]{:S(2)}) collective-permute-start(f32[2,1024]{1,0:T(2,128)S(1)} %add_add_fusion.1.refs_8_), channel_id=1, source_target_pairs={{0,64},{1,65},{2,66},{3,67},{4,68},{5,69},{6,70},{7,71},{8,72},{9,... | collective-permute-start | bytes 24584 | tf_op jit(solution)/shard_map/ppermute | solution.py:34
  61.2 4.9 %collective-permute-start.7 = (f32[2,1024]{1,0:T(2,128)S(1)}, f32[2,1024]{1,0:T(2,128)S(1)}, u32[]{:S(2)}, u32[]{:S(2)}) collective-permute-start(f32[2,1024]{1,0:T(2,128)S(1)} %add_add_fusion.1.refs_8_), channel_id=1, source_target_pairs={{0,192},{1,193},{2,194},{3,195},{4,196},{5,197},{6,198},{7,199},{8... | collective-permute-start | bytes 24584 | tf_op jit(solution)/shard_map/ppermute | solution.py:34
  66.1 5.5 %collective-permute-start.10 = (f32[2,1024]{1,0:T(2,128)S(1)}, f32[2,1024]{1,0:T(2,128)S(1)}, u32[]{:S(2)}, u32[]{:S(2)}) collective-permute-start(f32[2,1024]{1,0:T(2,128)S(1)} %add_add_fusion.y0), channel_id=1, source_target_pairs={{0,48},{1,49},{2,50},{3,51},{4,52},{5,53},{6,54},{7,55},{8,56},{9,... | collective-permute-start | bytes 24584 | tf_op jit(solution)/shard_map/ppermute | solution.py:34
  68.1 4.5 %collective-permute-start.8 = (f32[2,1024]{1,0:T(2,128)S(1)}, f32[2,1024]{1,0:T(2,128)S(1)}, u32[]{:S(2)}, u32[]{:S(2)}) collective-permute-start(f32[2,1024]{1,0:T(2,128)S(1)} %add_add_fusion.y0), channel_id=1, source_target_pairs={{0,32},{1,33},{2,34},{3,35},{4,36},{5,37},{6,38},{7,39},{8,40},{9,... | collective-permute-start | bytes 24584 | tf_op jit(solution)/shard_map/ppermute | solution.py:34
  68.9 3.8 %collective-permute-start.9 = (f32[2,1024]{1,0:T(2,128)S(1)}, f32[2,1024]{1,0:T(2,128)S(1)}, u32[]{:S(2)}, u32[]{:S(2)}) collective-permute-start(f32[2,1024]{1,0:T(2,128)S(1)} %add_add_fusion.y0), channel_id=1, source_target_pairs={{0,16},{1,17},{2,18},{3,19},{4,20},{5,21},{6,22},{7,23},{8,24},{9,... | collective-permute-start | bytes 24584 | tf_op jit(solution)/shard_map/ppermute | solution.py:34
  72.7 2.8 %copy-start.2 = (bf16[2,1024,1536]{2,1,0:T(8,128)(2,1)S(1)}, bf16[2,1024,1536]{2,1,0:T(8,128)(2,1)}, u32[]{:S(2)}) copy-start(bf16[2,1024,1536]{2,1,0:T(8,128)(2,1)} %param.10) | copy-start | bytes 18874372

commit v3 on v2

--- a/solution.py
+++ b/solution.py
@@ -98,7 +98,9 @@
     pay_ref[:, NMU:WIDTH] = block.astype(BF16)
 
 
-def own_kernel(where_ref, qmap_ref, pay_ref, z_ref, screening, rx_ref, first_ref, second_ref, lhs, sems):
+def fetch_kernel(where_ref, qmap_ref, basis, screening, z_ref, w_ref, sems):
+    whole = pltpu.make_async_copy(basis, z_ref, sems.at[16])
+    whole.start()
     own = where_ref[0]
     member = where_ref[1]
     partner = (own + 12) & 15
@@ -108,32 +110,29 @@
         for n in range(4):
             from_b = qmap_ref[0, partner * 16 + (member ^ (2 * n))]
             index = (((from_b >> 4) - (from_a >> 4)) & 15) * 16 + ((from_b - from_a) & 15)
-            target = first_ref if m < 2 else second_ref
-            at = (m & 1) * 4 + n
-            copy = pltpu.make_async_copy(
-                screening.at[pl.ds(index, 1)], target.at[pl.ds(at, 1)], sems.at[m * 4 + n]
-            )
+            at = m * 4 + n
+            copy = pltpu.make_async_copy(screening.at[pl.ds(index, 1)], w_ref.at[pl.ds(at, 1)], sems.at[at])
             copy.start()
             steps.append(copy)
-    waves = pay_ref[:, 0:NMU]
-    left = dot(spread(True), waves)
-    right = dot(spread(False), waves)
-    real, imag = conj_product(left[32:48], left[48:64], right[0:16], right[16:32])
-    lhs[0:16, 0:NMU] = real
-    lhs[0:16, NMU : 2 * NMU] = -imag
-    lhs[16:32, 0:NMU] = imag
-    lhs[16:32, NMU : 2 * NMU] = real
-    rx_ref[...] = dot(lhs[...], z_ref[...])
     for copy in steps:
         copy.wait()
-
-
-def transitions_kernel(a0, a1, a2, y_ref):
+    whole.wait()
+
+
+def transitions_kernel(a0, a1, a2, a3, b0, b1, b2, b3, y_ref, a_ref, b_ref, sems):
+    steps = []
+    for n, source in enumerate((a1, a3, a0, a2, b0, b1, b2, b3)):
+        target = a_ref if n < 4 else b_ref
+        copy = pltpu.make_async_copy(source, target.at[pl.ds(n % 4 * 16, 16)], sems.at[n])
+        copy.start()
+        steps.append(copy)
+    for copy in steps[:4]:
+        copy.wait()
     total_re = jnp.zeros((8, NMU), F32)
     total_im = jnp.zeros((8, NMU), F32)
-    for pay in (a0[...], a1[...], a2[0:16], a2[16:32]):
-        waves = pay[:, :NMU]
-        mixed = dot(pay[:, NMU : NMU + 16], waves)
+    for m in range(4):
+        waves = a_ref[m * 16 : m * 16 + 16, 0:NMU]
+        mixed = dot(a_ref[m * 16 : m * 16 + 16, NMU : NMU + 16], waves)
         waves = waves.astype(F32)
         val_re, val_im = waves[0:8], waves[8:16]
         mix_re, mix_im = mixed[0:8], mixed[8:16]
@@ -141,21 +140,34 @@
         total_im += val_re * mix_im - val_im * mix_re
     total_re = jnp.sum(total_re, 0, keepdims=True)
     total_im = jnp.sum(total_im, 0, keepdims=True)
-    y_ref[...] = jnp.concatenate([total_re, total_im], 0)
-
-
-def pair_kernel(from_core, *refs):
-    a_near, a_pair, b0, b1, b2, b3, w_ref, z_ref, _, out_ref, lhs, xa, xb, acc, ca, cb = refs
-    a_pays = (a_near[...], a_pair[from_core : from_core + 16])
-    b_pays = (b0[...], b1[...], b2[...], b3[...])
+    for j in range(8):
+        y_ref[j : j + 1] = total_re[:, j * 128 : j * 128 + 128]
+        y_ref[8 + j : 9 + j] = total_im[:, j * 128 : j * 128 + 128]
+    for copy in steps[4:]:
+        copy.wait()
+
+
+def pair_kernel(near, *refs):
+    if near:
+        a_ref, b_ref, w_ref, z_ref, far_ref, _, out_ref, rx_ref, lhs, own, xa, xb, acc, ca, cb = refs
+    else:
+        a_ref, b_ref, w_ref, z_ref, out_ref, lhs, xa, xb, acc, ca, cb = refs
+    base = 2 * near
+    a_pays = [a_ref[(base + m) * 16 : (base + m) * 16 + 16] for m in range(2)]
+    b_pays = [b_ref[n * 16 : n * 16 + 16] for n in range(4)]
     half = 2 * ROWS
 
-    def put(row, left, right, at):
-        real, imag = conj_product(left[at : at + 16], left[at + 16 : at + 32], right[at : at + 16], right[at + 16 : at + 32])
-        lhs[row : row + 16, 0:NMU] = real
-        lhs[row : row + 16, NMU : 2 * NMU] = -imag
-        lhs[half + row : half + row + 16, 0:NMU] = imag
-        lhs[half + row : half + row + 16, NMU : 2 * NMU] = real
+    def put(to, row, top, left, right, left_at, right_at):
+        real, imag = conj_product(
+            left[left_at : left_at + 16],
+            left[left_at + 16 : left_at + 32],
+            right[right_at : right_at + 16],
+            right[right_at + 16 : right_at + 32],
+        )
+        to[row : row + 16, 0:NMU] = real
+        to[row : row + 16, NMU : 2 * NMU] = -imag
+        to[top + row : top + row + 16, 0:NMU] = imag
+        to[top + row : top + row + 16, NMU : 2 * NMU] = real
 
     rep = spread(True)
     til = spread(False)
@@ -166,18 +178,20 @@
     for m in range(2):
         for n in range(4):
             row = (m * 4 + n) * 16
-            put(row, xa[m], xb[n], 0)
-            put(ROWS + row, xa[m], xb[n], 32)
+            put(lhs, row, half, xa[m], xb[n], 0, 0)
+            put(lhs, ROWS + row, half, xa[m], xb[n], 32, 32)
+    if near:
+        put(own, 0, 16, xa[0], dot(til, a_pays[0][:, 0:NMU]), 32, 0)
     acc[...] = jnp.zeros_like(acc)
     for at in range(0, NG, CHUNK):
         z = z_ref[:, at : at + CHUNK]
         con_re = dot(lhs[0:ROWS], z)
         for p in range(8):
-            weight = w_ref[p : p + 1, at : at + CHUNK]
+            weight = w_ref[4 * base + p : 4 * base + p + 1, at : at + CHUNK]
             ca[p * 16 : p * 16 + 16, 0:CHUNK] = (con_re[p * 16 : p * 16 + 16] * weight).astype(BF16)
         con_im = dot(lhs[half : half + ROWS], z)
         for p in range(8):
-            weight = w_ref[p : p + 1, at : at + CHUNK]
+            weight = w_ref[4 * base + p : 4 * base + p + 1, at : at + CHUNK]
             ca[p * 16 : p * 16 + 16, CHUNK : 2 * CHUNK] = (con_im[p * 16 : p * 16 + 16] * weight).astype(BF16)
         val_re = dot(lhs[ROWS:half], z).astype(BF16)
         cb[0:ROWS, 0:CHUNK] = val_re
@@ -186,6 +200,8 @@
         cb[0:ROWS, CHUNK : 2 * CHUNK] = val_im
         cb[ROWS:half, 0:CHUNK] = val_im
         acc[...] += dot_t(ca[...], cb[...])
+        if near:
+            rx_ref[:, at : at + CHUNK] = dot(own[...], z)
 
     pick_row = iota((8, 16), 0)
     pick_col = iota((8, 16), 1)
@@ -238,15 +254,28 @@
     to_b = onehot(row == 4 + ((col >> 4) & 3))
     high_d, low_d = split(sum_d)
     high_h, low_h = split(sum_h)
-    out_ref[...] = dot(to_a, high_d) + dot(to_a, low_d) + dot(to_b, high_h) + dot(to_b, low_h)
-
-
-def exchange_kernel(y0, y1, y2, y3, c_ref, rx_ref, z_ref, out_ref, lhs):
+    total = dot(to_a, high_d) + dot(to_a, low_d) + dot(to_b, high_h) + dot(to_b, low_h)
+    if near:
+        total += jnp.where(iota((8, 128), 0) >= 4, far_ref[...], 0.0)
+    out_ref[...] = total
+
+
+def mail_kernel(y0, y1, y2, y3, out_ref, *mails):
     total = y0[...] + y1[...] + y2[...] + y3[...]
-    swap = jnp.concatenate([-total[1:2], total[0:1]], 0)
-    high, low = split(jnp.concatenate([total, swap], 1))
-    pad = jnp.zeros((12, 2 * NMU), F32)
-    lhs[...] = jnp.concatenate([high.astype(F32), low.astype(F32), pad], 0).astype(BF16)
+    for n, mail in enumerate(mails):
+        mail[0:16] = total
+        mail[16:24] = jnp.broadcast_to(out_ref[4 + n : 5 + n], (8, 128))
+
+
+def exchange_kernel(y_ref, c_ref, rx_ref, z_ref, out_ref, lhs):
+    pad = jnp.zeros((12, 128), F32)
+    for j in range(8):
+        real = y_ref[j : j + 1]
+        imag = y_ref[8 + j : 9 + j]
+        for at, top, bottom in ((0, real, imag), (NMU, -imag, real)):
+            high, low = split(jnp.concatenate([top, bottom], 0))
+            rows = jnp.concatenate([high.astype(F32), low.astype(F32), pad], 0)
+            lhs[:, at + j * 128 : at + j * 128 + 128] = rows.astype(BF16)
     acc_re = jnp.zeros((16, 128), F32)
     acc_im = jnp.zeros((16, 128), F32)
     for start in range(0, NG, CHUNK):
@@ -277,14 +306,19 @@
     return pl.CostEstimate(flops=2 * rows * 2 * NMU * NG, bytes_accessed=4 * NMU * NG, transcendentals=0)
 
 
-def pair_call(from_core, a_near, a_pair, b_pays, weights, basis, after):
+def pair_call(near, operands):
+    scratch = [pltpu.VMEM((4 * ROWS, 2 * NMU), BF16)]
+    out_shape = [jax.ShapeDtypeStruct((8, 128), F32)]
+    if near:
+        scratch.append(pltpu.VMEM((32, 2 * NMU), BF16))
+        out_shape.append(pltpu.VMEM((32, NG), F32))
     return pl.pallas_call(
-        functools.partial(pair_kernel, from_core),
-        in_specs=[VMEM] * 8 + [ANY],
-        out_specs=VMEM,
-        out_shape=jax.ShapeDtypeStruct((8, 128), F32),
-        scratch_shapes=[
-            pltpu.VMEM((4 * ROWS, 2 * NMU), BF16),
+        functools.partial(pair_kernel, near),
+        in_specs=[VMEM] * 4 + [VMEM, ANY] * near,
+        out_specs=[VMEM] * len(out_shape),
+        out_shape=out_shape,
+        scratch_shapes=scratch
+        + [
             pltpu.VMEM((2, 64, NMU), F32),
             pltpu.VMEM((4, 64, NMU), F32),
             pltpu.VMEM((ROWS, 2 * ROWS), F32),
@@ -293,63 +327,69 @@
         ],
         compiler_params=params(24),
         cost_estimate=cost(4 * ROWS),
-    )(a_near, a_pair, *b_pays, weights, basis, after)
+    )(*operands)
 
 
 def on_device(waves, vector, energies, basis, screening, coulomb, qmap):
-    basis = basis.reshape(2 * NMU, NG)
     pay = pl.pallas_call(
         pack_kernel,
         in_specs=[VMEM] * 2,
         out_specs=VMEM,
         out_shape=jax.ShapeDtypeStruct((16, WIDTH), BF16),
     )(waves.reshape(16, NMU), vector.reshape(2, NT))
+    a1 = move(pay, far=1)
     b0 = move(pay, step=1)
-    a1 = move(pay, far=1)
+    a2 = move(pay, core=1)
     where = jnp.stack([lax.axis_index("grp"), lax.axis_index("kin")]).astype(jnp.int32)
-    rx, far_weights, near_weights = pl.pallas_call(
-        own_kernel,
-        in_specs=[SMEM, SMEM, VMEM, VMEM, ANY],
+    z, weights = pl.pallas_call(
+        fetch_kernel,
+        in_specs=[SMEM, SMEM, ANY, ANY],
+        out_specs=[VMEM] * 2,
+        out_shape=[pltpu.VMEM((2 * NMU, NG), BF16), pltpu.VMEM((16, NG), F32)],
+        scratch_shapes=[pltpu.SemaphoreType.DMA((17,))],
+        compiler_params=params(50),
+        cost_estimate=cost(128),
+    )(where, qmap, basis.reshape(2 * NMU, NG), screening)
+    b1, b2, b3 = (move(b0, y=n) for n in (1, 2, 3))
+    a3 = move(a1, core=1)
+    y, a_all, b_all = pl.pallas_call(
+        transitions_kernel,
+        in_specs=[ANY] * 8,
         out_specs=[VMEM] * 3,
         out_shape=[
-            jax.ShapeDtypeStruct((32, NG), F32),
-            jax.ShapeDtypeStruct((8, NG), F32),
-            jax.ShapeDtypeStruct((8, NG), F32),
+            jax.ShapeDtypeStruct((16, 128), F32),
+            pltpu.VMEM((64, WIDTH), BF16),
+            pltpu.VMEM((64, WIDTH), BF16),
         ],
-        scratch_shapes=[pltpu.VMEM((32, 2 * NMU), BF16), pltpu.SemaphoreType.DMA((16,))],
-        compiler_params=params(24),
-        cost_estimate=cost(128),
-    )(where, qmap, pay, basis, screening)
-    b2 = move(b0, y=2)
-    b1 = move(b0, y=1)
-    b3 = move(b0, y=3)
-    a23 = move(jnp.concatenate([pay, a1], 0), core=1)
-    y = pl.pallas_call(
-        transitions_kernel,
-        in_specs=[VMEM] * 3,
-        out_specs=VMEM,
-        out_shape=jax.ShapeDtypeStruct((2, NMU), F32),
-    )(pay, a1, a23)
-    b_pays = (b0, b1, b2, b3)
-    far_out = pair_call(16, a1, a23, b_pays, far_weights, basis, y)
-    y = y + move(y, y=2) + move(y, y=1) + move(y, y=3)
-    near_out = pair_call(0, pay, a23, b_pays, near_weights, basis, y)
-    y = y + move(y, x=2) + move(y, x=1) + move(y, x=3)
-    others = [move(y, z=n) for n in (2, 1, 3)]
+        scratch_shapes=[pltpu.SemaphoreType.DMA((8,))],
+    )(pay, a1, a2, a3, b0, b1, b2, b3)
+    (far_out,) = pair_call(0, (a_all, b_all, weights, z))
+    far_sum = far_out[0:1] + move(far_out[1:2], core=1)
+    y = y + move(y, z=2) + move(y, z=1) + move(y, z=3)
+    near_out, rx = pair_call(1, (a_all, b_all, weights, z, far_out, y))
+    mail = pl.pallas_call(
+        mail_kernel,
+        in_specs=[VMEM] * 5,
+        out_specs=[VMEM] * 4,
+        out_shape=[jax.ShapeDtypeStruct((24, 128), F32)] * 4,
+    )(y, *(move(y, x=n) for n in (2, 1, 3)), near_out)
+    mail = mail[0] + move(mail[2], y=2) + move(mail[1], y=1) + move(mail[3], y=3)
     exchange = pl.pallas_call(
         exchange_kernel,
-        in_specs=[VMEM] * 7,
+        in_specs=[VMEM] * 4,
         out_specs=VMEM,
         out_shape=jax.ShapeDtypeStruct((2, NT), F32),
         scratch_shapes=[pltpu.VMEM((16, 2 * NMU), BF16)],
         compiler_params=params(24),
         cost_estimate=cost(128),
-    )(y, *others, coulomb.reshape(1, NG), rx, basis)
-
-    far_sum = far_out[0:1] + move(far_out[1:2], core=1)
-    herm = far_out[4:8] + near_out[4:8]
-    herm = herm[0:1] + move(herm[2:3], y=2) + move(herm[1:2], y=1) + move(herm[3:4], y=3)
-    terms = near_out[0:1] + move(near_out[1:2], core=1) + move(far_sum, far=1) + move(herm, step=3)
+    )(mail, coulomb.reshape(1, NG), rx, z)
+
+    terms = (
+        near_out[0:1]
+        + move(near_out[1:2], core=1)
+        + move(far_sum, far=1)
+        + move(mail[16:17], step=3)
+    )
     terms = terms[:, 0:32].reshape(1, 2, NT)
     scale = jnp.float32(1.0 / 256)
     return energies[:, None, :] * vector + 2.0 * scale * exchange[None] - scale * terms

time: 78.1 us -> 67.7 us (0.87)
  the two profiles are of different devices: /device:TPU:6 before, /device:TPU:1 now
where the time goes in v3:
time: 67.7 us; the launch traced here: 67.3 us
  starting transfers between devices  32.2 us (48%)
  Pallas kernels  20.8 us (31%)
  local copies, waits for them, and re-layouts  11.4 us (17%)
  other arithmetic  2.64 us (4%)
    ppermute x20, starting transfers between devices, move(): return lax.ppermute(value, ('grp', 'kin'), pairs)  32.2 us
    pallas_call x2, Pallas kernels, pair_call(): pl.pallas_call(functools.partial(pair_kernel, near), in_specs=[VMEM] * 4...  11.4 us
    unnamed x38, local copies, waits for them, and re-layouts  10.6 us
    pallas_call x1, Pallas kernels, on_device(): pl.pallas_call(fetch_kernel, in_specs=[SMEM, SMEM, ANY, ANY], out_specs=[...  3.65 us
    pallas_call x1, Pallas kernels, on_device(): pl.pallas_call(transitions_kernel, in_specs=[ANY] * 8, out_specs=[VMEM] *...  1.67 us
    pallas_call x1, Pallas kernels, on_device(): pl.pallas_call(pack_kernel, in_specs=[VMEM] * 2, out_specs=VMEM, out_shap...  1.63 us
    pallas_call x1, Pallas kernels, on_device(): pl.pallas_call(mail_kernel, in_specs=[VMEM] * 5, out_specs=[VMEM] * 4, ou...  1.38 us
  transfers between devices with their start and end apart: 20, of which 0 were waited for; matrix products, arithmetic and copies ran while one was open for 3% of the time, Pallas kernels for 26%

profile of v3, /device:TPU:1, one launch (start us, length us, event | category | flops | bytes accessed | tf_op | source)
XLA Modules:
  0.0 67.3 jit_solution(2363853643818129508)
XLA Ops:
  0.0 1.6 %shard_map.73.a0 = bf16[16,1152]{1,0:T(8,128)(2,1)} custom-call(bf16[16,1024]{1,0:T(8,128)(2,1)} %bitcast.11, f32[2,16]{1,0:T(2,128)} %bitcast.12), custom_call_target="tpu_custom_call" | custom-call | tf_op jit(solution)/shard_map/pallas_call | solution.py:334
  1.6 2.0 %collective-permute-start.3 = (bf16[16,1152]{1,0:T(8,128)(2,1)}, bf16[16,1152]{1,0:T(8,128)(2,1)S(1)}, u32[]{:S(2)}, u32[]{:S(2)}) collective-permute-start(bf16[16,1152]{1,0:T(8,128)(2,1)} %shard_map.73.a0), channel_id=1, source_target_pairs={{0,64},{1,65},{2,66},{3,67},{4,68},{5,69},{6,70},{7,71},{8,72},{9,... | collective-permute-start | bytes 110600 | tf_op jit(solution)/shard_map/ppermute | solution.py:34
  3.7 6.9 %collective-permute-start = (bf16[16,1152]{1,0:T(8,128)(2,1)}, bf16[16,1152]{1,0:T(8,128)(2,1)S(1)}, u32[]{:S(2)}, u32[]{:S(2)}) collective-permute-start(bf16[16,1152]{1,0:T(8,128)(2,1)} %shard_map.73.a0), channel_id=1, source_target_pairs={{0,8},{1,9},{2,10},{3,11},{4,12},{5,13},{6,14},{7,15},{8,0},{9,1},... | collective-permute-start | bytes 110600 | tf_op jit(solution)/shard_map/ppermute | solution.py:34
  10.6 1.2 %collective-permute-start.1 = (bf16[16,1152]{1,0:T(8,128)(2,1)}, bf16[16,1152]{1,0:T(8,128)(2,1)S(1)}, u32[]{:S(2)}, u32[]{:S(2)}) collective-permute-start(bf16[16,1152]{1,0:T(8,128)(2,1)} %shard_map.73.a0), channel_id=1, source_target_pairs={{0,1},{1,0},{2,3},{3,2},{4,5},{5,4},{6,7},{7,6},{8,9},{9,8},{10,11... | collective-permute-start | bytes 110600 | tf_op jit(solution)/shard_map/ppermute | solution.py:34
  11.8 0.6 pad_add_fusion.where_ref
  12.5 0.0 collective-permute-done.3.b0
  12.5 1.3 %collective-permute-start.4 = (bf16[16,1152]{1,0:T(8,128)(2,1)S(1)}, bf16[16,1152]{1,0:T(8,128)(2,1)S(1)}, u32[]{:S(2)}, u32[]{:S(2)}) collective-permute-start(bf16[16,1152]{1,0:T(8,128)(2,1)S(1)} %collective-permute-done.3.b0), channel_id=1, source_target_pairs={{0,2},{1,3},{2,0},{3,1},{4,6},{5,7},{6,4},{7,5},{8,10},{9,11},{10,... | collective-permute-start | bytes 110600 | tf_op jit(solution)/shard_map/ppermute | solution.py:34
  13.8 2.6 %collective-permute-start.5 = (bf16[16,1152]{1,0:T(8,128)(2,1)S(1)}, bf16[16,1152]{1,0:T(8,128)(2,1)S(1)}, u32[]{:S(2)}, u32[]{:S(2)}) collective-permute-start(bf16[16,1152]{1,0:T(8,128)(2,1)S(1)} %collective-permute-done.3.b0), channel_id=1, source_target_pairs={{0,4},{1,5},{2,6},{3,7},{4,0},{5,1},{6,2},{7,3},{8,12},{9,13},{10,... | collective-permute-start | bytes 110600 | tf_op jit(solution)/shard_map/ppermute | solution.py:34
  16.4 0.0 collective-permute-done.a1
  16.4 0.8 %collective-permute-start.2 = (bf16[16,1152]{1,0:T(8,128)(2,1)S(1)}, bf16[16,1152]{1,0:T(8,128)(2,1)S(1)}, u32[]{:S(2)}, u32[]{:S(2)}) collective-permute-start(bf16[16,1152]{1,0:T(8,128)(2,1)S(1)} %collective-permute-done.a1), channel_id=1, source_target_pairs={{0,1},{1,0},{2,3},{3,2},{4,5},{5,4},{6,7},{7,6},{8,9},{9,8},{10,11... | collective-permute-start | bytes 110600 | tf_op jit(solution)/shard_map/ppermute | solution.py:34
  17.2 3.6 %shard_map.75 = (bf16[2048,1536]{1,0:T(8,128)(2,1)S(1)}, f32[16,1536]{1,0:T(8,128)S(1)}) custom-call(s32[2]{0:T(128)} %pad_add_fusion.where_ref, s32[1,256]{1,0:T(1,128)} %qmap_ref.1, bf16[2048,1536]{1,0:T(8,128)(2,1)} %bitcast.10, f32[256,1536]{1,0:T(8,128)} %screening.1), custom_call_target="tpu_custom_call" | custom-call | flops 805306368 | bytes 6291456 | tf_op jit(solution)/shard_map/pallas_call | solution.py:344
  20.8 2.6 %copy-done = bf16[2048,1536]{1,0:T(8,128)(2,1)} copy-done((bf16[2048,1536]{1,0:T(8,128)(2,1)}, bf16[2048,1536]{1,0:T(8,128)(2,1)S(1)}, u32[]{:S(2)}) %copy-start) | copy-done | bytes 6291480
  23.5 0.0 collective-permute-done.5.b2
  23.6 0.5 copy-done.7
  24.1 0.0 copy-done.8
  24.1 0.0 copy-done.9
  24.2 0.0 copy-done.10
  24.2 0.6 copy-done.11
  24.8 1.7 %shard_map.74 = (f32[16,128]{1,0:T(8,128)}, bf16[64,1152]{1,0:T(8,128)(2,1)S(1)}, bf16[64,1152]{1,0:T(8,128)(2,1)S(1)}) custom-call(bf16[16,1152]{1,0:T(8,128)(2,1)} %shard_map.73.a0, bf16[16,1152]{1,0:T(8,128)(2,1)} %copy-done.6, bf16[16,1152]{1,0:T(8,128)(2,1)} %copy-done.7, bf16[16,1152]{1,0:T(8,128)(2,1)} %copy-done.11, bf16[16,1152]{1,0:T(8,128)(2,1)} %copy-done.5, ...), custom_call_target="tpu_custom_call" | custom-call | tf_op jit(solution)/shard_map/pallas_call | solution.py:355
  26.5 1.3 %collective-permute-start.7 = (f32[16,128]{1,0:T(8,128)}, f32[16,128]{1,0:T(8,128)S(1)}, u32[]{:S(2)}, u32[]{:S(2)}) collective-permute-start(f32[16,128]{1,0:T(8,128)} %get-tuple-element.16), channel_id=1, source_target_pairs={{0,32},{1,33},{2,34},{3,35},{4,36},{5,37},{6,38},{7,39},{8,40},{9,... | collective-permute-start | bytes 24584 | tf_op jit(solution)/shard_map/ppermute | solution.py:34
  27.7 0.7 %collective-permute-start.8 = (f32[16,128]{1,0:T(8,128)}, f32[16,128]{1,0:T(8,128)S(1)}, u32[]{:S(2)}, u32[]{:S(2)}) collective-permute-start(f32[16,128]{1,0:T(8,128)} %get-tuple-element.16), channel_id=1, source_target_pairs={{0,16},{1,17},{2,18},{3,19},{4,20},{5,21},{6,22},{7,23},{8,24},{9,... | collective-permute-start | bytes 24584 | tf_op jit(solution)/shard_map/ppermute | solution.py:34
  28.5 1.6 %collective-permute-start.9 = (f32[16,128]{1,0:T(8,128)}, f32[16,128]{1,0:T(8,128)S(1)}, u32[]{:S(2)}, u32[]{:S(2)}) collective-permute-start(f32[16,128]{1,0:T(8,128)} %get-tuple-element.16), channel_id=1, source_target_pairs={{0,48},{1,49},{2,50},{3,51},{4,52},{5,53},{6,54},{7,55},{8,56},{9,... | collective-permute-start | bytes 24584 | tf_op jit(solution)/shard_map/ppermute | solution.py:34
  30.1 2.8 %copy-done.1 = bf16[2048,1536]{1,0:T(8,128)(2,1)S(1)} copy-done((bf16[2048,1536]{1,0:T(8,128)(2,1)S(1)}, bf16[2048,1536]{1,0:T(8,128)(2,1)}, u32[]{:S(2)}) %copy-start.1) | copy-done | bytes 6291480
  32.9 5.3 %shard_map.76.refs_4_ = f32[8,128]{1,0:T(8,128)S(1)} custom-call(bf16[64,1152]{1,0:T(8,128)(2,1)S(1)} %get-tuple-element.17.refs_0_, bf16[64,1152]{1,0:T(8,128)(2,1)S(1)} %get-tuple-element.18.refs_1_, f32[16,1536]{1,0:T(8,128)S(1)} %get-tuple-element.19.refs_2_, bf16[2048,1536]{1,0:T(8,128)(2,1)S(1)} %copy-done.1), custom_call_target="tpu_custom_call" | custom-call | flops 3221225472 | bytes 6291456 | tf_op jit(solution)/shard_map/pallas_call | solution.py:315
  38.2 0.9 %collective-permute-start.17 = (f32[1,128]{1,0:T(1,128)S(1)}, f32[1,128]{1,0:T(1,128)S(1)}, u32[]{:S(2)}, u32[]{:S(2)}) collective-permute-start(f32[1,128]{1,0:T(1,128)S(1)} %slice.21), channel_id=1, source_target_pairs={{0,1},{1,0},{2,3},{3,2},{4,5},{5,4},{6,7},{7,6},{8,9},{9,8},{10,11... | collective-permute-start | bytes 1544 | tf_op jit(solution)/shard_map/ppermute | solution.py:34
  39.1 0.0 collective-permute-done.7
  39.2 2.5 %collective-permute-start.10 = (f32[16,128]{1,0:T(8,128)S(1)}, f32[16,128]{1,0:T(8,128)S(1)}, u32[]{:S(2)}, u32[]{:S(2)}) collective-permute-start(f32[16,128]{1,0:T(8,128)S(1)} %add_add_fusion.1.refs_5_.y0), channel_id=1, source_target_pairs={{0,128},{1,129},{2,130},{3,131},{4,132},{5,133},{6,134},{7,135},{8... | collective-permute-start | bytes 24584 | tf_op jit(solution)/shard_map/ppermute | solution.py:34
  41.7 0.0 collective-permute-start.11
  41.7 1.1 %collective-permute-start.12 = (f32[16,128]{1,0:T(8,128)S(1)}, f32[16,128]{1,0:T(8,128)S(1)}, u32[]{:S(2)}, u32[]{:S(2)}) collective-permute-start(f32[16,128]{1,0:T(8,128)S(1)} %add_add_fusion.1.refs_5_.y0), channel_id=1, source_target_pairs={{0,192},{1,193},{2,194},{3,195},{4,196},{5,197},{6,198},{7,199},{8... | collective-permute-start | bytes 24584 | tf_op jit(solution)/shard_map/ppermute | solution.py:34
  42.9 6.0 %shard_map.77 = (f32[8,128]{1,0:T(8,128)S(1)}, f32[32,1536]{1,0:T(8,128)S(1)}) custom-call(bf16[64,1152]{1,0:T(8,128)(2,1)S(1)} %get-tuple-element.17.refs_0_, bf16[64,1152]{1,0:T(8,128)(2,1)S(1)} %get-tuple-element.18.refs_1_, f32[16,1536]{1,0:T(8,128)S(1)} %get-tuple-element.19.refs_2_, bf16[2048,1536]{1,0:T(8,128)(2,1)S(1)} %copy-done.1, ...), custom_call_target="tpu_custom_call" | custom-call | flops 3221225472 | bytes 6291456 | tf_op jit(solution)/shard_map/pallas_call | solution.py:315
  48.9 0.6 copy-done.4
  49.6 0.5 copy-done.14
  50.1 0.0 copy-done.15
  50.1 0.0 copy-done.16
  50.1 1.4 %shard_map.78 = (f32[24,128]{1,0:T(8,128)}, f32[24,128]{1,0:T(8,128)}, f32[24,128]{1,0:T(8,128)}, f32[24,128]{1,0:T(8,128)}) custom-call(f32[16,128]{1,0:T(8,128)} %copy-done.3, f32[16,128]{1,0:T(8,128)} %copy-done.14, f32[16,128]{1,0:T(8,128)} %copy-done.15, f32[16,128]{1,0:T(8,128)} %copy-done.16, f32[8,128]{1,0:T(8,128)} %copy-done.4), custom_call_target="tpu_custom_call" | custom-call | tf_op jit(solution)/shard_map/pallas_call | solution.py:370
  51.5 1.7 %collective-permute-start.13 = (f32[24,128]{1,0:T(8,128)}, f32[24,128]{1,0:T(8,128)S(1)}, u32[]{:S(2)}, u32[]{:S(2)}) collective-permute-start(f32[24,128]{1,0:T(8,128)} %get-tuple-element.23), channel_id=1, source_target_pairs={{0,4},{1,5},{2,6},{3,7},{4,0},{5,1},{6,2},{7,3},{8,12},{9,13},{10,... | collective-permute-start | bytes 36872 | tf_op jit(solution)/shard_map/ppermute | solution.py:34
  53.2 1.6 %collective-permute-start.14 = (f32[24,128]{1,0:T(8,128)}, f32[24,128]{1,0:T(8,128)S(1)}, u32[]{:S(2)}, u32[]{:S(2)}) collective-permute-start(f32[24,128]{1,0:T(8,128)} %get-tuple-element.24), channel_id=1, source_target_pairs={{0,2},{1,3},{2,0},{3,1},{4,6},{5,7},{6,4},{7,5},{8,10},{9,11},{10,... | collective-permute-start | bytes 36872 | tf_op jit(solution)/shard_map/ppermute | solution.py:34
  54.9 2.8 %collective-permute-start.18 = (f32[1,128]{1,0:T(1,128)S(1)}, f32[1,128]{1,0:T(1,128)S(1)}, u32[]{:S(2)}, u32[]{:S(2)}) collective-permute-start(f32[1,128]{1,0:T(1,128)S(1)} %slice_add_fusion), channel_id=1, source_target_pairs={{0,8},{1,9},{2,10},{3,11},{4,12},{5,13},{6,14},{7,15},{8,0},{9,1},... | collective-permute-start | bytes 1544 | tf_op jit(solution)/shard_map/ppermute | solution.py:34
  57.7 0.7 %slice.19 = f32[1,128]{1,0:T(1,128)S(1)} slice(f32[8,128]{1,0:T(8,128)} %copy-done.4), slice={[1:2], [0:128]} | slice | bytes 1024 | tf_op jit(solution)/shard_map/slice | solution.py:389
  58.3 1.7 %collective-permute-start.16 = (f32[1,128]{1,0:T(1,128)S(1)}, f32[1,128]{1,0:T(1,128)S(1)}, u32[]{:S(2)}, u32[]{:S(2)}) collective-permute-start(f32[1,128]{1,0:T(1,128)S(1)} %slice.19), channel_id=1, source_target_pairs={{0,1},{1,0},{2,3},{3,2},{4,5},{5,4},{6,7},{7,6},{8,9},{9,8},{10,11... | collective-permute-start | bytes 1544 | tf_op jit(solution)/shard_map/ppermute | solution.py:34
  60.1 0.7 %add_add_fusion.y_ref = f32[24,128]{1,0:T(8,128)S(1)} fusion(f32[24,128]{1,0:T(8,128)S(1)} %collective-permute-done.15, f32[24,128]{1,0:T(8,128)S(1)} %collective-permute-done.14, f32[24,128]{1,0:T(8,128)} %get-tuple-element.22, f32[24,128]{1,0:T(8,128)S(1)} %collective-permute-done.13), kind=kLoop, calls=%fused_computation | loop fusion | flops 9216 | bytes 61440 | tf_op jit(solution)/shard_map/add | solution.py:376
  60.8 1.3 %collective-permute-start.19 = (f32[1,128]{1,0:T(1,128)S(1)}, f32[1,128]{1,0:T(1,128)S(1)}, u32[]{:S(2)}, u32[]{:S(2)}) collective-permute-start(f32[1,128]{1,0:T(1,128)S(1)} %slice.24), channel_id=1, source_target_pairs={{0,192},{1,193},{2,194},{3,195},{4,196},{5,197},{6,198},{7,199},{8... | collective-permute-start | bytes 1544 | tf_op jit(solution)/shard_map/ppermute | solution.py:34
  62.0 2.8 %copy-done.2 = bf16[2048,1536]{1,0:T(8,128)(2,1)S(1)} copy-done((bf16[2048,1536]{1,0:T(8,128)(2,1)S(1)}, bf16[2048,1536]{1,0:T(8,128)(2,1)}, u32[]{:S(2)}) %copy-start.2) | copy-done | bytes 6291480
  64.8 1.1 %shard_map.79 = f32[2,16]{1,0:T(2,128)S(1)} custom-call(f32[24,128]{1,0:T(8,128)S(1)} %add_add_fusion.y_ref, f32[1,1536]{1,0:T(1,128)S(1)} %reshape.34.c_ref, f32[32,1536]{1,0:T(8,128)S(1)} %get-tuple-element.26.rx_ref, bf16[2048,1536]{1,0:T(8,128)(2,1)S(1)} %copy-done.2), custom_call_target="tpu_custom_call" | custom-call | flops 805306368 | bytes 6291456 | tf_op jit(solution)/shard_map/pallas_call | solution.py:377
  65.9 0.0 collective-permute-done.19
  65.9 0.7 %add_add_fusion.2 = f32[1,128]{1,0:T(1,128)S(1)} fusion(f32[1,128]{1,0:T(1,128)S(1)} %collective-permute-done.19, f32[1,128]{1,0:T(1,128)S(1)} %collective-permute-done.18, f32[1,128]{1,0:T(1,128)S(1)} %collective-permute-done.16, f32[8,128]{1,0:T(8,128)} %copy-done.4), kind=kLoop, calls=%fused_computation.6 | loop fusion | flops 384 | bytes 2560 | tf_op jit(solution)/shard_map/add | solution.py:388
  66.6 0.1 mul.44
  66.7 0.6 fusion
  (49 shorter events, 0.1 us)
Async XLA Ops:
  0.0 23.5 %copy-start.13 = (f32[1536]{0:T(1024)S(1)}, f32[1536]{0:T(1024)}, u32[]{:S(2)}) copy-start(f32[1536]{0:T(1024)} %param.12) | copy-start | bytes 18436
  1.6 10.8 %collective-permute-start.3 = (bf16[16,1152]{1,0:T(8,128)(2,1)}, bf16[16,1152]{1,0:T(8,128)(2,1)S(1)}, u32[]{:S(2)}, u32[]{:S(2)}) collective-permute-start(bf16[16,1152]{1,0:T(8,128)(2,1)} %shard_map.73.a0), channel_id=1, source_target_pairs={{0,64},{1,65},{2,66},{3,67},{4,68},{5,69},{6,70},{7,71},{8,72},{9,... | collective-permute-start | bytes 110600 | tf_op jit(solution)/shard_map/ppermute | solution.py:34
  3.7 12.7 %collective-permute-start = (bf16[16,1152]{1,0:T(8,128)(2,1)}, bf16[16,1152]{1,0:T(8,128)(2,1)S(1)}, u32[]{:S(2)}, u32[]{:S(2)}) collective-permute-start(bf16[16,1152]{1,0:T(8,128)(2,1)} %shard_map.73.a0), channel_id=1, source_target_pairs={{0,8},{1,9},{2,10},{3,11},{4,12},{5,13},{6,14},{7,15},{8,0},{9,1},... | collective-permute-start | bytes 110600 | tf_op jit(solution)/shard_map/ppermute | solution.py:34
  10.6 12.9 %collective-permute-start.1 = (bf16[16,1152]{1,0:T(8,128)(2,1)}, bf16[16,1152]{1,0:T(8,128)(2,1)S(1)}, u32[]{:S(2)}, u32[]{:S(2)}) collective-permute-start(bf16[16,1152]{1,0:T(8,128)(2,1)} %shard_map.73.a0), channel_id=1, source_target_pairs={{0,1},{1,0},{2,3},{3,2},{4,5},{5,4},{6,7},{7,6},{8,9},{9,8},{10,11... | collective-permute-start | bytes 110600 | tf_op jit(solution)/shard_map/ppermute | solution.py:34
  12.5 11.1 %copy-start.5 = (bf16[16,1152]{1,0:T(8,128)(2,1)}, bf16[16,1152]{1,0:T(8,128)(2,1)S(1)}, u32[]{:S(2)}) copy-start(bf16[16,1152]{1,0:T(8,128)(2,1)S(1)} %collective-permute-done.3.b0) | copy-start | bytes 110596
  12.5 11.0 %collective-permute-start.4 = (bf16[16,1152]{1,0:T(8,128)(2,1)S(1)}, bf16[16,1152]{1,0:T(8,128)(2,1)S(1)}, u32[]{:S(2)}, u32[]{:S(2)}) collective-permute-start(bf16[16,1152]{1,0:T(8,128)(2,1)S(1)} %collective-permute-done.3.b0), channel_id=1, source_target_pairs={{0,2},{1,3},{2,0},{3,1},{4,6},{5,7},{6,4},{7,5},{8,10},{9,11},{10,... | collective-permute-start | bytes 110600 | tf_op jit(solution)/shard_map/ppermute | solution.py:34
  13.8 9.8 %collective-permute-start.5 = (bf16[16,1152]{1,0:T(8,128)(2,1)S(1)}, bf16[16,1152]{1,0:T(8,128)(2,1)S(1)}, u32[]{:S(2)}, u32[]{:S(2)}) collective-permute-start(bf16[16,1152]{1,0:T(8,128)(2,1)S(1)} %collective-permute-done.3.b0), channel_id=1, source_target_pairs={{0,4},{1,5},{2,6},{3,7},{4,0},{5,1},{6,2},{7,3},{8,12},{9,13},{10,... | collective-permute-start | bytes 110600 | tf_op jit(solution)/shard_map/ppermute | solution.py:34
  16.4 7.2 %collective-permute-start.6 = (bf16[16,1152]{1,0:T(8,128)(2,1)S(1)}, bf16[16,1152]{1,0:T(8,128)(2,1)S(1)}, u32[]{:S(2)}, u32[]{:S(2)}) collective-permute-start(bf16[16,1152]{1,0:T(8,128)(2,1)S(1)} %collective-permute-done.3.b0), channel_id=1, source_target_pairs={{0,6},{1,7},{2,4},{3,5},{4,2},{5,3},{6,0},{7,1},{8,14},{9,15},{10,... | collective-permute-start | bytes 110600 | tf_op jit(solution)/shard_map/ppermute | solution.py:34
  16.4 7.2 %copy-start.6 = (bf16[16,1152]{1,0:T(8,128)(2,1)}, bf16[16,1152]{1,0:T(8,128)(2,1)S(1)}, u32[]{:S(2)}) copy-start(bf16[16,1152]{1,0:T(8,128)(2,1)S(1)} %collective-permute-done.a1) | copy-start | bytes 110596
  16.4 7.2 %collective-permute-start.2 = (bf16[16,1152]{1,0:T(8,128)(2,1)S(1)}, bf16[16,1152]{1,0:T(8,128)(2,1)S(1)}, u32[]{:S(2)}, u32[]{:S(2)}) collective-permute-start(bf16[16,1152]{1,0:T(8,128)(2,1)S(1)} %collective-permute-done.a1), channel_id=1, source_target_pairs={{0,1},{1,0},{2,3},{3,2},{4,5},{5,4},{6,7},{7,6},{8,9},{9,8},{10,11... | collective-permute-start | bytes 110600 | tf_op jit(solution)/shard_map/ppermute | solution.py:34
  20.8 2.6 %copy-start = (bf16[2048,1536]{1,0:T(8,128)(2,1)}, bf16[2048,1536]{1,0:T(8,128)(2,1)S(1)}, u32[]{:S(2)}) copy-start(bf16[2048,1536]{1,0:T(8,128)(2,1)S(1)} %get-tuple-element.20.refs_3_.z_ref) | copy-start | bytes 18874372
  23.5 0.6 copy-start.7
  23.5 0.6 copy-start.8
  23.5 0.6 copy-start.9
  23.6 0.6 copy-start.10
  24.2 0.6 copy-start.11
  26.5 12.7 %copy-start.12 = (f32[16,128]{1,0:T(8,128)S(1)}, f32[16,128]{1,0:T(8,128)}, u32[]{:S(2)}) copy-start(f32[16,128]{1,0:T(8,128)} %get-tuple-element.16) | copy-start | bytes 24580
  26.5 12.6 %collective-permute-start.7 = (f32[16,128]{1,0:T(8,128)}, f32[16,128]{1,0:T(8,128)S(1)}, u32[]{:S(2)}, u32[]{:S(2)}) collective-permute-start(f32[16,128]{1,0:T(8,128)} %get-tuple-element.16), channel_id=1, source_target_pairs={{0,32},{1,33},{2,34},{3,35},{4,36},{5,37},{6,38},{7,39},{8,40},{9,... | collective-permute-start | bytes 24584 | tf_op jit(solution)/shard_map/ppermute | solution.py:34
  27.7 11.4 %collective-permute-start.8 = (f32[16,128]{1,0:T(8,128)}, f32[16,128]{1,0:T(8,128)S(1)}, u32[]{:S(2)}, u32[]{:S(2)}) collective-permute-start(f32[16,128]{1,0:T(8,128)} %get-tuple-element.16), channel_id=1, source_target_pairs={{0,16},{1,17},{2,18},{3,19},{4,20},{5,21},{6,22},{7,23},{8,24},{9,... | collective-permute-start | bytes 24584 | tf_op jit(solution)/shard_map/ppermute | solution.py:34
  28.5 10.6 %collective-permute-start.9 = (f32[16,128]{1,0:T(8,128)}, f32[16,128]{1,0:T(8,128)S(1)}, u32[]{:S(2)}, u32[]{:S(2)}) collective-permute-start(f32[16,128]{1,0:T(8,128)} %get-tuple-element.16), channel_id=1, source_target_pairs={{0,48},{1,49},{2,50},{3,51},{4,52},{5,53},{6,54},{7,55},{8,56},{9,... | collective-permute-start | bytes 24584 | tf_op jit(solution)/shard_map/ppermute | solution.py:34
  30.1 2.8 %copy-start.1 = (bf16[2048,1536]{1,0:T(8,128)(2,1)S(1)}, bf16[2048,1536]{1,0:T(8,128)(2,1)}, u32[]{:S(2)}) copy-start(bf16[2048,1536]{1,0:T(8,128)(2,1)} %copy-done) | copy-start | bytes 18874372
  38.2 16.6 %collective-permute-start.17 = (f32[1,128]{1,0:T(1,128)S(1)}, f32[1,128]{1,0:T(1,128)S(1)}, u32[]{:S(2)}, u32[]{:S(2)}) collective-permute-start(f32[1,128]{1,0:T(1,128)S(1)} %slice.21), channel_id=1, source_target_pairs={{0,1},{1,0},{2,3},{3,2},{4,5},{5,4},{6,7},{7,6},{8,9},{9,8},{10,11... | collective-permute-start | bytes 1544 | tf_op jit(solution)/shard_map/ppermute | solution.py:34
  39.2 10.4 %copy-start.3 = (f32[16,128]{1,0:T(8,128)}, f32[16,128]{1,0:T(8,128)S(1)}, u32[]{:S(2)}) copy-start(f32[16,128]{1,0:T(8,128)S(1)} %add_add_fusion.1.refs_5_.y0) | copy-start | bytes 24580
  39.2 10.4 %collective-permute-start.10 = (f32[16,128]{1,0:T(8,128)S(1)}, f32[16,128]{1,0:T(8,128)S(1)}, u32[]{:S(2)}, u32[]{:S(2)}) collective-permute-start(f32[16,128]{1,0:T(8,128)S(1)} %add_add_fusion.1.refs_5_.y0), channel_id=1, source_target_pairs={{0,128},{1,129},{2,130},{3,131},{4,132},{5,133},{6,134},{7,135},{8... | collective-permute-start | bytes 24584 | tf_op jit(solution)/shard_map/ppermute | solution.py:34
  41.7 7.8 %collective-permute-start.11 = (f32[16,128]{1,0:T(8,128)S(1)}, f32[16,128]{1,0:T(8,128)S(1)}, u32[]{:S(2)}, u32[]{:S(2)}) collective-permute-start(f32[16,128]{1,0:T(8,128)S(1)} %add_add_fusion.1.refs_5_.y0), channel_id=1, source_target_pairs={{0,64},{1,65},{2,66},{3,67},{4,68},{5,69},{6,70},{7,71},{8,72},{9,... | collective-permute-start | bytes 24584 | tf_op jit(solution)/shard_map/ppermute | solution.py:34
  41.7 7.8 %collective-permute-start.12 = (f32[16,128]{1,0:T(8,128)S(1)}, f32[16,128]{1,0:T(8,128)S(1)}, u32[]{:S(2)}, u32[]{:S(2)}) collective-permute-start(f32[16,128]{1,0:T(8,128)S(1)} %add_add_fusion.1.refs_5_.y0), channel_id=1, source_target_pairs={{0,192},{1,193},{2,194},{3,195},{4,196},{5,197},{6,198},{7,199},{8... | collective-permute-start | bytes 24584 | tf_op jit(solution)/shard_map/ppermute | solution.py:34
  48.9 0.6 copy-start.4
  49.5 17.2 %copy-start.17 = (f32[1,2,16]{2,1,0:T(2,128)S(1)}, f32[1,2,16]{2,1,0:T(2,128)}, u32[]{:S(2)}) copy-start(f32[1,2,16]{2,1,0:T(2,128)} %param.8) | copy-start | bytes 388
  49.5 17.2 %copy-start.18 = (f32[1,16]{1,0:T(1,128)S(1)}, f32[1,16]{1,0:T(1,128)}, u32[]{:S(2)}) copy-start(f32[1,16]{1,0:T(1,128)} %param.9) | copy-start | bytes 196
  49.5 0.6 copy-start.14
  49.5 0.6 copy-start.15
  49.6 0.6 copy-start.16
  51.5 8.5 %collective-permute-start.13 = (f32[24,128]{1,0:T(8,128)}, f32[24,128]{1,0:T(8,128)S(1)}, u32[]{:S(2)}, u32[]{:S(2)}) collective-permute-start(f32[24,128]{1,0:T(8,128)} %get-tuple-element.23), channel_id=1, source_target_pairs={{0,4},{1,5},{2,6},{3,7},{4,0},{5,1},{6,2},{7,3},{8,12},{9,13},{10,... | collective-permute-start | bytes 36872 | tf_op jit(solution)/shard_map/ppermute | solution.py:34
  53.2 6.8 %collective-permute-start.14 = (f32[24,128]{1,0:T(8,128)}, f32[24,128]{1,0:T(8,128)S(1)}, u32[]{:S(2)}, u32[]{:S(2)}) collective-permute-start(f32[24,128]{1,0:T(8,128)} %get-tuple-element.24), channel_id=1, source_target_pairs={{0,2},{1,3},{2,0},{3,1},{4,6},{5,7},{6,4},{7,5},{8,10},{9,11},{10,... | collective-permute-start | bytes 36872 | tf_op jit(solution)/shard_map/ppermute | solution.py:34
  54.8 5.2 %collective-permute-start.15 = (f32[24,128]{1,0:T(8,128)}, f32[24,128]{1,0:T(8,128)S(1)}, u32[]{:S(2)}, u32[]{:S(2)}) collective-permute-start(f32[24,128]{1,0:T(8,128)} %get-tuple-element.25), channel_id=1, source_target_pairs={{0,6},{1,7},{2,4},{3,5},{4,2},{5,3},{6,0},{7,1},{8,14},{9,15},{10,... | collective-permute-start | bytes 36872 | tf_op jit(solution)/shard_map/ppermute | solution.py:34
  54.9 11.1 %collective-permute-start.18 = (f32[1,128]{1,0:T(1,128)S(1)}, f32[1,128]{1,0:T(1,128)S(1)}, u32[]{:S(2)}, u32[]{:S(2)}) collective-permute-start(f32[1,128]{1,0:T(1,128)S(1)} %slice_add_fusion), channel_id=1, source_target_pairs={{0,8},{1,9},{2,10},{3,11},{4,12},{5,13},{6,14},{7,15},{8,0},{9,1},... | collective-permute-start | bytes 1544 | tf_op jit(solution)/shard_map/ppermute | solution.py:34
  58.3 7.6 %collective-permute-start.16 = (f32[1,128]{1,0:T(1,128)S(1)}, f32[1,128]{1,0:T(1,128)S(1)}, u32[]{:S(2)}, u32[]{:S(2)}) collective-permute-start(f32[1,128]{1,0:T(1,128)S(1)} %slice.19), channel_id=1, source_target_pairs={{0,1},{1,0},{2,3},{3,2},{4,5},{5,4},{6,7},{7,6},{8,9},{9,8},{10,11... | collective-permute-start | bytes 1544 | tf_op jit(solution)/shard_map/ppermute | solution.py:34
  60.8 5.1 %collective-permute-start.19 = (f32[1,128]{1,0:T(1,128)S(1)}, f32[1,128]{1,0:T(1,128)S(1)}, u32[]{:S(2)}, u32[]{:S(2)}) collective-permute-start(f32[1,128]{1,0:T(1,128)S(1)} %slice.24), channel_id=1, source_target_pairs={{0,192},{1,193},{2,194},{3,195},{4,196},{5,197},{6,198},{7,199},{8... | collective-permute-start | bytes 1544 | tf_op jit(solution)/shard_map/ppermute | solution.py:34
  62.0 2.8 %copy-start.2 = (bf16[2048,1536]{1,0:T(8,128)(2,1)S(1)}, bf16[2048,1536]{1,0:T(8,128)(2,1)}, u32[]{:S(2)}) copy-start(bf16[2048,1536]{1,0:T(8,128)(2,1)} %copy-done) | copy-start | bytes 18874372

commit v4 on v3

--- a/solution.py
+++ b/solution.py
@@ -74,7 +74,14 @@
     return real, imag
 
 
-def pack_kernel(waves_ref, vector_ref, pay_ref):
+def pack_kernel(waves, vector, pay_ref, vector_ref, sems):
+    copies = (
+        pltpu.make_async_copy(vector, vector_ref, sems.at[0]),
+        pltpu.make_async_copy(waves, pay_ref.at[:, pl.ds(0, NMU)], sems.at[1]),
+    )
+    for copy in copies:
+        copy.start()
+    copies[0].wait()
     coarse = vector_ref[...].astype(BF16).astype(F32)
     real = jnp.broadcast_to(coarse[0:1], (16, 16))
     imag = jnp.broadcast_to(coarse[1:2], (16, 16))
@@ -94,8 +101,8 @@
     row = iota((16, 128), 0)
     lane = iota((16, 128), 1)
     block = dot(mixer, onehot(lane == row)) + dot(line_re, onehot(lane == row + 16)) + dot(line_im, onehot(lane == row + 32))
-    pay_ref[:, 0:NMU] = waves_ref[...]
     pay_ref[:, NMU:WIDTH] = block.astype(BF16)
+    copies[1].wait()
 
 
 def fetch_kernel(where_ref, qmap_ref, basis, screening, z_ref, w_ref, sems):
@@ -119,20 +126,12 @@
     whole.wait()
 
 
-def transitions_kernel(a0, a1, a2, a3, b0, b1, b2, b3, y_ref, a_ref, b_ref, sems):
-    steps = []
-    for n, source in enumerate((a1, a3, a0, a2, b0, b1, b2, b3)):
-        target = a_ref if n < 4 else b_ref
-        copy = pltpu.make_async_copy(source, target.at[pl.ds(n % 4 * 16, 16)], sems.at[n])
-        copy.start()
-        steps.append(copy)
-    for copy in steps[:4]:
-        copy.wait()
+def transitions_kernel(a0, a1, a2, a3, y_ref):
     total_re = jnp.zeros((8, NMU), F32)
     total_im = jnp.zeros((8, NMU), F32)
-    for m in range(4):
-        waves = a_ref[m * 16 : m * 16 + 16, 0:NMU]
-        mixed = dot(a_ref[m * 16 : m * 16 + 16, NMU : NMU + 16], waves)
+    for pay in (a0, a1, a2, a3):
+        waves = pay[:, 0:NMU]
+        mixed = dot(pay[:, NMU : NMU + 16], waves)
         waves = waves.astype(F32)
         val_re, val_im = waves[0:8], waves[8:16]
         mix_re, mix_im = mixed[0:8], mixed[8:16]
@@ -143,18 +142,16 @@
     for j in range(8):
         y_ref[j : j + 1] = total_re[:, j * 128 : j * 128 + 128]
         y_ref[8 + j : 9 + j] = total_im[:, j * 128 : j * 128 + 128]
-    for copy in steps[4:]:
-        copy.wait()
 
 
 def pair_kernel(near, *refs):
     if near:
-        a_ref, b_ref, w_ref, z_ref, far_ref, _, out_ref, rx_ref, lhs, own, xa, xb, acc, ca, cb = refs
+        w_ref, z_ref, far_ref, _, out_ref, rx_ref, lhs, own, xa, xb, acc, ca, cb = refs[6:]
     else:
-        a_ref, b_ref, w_ref, z_ref, out_ref, lhs, xa, xb, acc, ca, cb = refs
+        w_ref, z_ref, _, out_ref, lhs, xa, xb, acc, ca, cb = refs[6:]
     base = 2 * near
-    a_pays = [a_ref[(base + m) * 16 : (base + m) * 16 + 16] for m in range(2)]
-    b_pays = [b_ref[n * 16 : n * 16 + 16] for n in range(4)]
+    a_pays = refs[0:2]
+    b_pays = refs[2:6]
     half = 2 * ROWS
 
     def put(to, row, top, left, right, left_at, right_at):
@@ -298,6 +295,18 @@
     out_ref[...] = jnp.concatenate(out, 0)
 
 
+def final_kernel(energy_ref, vector_ref, exchange_ref, near_ref, d0, d1, d2, out_ref):
+    scale = 1.0 / 256
+    terms = near_ref[0:1] + d0[...] + d1[...] + d2[...]
+    for part in range(2):
+        term = terms[:, part * NT : part * NT + NT]
+        out_ref[part : part + 1] = (
+            energy_ref[...] * vector_ref[part : part + 1]
+            + (2.0 * scale) * exchange_ref[part : part + 1]
+            - scale * term
+        )
+
+
 def params(mib):
     return pltpu.CompilerParams(vmem_limit_bytes=mib * 1024 * 1024)
 
@@ -314,7 +323,7 @@
         out_shape.append(pltpu.VMEM((32, NG), F32))
     return pl.pallas_call(
         functools.partial(pair_kernel, near),
-        in_specs=[VMEM] * 4 + [VMEM, ANY] * near,
+        in_specs=[VMEM] * 8 + [VMEM] * near + [ANY],
         out_specs=[VMEM] * len(out_shape),
         out_shape=out_shape,
         scratch_shapes=scratch
@@ -333,9 +342,11 @@
 def on_device(waves, vector, energies, basis, screening, coulomb, qmap):
     pay = pl.pallas_call(
         pack_kernel,
-        in_specs=[VMEM] * 2,
+        in_specs=[ANY] * 2,
         out_specs=VMEM,
-        out_shape=jax.ShapeDtypeStruct((16, WIDTH), BF16),
+        out_shape=pltpu.VMEM((16, WIDTH), BF16),
+        scratch_shapes=[pltpu.VMEM((2, NT), F32), pltpu.SemaphoreType.DMA((2,))],
+        compiler_params=params(56),
     )(waves.reshape(16, NMU), vector.reshape(2, NT))
     a1 = move(pay, far=1)
     b0 = move(pay, step=1)
@@ -352,26 +363,24 @@
     )(where, qmap, basis.reshape(2 * NMU, NG), screening)
     b1, b2, b3 = (move(b0, y=n) for n in (1, 2, 3))
     a3 = move(a1, core=1)
-    y, a_all, b_all = pl.pallas_call(
+    y = pl.pallas_call(
         transitions_kernel,
-        in_specs=[ANY] * 8,
-        out_specs=[VMEM] * 3,
-        out_shape=[
-            jax.ShapeDtypeStruct((16, 128), F32),
-            pltpu.VMEM((64, WIDTH), BF16),
-            pltpu.VMEM((64, WIDTH), BF16),
-        ],
-        scratch_shapes=[pltpu.SemaphoreType.DMA((8,))],
-    )(pay, a1, a2, a3, b0, b1, b2, b3)
-    (far_out,) = pair_call(0, (a_all, b_all, weights, z))
+        in_specs=[VMEM] * 4,
+        out_specs=VMEM,
+        out_shape=jax.ShapeDtypeStruct((16, 128), F32),
+        compiler_params=params(8),
+    )(pay, a1, a2, a3)
+    b_pays = (b0, b1, b2, b3)
+    (far_out,) = pair_call(0, (a1, a3, *b_pays, weights, z, y))
     far_sum = far_out[0:1] + move(far_out[1:2], core=1)
     y = y + move(y, z=2) + move(y, z=1) + move(y, z=3)
-    near_out, rx = pair_call(1, (a_all, b_all, weights, z, far_out, y))
+    near_out, rx = pair_call(1, (pay, a2, *b_pays, weights, z, far_out, y))
     mail = pl.pallas_call(
         mail_kernel,
         in_specs=[VMEM] * 5,
         out_specs=[VMEM] * 4,
         out_shape=[jax.ShapeDtypeStruct((24, 128), F32)] * 4,
+        compiler_params=params(4),
     )(y, *(move(y, x=n) for n in (2, 1, 3)), near_out)
     mail = mail[0] + move(mail[2], y=2) + move(mail[1], y=1) + move(mail[3], y=3)
     exchange = pl.pallas_call(
@@ -384,15 +393,22 @@
         cost_estimate=cost(128),
     )(mail, coulomb.reshape(1, NG), rx, z)
 
-    terms = (
-        near_out[0:1]
-        + move(near_out[1:2], core=1)
-        + move(far_sum, far=1)
-        + move(mail[16:17], step=3)
+    out = pl.pallas_call(
+        final_kernel,
+        in_specs=[VMEM] * 7,
+        out_specs=VMEM,
+        out_shape=jax.ShapeDtypeStruct((2, NT), F32),
+        compiler_params=params(4),
+    )(
+        energies,
+        vector.reshape(2, NT),
+        exchange,
+        near_out,
+        move(near_out[1:2], core=1),
+        move(far_sum, far=1),
+        move(mail[16:17], step=3),
     )
-    terms = terms[:, 0:32].reshape(1, 2, NT)
-    scale = jnp.float32(1.0 / 256)
-    return energies[:, None, :] * vector + 2.0 * scale * exchange[None] - scale * terms
+    return out.reshape(1, 2, NT)
 
 
 def solution(mesh):

time: 67.7 us -> 54.5 us (0.81)
  the two profiles are of different devices: /device:TPU:1 before, /device:TPU:6 now
where the time goes in v4:
time: 54.5 us; the launch traced here: 54.4 us
  starting transfers between devices  26.4 us (48%)
  Pallas kernels  16.9 us (31%)
  waiting for transfers between devices  10.3 us (19%)
  other arithmetic  0.6 us (1%)
    ppermute x20, starting transfers between devices, move(): return lax.ppermute(value, ('grp', 'kin'), pairs)  26.4 us
    pallas_call x2, Pallas kernels, pair_call(): pl.pallas_call(functools.partial(pair_kernel, near), in_specs=[VMEM] * 8...  10.4 us
    ppermute x20, waiting for transfers between devices, move(): return lax.ppermute(value, ('grp', 'kin'), pairs)  10.3 us
    pallas_call x1, Pallas kernels, on_device(): pl.pallas_call(fetch_kernel, in_specs=[SMEM, SMEM, ANY, ANY], out_specs=[...  3.63 us
  transfers between devices with their start and end apart: 20, of which 6 were waited for; matrix products, arithmetic and copies ran while one was open for 1% of the time, Pallas kernels for 28%

profile of v4, /device:TPU:6, one launch (start us, length us, event | category | flops | bytes accessed | tf_op | source)
XLA Modules:
  0.0 54.4 jit_solution(16714952929811025978)
XLA Ops:
  0.0 1.0 %shard_map.73.a0.refs_0_ = bf16[16,1152]{1,0:T(8,128)(2,1)S(1)} custom-call(bf16[16,1024]{1,0:T(8,128)(2,1)} %bitcast.9, f32[2,16]{1,0:T(2,128)} %bitcast.6), custom_call_target="tpu_custom_call" | custom-call | tf_op jit(solution)/shard_map/pallas_call | solution.py:343
  1.0 7.3 %collective-permute-start = (bf16[16,1152]{1,0:T(8,128)(2,1)S(1)}, bf16[16,1152]{1,0:T(8,128)(2,1)S(1)}, u32[]{:S(2)}, u32[]{:S(2)}) collective-permute-start(bf16[16,1152]{1,0:T(8,128)(2,1)S(1)} %shard_map.73.a0.refs_0_), channel_id=1, source_target_pairs={{0,8},{1,9},{2,10},{3,11},{4,12},{5,13},{6,14},{7,15},{8,0},{9,1},... | collective-permute-start | bytes 110600 | tf_op jit(solution)/shard_map/ppermute | solution.py:34
  8.2 0.0 collective-permute-start.1
  8.3 0.5 collective-permute-start.9
  8.7 0.6 %pad_add_fusion.where_ref = s32[2]{0:T(128)} fusion(s32[1]{0:T(128)} %bitcast.3, s32[1]{0:T(128)} %bitcast.2), kind=kLoop, calls=%fused_computation.2 | loop fusion | flops 2 | bytes 16 | tf_op jit(solution)/shard_map/stack | solution.py:354
  9.3 2.9 %collective-permute-done.9.refs_2_ = bf16[16,1152]{1,0:T(8,128)(2,1)S(1)} collective-permute-done((bf16[16,1152]{1,0:T(8,128)(2,1)S(1)}, bf16[16,1152]{1,0:T(8,128)(2,1)S(1)}, u32[]{:S(2)}, u32[]{:S(2)}) %collective-permute-start.9) | collective-permute-done | bytes 36896 | tf_op jit(solution)/shard_map/ppermute | solution.py:34
  12.2 1.6 %collective-permute-start.10 = (bf16[16,1152]{1,0:T(8,128)(2,1)S(1)}, bf16[16,1152]{1,0:T(8,128)(2,1)S(1)}, u32[]{:S(2)}, u32[]{:S(2)}) collective-permute-start(bf16[16,1152]{1,0:T(8,128)(2,1)S(1)} %collective-permute-done.9.refs_2_), channel_id=1, source_target_pairs={{0,2},{1,3},{2,0},{3,1},{4,6},{5,7},{6,4},{7,5},{8,10},{9,11},{10,... | collective-permute-start | bytes 110600 | tf_op jit(solution)/shard_map/ppermute | solution.py:34
  13.8 2.9 %collective-permute-start.11 = (bf16[16,1152]{1,0:T(8,128)(2,1)S(1)}, bf16[16,1152]{1,0:T(8,128)(2,1)S(1)}, u32[]{:S(2)}, u32[]{:S(2)}) collective-permute-start(bf16[16,1152]{1,0:T(8,128)(2,1)S(1)} %collective-permute-done.9.refs_2_), channel_id=1, source_target_pairs={{0,4},{1,5},{2,6},{3,7},{4,0},{5,1},{6,2},{7,3},{8,12},{9,13},{10,... | collective-permute-start | bytes 110600 | tf_op jit(solution)/shard_map/ppermute | solution.py:34
  16.7 0.2 collective-permute-start.12
  16.9 0.0 collective-permute-done.a1.refs_0_
  16.9 0.0 collective-permute-start.2
  16.9 3.6 %shard_map.75 = (bf16[2048,1536]{1,0:T(8,128)(2,1)S(1)}, f32[16,1536]{1,0:T(8,128)S(1)}) custom-call(s32[2]{0:T(128)} %pad_add_fusion.where_ref, s32[1,256]{1,0:T(1,128)} %qmap_ref.1, bf16[2048,1536]{1,0:T(8,128)(2,1)} %bitcast.8, f32[256,1536]{1,0:T(8,128)} %screening.1), custom_call_target="tpu_custom_call" | custom-call | flops 805306368 | bytes 6291456 | tf_op jit(solution)/shard_map/pallas_call | solution.py:355
  20.6 0.0 collective-permute-done.1.a2.refs_1_
  20.6 0.0 collective-permute-done.2.a3.refs_1_
  20.6 0.2 shard_map.74.refs_8_
  20.8 1.6 %collective-permute-start.3 = (f32[16,128]{1,0:T(8,128)S(1)}, f32[16,128]{1,0:T(8,128)S(1)}, u32[]{:S(2)}, u32[]{:S(2)}) collective-permute-start(f32[16,128]{1,0:T(8,128)S(1)} %shard_map.74.refs_8_), channel_id=1, source_target_pairs={{0,32},{1,33},{2,34},{3,35},{4,36},{5,37},{6,38},{7,39},{8,40},{9,... | collective-permute-start | bytes 24584 | tf_op jit(solution)/shard_map/ppermute | solution.py:34
  22.4 1.0 %collective-permute-start.4 = (f32[16,128]{1,0:T(8,128)S(1)}, f32[16,128]{1,0:T(8,128)S(1)}, u32[]{:S(2)}, u32[]{:S(2)}) collective-permute-start(f32[16,128]{1,0:T(8,128)S(1)} %shard_map.74.refs_8_), channel_id=1, source_target_pairs={{0,16},{1,17},{2,18},{3,19},{4,20},{5,21},{6,22},{7,23},{8,24},{9,... | collective-permute-start | bytes 24584 | tf_op jit(solution)/shard_map/ppermute | solution.py:34
  23.4 0.0 collective-permute-done.10.refs_3_
  23.4 1.9 %collective-permute-start.5 = (f32[16,128]{1,0:T(8,128)S(1)}, f32[16,128]{1,0:T(8,128)S(1)}, u32[]{:S(2)}, u32[]{:S(2)}) collective-permute-start(f32[16,128]{1,0:T(8,128)S(1)} %shard_map.74.refs_8_), channel_id=1, source_target_pairs={{0,48},{1,49},{2,50},{3,51},{4,52},{5,53},{6,54},{7,55},{8,56},{9,... | collective-permute-start | bytes 24584 | tf_op jit(solution)/shard_map/ppermute | solution.py:34
  25.3 0.0 collective-permute-done.11.refs_4_
  25.3 0.0 collective-permute-done.12.refs_5_
  25.3 4.9 %shard_map.76.refs_8_ = f32[8,128]{1,0:T(8,128)S(1)} custom-call(bf16[16,1152]{1,0:T(8,128)(2,1)S(1)} %collective-permute-done.a1.refs_0_, bf16[16,1152]{1,0:T(8,128)(2,1)S(1)} %collective-permute-done.2.a3.refs_1_, bf16[16,1152]{1,0:T(8,128)(2,1)S(1)} %collective-permute-done.9.refs_2_, bf16[16,1152]{1,0:T(8,128)(2,1)S(1)} %collective-permute-done.10.refs_3_, ...), custom_call_target="tpu_custom_call" | custom-call | flops 3221225472 | bytes 6291456 | tf_op jit(solution)/shard_map/pallas_call | solution.py:324
  30.2 0.0 collective-permute-start.17
  30.2 0.0 collective-permute-done.3
  30.2 0.0 collective-permute-done.4
  30.2 0.0 collective-permute-done.5
  30.3 1.5 %collective-permute-start.6 = (f32[16,128]{1,0:T(8,128)S(1)}, f32[16,128]{1,0:T(8,128)S(1)}, u32[]{:S(2)}, u32[]{:S(2)}) collective-permute-start(f32[16,128]{1,0:T(8,128)S(1)} %add_add_fusion.1.refs_9_.y0), channel_id=1, source_target_pairs={{0,128},{1,129},{2,130},{3,131},{4,132},{5,133},{6,134},{7,135},{8... | collective-permute-start | bytes 24584 | tf_op jit(solution)/shard_map/ppermute | solution.py:34
  31.8 1.1 %collective-permute-start.7 = (f32[16,128]{1,0:T(8,128)S(1)}, f32[16,128]{1,0:T(8,128)S(1)}, u32[]{:S(2)}, u32[]{:S(2)}) collective-permute-start(f32[16,128]{1,0:T(8,128)S(1)} %add_add_fusion.1.refs_9_.y0), channel_id=1, source_target_pairs={{0,64},{1,65},{2,66},{3,67},{4,68},{5,69},{6,70},{7,71},{8,72},{9,... | collective-permute-start | bytes 24584 | tf_op jit(solution)/shard_map/ppermute | solution.py:34
  32.9 1.5 %collective-permute-start.8 = (f32[16,128]{1,0:T(8,128)S(1)}, f32[16,128]{1,0:T(8,128)S(1)}, u32[]{:S(2)}, u32[]{:S(2)}) collective-permute-start(f32[16,128]{1,0:T(8,128)S(1)} %add_add_fusion.1.refs_9_.y0), channel_id=1, source_target_pairs={{0,192},{1,193},{2,194},{3,195},{4,196},{5,197},{6,198},{7,199},{8... | collective-permute-start | bytes 24584 | tf_op jit(solution)/shard_map/ppermute | solution.py:34
  34.5 5.5 %shard_map.77 = (f32[8,128]{1,0:T(8,128)S(1)}, f32[32,1536]{1,0:T(8,128)S(1)}) custom-call(bf16[16,1152]{1,0:T(8,128)(2,1)S(1)} %shard_map.73.a0.refs_0_, bf16[16,1152]{1,0:T(8,128)(2,1)S(1)} %collective-permute-done.1.a2.refs_1_, bf16[16,1152]{1,0:T(8,128)(2,1)S(1)} %collective-permute-done.9.refs_2_, bf16[16,1152]{1,0:T(8,128)(2,1)S(1)} %collective-permute-done.10.refs_3_, ...), custom_call_target="tpu_custom_call" | custom-call | flops 3221225472 | bytes 6291456 | tf_op jit(solution)/shard_map/pallas_call | solution.py:324
  40.0 0.0 collective-permute-done.6.y1
  40.0 0.0 collective-permute-done.7.y2
  40.0 0.0 collective-permute-done.8.y3
  40.0 2.1 %collective-permute-start.13 = (f32[24,128]{1,0:T(8,128)S(1)}, f32[24,128]{1,0:T(8,128)S(1)}, u32[]{:S(2)}, u32[]{:S(2)}) collective-permute-start(f32[24,128]{1,0:T(8,128)S(1)} %get-tuple-element.17), channel_id=1, source_target_pairs={{0,4},{1,5},{2,6},{3,7},{4,0},{5,1},{6,2},{7,3},{8,12},{9,13},{10,... | collective-permute-start | bytes 36872 | tf_op jit(solution)/shard_map/ppermute | solution.py:34
  42.1 1.9 %collective-permute-start.14 = (f32[24,128]{1,0:T(8,128)S(1)}, f32[24,128]{1,0:T(8,128)S(1)}, u32[]{:S(2)}, u32[]{:S(2)}) collective-permute-start(f32[24,128]{1,0:T(8,128)S(1)} %get-tuple-element.18), channel_id=1, source_target_pairs={{0,2},{1,3},{2,0},{3,1},{4,6},{5,7},{6,4},{7,5},{8,10},{9,11},{10,... | collective-permute-start | bytes 36872 | tf_op jit(solution)/shard_map/ppermute | solution.py:34
  44.0 0.2 collective-permute-start.15
  44.2 0.0 collective-permute-done.17
  44.2 0.2 collective-permute-start.18
  44.4 0.0 collective-permute-start.16
  44.4 0.9 %collective-permute-done.13 = f32[24,128]{1,0:T(8,128)S(1)} collective-permute-done((f32[24,128]{1,0:T(8,128)S(1)}, f32[24,128]{1,0:T(8,128)S(1)}, u32[]{:S(2)}, u32[]{:S(2)}) %collective-permute-start.13) | collective-permute-done | bytes 12320 | tf_op jit(solution)/shard_map/ppermute | solution.py:34
  45.3 0.5 collective-permute-done.14
  45.8 3.1 %collective-permute-done.15 = f32[24,128]{1,0:T(8,128)S(1)} collective-permute-done((f32[24,128]{1,0:T(8,128)S(1)}, f32[24,128]{1,0:T(8,128)S(1)}, u32[]{:S(2)}, u32[]{:S(2)}) %collective-permute-start.15) | collective-permute-done | bytes 12320 | tf_op jit(solution)/shard_map/ppermute | solution.py:34
  48.9 0.9 %collective-permute-start.19 = (f32[1,128]{1,0:T(1,128)S(1)}, f32[1,128]{1,0:T(1,128)S(1)}, u32[]{:S(2)}, u32[]{:S(2)}) collective-permute-start(f32[1,128]{1,0:T(1,128)S(1)} %slice.16), channel_id=1, source_target_pairs={{0,192},{1,193},{2,194},{3,195},{4,196},{5,197},{6,198},{7,199},{8... | collective-permute-start | bytes 1544 | tf_op jit(solution)/shard_map/ppermute | solution.py:34
  49.8 1.1 %shard_map.79.exchange_ref = f32[2,16]{1,0:T(2,128)S(1)} custom-call(f32[24,128]{1,0:T(8,128)S(1)} %add_add_fusion.y_ref, f32[1,1536]{1,0:T(1,128)S(1)} %reshape.19.c_ref, f32[32,1536]{1,0:T(8,128)S(1)} %get-tuple-element.20.rx_ref, bf16[2048,1536]{1,0:T(8,128)(2,1)S(1)} %get-tuple-element.14.refs_7_.z_ref), custom_call_target="tpu_custom_call" | custom-call | flops 805306368 | bytes 6291456 | tf_op jit(solution)/shard_map/pallas_call | solution.py:386
  50.9 0.8 %collective-permute-done.18.d1 = f32[1,128]{1,0:T(1,128)S(1)} collective-permute-done((f32[1,128]{1,0:T(1,128)S(1)}, f32[1,128]{1,0:T(1,128)S(1)}, u32[]{:S(2)}, u32[]{:S(2)}) %collective-permute-start.18) | collective-permute-done | bytes 544 | tf_op jit(solution)/shard_map/ppermute | solution.py:34
  51.7 0.0 collective-permute-done.16.d0
  51.7 2.1 %collective-permute-done.19.d2 = f32[1,128]{1,0:T(1,128)S(1)} collective-permute-done((f32[1,128]{1,0:T(1,128)S(1)}, f32[1,128]{1,0:T(1,128)S(1)}, u32[]{:S(2)}, u32[]{:S(2)}) %collective-permute-start.19) | collective-permute-done | bytes 544 | tf_op jit(solution)/shard_map/ppermute | solution.py:34
  53.7 0.6 %shard_map.80 = f32[2,16]{1,0:T(2,128)} custom-call(f32[1,16]{1,0:T(1,128)S(1)} %copy-done.1, f32[2,16]{1,0:T(2,128)S(1)} %bitcast.7, f32[2,16]{1,0:T(2,128)S(1)} %shard_map.79.exchange_ref, f32[8,128]{1,0:T(8,128)S(1)} %get-tuple-element.15.out_ref.near_ref, f32[1,128]{1,0:T(1,128)S(1)} %collective-permute-done.16.d0, ...), custom_call_target="tpu_custom_call" | custom-call | tf_op jit(solution)/shard_map/pallas_call | solution.py:396
  (14 shorter events, 0.1 us)
Async XLA Ops:
  0.0 20.6 %copy-start.2 = (f32[1536]{0:T(1024)S(1)}, f32[1536]{0:T(1024)}, u32[]{:S(2)}) copy-start(f32[1536]{0:T(1024)} %param.12) | copy-start | bytes 18436
  1.0 15.9 %collective-permute-start = (bf16[16,1152]{1,0:T(8,128)(2,1)S(1)}, bf16[16,1152]{1,0:T(8,128)(2,1)S(1)}, u32[]{:S(2)}, u32[]{:S(2)}) collective-permute-start(bf16[16,1152]{1,0:T(8,128)(2,1)S(1)} %shard_map.73.a0.refs_0_), channel_id=1, source_target_pairs={{0,8},{1,9},{2,10},{3,11},{4,12},{5,13},{6,14},{7,15},{8,0},{9,1},... | collective-permute-start | bytes 110600 | tf_op jit(solution)/shard_map/ppermute | solution.py:34
  8.2 12.3 %collective-permute-start.1 = (bf16[16,1152]{1,0:T(8,128)(2,1)S(1)}, bf16[16,1152]{1,0:T(8,128)(2,1)S(1)}, u32[]{:S(2)}, u32[]{:S(2)}) collective-permute-start(bf16[16,1152]{1,0:T(8,128)(2,1)S(1)} %shard_map.73.a0.refs_0_), channel_id=1, source_target_pairs={{0,1},{1,0},{2,3},{3,2},{4,5},{5,4},{6,7},{7,6},{8,9},{9,8},{10,11... | collective-permute-start | bytes 110600 | tf_op jit(solution)/shard_map/ppermute | solution.py:34
  8.3 4.0 %collective-permute-start.9 = (bf16[16,1152]{1,0:T(8,128)(2,1)S(1)}, bf16[16,1152]{1,0:T(8,128)(2,1)S(1)}, u32[]{:S(2)}, u32[]{:S(2)}) collective-permute-start(bf16[16,1152]{1,0:T(8,128)(2,1)S(1)} %shard_map.73.a0.refs_0_), channel_id=1, source_target_pairs={{0,64},{1,65},{2,66},{3,67},{4,68},{5,69},{6,70},{7,71},{8,72},{9,... | collective-permute-start | bytes 110600 | tf_op jit(solution)/shard_map/ppermute | solution.py:34
  12.2 11.2 %collective-permute-start.10 = (bf16[16,1152]{1,0:T(8,128)(2,1)S(1)}, bf16[16,1152]{1,0:T(8,128)(2,1)S(1)}, u32[]{:S(2)}, u32[]{:S(2)}) collective-permute-start(bf16[16,1152]{1,0:T(8,128)(2,1)S(1)} %collective-permute-done.9.refs_2_), channel_id=1, source_target_pairs={{0,2},{1,3},{2,0},{3,1},{4,6},{5,7},{6,4},{7,5},{8,10},{9,11},{10,... | collective-permute-start | bytes 110600 | tf_op jit(solution)/shard_map/ppermute | solution.py:34
  13.8 11.5 %collective-permute-start.11 = (bf16[16,1152]{1,0:T(8,128)(2,1)S(1)}, bf16[16,1152]{1,0:T(8,128)(2,1)S(1)}, u32[]{:S(2)}, u32[]{:S(2)}) collective-permute-start(bf16[16,1152]{1,0:T(8,128)(2,1)S(1)} %collective-permute-done.9.refs_2_), channel_id=1, source_target_pairs={{0,4},{1,5},{2,6},{3,7},{4,0},{5,1},{6,2},{7,3},{8,12},{9,13},{10,... | collective-permute-start | bytes 110600 | tf_op jit(solution)/shard_map/ppermute | solution.py:34
  16.7 8.6 %collective-permute-start.12 = (bf16[16,1152]{1,0:T(8,128)(2,1)S(1)}, bf16[16,1152]{1,0:T(8,128)(2,1)S(1)}, u32[]{:S(2)}, u32[]{:S(2)}) collective-permute-start(bf16[16,1152]{1,0:T(8,128)(2,1)S(1)} %collective-permute-done.9.refs_2_), channel_id=1, source_target_pairs={{0,6},{1,7},{2,4},{3,5},{4,2},{5,3},{6,0},{7,1},{8,14},{9,15},{10,... | collective-permute-start | bytes 110600 | tf_op jit(solution)/shard_map/ppermute | solution.py:34
  16.9 3.7 %collective-permute-start.2 = (bf16[16,1152]{1,0:T(8,128)(2,1)S(1)}, bf16[16,1152]{1,0:T(8,128)(2,1)S(1)}, u32[]{:S(2)}, u32[]{:S(2)}) collective-permute-start(bf16[16,1152]{1,0:T(8,128)(2,1)S(1)} %collective-permute-done.a1.refs_0_), channel_id=1, source_target_pairs={{0,1},{1,0},{2,3},{3,2},{4,5},{5,4},{6,7},{7,6},{8,9},{9,8},{10,11... | collective-permute-start | bytes 110600 | tf_op jit(solution)/shard_map/ppermute | solution.py:34
  20.8 9.4 %collective-permute-start.3 = (f32[16,128]{1,0:T(8,128)S(1)}, f32[16,128]{1,0:T(8,128)S(1)}, u32[]{:S(2)}, u32[]{:S(2)}) collective-permute-start(f32[16,128]{1,0:T(8,128)S(1)} %shard_map.74.refs_8_), channel_id=1, source_target_pairs={{0,32},{1,33},{2,34},{3,35},{4,36},{5,37},{6,38},{7,39},{8,40},{9,... | collective-permute-start | bytes 24584 | tf_op jit(solution)/shard_map/ppermute | solution.py:34
  22.4 7.9 %collective-permute-start.4 = (f32[16,128]{1,0:T(8,128)S(1)}, f32[16,128]{1,0:T(8,128)S(1)}, u32[]{:S(2)}, u32[]{:S(2)}) collective-permute-start(f32[16,128]{1,0:T(8,128)S(1)} %shard_map.74.refs_8_), channel_id=1, source_target_pairs={{0,16},{1,17},{2,18},{3,19},{4,20},{5,21},{6,22},{7,23},{8,24},{9,... | collective-permute-start | bytes 24584 | tf_op jit(solution)/shard_map/ppermute | solution.py:34
  23.4 6.9 %collective-permute-start.5 = (f32[16,128]{1,0:T(8,128)S(1)}, f32[16,128]{1,0:T(8,128)S(1)}, u32[]{:S(2)}, u32[]{:S(2)}) collective-permute-start(f32[16,128]{1,0:T(8,128)S(1)} %shard_map.74.refs_8_), channel_id=1, source_target_pairs={{0,48},{1,49},{2,50},{3,51},{4,52},{5,53},{6,54},{7,55},{8,56},{9,... | collective-permute-start | bytes 24584 | tf_op jit(solution)/shard_map/ppermute | solution.py:34
  30.2 14.0 %collective-permute-start.17 = (f32[1,128]{1,0:T(1,128)S(1)}, f32[1,128]{1,0:T(1,128)S(1)}, u32[]{:S(2)}, u32[]{:S(2)}) collective-permute-start(f32[1,128]{1,0:T(1,128)S(1)} %slice.14), channel_id=1, source_target_pairs={{0,1},{1,0},{2,3},{3,2},{4,5},{5,4},{6,7},{7,6},{8,9},{9,8},{10,11... | collective-permute-start | bytes 1544 | tf_op jit(solution)/shard_map/ppermute | solution.py:34
  30.3 9.7 %collective-permute-start.6 = (f32[16,128]{1,0:T(8,128)S(1)}, f32[16,128]{1,0:T(8,128)S(1)}, u32[]{:S(2)}, u32[]{:S(2)}) collective-permute-start(f32[16,128]{1,0:T(8,128)S(1)} %add_add_fusion.1.refs_9_.y0), channel_id=1, source_target_pairs={{0,128},{1,129},{2,130},{3,131},{4,132},{5,133},{6,134},{7,135},{8... | collective-permute-start | bytes 24584 | tf_op jit(solution)/shard_map/ppermute | solution.py:34
  31.8 8.2 %collective-permute-start.7 = (f32[16,128]{1,0:T(8,128)S(1)}, f32[16,128]{1,0:T(8,128)S(1)}, u32[]{:S(2)}, u32[]{:S(2)}) collective-permute-start(f32[16,128]{1,0:T(8,128)S(1)} %add_add_fusion.1.refs_9_.y0), channel_id=1, source_target_pairs={{0,64},{1,65},{2,66},{3,67},{4,68},{5,69},{6,70},{7,71},{8,72},{9,... | collective-permute-start | bytes 24584 | tf_op jit(solution)/shard_map/ppermute | solution.py:34
  32.9 7.1 %collective-permute-start.8 = (f32[16,128]{1,0:T(8,128)S(1)}, f32[16,128]{1,0:T(8,128)S(1)}, u32[]{:S(2)}, u32[]{:S(2)}) collective-permute-start(f32[16,128]{1,0:T(8,128)S(1)} %add_add_fusion.1.refs_9_.y0), channel_id=1, source_target_pairs={{0,192},{1,193},{2,194},{3,195},{4,196},{5,197},{6,198},{7,199},{8... | collective-permute-start | bytes 24584 | tf_op jit(solution)/shard_map/ppermute | solution.py:34
  40.0 13.8 %copy-start = (f32[1,2,16]{2,1,0:T(2,128)S(1)}, f32[1,2,16]{2,1,0:T(2,128)}, u32[]{:S(2)}) copy-start(f32[1,2,16]{2,1,0:T(2,128)} %param.8) | copy-start | bytes 388
  40.0 13.8 %copy-start.1 = (f32[1,16]{1,0:T(1,128)S(1)}, f32[1,16]{1,0:T(1,128)}, u32[]{:S(2)}) copy-start(f32[1,16]{1,0:T(1,128)} %energy_ref.1) | copy-start | bytes 196
  40.0 5.3 %collective-permute-start.13 = (f32[24,128]{1,0:T(8,128)S(1)}, f32[24,128]{1,0:T(8,128)S(1)}, u32[]{:S(2)}, u32[]{:S(2)}) collective-permute-start(f32[24,128]{1,0:T(8,128)S(1)} %get-tuple-element.17), channel_id=1, source_target_pairs={{0,4},{1,5},{2,6},{3,7},{4,0},{5,1},{6,2},{7,3},{8,12},{9,13},{10,... | collective-permute-start | bytes 36872 | tf_op jit(solution)/shard_map/ppermute | solution.py:34
  42.1 3.7 %collective-permute-start.14 = (f32[24,128]{1,0:T(8,128)S(1)}, f32[24,128]{1,0:T(8,128)S(1)}, u32[]{:S(2)}, u32[]{:S(2)}) collective-permute-start(f32[24,128]{1,0:T(8,128)S(1)} %get-tuple-element.18), channel_id=1, source_target_pairs={{0,2},{1,3},{2,0},{3,1},{4,6},{5,7},{6,4},{7,5},{8,10},{9,11},{10,... | collective-permute-start | bytes 36872 | tf_op jit(solution)/shard_map/ppermute | solution.py:34
  44.0 4.9 %collective-permute-start.15 = (f32[24,128]{1,0:T(8,128)S(1)}, f32[24,128]{1,0:T(8,128)S(1)}, u32[]{:S(2)}, u32[]{:S(2)}) collective-permute-start(f32[24,128]{1,0:T(8,128)S(1)} %get-tuple-element.19), channel_id=1, source_target_pairs={{0,6},{1,7},{2,4},{3,5},{4,2},{5,3},{6,0},{7,1},{8,14},{9,15},{10,... | collective-permute-start | bytes 36872 | tf_op jit(solution)/shard_map/ppermute | solution.py:34
  44.2 7.4 %collective-permute-start.18 = (f32[1,128]{1,0:T(1,128)S(1)}, f32[1,128]{1,0:T(1,128)S(1)}, u32[]{:S(2)}, u32[]{:S(2)}) collective-permute-start(f32[1,128]{1,0:T(1,128)S(1)} %slice_add_fusion), channel_id=1, source_target_pairs={{0,8},{1,9},{2,10},{3,11},{4,12},{5,13},{6,14},{7,15},{8,0},{9,1},... | collective-permute-start | bytes 1544 | tf_op jit(solution)/shard_map/ppermute | solution.py:34
  44.4 7.3 %collective-permute-start.16 = (f32[1,128]{1,0:T(1,128)S(1)}, f32[1,128]{1,0:T(1,128)S(1)}, u32[]{:S(2)}, u32[]{:S(2)}) collective-permute-start(f32[1,128]{1,0:T(1,128)S(1)} %slice.12), channel_id=1, source_target_pairs={{0,1},{1,0},{2,3},{3,2},{4,5},{5,4},{6,7},{7,6},{8,9},{9,8},{10,11... | collective-permute-start | bytes 1544 | tf_op jit(solution)/shard_map/ppermute | solution.py:34
  48.9 4.8 %collective-permute-start.19 = (f32[1,128]{1,0:T(1,128)S(1)}, f32[1,128]{1,0:T(1,128)S(1)}, u32[]{:S(2)}, u32[]{:S(2)}) collective-permute-start(f32[1,128]{1,0:T(1,128)S(1)} %slice.16), channel_id=1, source_target_pairs={{0,192},{1,193},{2,194},{3,195},{4,196},{5,197},{6,198},{7,199},{8... | collective-permute-start | bytes 1544 | tf_op jit(solution)/shard_map/ppermute | solution.py:34

commit v5 on v4

--- a/solution.py
+++ b/solution.py
@@ -11,6 +11,7 @@
 NMU = 1024
 NG = 1536
 WIDTH = NMU + 128
+PARTS = ((0, 256), (256, 512), (768, 512), (1280, 256))
 CHUNK = 512
 ROWS = 128
 F32 = jnp.float32
@@ -105,9 +106,7 @@
     copies[1].wait()
 
 
-def fetch_kernel(where_ref, qmap_ref, basis, screening, z_ref, w_ref, sems):
-    whole = pltpu.make_async_copy(basis, z_ref, sems.at[16])
-    whole.start()
+def weights_kernel(where_ref, qmap_ref, screening, w_ref, sems):
     own = where_ref[0]
     member = where_ref[1]
     partner = (own + 12) & 15
@@ -123,32 +122,40 @@
             steps.append(copy)
     for copy in steps:
         copy.wait()
-    whole.wait()
-
-
-def transitions_kernel(a0, a1, a2, a3, y_ref):
-    total_re = jnp.zeros((8, NMU), F32)
-    total_im = jnp.zeros((8, NMU), F32)
-    for pay in (a0, a1, a2, a3):
-        waves = pay[:, 0:NMU]
-        mixed = dot(pay[:, NMU : NMU + 16], waves)
-        waves = waves.astype(F32)
-        val_re, val_im = waves[0:8], waves[8:16]
-        mix_re, mix_im = mixed[0:8], mixed[8:16]
-        total_re += val_re * mix_re + val_im * mix_im
-        total_im += val_re * mix_im - val_im * mix_re
-    total_re = jnp.sum(total_re, 0, keepdims=True)
-    total_im = jnp.sum(total_im, 0, keepdims=True)
-    for j in range(8):
-        y_ref[j : j + 1] = total_re[:, j * 128 : j * 128 + 128]
-        y_ref[8 + j : 9 + j] = total_im[:, j * 128 : j * 128 + 128]
+
+
+def transitions_kernel(*refs):
+    y_ref = refs[8]
+    for group in range(2):
+        total_re = jnp.zeros((8, NMU), F32)
+        total_im = jnp.zeros((8, NMU), F32)
+        for pay in refs[group * 4 : group * 4 + 4]:
+            waves = pay[:, 0:NMU]
+            mixed = dot(pay[:, NMU : NMU + 16], waves)
+            waves = waves.astype(F32)
+            val_re, val_im = waves[0:8], waves[8:16]
+            mix_re, mix_im = mixed[0:8], mixed[8:16]
+            total_re += val_re * mix_re + val_im * mix_im
+            total_im += val_re * mix_im - val_im * mix_re
+        total_re = jnp.sum(total_re, 0, keepdims=True)
+        total_im = jnp.sum(total_im, 0, keepdims=True)
+        top = group * 16
+        for j in range(8):
+            y_ref[top + j : top + j + 1] = total_re[:, j * 128 : j * 128 + 128]
+            y_ref[top + 8 + j : top + 9 + j] = total_im[:, j * 128 : j * 128 + 128]
 
 
 def pair_kernel(near, *refs):
     if near:
         w_ref, z_ref, far_ref, _, out_ref, rx_ref, lhs, own, xa, xb, acc, ca, cb = refs[6:]
     else:
-        w_ref, z_ref, _, out_ref, lhs, xa, xb, acc, ca, cb = refs[6:]
+        w_ref, basis, _, out_ref, z_ref, lhs, xa, xb, acc, ca, cb, sems = refs[6:]
+        copies = []
+        for n, (at, width) in enumerate(PARTS):
+            part = pl.ds(at, width)
+            copies.append(pltpu.make_async_copy(basis.at[:, part], z_ref.at[:, part], sems.at[n]))
+        for copy in copies:
+            copy.start()
     base = 2 * near
     a_pays = refs[0:2]
     b_pays = refs[2:6]
@@ -180,25 +187,28 @@
     if near:
         put(own, 0, 16, xa[0], dot(til, a_pays[0][:, 0:NMU]), 32, 0)
     acc[...] = jnp.zeros_like(acc)
-    for at in range(0, NG, CHUNK):
-        z = z_ref[:, at : at + CHUNK]
+    for n, (at, width) in enumerate(PARTS):
+        part = pl.ds(at, width)
+        if not near:
+            copies[n].wait()
+        z = z_ref[:, part]
         con_re = dot(lhs[0:ROWS], z)
         for p in range(8):
-            weight = w_ref[4 * base + p : 4 * base + p + 1, at : at + CHUNK]
-            ca[p * 16 : p * 16 + 16, 0:CHUNK] = (con_re[p * 16 : p * 16 + 16] * weight).astype(BF16)
+            weight = w_ref[4 * base + p : 4 * base + p + 1, part]
+            ca[p * 16 : p * 16 + 16, 0:width] = (con_re[p * 16 : p * 16 + 16] * weight).astype(BF16)
         con_im = dot(lhs[half : half + ROWS], z)
         for p in range(8):
-            weight = w_ref[4 * base + p : 4 * base + p + 1, at : at + CHUNK]
-            ca[p * 16 : p * 16 + 16, CHUNK : 2 * CHUNK] = (con_im[p * 16 : p * 16 + 16] * weight).astype(BF16)
+            weight = w_ref[4 * base + p : 4 * base + p + 1, part]
+            ca[p * 16 : p * 16 + 16, width : 2 * width] = (con_im[p * 16 : p * 16 + 16] * weight).astype(BF16)
         val_re = dot(lhs[ROWS:half], z).astype(BF16)
-        cb[0:ROWS, 0:CHUNK] = val_re
-        cb[ROWS:half, CHUNK : 2 * CHUNK] = -val_re
+        cb[0:ROWS, 0:width] = val_re
+        cb[ROWS:half, width : 2 * width] = -val_re
         val_im = dot(lhs[half + ROWS : 2 * half], z).astype(BF16)
-        cb[0:ROWS, CHUNK : 2 * CHUNK] = val_im
-        cb[ROWS:half, 0:CHUNK] = val_im
-        acc[...] += dot_t(ca[...], cb[...])
+        cb[0:ROWS, width : 2 * width] = val_im
+        cb[ROWS:half, 0:width] = val_im
+        acc[...] += dot_t(ca[:, 0 : 2 * width], cb[:, 0 : 2 * width])
         if near:
-            rx_ref[:, at : at + CHUNK] = dot(own[...], z)
+            rx_ref[:, part] = dot(own[...], z)
 
     pick_row = iota((8, 16), 0)
     pick_col = iota((8, 16), 1)
@@ -257,18 +267,25 @@
     out_ref[...] = total
 
 
-def mail_kernel(y0, y1, y2, y3, out_ref, *mails):
-    total = y0[...] + y1[...] + y2[...] + y3[...]
+def mail_kernel(y0, y1, out_ref, *mails):
+    total = y0[...] + y1[...]
     for n, mail in enumerate(mails):
-        mail[0:16] = total
-        mail[16:24] = jnp.broadcast_to(out_ref[4 + n : 5 + n], (8, 128))
-
-
-def exchange_kernel(y_ref, c_ref, rx_ref, z_ref, out_ref, lhs):
+        mail[0:16] = total[0:16] if n < 4 else total[16:32]
+        row = 4 + n if n < 4 else 1
+        mail[16:24] = jnp.broadcast_to(out_ref[row : row + 1], (8, 128))
+
+
+def far_mail_kernel(m0, m1, d0, d1, mail):
+    mail[0:16] = m0[0:16] + m1[0:16]
+    mail[16:24] = jnp.broadcast_to(d0[0:1] + d1[...], (8, 128))
+
+
+def exchange_kernel(y_ref, first_ref, second_ref, c_ref, rx_ref, z_ref, out_ref, lhs):
+    y = y_ref[0:16] + first_ref[0:16] + second_ref[0:16]
     pad = jnp.zeros((12, 128), F32)
     for j in range(8):
-        real = y_ref[j : j + 1]
-        imag = y_ref[8 + j : 9 + j]
+        real = y[j : j + 1]
+        imag = y[8 + j : 9 + j]
         for at, top, bottom in ((0, real, imag), (NMU, -imag, real)):
             high, low = split(jnp.concatenate([top, bottom], 0))
             rows = jnp.concatenate([high.astype(F32), low.astype(F32), pad], 0)
@@ -295,9 +312,9 @@
     out_ref[...] = jnp.concatenate(out, 0)
 
 
-def final_kernel(energy_ref, vector_ref, exchange_ref, near_ref, d0, d1, d2, out_ref):
+def final_kernel(energy_ref, vector_ref, exchange_ref, near_ref, core_ref, far_ref, herm_ref, out_ref):
     scale = 1.0 / 256
-    terms = near_ref[0:1] + d0[...] + d1[...] + d2[...]
+    terms = near_ref[0:1] + core_ref[16:17] + far_ref[16:17] + herm_ref[...]
     for part in range(2):
         term = terms[:, part * NT : part * NT + NT]
         out_ref[part : part + 1] = (
@@ -321,10 +338,12 @@
     if near:
         scratch.append(pltpu.VMEM((32, 2 * NMU), BF16))
         out_shape.append(pltpu.VMEM((32, NG), F32))
+    else:
+        out_shape.append(pltpu.VMEM((2 * NMU, NG), BF16))
     return pl.pallas_call(
         functools.partial(pair_kernel, near),
-        in_specs=[VMEM] * 8 + [VMEM] * near + [ANY],
-        out_specs=[VMEM] * len(out_shape),
+        in_specs=[VMEM] * 7 + ([VMEM, VMEM, ANY] if near else [ANY, ANY]),
+        out_specs=[VMEM] * 2,
         out_shape=out_shape,
         scratch_shapes=scratch
         + [
@@ -333,9 +352,20 @@
             pltpu.VMEM((ROWS, 2 * ROWS), F32),
             pltpu.VMEM((ROWS, 2 * CHUNK), BF16),
             pltpu.VMEM((2 * ROWS, 2 * CHUNK), BF16),
-        ],
-        compiler_params=params(24),
+        ]
+        + [pltpu.SemaphoreType.DMA((len(PARTS),))] * (1 - near),
+        compiler_params=params(24 if near else 42),
         cost_estimate=cost(4 * ROWS),
+    )(*operands)
+
+
+def small_call(kernel, shapes, *operands):
+    return pl.pallas_call(
+        kernel,
+        in_specs=[VMEM] * len(operands),
+        out_specs=[VMEM] * len(shapes),
+        out_shape=[jax.ShapeDtypeStruct(shape, F32) for shape in shapes],
+        compiler_params=params(8),
     )(*operands)
 
 
@@ -348,65 +378,52 @@
         scratch_shapes=[pltpu.VMEM((2, NT), F32), pltpu.SemaphoreType.DMA((2,))],
         compiler_params=params(56),
     )(waves.reshape(16, NMU), vector.reshape(2, NT))
+    b0 = move(pay, step=1)
     a1 = move(pay, far=1)
-    b0 = move(pay, step=1)
     a2 = move(pay, core=1)
-    where = jnp.stack([lax.axis_index("grp"), lax.axis_index("kin")]).astype(jnp.int32)
-    z, weights = pl.pallas_call(
-        fetch_kernel,
-        in_specs=[SMEM, SMEM, ANY, ANY],
-        out_specs=[VMEM] * 2,
-        out_shape=[pltpu.VMEM((2 * NMU, NG), BF16), pltpu.VMEM((16, NG), F32)],
-        scratch_shapes=[pltpu.SemaphoreType.DMA((17,))],
-        compiler_params=params(50),
-        cost_estimate=cost(128),
-    )(where, qmap, basis.reshape(2 * NMU, NG), screening)
     b1, b2, b3 = (move(b0, y=n) for n in (1, 2, 3))
     a3 = move(a1, core=1)
-    y = pl.pallas_call(
-        transitions_kernel,
-        in_specs=[VMEM] * 4,
+    where = jnp.stack([lax.axis_index("grp"), lax.axis_index("kin")]).astype(jnp.int32)
+    weights = pl.pallas_call(
+        weights_kernel,
+        in_specs=[SMEM, SMEM, ANY],
         out_specs=VMEM,
-        out_shape=jax.ShapeDtypeStruct((16, 128), F32),
-        compiler_params=params(8),
-    )(pay, a1, a2, a3)
+        out_shape=pltpu.VMEM((16, NG), F32),
+        scratch_shapes=[pltpu.SemaphoreType.DMA((16,))],
+        compiler_params=params(56),
+    )(where, qmap, screening)
     b_pays = (b0, b1, b2, b3)
-    (far_out,) = pair_call(0, (a1, a3, *b_pays, weights, z, y))
-    far_sum = far_out[0:1] + move(far_out[1:2], core=1)
+    (y,) = small_call(transitions_kernel, [(32, 128)], pay, a1, a2, a3, *b_pays)
+    far_out, z = pair_call(0, (a1, a3, *b_pays, weights, basis.reshape(2 * NMU, NG), y))
     y = y + move(y, z=2) + move(y, z=1) + move(y, z=3)
     near_out, rx = pair_call(1, (pay, a2, *b_pays, weights, z, far_out, y))
-    mail = pl.pallas_call(
-        mail_kernel,
-        in_specs=[VMEM] * 5,
-        out_specs=[VMEM] * 4,
-        out_shape=[jax.ShapeDtypeStruct((24, 128), F32)] * 4,
-        compiler_params=params(4),
-    )(y, *(move(y, x=n) for n in (2, 1, 3)), near_out)
-    mail = mail[0] + move(mail[2], y=2) + move(mail[1], y=1) + move(mail[3], y=3)
+    mails = small_call(mail_kernel, [(24, 128)] * 5, y, move(y, x=2), near_out)
+    core_mail = move(mails[4], core=1)
+    (far_mail,) = small_call(
+        far_mail_kernel, [(24, 128)], mails[4], core_mail, far_out, move(far_out[1:2], core=1)
+    )
+    far_back = move(far_mail, far=1)
+    mail = mails[0] + move(mails[2], y=2) + move(mails[1], y=1) + move(mails[3], y=3)
+    herm = move(mail[16:17], step=3)
     exchange = pl.pallas_call(
         exchange_kernel,
-        in_specs=[VMEM] * 4,
+        in_specs=[VMEM] * 6,
         out_specs=VMEM,
         out_shape=jax.ShapeDtypeStruct((2, NT), F32),
         scratch_shapes=[pltpu.VMEM((16, 2 * NMU), BF16)],
         compiler_params=params(24),
         cost_estimate=cost(128),
-    )(mail, coulomb.reshape(1, NG), rx, z)
-
-    out = pl.pallas_call(
+    )(mail, far_mail, far_back, coulomb.reshape(1, NG), rx, z)
+    (out,) = small_call(
         final_kernel,
-        in_specs=[VMEM] * 7,
-        out_specs=VMEM,
-        out_shape=jax.ShapeDtypeStruct((2, NT), F32),
-        compiler_params=params(4),
-    )(
+        [(2, NT)],
         energies,
         vector.reshape(2, NT),
         exchange,
         near_out,
-        move(near_out[1:2], core=1),
-        move(far_sum, far=1),
-        move(mail[16:17], step=3),
+        core_mail,
+        far_back,
+        herm,
     )
     return out.reshape(1, 2, NT)
 

time: 54.5 us -> 55.1 us (1.011)
  the two profiles are of different devices: /device:TPU:6 before, /device:TPU:1 now
where the time goes in v5:
time: 55.1 us; the launch traced here: 54.9 us
  starting transfers between devices  31.9 us (58%)
  Pallas kernels  17.5 us (32%)
  waiting for transfers between devices  4.72 us (9%)
  other arithmetic  0.61 us (1%)
    ppermute x18, starting transfers between devices, move(): return lax.ppermute(value, ('grp', 'kin'), pairs)  31.9 us
    pallas_call x2, Pallas kernels, pair_call(): pl.pallas_call(functools.partial(pair_kernel, near), in_specs=[VMEM] * 7...  12.8 us
    ppermute x18, waiting for transfers between devices, move(): return lax.ppermute(value, ('grp', 'kin'), pairs)  4.72 us
    pallas_call x1, Pallas kernels, on_device(): pl.pallas_call(weights_kernel, in_specs=[SMEM, SMEM, ANY], out_specs=VMEM...  1.74 us
  transfers between devices with their start and end apart: 18, of which 3 were waited for; matrix products, arithmetic and copies ran while one was open for 1% of the time, Pallas kernels for 29%

profile of v5, /device:TPU:1, one launch (start us, length us, event | category | flops | bytes accessed | tf_op | source)
XLA Modules:
  0.0 54.9 jit_solution(8213527465507149711)
XLA Ops:
  0.0 0.9 %shard_map.73.refs_0_ = bf16[16,1152]{1,0:T(8,128)(2,1)S(1)} custom-call(bf16[16,1024]{1,0:T(8,128)(2,1)} %bitcast.8, f32[2,16]{1,0:T(2,128)} %bitcast.6), custom_call_target="tpu_custom_call" | custom-call | tf_op jit(solution)/shard_map/pallas_call | solution.py:373
  1.0 2.1 %collective-permute-start.3 = (bf16[16,1152]{1,0:T(8,128)(2,1)S(1)}, bf16[16,1152]{1,0:T(8,128)(2,1)S(1)}, u32[]{:S(2)}, u32[]{:S(2)}) collective-permute-start(bf16[16,1152]{1,0:T(8,128)(2,1)S(1)} %shard_map.73.refs_0_), channel_id=1, source_target_pairs={{0,64},{1,65},{2,66},{3,67},{4,68},{5,69},{6,70},{7,71},{8,72},{9,... | collective-permute-start | bytes 110600 | tf_op jit(solution)/shard_map/ppermute | solution.py:35
  3.1 6.9 %collective-permute-start = (bf16[16,1152]{1,0:T(8,128)(2,1)S(1)}, bf16[16,1152]{1,0:T(8,128)(2,1)S(1)}, u32[]{:S(2)}, u32[]{:S(2)}) collective-permute-start(bf16[16,1152]{1,0:T(8,128)(2,1)S(1)} %shard_map.73.refs_0_), channel_id=1, source_target_pairs={{0,8},{1,9},{2,10},{3,11},{4,12},{5,13},{6,14},{7,15},{8,0},{9,1},... | collective-permute-start | bytes 110600 | tf_op jit(solution)/shard_map/ppermute | solution.py:35
  10.0 1.2 %collective-permute-start.1 = (bf16[16,1152]{1,0:T(8,128)(2,1)S(1)}, bf16[16,1152]{1,0:T(8,128)(2,1)S(1)}, u32[]{:S(2)}, u32[]{:S(2)}) collective-permute-start(bf16[16,1152]{1,0:T(8,128)(2,1)S(1)} %shard_map.73.refs_0_), channel_id=1, source_target_pairs={{0,1},{1,0},{2,3},{3,2},{4,5},{5,4},{6,7},{7,6},{8,9},{9,8},{10,11... | collective-permute-start | bytes 110600 | tf_op jit(solution)/shard_map/ppermute | solution.py:35
  11.2 0.0 collective-permute-done.3.refs_4_.refs_2_
  11.2 1.3 %collective-permute-start.4 = (bf16[16,1152]{1,0:T(8,128)(2,1)S(1)}, bf16[16,1152]{1,0:T(8,128)(2,1)S(1)}, u32[]{:S(2)}, u32[]{:S(2)}) collective-permute-start(bf16[16,1152]{1,0:T(8,128)(2,1)S(1)} %collective-permute-done.3.refs_4_.refs_2_), channel_id=1, source_target_pairs={{0,2},{1,3},{2,0},{3,1},{4,6},{5,7},{6,4},{7,5},{8,10},{9,11},{10,... | collective-permute-start | bytes 110600 | tf_op jit(solution)/shard_map/ppermute | solution.py:35
  12.5 2.6 %collective-permute-start.5 = (bf16[16,1152]{1,0:T(8,128)(2,1)S(1)}, bf16[16,1152]{1,0:T(8,128)(2,1)S(1)}, u32[]{:S(2)}, u32[]{:S(2)}) collective-permute-start(bf16[16,1152]{1,0:T(8,128)(2,1)S(1)} %collective-permute-done.3.refs_4_.refs_2_), channel_id=1, source_target_pairs={{0,4},{1,5},{2,6},{3,7},{4,0},{5,1},{6,2},{7,3},{8,12},{9,13},{10,... | collective-permute-start | bytes 110600 | tf_op jit(solution)/shard_map/ppermute | solution.py:35
  15.1 0.0 collective-permute-start.6
  15.1 0.0 collective-permute-done.refs_1_.refs_0_
  15.1 0.8 %collective-permute-start.2 = (bf16[16,1152]{1,0:T(8,128)(2,1)S(1)}, bf16[16,1152]{1,0:T(8,128)(2,1)S(1)}, u32[]{:S(2)}, u32[]{:S(2)}) collective-permute-start(bf16[16,1152]{1,0:T(8,128)(2,1)S(1)} %collective-permute-done.refs_1_.refs_0_), channel_id=1, source_target_pairs={{0,1},{1,0},{2,3},{3,2},{4,5},{5,4},{6,7},{7,6},{8,9},{9,8},{10,11... | collective-permute-start | bytes 110600 | tf_op jit(solution)/shard_map/ppermute | solution.py:35
  15.9 0.6 %pad_add_fusion.where_ref = s32[2]{0:T(128)} fusion(s32[1]{0:T(128)} %bitcast.3, s32[1]{0:T(128)} %bitcast.2), kind=kLoop, calls=%fused_computation.2 | loop fusion | flops 2 | bytes 16 | tf_op jit(solution)/shard_map/stack | solution.py:386
  16.5 1.7 %shard_map.75.refs_6_ = f32[16,1536]{1,0:T(8,128)S(1)} custom-call(s32[2]{0:T(128)} %pad_add_fusion.where_ref, s32[1,256]{1,0:T(1,128)} %qmap_ref.1, f32[256,1536]{1,0:T(8,128)} %screening.1), custom_call_target="tpu_custom_call" | custom-call | tf_op jit(solution)/shard_map/pallas_call | solution.py:387
  18.3 0.0 collective-permute-done.1.refs_2_.refs_1_
  18.3 0.0 collective-permute-done.4.refs_5_.refs_3_
  18.3 0.0 collective-permute-done.5.refs_6_.refs_4_
  18.3 0.9 %collective-permute-done.6.refs_7_.refs_5_ = bf16[16,1152]{1,0:T(8,128)(2,1)S(1)} collective-permute-done((bf16[16,1152]{1,0:T(8,128)(2,1)S(1)}, bf16[16,1152]{1,0:T(8,128)(2,1)S(1)}, u32[]{:S(2)}, u32[]{:S(2)}) %collective-permute-start.6) | collective-permute-done | bytes 36896 | tf_op jit(solution)/shard_map/ppermute | solution.py:35
  19.2 0.0 collective-permute-done.2.refs_3_.refs_1_
  19.2 0.3 shard_map.74.refs_8_
  19.4 1.3 %collective-permute-start.7 = (f32[32,128]{1,0:T(8,128)S(1)}, f32[32,128]{1,0:T(8,128)S(1)}, u32[]{:S(2)}, u32[]{:S(2)}) collective-permute-start(f32[32,128]{1,0:T(8,128)S(1)} %shard_map.74.refs_8_), channel_id=1, source_target_pairs={{0,32},{1,33},{2,34},{3,35},{4,36},{5,37},{6,38},{7,39},{8,40},{9,... | collective-permute-start | bytes 49160 | tf_op jit(solution)/shard_map/ppermute | solution.py:35
  20.7 0.7 %collective-permute-start.8 = (f32[32,128]{1,0:T(8,128)S(1)}, f32[32,128]{1,0:T(8,128)S(1)}, u32[]{:S(2)}, u32[]{:S(2)}) collective-permute-start(f32[32,128]{1,0:T(8,128)S(1)} %shard_map.74.refs_8_), channel_id=1, source_target_pairs={{0,16},{1,17},{2,18},{3,19},{4,20},{5,21},{6,22},{7,23},{8,24},{9,... | collective-permute-start | bytes 49160 | tf_op jit(solution)/shard_map/ppermute | solution.py:35
  21.4 1.6 %collective-permute-start.9 = (f32[32,128]{1,0:T(8,128)S(1)}, f32[32,128]{1,0:T(8,128)S(1)}, u32[]{:S(2)}, u32[]{:S(2)}) collective-permute-start(f32[32,128]{1,0:T(8,128)S(1)} %shard_map.74.refs_8_), channel_id=1, source_target_pairs={{0,48},{1,49},{2,50},{3,51},{4,52},{5,53},{6,54},{7,55},{8,56},{9,... | collective-permute-start | bytes 49160 | tf_op jit(solution)/shard_map/ppermute | solution.py:35
  23.1 6.8 %shard_map.76 = (f32[8,128]{1,0:T(8,128)S(1)}, bf16[2048,1536]{1,0:T(8,128)(2,1)S(1)}) custom-call(bf16[16,1152]{1,0:T(8,128)(2,1)S(1)} %collective-permute-done.refs_1_.refs_0_, bf16[16,1152]{1,0:T(8,128)(2,1)S(1)} %collective-permute-done.2.refs_3_.refs_1_, bf16[16,1152]{1,0:T(8,128)(2,1)S(1)} %collective-permute-done.3.refs_4_.refs_2_, ...), custom_call_target="tpu_custom_call" | custom-call | flops 3221225472 | bytes 6291456 | tf_op jit(solution)/shard_map/pallas_call | solution.py:343
  29.9 0.0 copy-start.2
  29.9 0.0 collective-permute-done.7
  29.9 0.0 collective-permute-done.8
  29.9 0.0 collective-permute-done.9
  30.0 2.7 %collective-permute-start.10 = (f32[32,128]{1,0:T(8,128)S(1)}, f32[32,128]{1,0:T(8,128)S(1)}, u32[]{:S(2)}, u32[]{:S(2)}) collective-permute-start(f32[32,128]{1,0:T(8,128)S(1)} %add_add_fusion.refs_9_.y0), channel_id=1, source_target_pairs={{0,128},{1,129},{2,130},{3,131},{4,132},{5,133},{6,134},{7,135},{8... | collective-permute-start | bytes 49160 | tf_op jit(solution)/shard_map/ppermute | solution.py:35
  32.7 6.0 %shard_map.77 = (f32[8,128]{1,0:T(8,128)S(1)}, f32[32,1536]{1,0:T(8,128)S(1)}) custom-call(bf16[16,1152]{1,0:T(8,128)(2,1)S(1)} %shard_map.73.refs_0_, bf16[16,1152]{1,0:T(8,128)(2,1)S(1)} %collective-permute-done.1.refs_2_.refs_1_, bf16[16,1152]{1,0:T(8,128)(2,1)S(1)} %collective-permute-done.3.refs_4_.refs_2_, ...), custom_call_target="tpu_custom_call" | custom-call | flops 3221225472 | bytes 6291456 | tf_op jit(solution)/shard_map/pallas_call | solution.py:343
  38.7 0.0 collective-permute-done.10.y1
  38.7 2.9 %collective-permute-start.14 = (f32[24,128]{1,0:T(8,128)S(1)}, f32[24,128]{1,0:T(8,128)S(1)}, u32[]{:S(2)}, u32[]{:S(2)}) collective-permute-start(f32[24,128]{1,0:T(8,128)S(1)} %get-tuple-element.21.m0), channel_id=1, source_target_pairs={{0,1},{1,0},{2,3},{3,2},{4,5},{5,4},{6,7},{7,6},{8,9},{9,8},{10,11... | collective-permute-start | bytes 36872 | tf_op jit(solution)/shard_map/ppermute | solution.py:35
  41.6 0.0 collective-permute-start.11
  41.7 0.7 %collective-permute-start.12 = (f32[24,128]{1,0:T(8,128)S(1)}, f32[24,128]{1,0:T(8,128)S(1)}, u32[]{:S(2)}, u32[]{:S(2)}) collective-permute-start(f32[24,128]{1,0:T(8,128)S(1)} %get-tuple-element.19), channel_id=1, source_target_pairs={{0,2},{1,3},{2,0},{3,1},{4,6},{5,7},{6,4},{7,5},{8,10},{9,11},{10,... | collective-permute-start | bytes 36872 | tf_op jit(solution)/shard_map/ppermute | solution.py:35
  42.4 2.5 %collective-permute-start.13 = (f32[24,128]{1,0:T(8,128)S(1)}, f32[24,128]{1,0:T(8,128)S(1)}, u32[]{:S(2)}, u32[]{:S(2)}) collective-permute-start(f32[24,128]{1,0:T(8,128)S(1)} %get-tuple-element.20), channel_id=1, source_target_pairs={{0,6},{1,7},{2,4},{3,5},{4,2},{5,3},{6,0},{7,1},{8,14},{9,15},{10,... | collective-permute-start | bytes 36872 | tf_op jit(solution)/shard_map/ppermute | solution.py:35
  44.9 0.9 %collective-permute-start.15 = (f32[1,128]{1,0:T(1,128)S(1)}, f32[1,128]{1,0:T(1,128)S(1)}, u32[]{:S(2)}, u32[]{:S(2)}) collective-permute-start(f32[1,128]{1,0:T(1,128)S(1)} %slice.6), channel_id=1, source_target_pairs={{0,1},{1,0},{2,3},{3,2},{4,5},{5,4},{6,7},{7,6},{8,9},{9,8},{10,11... | collective-permute-start | bytes 1544 | tf_op jit(solution)/shard_map/ppermute | solution.py:35
  45.8 0.0 copy-done.2
  45.9 0.8 %collective-permute-done.15.d1 = f32[1,128]{1,0:T(1,128)S(1)} collective-permute-done((f32[1,128]{1,0:T(1,128)S(1)}, f32[1,128]{1,0:T(1,128)S(1)}, u32[]{:S(2)}, u32[]{:S(2)}) %collective-permute-start.15) | collective-permute-done | bytes 544 | tf_op jit(solution)/shard_map/ppermute | solution.py:35
  46.7 0.0 collective-permute-done.14.m1.core_ref
  46.7 2.5 %collective-permute-start.16 = (f32[24,128]{1,0:T(8,128)S(1)}, f32[24,128]{1,0:T(8,128)S(1)}, u32[]{:S(2)}, u32[]{:S(2)}) collective-permute-start(f32[24,128]{1,0:T(8,128)S(1)} %shard_map.79.first_ref), channel_id=1, source_target_pairs={{0,8},{1,9},{2,10},{3,11},{4,12},{5,13},{6,14},{7,15},{8,0},{9,1},... | collective-permute-start | bytes 36872 | tf_op jit(solution)/shard_map/ppermute | solution.py:35
  49.2 0.0 collective-permute-done.11
  49.2 0.0 collective-permute-done.12
  49.2 0.0 collective-permute-done.13
  49.2 0.9 %collective-permute-start.17 = (f32[1,128]{1,0:T(1,128)S(1)}, f32[1,128]{1,0:T(1,128)S(1)}, u32[]{:S(2)}, u32[]{:S(2)}) collective-permute-start(f32[1,128]{1,0:T(1,128)S(1)} %slice.8), channel_id=1, source_target_pairs={{0,192},{1,193},{2,194},{3,195},{4,196},{5,197},{6,198},{7,199},{8... | collective-permute-start | bytes 1544 | tf_op jit(solution)/shard_map/ppermute | solution.py:35
  50.2 3.0 %collective-permute-done.16.second_ref.far_ref = f32[24,128]{1,0:T(8,128)S(1)} collective-permute-done((f32[24,128]{1,0:T(8,128)S(1)}, f32[24,128]{1,0:T(8,128)S(1)}, u32[]{:S(2)}, u32[]{:S(2)}) %collective-permute-start.16) | collective-permute-done | bytes 12320 | tf_op jit(solution)/shard_map/ppermute | solution.py:35
  53.2 1.1 %shard_map.80.exchange_ref = f32[2,16]{1,0:T(2,128)S(1)} custom-call(f32[24,128]{1,0:T(8,128)S(1)} %add_add_fusion.1.y_ref, f32[24,128]{1,0:T(8,128)S(1)} %shard_map.79.first_ref, f32[24,128]{1,0:T(8,128)S(1)} %collective-permute-done.16.second_ref.far_ref, f32[1,1536]{1,0:T(1,128)S(1)} %reshape.19.c_ref, f32[32,1536]{1,0:T(8,128)S(1)} %get-tuple-element.22.rx_ref, ...), custom_call_target="tpu_custom_call" | custom-call | flops 805306368 | bytes 6291456 | tf_op jit(solution)/shard_map/pallas_call | solution.py:408
  54.2 0.0 collective-permute-done.17.herm_ref
  54.2 0.0 copy-done
  54.2 0.0 copy-done.1
  54.2 0.6 %shard_map.81 = f32[2,16]{1,0:T(2,128)} custom-call(f32[1,16]{1,0:T(1,128)S(1)} %copy-done.1, f32[2,16]{1,0:T(2,128)S(1)} %bitcast.7, f32[2,16]{1,0:T(2,128)S(1)} %shard_map.80.exchange_ref, f32[8,128]{1,0:T(8,128)S(1)} %get-tuple-element.16.out_ref.near_ref, f32[24,128]{1,0:T(8,128)S(1)} %collective-permute-done.14.m1.core_ref, ...), custom_call_target="tpu_custom_call" | custom-call | tf_op jit(solution)/shard_map/pallas_call | solution.py:363
  (9 shorter events, 0.0 us)
Async XLA Ops:
  1.0 10.3 %collective-permute-start.3 = (bf16[16,1152]{1,0:T(8,128)(2,1)S(1)}, bf16[16,1152]{1,0:T(8,128)(2,1)S(1)}, u32[]{:S(2)}, u32[]{:S(2)}) collective-permute-start(bf16[16,1152]{1,0:T(8,128)(2,1)S(1)} %shard_map.73.refs_0_), channel_id=1, source_target_pairs={{0,64},{1,65},{2,66},{3,67},{4,68},{5,69},{6,70},{7,71},{8,72},{9,... | collective-permute-start | bytes 110600 | tf_op jit(solution)/shard_map/ppermute | solution.py:35
  3.1 12.1 %collective-permute-start = (bf16[16,1152]{1,0:T(8,128)(2,1)S(1)}, bf16[16,1152]{1,0:T(8,128)(2,1)S(1)}, u32[]{:S(2)}, u32[]{:S(2)}) collective-permute-start(bf16[16,1152]{1,0:T(8,128)(2,1)S(1)} %shard_map.73.refs_0_), channel_id=1, source_target_pairs={{0,8},{1,9},{2,10},{3,11},{4,12},{5,13},{6,14},{7,15},{8,0},{9,1},... | collective-permute-start | bytes 110600 | tf_op jit(solution)/shard_map/ppermute | solution.py:35
  10.0 8.3 %collective-permute-start.1 = (bf16[16,1152]{1,0:T(8,128)(2,1)S(1)}, bf16[16,1152]{1,0:T(8,128)(2,1)S(1)}, u32[]{:S(2)}, u32[]{:S(2)}) collective-permute-start(bf16[16,1152]{1,0:T(8,128)(2,1)S(1)} %shard_map.73.refs_0_), channel_id=1, source_target_pairs={{0,1},{1,0},{2,3},{3,2},{4,5},{5,4},{6,7},{7,6},{8,9},{9,8},{10,11... | collective-permute-start | bytes 110600 | tf_op jit(solution)/shard_map/ppermute | solution.py:35
  11.2 7.1 %collective-permute-start.4 = (bf16[16,1152]{1,0:T(8,128)(2,1)S(1)}, bf16[16,1152]{1,0:T(8,128)(2,1)S(1)}, u32[]{:S(2)}, u32[]{:S(2)}) collective-permute-start(bf16[16,1152]{1,0:T(8,128)(2,1)S(1)} %collective-permute-done.3.refs_4_.refs_2_), channel_id=1, source_target_pairs={{0,2},{1,3},{2,0},{3,1},{4,6},{5,7},{6,4},{7,5},{8,10},{9,11},{10,... | collective-permute-start | bytes 110600 | tf_op jit(solution)/shard_map/ppermute | solution.py:35
  12.5 5.8 %collective-permute-start.5 = (bf16[16,1152]{1,0:T(8,128)(2,1)S(1)}, bf16[16,1152]{1,0:T(8,128)(2,1)S(1)}, u32[]{:S(2)}, u32[]{:S(2)}) collective-permute-start(bf16[16,1152]{1,0:T(8,128)(2,1)S(1)} %collective-permute-done.3.refs_4_.refs_2_), channel_id=1, source_target_pairs={{0,4},{1,5},{2,6},{3,7},{4,0},{5,1},{6,2},{7,3},{8,12},{9,13},{10,... | collective-permute-start | bytes 110600 | tf_op jit(solution)/shard_map/ppermute | solution.py:35
  15.1 4.0 %collective-permute-start.6 = (bf16[16,1152]{1,0:T(8,128)(2,1)S(1)}, bf16[16,1152]{1,0:T(8,128)(2,1)S(1)}, u32[]{:S(2)}, u32[]{:S(2)}) collective-permute-start(bf16[16,1152]{1,0:T(8,128)(2,1)S(1)} %collective-permute-done.3.refs_4_.refs_2_), channel_id=1, source_target_pairs={{0,6},{1,7},{2,4},{3,5},{4,2},{5,3},{6,0},{7,1},{8,14},{9,15},{10,... | collective-permute-start | bytes 110600 | tf_op jit(solution)/shard_map/ppermute | solution.py:35
  15.1 4.0 %collective-permute-start.2 = (bf16[16,1152]{1,0:T(8,128)(2,1)S(1)}, bf16[16,1152]{1,0:T(8,128)(2,1)S(1)}, u32[]{:S(2)}, u32[]{:S(2)}) collective-permute-start(bf16[16,1152]{1,0:T(8,128)(2,1)S(1)} %collective-permute-done.refs_1_.refs_0_), channel_id=1, source_target_pairs={{0,1},{1,0},{2,3},{3,2},{4,5},{5,4},{6,7},{7,6},{8,9},{9,8},{10,11... | collective-permute-start | bytes 110600 | tf_op jit(solution)/shard_map/ppermute | solution.py:35
  19.4 10.5 %collective-permute-start.7 = (f32[32,128]{1,0:T(8,128)S(1)}, f32[32,128]{1,0:T(8,128)S(1)}, u32[]{:S(2)}, u32[]{:S(2)}) collective-permute-start(f32[32,128]{1,0:T(8,128)S(1)} %shard_map.74.refs_8_), channel_id=1, source_target_pairs={{0,32},{1,33},{2,34},{3,35},{4,36},{5,37},{6,38},{7,39},{8,40},{9,... | collective-permute-start | bytes 49160 | tf_op jit(solution)/shard_map/ppermute | solution.py:35
  20.7 9.2 %collective-permute-start.8 = (f32[32,128]{1,0:T(8,128)S(1)}, f32[32,128]{1,0:T(8,128)S(1)}, u32[]{:S(2)}, u32[]{:S(2)}) collective-permute-start(f32[32,128]{1,0:T(8,128)S(1)} %shard_map.74.refs_8_), channel_id=1, source_target_pairs={{0,16},{1,17},{2,18},{3,19},{4,20},{5,21},{6,22},{7,23},{8,24},{9,... | collective-permute-start | bytes 49160 | tf_op jit(solution)/shard_map/ppermute | solution.py:35
  21.4 8.5 %collective-permute-start.9 = (f32[32,128]{1,0:T(8,128)S(1)}, f32[32,128]{1,0:T(8,128)S(1)}, u32[]{:S(2)}, u32[]{:S(2)}) collective-permute-start(f32[32,128]{1,0:T(8,128)S(1)} %shard_map.74.refs_8_), channel_id=1, source_target_pairs={{0,48},{1,49},{2,50},{3,51},{4,52},{5,53},{6,54},{7,55},{8,56},{9,... | collective-permute-start | bytes 49160 | tf_op jit(solution)/shard_map/ppermute | solution.py:35
  29.9 15.9 %copy-start.2 = (f32[1536]{0:T(1024)S(1)}, f32[1536]{0:T(1024)}, u32[]{:S(2)}) copy-start(f32[1536]{0:T(1024)} %param.12) | copy-start | bytes 18436
  30.0 8.7 %collective-permute-start.10 = (f32[32,128]{1,0:T(8,128)S(1)}, f32[32,128]{1,0:T(8,128)S(1)}, u32[]{:S(2)}, u32[]{:S(2)}) collective-permute-start(f32[32,128]{1,0:T(8,128)S(1)} %add_add_fusion.refs_9_.y0), channel_id=1, source_target_pairs={{0,128},{1,129},{2,130},{3,131},{4,132},{5,133},{6,134},{7,135},{8... | collective-permute-start | bytes 49160 | tf_op jit(solution)/shard_map/ppermute | solution.py:35
  38.7 15.5 %copy-start = (f32[1,2,16]{2,1,0:T(2,128)S(1)}, f32[1,2,16]{2,1,0:T(2,128)}, u32[]{:S(2)}) copy-start(f32[1,2,16]{2,1,0:T(2,128)} %param.8) | copy-start | bytes 388
  38.7 15.6 %copy-start.1 = (f32[1,16]{1,0:T(1,128)S(1)}, f32[1,16]{1,0:T(1,128)}, u32[]{:S(2)}) copy-start(f32[1,16]{1,0:T(1,128)} %energy_ref.1) | copy-start | bytes 196
  38.7 7.9 %collective-permute-start.14 = (f32[24,128]{1,0:T(8,128)S(1)}, f32[24,128]{1,0:T(8,128)S(1)}, u32[]{:S(2)}, u32[]{:S(2)}) collective-permute-start(f32[24,128]{1,0:T(8,128)S(1)} %get-tuple-element.21.m0), channel_id=1, source_target_pairs={{0,1},{1,0},{2,3},{3,2},{4,5},{5,4},{6,7},{7,6},{8,9},{9,8},{10,11... | collective-permute-start | bytes 36872 | tf_op jit(solution)/shard_map/ppermute | solution.py:35
  41.6 7.5 %collective-permute-start.11 = (f32[24,128]{1,0:T(8,128)S(1)}, f32[24,128]{1,0:T(8,128)S(1)}, u32[]{:S(2)}, u32[]{:S(2)}) collective-permute-start(f32[24,128]{1,0:T(8,128)S(1)} %get-tuple-element.18), channel_id=1, source_target_pairs={{0,4},{1,5},{2,6},{3,7},{4,0},{5,1},{6,2},{7,3},{8,12},{9,13},{10,... | collective-permute-start | bytes 36872 | tf_op jit(solution)/shard_map/ppermute | solution.py:35
  41.7 7.5 %collective-permute-start.12 = (f32[24,128]{1,0:T(8,128)S(1)}, f32[24,128]{1,0:T(8,128)S(1)}, u32[]{:S(2)}, u32[]{:S(2)}) collective-permute-start(f32[24,128]{1,0:T(8,128)S(1)} %get-tuple-element.19), channel_id=1, source_target_pairs={{0,2},{1,3},{2,0},{3,1},{4,6},{5,7},{6,4},{7,5},{8,10},{9,11},{10,... | collective-permute-start | bytes 36872 | tf_op jit(solution)/shard_map/ppermute | solution.py:35
  42.4 6.8 %collective-permute-start.13 = (f32[24,128]{1,0:T(8,128)S(1)}, f32[24,128]{1,0:T(8,128)S(1)}, u32[]{:S(2)}, u32[]{:S(2)}) collective-permute-start(f32[24,128]{1,0:T(8,128)S(1)} %get-tuple-element.20), channel_id=1, source_target_pairs={{0,6},{1,7},{2,4},{3,5},{4,2},{5,3},{6,0},{7,1},{8,14},{9,15},{10,... | collective-permute-start | bytes 36872 | tf_op jit(solution)/shard_map/ppermute | solution.py:35
  44.9 1.7 %collective-permute-start.15 = (f32[1,128]{1,0:T(1,128)S(1)}, f32[1,128]{1,0:T(1,128)S(1)}, u32[]{:S(2)}, u32[]{:S(2)}) collective-permute-start(f32[1,128]{1,0:T(1,128)S(1)} %slice.6), channel_id=1, source_target_pairs={{0,1},{1,0},{2,3},{3,2},{4,5},{5,4},{6,7},{7,6},{8,9},{9,8},{10,11... | collective-permute-start | bytes 1544 | tf_op jit(solution)/shard_map/ppermute | solution.py:35
  46.7 6.5 %collective-permute-start.16 = (f32[24,128]{1,0:T(8,128)S(1)}, f32[24,128]{1,0:T(8,128)S(1)}, u32[]{:S(2)}, u32[]{:S(2)}) collective-permute-start(f32[24,128]{1,0:T(8,128)S(1)} %shard_map.79.first_ref), channel_id=1, source_target_pairs={{0,8},{1,9},{2,10},{3,11},{4,12},{5,13},{6,14},{7,15},{8,0},{9,1},... | collective-permute-start | bytes 36872 | tf_op jit(solution)/shard_map/ppermute | solution.py:35
  49.2 5.0 %collective-permute-start.17 = (f32[1,128]{1,0:T(1,128)S(1)}, f32[1,128]{1,0:T(1,128)S(1)}, u32[]{:S(2)}, u32[]{:S(2)}) collective-permute-start(f32[1,128]{1,0:T(1,128)S(1)} %slice.8), channel_id=1, source_target_pairs={{0,192},{1,193},{2,194},{3,195},{4,196},{5,197},{6,198},{7,199},{8... | collective-permute-start | bytes 1544 | tf_op jit(solution)/shard_map/ppermute | solution.py:35

commit v6 on v4

--- a/solution.py
+++ b/solution.py
@@ -105,11 +105,9 @@
     copies[1].wait()
 
 
-def fetch_kernel(where_ref, qmap_ref, basis, screening, z_ref, w_ref, sems):
-    whole = pltpu.make_async_copy(basis, z_ref, sems.at[16])
-    whole.start()
-    own = where_ref[0]
-    member = where_ref[1]
+def weights_kernel(qmap_ref, screening, w_ref, sems):
+    own = lax.axis_index("grp")
+    member = lax.axis_index("kin")
     partner = (own + 12) & 15
     steps = []
     for m, flip in enumerate((8, 9, 0, 1)):
@@ -123,7 +121,6 @@
             steps.append(copy)
     for copy in steps:
         copy.wait()
-    whole.wait()
 
 
 def transitions_kernel(a0, a1, a2, a3, y_ref):
@@ -351,16 +348,16 @@
     a1 = move(pay, far=1)
     b0 = move(pay, step=1)
     a2 = move(pay, core=1)
-    where = jnp.stack([lax.axis_index("grp"), lax.axis_index("kin")]).astype(jnp.int32)
-    z, weights = pl.pallas_call(
-        fetch_kernel,
-        in_specs=[SMEM, SMEM, ANY, ANY],
-        out_specs=[VMEM] * 2,
-        out_shape=[pltpu.VMEM((2 * NMU, NG), BF16), pltpu.VMEM((16, NG), F32)],
-        scratch_shapes=[pltpu.SemaphoreType.DMA((17,))],
-        compiler_params=params(50),
-        cost_estimate=cost(128),
-    )(where, qmap, basis.reshape(2 * NMU, NG), screening)
+    z = basis.reshape(2 * NMU, NG)
+    weights = pl.pallas_call(
+        weights_kernel,
+        in_specs=[SMEM, ANY],
+        out_specs=VMEM,
+        out_shape=pltpu.VMEM((16, NG), F32),
+        scratch_shapes=[pltpu.SemaphoreType.DMA((16,))],
+        compiler_params=params(54),
+        cost_estimate=pl.CostEstimate(flops=4000000000, bytes_accessed=1024, transcendentals=0),
+    )(qmap, screening)
     b1, b2, b3 = (move(b0, y=n) for n in (1, 2, 3))
     a3 = move(a1, core=1)
     y = pl.pallas_call(

time: 54.5 us -> 49.5 us (0.908)
  waiting for transfers between devices: 10.3 us -> 3.64 us
  starting transfers between devices: 26.4 us -> 30.3 us
  Pallas kernels: 16.9 us -> 15.1 us
  other arithmetic: 0.6 us -> 0.02 us
    ppermute x20, waiting for transfers between devices: 10.3 us -> 3.64 us  [move(): return lax.ppermute(value, ('grp', 'kin'), pairs)]
    ppermute x20, starting transfers between devices: 26.4 us -> 30.3 us  [move(): return lax.ppermute(value, ('grp', 'kin'), pairs)]
    pallas_call x1, Pallas kernels: 3.63 us -> 1.74 us  [on_device(): pl.pallas_call(weights_kernel, in_specs=[SMEM, ANY], out_specs=VMEM, out_...]
    another operation x1 -> x0, other arithmetic: 0.59 us -> none  [on_device(): jnp.stack([lax.axis_index('grp'), lax.axis_index('kin')]).astype(jnp.int32)]
  transfers between devices with their start and end apart: 20 -> 20, of which waited for: 6 -> 3; matrix products, arithmetic and copies ran while one was open for 1% -> 0% of each run, Pallas kernels for 28% -> 27%
where the time goes in v6:
time: 49.5 us; the launch traced here: 49.3 us
  starting transfers between devices  30.3 us (61%)
  Pallas kernels  15.1 us (31%)
  waiting for transfers between devices  3.64 us (7%)
    ppermute x20, starting transfers between devices, move(): return lax.ppermute(value, ('grp', 'kin'), pairs)  30.3 us
    pallas_call x2, Pallas kernels, pair_call(): pl.pallas_call(functools.partial(pair_kernel, near), in_specs=[VMEM] * 8...  10.4 us
    ppermute x20, waiting for transfers between devices, move(): return lax.ppermute(value, ('grp', 'kin'), pairs)  3.64 us
    pallas_call x1, Pallas kernels, on_device(): pl.pallas_call(weights_kernel, in_specs=[SMEM, ANY], out_specs=VMEM, out_...  1.74 us
    pallas_call x1, Pallas kernels, on_device(): pl.pallas_call(pack_kernel, in_specs=[ANY] * 2, out_specs=VMEM, out_shape...  1.1 us
    pallas_call x1, Pallas kernels, on_device(): pl.pallas_call(exchange_kernel, in_specs=[VMEM] * 4, out_specs=VMEM, out_...  1.06 us
  transfers between devices with their start and end apart: 20, of which 3 were waited for; matrix products, arithmetic and copies ran while one was open for 0% of the time, Pallas kernels for 27%

profile of v6, /device:TPU:6, one launch (start us, length us, event | category | flops | bytes accessed | tf_op | source)
XLA Modules:
  0.0 49.3 jit_solution(7955427308123735690)
XLA Ops:
  0.0 1.1 %shard_map.73.a0.refs_0_ = bf16[16,1152]{1,0:T(8,128)(2,1)S(1)} custom-call(bf16[16,1024]{1,0:T(8,128)(2,1)} %bitcast.11, f32[2,16]{1,0:T(2,128)} %bitcast.9), custom_call_target="tpu_custom_call" | custom-call | tf_op jit(solution)/shard_map/pallas_call | solution.py:340
  1.1 0.0 copy-start.2
  1.1 0.0 slice-start.1
  1.1 2.3 %collective-permute-start.9 = (bf16[16,1152]{1,0:T(8,128)(2,1)S(1)}, bf16[16,1152]{1,0:T(8,128)(2,1)S(1)}, u32[]{:S(2)}, u32[]{:S(2)}) collective-permute-start(bf16[16,1152]{1,0:T(8,128)(2,1)S(1)} %shard_map.73.a0.refs_0_), channel_id=1, source_target_pairs={{0,64},{1,65},{2,66},{3,67},{4,68},{5,69},{6,70},{7,71},{8,72},{9,... | collective-permute-start | bytes 110600 | tf_op jit(solution)/shard_map/ppermute | solution.py:34
  3.4 5.5 %collective-permute-start = (bf16[16,1152]{1,0:T(8,128)(2,1)S(1)}, bf16[16,1152]{1,0:T(8,128)(2,1)S(1)}, u32[]{:S(2)}, u32[]{:S(2)}) collective-permute-start(bf16[16,1152]{1,0:T(8,128)(2,1)S(1)} %shard_map.73.a0.refs_0_), channel_id=1, source_target_pairs={{0,8},{1,9},{2,10},{3,11},{4,12},{5,13},{6,14},{7,15},{8,0},{9,1},... | collective-permute-start | bytes 110600 | tf_op jit(solution)/shard_map/ppermute | solution.py:34
  8.9 0.0 collective-permute-start.1
  8.9 0.0 collective-permute-done.9.refs_2_
  8.9 1.6 %collective-permute-start.10 = (bf16[16,1152]{1,0:T(8,128)(2,1)S(1)}, bf16[16,1152]{1,0:T(8,128)(2,1)S(1)}, u32[]{:S(2)}, u32[]{:S(2)}) collective-permute-start(bf16[16,1152]{1,0:T(8,128)(2,1)S(1)} %collective-permute-done.9.refs_2_), channel_id=1, source_target_pairs={{0,2},{1,3},{2,0},{3,1},{4,6},{5,7},{6,4},{7,5},{8,10},{9,11},{10,... | collective-permute-start | bytes 110600 | tf_op jit(solution)/shard_map/ppermute | solution.py:34
  10.5 2.9 %collective-permute-start.11 = (bf16[16,1152]{1,0:T(8,128)(2,1)S(1)}, bf16[16,1152]{1,0:T(8,128)(2,1)S(1)}, u32[]{:S(2)}, u32[]{:S(2)}) collective-permute-start(bf16[16,1152]{1,0:T(8,128)(2,1)S(1)} %collective-permute-done.9.refs_2_), channel_id=1, source_target_pairs={{0,4},{1,5},{2,6},{3,7},{4,0},{5,1},{6,2},{7,3},{8,12},{9,13},{10,... | collective-permute-start | bytes 110600 | tf_op jit(solution)/shard_map/ppermute | solution.py:34
  13.4 0.2 collective-permute-start.12
  13.6 0.0 collective-permute-done.a1.refs_0_
  13.6 0.0 collective-permute-start.2
  13.6 1.7 %shard_map.75.refs_6_ = f32[16,1536]{1,0:T(8,128)S(1)} custom-call(s32[1,256]{1,0:T(1,128)} %qmap_ref.1, f32[256,1536]{1,0:T(8,128)} %screening.1), custom_call_target="tpu_custom_call" | custom-call | flops 4000000000 | bytes 1024 | tf_op jit(solution)/shard_map/pallas_call | solution.py:352
  15.4 0.0 collective-permute-done.1.a2.refs_1_
  15.4 0.0 collective-permute-done.2.a3.refs_1_
  15.4 0.2 shard_map.74.refs_8_
  15.6 1.6 %collective-permute-start.3 = (f32[16,128]{1,0:T(8,128)S(1)}, f32[16,128]{1,0:T(8,128)S(1)}, u32[]{:S(2)}, u32[]{:S(2)}) collective-permute-start(f32[16,128]{1,0:T(8,128)S(1)} %shard_map.74.refs_8_), channel_id=1, source_target_pairs={{0,32},{1,33},{2,34},{3,35},{4,36},{5,37},{6,38},{7,39},{8,40},{9,... | collective-permute-start | bytes 24584 | tf_op jit(solution)/shard_map/ppermute | solution.py:34
  17.1 1.0 %collective-permute-start.4 = (f32[16,128]{1,0:T(8,128)S(1)}, f32[16,128]{1,0:T(8,128)S(1)}, u32[]{:S(2)}, u32[]{:S(2)}) collective-permute-start(f32[16,128]{1,0:T(8,128)S(1)} %shard_map.74.refs_8_), channel_id=1, source_target_pairs={{0,16},{1,17},{2,18},{3,19},{4,20},{5,21},{6,22},{7,23},{8,24},{9,... | collective-permute-start | bytes 24584 | tf_op jit(solution)/shard_map/ppermute | solution.py:34
  18.2 0.0 collective-permute-done.10.refs_3_
  18.2 1.9 %collective-permute-start.5 = (f32[16,128]{1,0:T(8,128)S(1)}, f32[16,128]{1,0:T(8,128)S(1)}, u32[]{:S(2)}, u32[]{:S(2)}) collective-permute-start(f32[16,128]{1,0:T(8,128)S(1)} %shard_map.74.refs_8_), channel_id=1, source_target_pairs={{0,48},{1,49},{2,50},{3,51},{4,52},{5,53},{6,54},{7,55},{8,56},{9,... | collective-permute-start | bytes 24584 | tf_op jit(solution)/shard_map/ppermute | solution.py:34
  20.1 0.0 collective-permute-done.11.refs_4_
  20.1 0.0 collective-permute-done.12.refs_5_
  20.1 4.9 %shard_map.76.refs_8_ = f32[8,128]{1,0:T(8,128)S(1)} custom-call(bf16[16,1152]{1,0:T(8,128)(2,1)S(1)} %collective-permute-done.a1.refs_0_, bf16[16,1152]{1,0:T(8,128)(2,1)S(1)} %collective-permute-done.2.a3.refs_1_, bf16[16,1152]{1,0:T(8,128)(2,1)S(1)} %collective-permute-done.9.refs_2_, bf16[16,1152]{1,0:T(8,128)(2,1)S(1)} %collective-permute-done.10.refs_3_, ...), custom_call_target="tpu_custom_call" | custom-call | flops 3221225472 | bytes 6291456 | tf_op jit(solution)/shard_map/pallas_call | solution.py:321
  25.0 0.0 collective-permute-start.17
  25.0 0.0 collective-permute-done.3
  25.0 0.0 collective-permute-done.4
  25.0 0.0 collective-permute-done.5
  25.1 2.5 %collective-permute-start.6 = (f32[16,128]{1,0:T(8,128)S(1)}, f32[16,128]{1,0:T(8,128)S(1)}, u32[]{:S(2)}, u32[]{:S(2)}) collective-permute-start(f32[16,128]{1,0:T(8,128)S(1)} %add_add_fusion.1.refs_9_.y0), channel_id=1, source_target_pairs={{0,128},{1,129},{2,130},{3,131},{4,132},{5,133},{6,134},{7,135},{8... | collective-permute-start | bytes 24584 | tf_op jit(solution)/shard_map/ppermute | solution.py:34
  27.6 0.0 collective-permute-start.7
  27.6 1.8 %collective-permute-start.8 = (f32[16,128]{1,0:T(8,128)S(1)}, f32[16,128]{1,0:T(8,128)S(1)}, u32[]{:S(2)}, u32[]{:S(2)}) collective-permute-start(f32[16,128]{1,0:T(8,128)S(1)} %add_add_fusion.1.refs_9_.y0), channel_id=1, source_target_pairs={{0,192},{1,193},{2,194},{3,195},{4,196},{5,197},{6,198},{7,199},{8... | collective-permute-start | bytes 24584 | tf_op jit(solution)/shard_map/ppermute | solution.py:34
  29.4 5.5 %shard_map.77 = (f32[8,128]{1,0:T(8,128)S(1)}, f32[32,1536]{1,0:T(8,128)S(1)}) custom-call(bf16[16,1152]{1,0:T(8,128)(2,1)S(1)} %shard_map.73.a0.refs_0_, bf16[16,1152]{1,0:T(8,128)(2,1)S(1)} %collective-permute-done.1.a2.refs_1_, bf16[16,1152]{1,0:T(8,128)(2,1)S(1)} %collective-permute-done.9.refs_2_, bf16[16,1152]{1,0:T(8,128)(2,1)S(1)} %collective-permute-done.10.refs_3_, ...), custom_call_target="tpu_custom_call" | custom-call | flops 3221225472 | bytes 6291456 | tf_op jit(solution)/shard_map/pallas_call | solution.py:321
  34.9 0.0 collective-permute-done.6.y1
  34.9 0.0 collective-permute-done.7.y2
  34.9 0.0 collective-permute-done.8.y3
  35.0 2.1 %collective-permute-start.13 = (f32[24,128]{1,0:T(8,128)S(1)}, f32[24,128]{1,0:T(8,128)S(1)}, u32[]{:S(2)}, u32[]{:S(2)}) collective-permute-start(f32[24,128]{1,0:T(8,128)S(1)} %get-tuple-element.13), channel_id=1, source_target_pairs={{0,4},{1,5},{2,6},{3,7},{4,0},{5,1},{6,2},{7,3},{8,12},{9,13},{10,... | collective-permute-start | bytes 36872 | tf_op jit(solution)/shard_map/ppermute | solution.py:34
  37.0 1.9 %collective-permute-start.14 = (f32[24,128]{1,0:T(8,128)S(1)}, f32[24,128]{1,0:T(8,128)S(1)}, u32[]{:S(2)}, u32[]{:S(2)}) collective-permute-start(f32[24,128]{1,0:T(8,128)S(1)} %get-tuple-element.14), channel_id=1, source_target_pairs={{0,2},{1,3},{2,0},{3,1},{4,6},{5,7},{6,4},{7,5},{8,10},{9,11},{10,... | collective-permute-start | bytes 36872 | tf_op jit(solution)/shard_map/ppermute | solution.py:34
  38.9 0.2 collective-permute-start.15
  39.1 0.0 collective-permute-done.17
  39.2 3.3 %collective-permute-start.18 = (f32[1,128]{1,0:T(1,128)S(1)}, f32[1,128]{1,0:T(1,128)S(1)}, u32[]{:S(2)}, u32[]{:S(2)}) collective-permute-start(f32[1,128]{1,0:T(1,128)S(1)} %slice_add_fusion), channel_id=1, source_target_pairs={{0,8},{1,9},{2,10},{3,11},{4,12},{5,13},{6,14},{7,15},{8,0},{9,1},... | collective-permute-start | bytes 1544 | tf_op jit(solution)/shard_map/ppermute | solution.py:34
  42.5 0.0 collective-permute-start.16
  42.5 0.0 collective-permute-done.13
  42.5 1.3 %collective-permute-done.15 = f32[24,128]{1,0:T(8,128)S(1)} collective-permute-done((f32[24,128]{1,0:T(8,128)S(1)}, f32[24,128]{1,0:T(8,128)S(1)}, u32[]{:S(2)}, u32[]{:S(2)}) %collective-permute-start.15) | collective-permute-done | bytes 12320 | tf_op jit(solution)/shard_map/ppermute | solution.py:34
  43.9 1.5 %collective-permute-start.19 = (f32[1,128]{1,0:T(1,128)S(1)}, f32[1,128]{1,0:T(1,128)S(1)}, u32[]{:S(2)}, u32[]{:S(2)}) collective-permute-start(f32[1,128]{1,0:T(1,128)S(1)} %slice.16), channel_id=1, source_target_pairs={{0,192},{1,193},{2,194},{3,195},{4,196},{5,197},{6,198},{7,199},{8... | collective-permute-start | bytes 1544 | tf_op jit(solution)/shard_map/ppermute | solution.py:34
  45.3 1.1 %shard_map.79.exchange_ref = f32[2,16]{1,0:T(2,128)S(1)} custom-call(f32[24,128]{1,0:T(8,128)S(1)} %add_add_fusion.y_ref, f32[1,1536]{1,0:T(1,128)S(1)} %reshape.19.c_ref, f32[32,1536]{1,0:T(8,128)S(1)} %get-tuple-element.16.rx_ref, bf16[2048,1536]{1,0:T(8,128)(2,1)S(1)} %bitcast.8), custom_call_target="tpu_custom_call" | custom-call | flops 805306368 | bytes 6291456 | tf_op jit(solution)/shard_map/pallas_call | solution.py:383
  46.4 0.2 collective-permute-done.18.d1
  46.6 0.0 collective-permute-done.16.d0
  46.6 2.1 %collective-permute-done.19.d2 = f32[1,128]{1,0:T(1,128)S(1)} collective-permute-done((f32[1,128]{1,0:T(1,128)S(1)}, f32[1,128]{1,0:T(1,128)S(1)}, u32[]{:S(2)}, u32[]{:S(2)}) %collective-permute-start.19) | collective-permute-done | bytes 544 | tf_op jit(solution)/shard_map/ppermute | solution.py:34
  48.7 0.6 %shard_map.80 = f32[2,16]{1,0:T(2,128)} custom-call(f32[1,16]{1,0:T(1,128)S(1)} %copy-done.1, f32[2,16]{1,0:T(2,128)S(1)} %bitcast.10, f32[2,16]{1,0:T(2,128)S(1)} %shard_map.79.exchange_ref, f32[8,128]{1,0:T(8,128)S(1)} %get-tuple-element.11.out_ref.near_ref, f32[1,128]{1,0:T(1,128)S(1)} %collective-permute-done.16.d0, ...), custom_call_target="tpu_custom_call" | custom-call | tf_op jit(solution)/shard_map/pallas_call | solution.py:393
  (18 shorter events, 0.1 us)
Async XLA Ops:
  0.0 20.1 %slice-start = ((s8[6291456]{0:T(1024)(128)(4,1)}), s8[2097152]{0:T(1024)(128)(4,1)S(1)}, s32[]{:S(2)}) async-start(s8[6291456]{0:T(1024)(128)(4,1)} %bitcast.4), calls=%async_computation | async-start | bytes 4194304
  1.1 14.2 %copy-start.2 = (f32[1536]{0:T(1024)S(1)}, f32[1536]{0:T(1024)}, u32[]{:S(2)}) copy-start(f32[1536]{0:T(1024)} %param.12) | copy-start | bytes 18436
  1.1 19.0 %slice-start.1 = ((s8[6291456]{0:T(1024)(128)(4,1)}), s8[4194304]{0:T(1024)(128)(4,1)S(1)}, s32[]{:S(2)}) async-start(s8[6291456]{0:T(1024)(128)(4,1)} %bitcast.4), calls=%async_computation.1 | async-start | bytes 8388608
  1.1 7.8 %collective-permute-start.9 = (bf16[16,1152]{1,0:T(8,128)(2,1)S(1)}, bf16[16,1152]{1,0:T(8,128)(2,1)S(1)}, u32[]{:S(2)}, u32[]{:S(2)}) collective-permute-start(bf16[16,1152]{1,0:T(8,128)(2,1)S(1)} %shard_map.73.a0.refs_0_), channel_id=1, source_target_pairs={{0,64},{1,65},{2,66},{3,67},{4,68},{5,69},{6,70},{7,71},{8,72},{9,... | collective-permute-start | bytes 110600 | tf_op jit(solution)/shard_map/ppermute | solution.py:34
  3.4 10.2 %collective-permute-start = (bf16[16,1152]{1,0:T(8,128)(2,1)S(1)}, bf16[16,1152]{1,0:T(8,128)(2,1)S(1)}, u32[]{:S(2)}, u32[]{:S(2)}) collective-permute-start(bf16[16,1152]{1,0:T(8,128)(2,1)S(1)} %shard_map.73.a0.refs_0_), channel_id=1, source_target_pairs={{0,8},{1,9},{2,10},{3,11},{4,12},{5,13},{6,14},{7,15},{8,0},{9,1},... | collective-permute-start | bytes 110600 | tf_op jit(solution)/shard_map/ppermute | solution.py:34
  8.9 6.5 %collective-permute-start.1 = (bf16[16,1152]{1,0:T(8,128)(2,1)S(1)}, bf16[16,1152]{1,0:T(8,128)(2,1)S(1)}, u32[]{:S(2)}, u32[]{:S(2)}) collective-permute-start(bf16[16,1152]{1,0:T(8,128)(2,1)S(1)} %shard_map.73.a0.refs_0_), channel_id=1, source_target_pairs={{0,1},{1,0},{2,3},{3,2},{4,5},{5,4},{6,7},{7,6},{8,9},{9,8},{10,11... | collective-permute-start | bytes 110600 | tf_op jit(solution)/shard_map/ppermute | solution.py:34
  8.9 9.3 %collective-permute-start.10 = (bf16[16,1152]{1,0:T(8,128)(2,1)S(1)}, bf16[16,1152]{1,0:T(8,128)(2,1)S(1)}, u32[]{:S(2)}, u32[]{:S(2)}) collective-permute-start(bf16[16,1152]{1,0:T(8,128)(2,1)S(1)} %collective-permute-done.9.refs_2_), channel_id=1, source_target_pairs={{0,2},{1,3},{2,0},{3,1},{4,6},{5,7},{6,4},{7,5},{8,10},{9,11},{10,... | collective-permute-start | bytes 110600 | tf_op jit(solution)/shard_map/ppermute | solution.py:34
  10.5 9.6 %collective-permute-start.11 = (bf16[16,1152]{1,0:T(8,128)(2,1)S(1)}, bf16[16,1152]{1,0:T(8,128)(2,1)S(1)}, u32[]{:S(2)}, u32[]{:S(2)}) collective-permute-start(bf16[16,1152]{1,0:T(8,128)(2,1)S(1)} %collective-permute-done.9.refs_2_), channel_id=1, source_target_pairs={{0,4},{1,5},{2,6},{3,7},{4,0},{5,1},{6,2},{7,3},{8,12},{9,13},{10,... | collective-permute-start | bytes 110600 | tf_op jit(solution)/shard_map/ppermute | solution.py:34
  13.4 6.7 %collective-permute-start.12 = (bf16[16,1152]{1,0:T(8,128)(2,1)S(1)}, bf16[16,1152]{1,0:T(8,128)(2,1)S(1)}, u32[]{:S(2)}, u32[]{:S(2)}) collective-permute-start(bf16[16,1152]{1,0:T(8,128)(2,1)S(1)} %collective-permute-done.9.refs_2_), channel_id=1, source_target_pairs={{0,6},{1,7},{2,4},{3,5},{4,2},{5,3},{6,0},{7,1},{8,14},{9,15},{10,... | collective-permute-start | bytes 110600 | tf_op jit(solution)/shard_map/ppermute | solution.py:34
  13.6 1.8 %collective-permute-start.2 = (bf16[16,1152]{1,0:T(8,128)(2,1)S(1)}, bf16[16,1152]{1,0:T(8,128)(2,1)S(1)}, u32[]{:S(2)}, u32[]{:S(2)}) collective-permute-start(bf16[16,1152]{1,0:T(8,128)(2,1)S(1)} %collective-permute-done.a1.refs_0_), channel_id=1, source_target_pairs={{0,1},{1,0},{2,3},{3,2},{4,5},{5,4},{6,7},{7,6},{8,9},{9,8},{10,11... | collective-permute-start | bytes 110600 | tf_op jit(solution)/shard_map/ppermute | solution.py:34
  15.6 9.5 %collective-permute-start.3 = (f32[16,128]{1,0:T(8,128)S(1)}, f32[16,128]{1,0:T(8,128)S(1)}, u32[]{:S(2)}, u32[]{:S(2)}) collective-permute-start(f32[16,128]{1,0:T(8,128)S(1)} %shard_map.74.refs_8_), channel_id=1, source_target_pairs={{0,32},{1,33},{2,34},{3,35},{4,36},{5,37},{6,38},{7,39},{8,40},{9,... | collective-permute-start | bytes 24584 | tf_op jit(solution)/shard_map/ppermute | solution.py:34
  17.1 7.9 %collective-permute-start.4 = (f32[16,128]{1,0:T(8,128)S(1)}, f32[16,128]{1,0:T(8,128)S(1)}, u32[]{:S(2)}, u32[]{:S(2)}) collective-permute-start(f32[16,128]{1,0:T(8,128)S(1)} %shard_map.74.refs_8_), channel_id=1, source_target_pairs={{0,16},{1,17},{2,18},{3,19},{4,20},{5,21},{6,22},{7,23},{8,24},{9,... | collective-permute-start | bytes 24584 | tf_op jit(solution)/shard_map/ppermute | solution.py:34
  18.2 6.9 %collective-permute-start.5 = (f32[16,128]{1,0:T(8,128)S(1)}, f32[16,128]{1,0:T(8,128)S(1)}, u32[]{:S(2)}, u32[]{:S(2)}) collective-permute-start(f32[16,128]{1,0:T(8,128)S(1)} %shard_map.74.refs_8_), channel_id=1, source_target_pairs={{0,48},{1,49},{2,50},{3,51},{4,52},{5,53},{6,54},{7,55},{8,56},{9,... | collective-permute-start | bytes 24584 | tf_op jit(solution)/shard_map/ppermute | solution.py:34
  25.0 14.2 %collective-permute-start.17 = (f32[1,128]{1,0:T(1,128)S(1)}, f32[1,128]{1,0:T(1,128)S(1)}, u32[]{:S(2)}, u32[]{:S(2)}) collective-permute-start(f32[1,128]{1,0:T(1,128)S(1)} %slice.14), channel_id=1, source_target_pairs={{0,1},{1,0},{2,3},{3,2},{4,5},{5,4},{6,7},{7,6},{8,9},{9,8},{10,11... | collective-permute-start | bytes 1544 | tf_op jit(solution)/shard_map/ppermute | solution.py:34
  25.1 9.8 %collective-permute-start.6 = (f32[16,128]{1,0:T(8,128)S(1)}, f32[16,128]{1,0:T(8,128)S(1)}, u32[]{:S(2)}, u32[]{:S(2)}) collective-permute-start(f32[16,128]{1,0:T(8,128)S(1)} %add_add_fusion.1.refs_9_.y0), channel_id=1, source_target_pairs={{0,128},{1,129},{2,130},{3,131},{4,132},{5,133},{6,134},{7,135},{8... | collective-permute-start | bytes 24584 | tf_op jit(solution)/shard_map/ppermute | solution.py:34
  27.6 7.3 %collective-permute-start.7 = (f32[16,128]{1,0:T(8,128)S(1)}, f32[16,128]{1,0:T(8,128)S(1)}, u32[]{:S(2)}, u32[]{:S(2)}) collective-permute-start(f32[16,128]{1,0:T(8,128)S(1)} %add_add_fusion.1.refs_9_.y0), channel_id=1, source_target_pairs={{0,64},{1,65},{2,66},{3,67},{4,68},{5,69},{6,70},{7,71},{8,72},{9,... | collective-permute-start | bytes 24584 | tf_op jit(solution)/shard_map/ppermute | solution.py:34
  27.6 7.4 %collective-permute-start.8 = (f32[16,128]{1,0:T(8,128)S(1)}, f32[16,128]{1,0:T(8,128)S(1)}, u32[]{:S(2)}, u32[]{:S(2)}) collective-permute-start(f32[16,128]{1,0:T(8,128)S(1)} %add_add_fusion.1.refs_9_.y0), channel_id=1, source_target_pairs={{0,192},{1,193},{2,194},{3,195},{4,196},{5,197},{6,198},{7,199},{8... | collective-permute-start | bytes 24584 | tf_op jit(solution)/shard_map/ppermute | solution.py:34
  34.9 13.8 %copy-start = (f32[1,2,16]{2,1,0:T(2,128)S(1)}, f32[1,2,16]{2,1,0:T(2,128)}, u32[]{:S(2)}) copy-start(f32[1,2,16]{2,1,0:T(2,128)} %param.8) | copy-start | bytes 388
  34.9 13.8 %copy-start.1 = (f32[1,16]{1,0:T(1,128)S(1)}, f32[1,16]{1,0:T(1,128)}, u32[]{:S(2)}) copy-start(f32[1,16]{1,0:T(1,128)} %energy_ref.1) | copy-start | bytes 196
  35.0 7.5 %collective-permute-start.13 = (f32[24,128]{1,0:T(8,128)S(1)}, f32[24,128]{1,0:T(8,128)S(1)}, u32[]{:S(2)}, u32[]{:S(2)}) collective-permute-start(f32[24,128]{1,0:T(8,128)S(1)} %get-tuple-element.13), channel_id=1, source_target_pairs={{0,4},{1,5},{2,6},{3,7},{4,0},{5,1},{6,2},{7,3},{8,12},{9,13},{10,... | collective-permute-start | bytes 36872 | tf_op jit(solution)/shard_map/ppermute | solution.py:34
  37.0 5.5 %collective-permute-start.14 = (f32[24,128]{1,0:T(8,128)S(1)}, f32[24,128]{1,0:T(8,128)S(1)}, u32[]{:S(2)}, u32[]{:S(2)}) collective-permute-start(f32[24,128]{1,0:T(8,128)S(1)} %get-tuple-element.14), channel_id=1, source_target_pairs={{0,2},{1,3},{2,0},{3,1},{4,6},{5,7},{6,4},{7,5},{8,10},{9,11},{10,... | collective-permute-start | bytes 36872 | tf_op jit(solution)/shard_map/ppermute | solution.py:34
  38.9 4.9 %collective-permute-start.15 = (f32[24,128]{1,0:T(8,128)S(1)}, f32[24,128]{1,0:T(8,128)S(1)}, u32[]{:S(2)}, u32[]{:S(2)}) collective-permute-start(f32[24,128]{1,0:T(8,128)S(1)} %get-tuple-element.15), channel_id=1, source_target_pairs={{0,6},{1,7},{2,4},{3,5},{4,2},{5,3},{6,0},{7,1},{8,14},{9,15},{10,... | collective-permute-start | bytes 36872 | tf_op jit(solution)/shard_map/ppermute | solution.py:34
  39.2 7.4 %collective-permute-start.18 = (f32[1,128]{1,0:T(1,128)S(1)}, f32[1,128]{1,0:T(1,128)S(1)}, u32[]{:S(2)}, u32[]{:S(2)}) collective-permute-start(f32[1,128]{1,0:T(1,128)S(1)} %slice_add_fusion), channel_id=1, source_target_pairs={{0,8},{1,9},{2,10},{3,11},{4,12},{5,13},{6,14},{7,15},{8,0},{9,1},... | collective-permute-start | bytes 1544 | tf_op jit(solution)/shard_map/ppermute | solution.py:34
  42.5 4.1 %collective-permute-start.16 = (f32[1,128]{1,0:T(1,128)S(1)}, f32[1,128]{1,0:T(1,128)S(1)}, u32[]{:S(2)}, u32[]{:S(2)}) collective-permute-start(f32[1,128]{1,0:T(1,128)S(1)} %slice.12), channel_id=1, source_target_pairs={{0,1},{1,0},{2,3},{3,2},{4,5},{5,4},{6,7},{7,6},{8,9},{9,8},{10,11... | collective-permute-start | bytes 1544 | tf_op jit(solution)/shard_map/ppermute | solution.py:34
  43.9 4.8 %collective-permute-start.19 = (f32[1,128]{1,0:T(1,128)S(1)}, f32[1,128]{1,0:T(1,128)S(1)}, u32[]{:S(2)}, u32[]{:S(2)}) collective-permute-start(f32[1,128]{1,0:T(1,128)S(1)} %slice.16), channel_id=1, source_target_pairs={{0,192},{1,193},{2,194},{3,195},{4,196},{5,197},{6,198},{7,199},{8... | collective-permute-start | bytes 1544 | tf_op jit(solution)/shard_map/ppermute | solution.py:34

commit v7 on v6

--- a/solution.py
+++ b/solution.py
@@ -11,7 +11,7 @@
 NMU = 1024
 NG = 1536
 WIDTH = NMU + 128
-CHUNK = 512
+CHUNK = 1536
 ROWS = 128
 F32 = jnp.float32
 BF16 = jnp.bfloat16
@@ -110,10 +110,10 @@
     member = lax.axis_index("kin")
     partner = (own + 12) & 15
     steps = []
-    for m, flip in enumerate((8, 9, 0, 1)):
+    for m, flip in enumerate((4, 6, 0, 2)):
         from_a = qmap_ref[0, own * 16 + (member ^ flip)]
-        for n in range(4):
-            from_b = qmap_ref[0, partner * 16 + (member ^ (2 * n))]
+        for n, other in enumerate((0, 8, 1, 9)):
+            from_b = qmap_ref[0, partner * 16 + (member ^ other)]
             index = (((from_b >> 4) - (from_a >> 4)) & 15) * 16 + ((from_b - from_a) & 15)
             at = m * 4 + n
             copy = pltpu.make_async_copy(screening.at[pl.ds(index, 1)], w_ref.at[pl.ds(at, 1)], sems.at[at])
@@ -123,7 +123,7 @@
         copy.wait()
 
 
-def transitions_kernel(a0, a1, a2, a3, y_ref):
+def transitions_kernel(a0, a1, a2, a3, _, __, y_ref):
     total_re = jnp.zeros((8, NMU), F32)
     total_im = jnp.zeros((8, NMU), F32)
     for pay in (a0, a1, a2, a3):
@@ -143,12 +143,12 @@
 
 def pair_kernel(near, *refs):
     if near:
-        w_ref, z_ref, far_ref, _, out_ref, rx_ref, lhs, own, xa, xb, acc, ca, cb = refs[6:]
+        w_ref, z_ref, far_ref, _, out_ref, rx_ref, lhs, own, xa, xb, acc, ca, cb = refs[5:]
     else:
-        w_ref, z_ref, _, out_ref, lhs, xa, xb, acc, ca, cb = refs[6:]
+        w_ref, z_ref, _, out_ref, lhs, xa, xb, acc, ca, cb = refs[5:]
     base = 2 * near
-    a_pays = refs[0:2]
-    b_pays = refs[2:6]
+    a_pays = [refs[0].at[pl.ds(m * 16, 16)] for m in range(2)]
+    b_pays = refs[1:5]
     half = 2 * ROWS
 
     def put(to, row, top, left, right, left_at, right_at):
@@ -254,26 +254,40 @@
     out_ref[...] = total
 
 
-def mail_kernel(y0, y1, y2, y3, out_ref, *mails):
-    total = y0[...] + y1[...] + y2[...] + y3[...]
-    for n, mail in enumerate(mails):
-        mail[0:16] = total
-        mail[16:24] = jnp.broadcast_to(out_ref[4 + n : 5 + n], (8, 128))
-
-
-def exchange_kernel(y_ref, c_ref, rx_ref, z_ref, out_ref, lhs):
+def first_mail_kernel(y0, y1, y2, y3, far_ref, mail):
+    mail[0:16] = y0[...] + y1[...] + y2[...] + y3[...]
+    mail[16:24] = far_ref[...]
+
+
+def second_mail_kernel(sent, received, near_ref, mail, herm):
+    mail[0:16] = sent[0:16] + received[0:16]
+    mail[16:24] = near_ref[...] + received[16:24]
+    herm[...] = near_ref[...]
+
+
+def row_kernel(herm, _, out_ref):
+    out_ref[...] = herm[0:1]
+
+
+def join_kernel(first, second, out_ref):
+    out_ref[0:16] = first[...]
+    out_ref[16:32] = second[...]
+
+
+def exchange_kernel(sent, received, c_ref, rx_ref, z_ref, out_ref, lhs):
+    y = sent[0:16] + received[0:16]
     pad = jnp.zeros((12, 128), F32)
     for j in range(8):
-        real = y_ref[j : j + 1]
-        imag = y_ref[8 + j : 9 + j]
+        real = y[j : j + 1]
+        imag = y[8 + j : 9 + j]
         for at, top, bottom in ((0, real, imag), (NMU, -imag, real)):
             high, low = split(jnp.concatenate([top, bottom], 0))
             rows = jnp.concatenate([high.astype(F32), low.astype(F32), pad], 0)
             lhs[:, at + j * 128 : at + j * 128 + 128] = rows.astype(BF16)
     acc_re = jnp.zeros((16, 128), F32)
     acc_im = jnp.zeros((16, 128), F32)
-    for start in range(0, NG, CHUNK):
-        part = pl.ds(start, CHUNK)
+    for start in range(0, NG, 512):
+        part = pl.ds(start, 512)
         total = dot(lhs[...], z_ref[:, part])
         pot_re = (total[0:1] + total[2:3]) * c_ref[:, part]
         pot_im = (total[1:2] + total[3:4]) * c_ref[:, part]
@@ -281,7 +295,7 @@
         rx_im = rx_ref[16:32, part]
         real = rx_re * pot_re + rx_im * pot_im
         imag = rx_re * pot_im - rx_im * pot_re
-        for at in range(0, CHUNK, 128):
+        for at in range(0, 512, 128):
             acc_re += real[:, at : at + 128]
             acc_im += imag[:, at : at + 128]
     ones = jnp.ones((8, 128), BF16)
@@ -292,9 +306,9 @@
     out_ref[...] = jnp.concatenate(out, 0)
 
 
-def final_kernel(energy_ref, vector_ref, exchange_ref, near_ref, d0, d1, d2, out_ref):
+def final_kernel(energy_ref, vector_ref, exchange_ref, sent, received, h0, h1, out_ref):
     scale = 1.0 / 256
-    terms = near_ref[0:1] + d0[...] + d1[...] + d2[...]
+    terms = sent[16:17] + received[17:18] + h0[...] + h1[...]
     for part in range(2):
         term = terms[:, part * NT : part * NT + NT]
         out_ref[part : part + 1] = (
@@ -320,7 +334,7 @@
         out_shape.append(pltpu.VMEM((32, NG), F32))
     return pl.pallas_call(
         functools.partial(pair_kernel, near),
-        in_specs=[VMEM] * 8 + [VMEM] * near + [ANY],
+        in_specs=[VMEM] * 7 + [VMEM] * near + [ANY],
         out_specs=[VMEM] * len(out_shape),
         out_shape=out_shape,
         scratch_shapes=scratch
@@ -336,6 +350,16 @@
     )(*operands)
 
 
+def small_call(kernel, shape, *operands, kind=F32, after=()):
+    return pl.pallas_call(
+        kernel,
+        in_specs=[VMEM] * len(operands) + [ANY] * len(after),
+        out_specs=VMEM,
+        out_shape=jax.ShapeDtypeStruct(shape, kind),
+        compiler_params=params(8),
+    )(*operands, *after)
+
+
 def on_device(waves, vector, energies, basis, screening, coulomb, qmap):
     pay = pl.pallas_call(
         pack_kernel,
@@ -345,10 +369,13 @@
         scratch_shapes=[pltpu.VMEM((2, NT), F32), pltpu.SemaphoreType.DMA((2,))],
         compiler_params=params(56),
     )(waves.reshape(16, NMU), vector.reshape(2, NT))
-    a1 = move(pay, far=1)
     b0 = move(pay, step=1)
-    a2 = move(pay, core=1)
-    z = basis.reshape(2 * NMU, NG)
+    b1 = move(pay, step=1, far=1)
+    a1 = move(pay, y=1)
+    near = small_call(join_kernel, (32, WIDTH), pay, a1, kind=BF16)
+    far = move(near, y=2)
+    b2 = move(b0, core=1)
+    b3 = move(b1, core=1)
     weights = pl.pallas_call(
         weights_kernel,
         in_specs=[SMEM, ANY],
@@ -358,52 +385,43 @@
         compiler_params=params(54),
         cost_estimate=pl.CostEstimate(flops=4000000000, bytes_accessed=1024, transcendentals=0),
     )(qmap, screening)
-    b1, b2, b3 = (move(b0, y=n) for n in (1, 2, 3))
-    a3 = move(a1, core=1)
-    y = pl.pallas_call(
-        transitions_kernel,
-        in_specs=[VMEM] * 4,
-        out_specs=VMEM,
-        out_shape=jax.ShapeDtypeStruct((16, 128), F32),
+    z = basis.reshape(2 * NMU, NG)
+    b_pays = (b0, b1, b2, b3)
+    y = small_call(transitions_kernel, (16, 128), *b_pays, after=(near, weights))
+    (far_out,) = pair_call(0, (far, *b_pays, weights, z, y))
+    y = y + move(y, z=2) + move(y, z=1) + move(y, z=3)
+    first = small_call(first_mail_kernel, (24, 128), y, *(move(y, x=n) for n in (2, 1, 3)), far_out)
+    near_out, rx = pair_call(1, (near, *b_pays, weights, z, far_out, first))
+    second, herm = pl.pallas_call(
+        second_mail_kernel,
+        in_specs=[VMEM] * 3,
+        out_specs=[VMEM] * 2,
+        out_shape=[jax.ShapeDtypeStruct((24, 128), F32), jax.ShapeDtypeStruct((8, 128), F32)],
         compiler_params=params(8),
-    )(pay, a1, a2, a3)
-    b_pays = (b0, b1, b2, b3)
-    (far_out,) = pair_call(0, (a1, a3, *b_pays, weights, z, y))
-    far_sum = far_out[0:1] + move(far_out[1:2], core=1)
-    y = y + move(y, z=2) + move(y, z=1) + move(y, z=3)
-    near_out, rx = pair_call(1, (pay, a2, *b_pays, weights, z, far_out, y))
-    mail = pl.pallas_call(
-        mail_kernel,
-        in_specs=[VMEM] * 5,
-        out_specs=[VMEM] * 4,
-        out_shape=[jax.ShapeDtypeStruct((24, 128), F32)] * 4,
-        compiler_params=params(4),
-    )(y, *(move(y, x=n) for n in (2, 1, 3)), near_out)
-    mail = mail[0] + move(mail[2], y=2) + move(mail[1], y=1) + move(mail[3], y=3)
+    )(first, move(first, y=2), near_out)
+    received = move(second, y=1)
+    herm = herm[4:6] + move(herm[6:8], core=1)
+    far_herm = move(herm[1:2], step=3, far=1)
+    near_herm = move(small_call(row_kernel, (1, 128), herm, after=(received,)), step=3)
     exchange = pl.pallas_call(
         exchange_kernel,
-        in_specs=[VMEM] * 4,
+        in_specs=[VMEM] * 5,
         out_specs=VMEM,
         out_shape=jax.ShapeDtypeStruct((2, NT), F32),
         scratch_shapes=[pltpu.VMEM((16, 2 * NMU), BF16)],
         compiler_params=params(24),
         cost_estimate=cost(128),
-    )(mail, coulomb.reshape(1, NG), rx, z)
-
-    out = pl.pallas_call(
+    )(second, received, coulomb.reshape(1, NG), rx, z)
+    out = small_call(
         final_kernel,
-        in_specs=[VMEM] * 7,
-        out_specs=VMEM,
-        out_shape=jax.ShapeDtypeStruct((2, NT), F32),
-        compiler_params=params(4),
-    )(
+        (2, NT),
         energies,
         vector.reshape(2, NT),
         exchange,
-        near_out,
-        move(near_out[1:2], core=1),
-        move(far_sum, far=1),
-        move(mail[16:17], step=3),
+        second,
+        received,
+        near_herm,
+        far_herm,
     )
     return out.reshape(1, 2, NT)
 

time: 49.5 us -> 53.9 us (1.089)
  starting transfers between devices: 30.3 us -> 32.5 us
  waiting for transfers between devices: 3.64 us -> 5.55 us
    ppermute x20 -> x17, starting transfers between devices: 30.3 us -> 32.5 us  [move(): return lax.ppermute(value, ('grp', 'kin'), pairs)]
    ppermute x20 -> x17, waiting for transfers between devices: 3.64 us -> 5.55 us  [move(): return lax.ppermute(value, ('grp', 'kin'), pairs)]
    pallas_call x6 -> x9, Pallas kernels: 12.3 us -> 12.3 us  [the longest x2 10.4 us: pair_call(): pl.pallas_call(functools.partial(pair_kernel, near), in_specs=[VMEM] * 7...]
  transfers between devices with their start and end apart: 20 -> 17, of which waited for: 3 -> 5; matrix products, arithmetic and copies ran while one was open for 0% -> 0% of each run, Pallas kernels for 27% -> 25%
where the time goes in v7:
time: 53.9 us; the launch traced here: 53.4 us
  starting transfers between devices  32.5 us (60%)
  Pallas kernels  15.1 us (28%)
  waiting for transfers between devices  5.55 us (10%)
    ppermute x17, starting transfers between devices, move(): return lax.ppermute(value, ('grp', 'kin'), pairs)  32.5 us
    pallas_call x2, Pallas kernels, pair_call(): pl.pallas_call(functools.partial(pair_kernel, near), in_specs=[VMEM] * 7...  10.4 us
    ppermute x17, waiting for transfers between devices, move(): return lax.ppermute(value, ('grp', 'kin'), pairs)  5.55 us
    pallas_call x1, Pallas kernels, on_device(): pl.pallas_call(weights_kernel, in_specs=[SMEM, ANY], out_specs=VMEM, out_...  1.74 us
    pallas_call x1, Pallas kernels, on_device(): pl.pallas_call(pack_kernel, in_specs=[ANY] * 2, out_specs=VMEM, out_shape...  1.1 us
  transfers between devices with their start and end apart: 17, of which 5 were waited for; matrix products, arithmetic and copies ran while one was open for 0% of the time, Pallas kernels for 25%

profile of v7, /device:TPU:6, one launch (start us, length us, event | category | flops | bytes accessed | tf_op | source)
XLA Modules:
  0.0 53.4 jit_solution(7237486711557443546)
XLA Ops:
  0.0 1.1 %shard_map.73.first = bf16[16,1152]{1,0:T(8,128)(2,1)S(1)} custom-call(bf16[16,1024]{1,0:T(8,128)(2,1)} %bitcast.11, f32[2,16]{1,0:T(2,128)} %bitcast.9), custom_call_target="tpu_custom_call" | custom-call | tf_op jit(solution)/shard_map/pallas_call | solution.py:364
  1.1 0.0 slice-start.1
  1.1 2.3 %collective-permute-start = (bf16[16,1152]{1,0:T(8,128)(2,1)S(1)}, bf16[16,1152]{1,0:T(8,128)(2,1)S(1)}, u32[]{:S(2)}, u32[]{:S(2)}) collective-permute-start(bf16[16,1152]{1,0:T(8,128)(2,1)S(1)} %shard_map.73.first), channel_id=1, source_target_pairs={{0,64},{1,65},{2,66},{3,67},{4,68},{5,69},{6,70},{7,71},{8,72},{9,... | collective-permute-start | bytes 110600 | tf_op jit(solution)/shard_map/ppermute | solution.py:34
  3.4 6.4 %collective-permute-start.1 = (bf16[16,1152]{1,0:T(8,128)(2,1)S(1)}, bf16[16,1152]{1,0:T(8,128)(2,1)S(1)}, u32[]{:S(2)}, u32[]{:S(2)}) collective-permute-start(bf16[16,1152]{1,0:T(8,128)(2,1)S(1)} %shard_map.73.first), channel_id=1, source_target_pairs={{0,72},{1,73},{2,74},{3,75},{4,76},{5,77},{6,78},{7,79},{8,64},{9,... | collective-permute-start | bytes 110600 | tf_op jit(solution)/shard_map/ppermute | solution.py:34
  9.8 1.6 %collective-permute-start.4 = (bf16[16,1152]{1,0:T(8,128)(2,1)S(1)}, bf16[16,1152]{1,0:T(8,128)(2,1)S(1)}, u32[]{:S(2)}, u32[]{:S(2)}) collective-permute-start(bf16[16,1152]{1,0:T(8,128)(2,1)S(1)} %shard_map.73.first), channel_id=1, source_target_pairs={{0,2},{1,3},{2,0},{3,1},{4,6},{5,7},{6,4},{7,5},{8,10},{9,11},{10,... | collective-permute-start | bytes 110600 | tf_op jit(solution)/shard_map/ppermute | solution.py:34
  11.4 0.0 collective-permute-done.a0.refs_1_
  11.4 0.0 collective-permute-start.2
  11.4 0.8 %collective-permute-done.1.a1.refs_2_ = bf16[16,1152]{1,0:T(8,128)(2,1)S(1)} collective-permute-done((bf16[16,1152]{1,0:T(8,128)(2,1)S(1)}, bf16[16,1152]{1,0:T(8,128)(2,1)S(1)}, u32[]{:S(2)}, u32[]{:S(2)}) %collective-permute-start.1) | collective-permute-done | bytes 36896 | tf_op jit(solution)/shard_map/ppermute | solution.py:34
  12.2 0.0 collective-permute-start.3
  12.2 1.7 %shard_map.75.__.refs_5_ = f32[16,1536]{1,0:T(8,128)S(1)} custom-call(s32[1,256]{1,0:T(1,128)} %qmap_ref.1, f32[256,1536]{1,0:T(8,128)} %screening.1), custom_call_target="tpu_custom_call" | custom-call | flops 4000000000 | bytes 1024 | tf_op jit(solution)/shard_map/pallas_call | solution.py:379
  13.9 0.0 collective-permute-done.4.second
  14.0 0.0 collective-permute-done.2.a2.refs_3_
  14.0 0.0 collective-permute-done.3.a3.refs_4_
  14.0 0.2 shard_map.76.refs_7_
  14.2 1.6 %collective-permute-start.5 = (f32[16,128]{1,0:T(8,128)S(1)}, f32[16,128]{1,0:T(8,128)S(1)}, u32[]{:S(2)}, u32[]{:S(2)}) collective-permute-start(f32[16,128]{1,0:T(8,128)S(1)} %shard_map.76.refs_7_), channel_id=1, source_target_pairs={{0,32},{1,33},{2,34},{3,35},{4,36},{5,37},{6,38},{7,39},{8,40},{9,... | collective-permute-start | bytes 24584 | tf_op jit(solution)/shard_map/ppermute | solution.py:34
  15.8 1.9 %collective-permute-start.6 = (f32[16,128]{1,0:T(8,128)S(1)}, f32[16,128]{1,0:T(8,128)S(1)}, u32[]{:S(2)}, u32[]{:S(2)}) collective-permute-start(f32[16,128]{1,0:T(8,128)S(1)} %shard_map.76.refs_7_), channel_id=1, source_target_pairs={{0,16},{1,17},{2,18},{3,19},{4,20},{5,21},{6,22},{7,23},{8,24},{9,... | collective-permute-start | bytes 24584 | tf_op jit(solution)/shard_map/ppermute | solution.py:34
  17.7 0.9 %collective-permute-start.7 = (f32[16,128]{1,0:T(8,128)S(1)}, f32[16,128]{1,0:T(8,128)S(1)}, u32[]{:S(2)}, u32[]{:S(2)}) collective-permute-start(f32[16,128]{1,0:T(8,128)S(1)} %shard_map.76.refs_7_), channel_id=1, source_target_pairs={{0,48},{1,49},{2,50},{3,51},{4,52},{5,53},{6,54},{7,55},{8,56},{9,... | collective-permute-start | bytes 24584 | tf_op jit(solution)/shard_map/ppermute | solution.py:34
  18.6 3.0 %collective-permute-start.11 = (bf16[32,1152]{1,0:T(8,128)(2,1)S(1)}, bf16[32,1152]{1,0:T(8,128)(2,1)S(1)}, u32[]{:S(2)}, u32[]{:S(2)}) collective-permute-start(bf16[32,1152]{1,0:T(8,128)(2,1)S(1)} %shard_map.74._.refs_0_), channel_id=1, source_target_pairs={{0,4},{1,5},{2,6},{3,7},{4,0},{5,1},{6,2},{7,3},{8,12},{9,13},{10,... | collective-permute-start | bytes 221192 | tf_op jit(solution)/shard_map/ppermute | solution.py:34
  21.6 0.0 collective-permute-done.5
  21.6 0.0 collective-permute-done.6
  21.6 1.5 %collective-permute-done.7 = f32[16,128]{1,0:T(8,128)S(1)} collective-permute-done((f32[16,128]{1,0:T(8,128)S(1)}, f32[16,128]{1,0:T(8,128)S(1)}, u32[]{:S(2)}, u32[]{:S(2)}) %collective-permute-start.7) | collective-permute-done | bytes 8224 | tf_op jit(solution)/shard_map/ppermute | solution.py:34
  23.2 2.7 %collective-permute-start.10 = (f32[16,128]{1,0:T(8,128)S(1)}, f32[16,128]{1,0:T(8,128)S(1)}, u32[]{:S(2)}, u32[]{:S(2)}) collective-permute-start(f32[16,128]{1,0:T(8,128)S(1)} %add_add_fusion.y0), channel_id=1, source_target_pairs={{0,192},{1,193},{2,194},{3,195},{4,196},{5,197},{6,198},{7,199},{8... | collective-permute-start | bytes 24584 | tf_op jit(solution)/shard_map/ppermute | solution.py:34
  25.9 0.9 %collective-permute-start.8 = (f32[16,128]{1,0:T(8,128)S(1)}, f32[16,128]{1,0:T(8,128)S(1)}, u32[]{:S(2)}, u32[]{:S(2)}) collective-permute-start(f32[16,128]{1,0:T(8,128)S(1)} %add_add_fusion.y0), channel_id=1, source_target_pairs={{0,128},{1,129},{2,130},{3,131},{4,132},{5,133},{6,134},{7,135},{8... | collective-permute-start | bytes 24584 | tf_op jit(solution)/shard_map/ppermute | solution.py:34
  26.8 0.5 collective-permute-start.9
  27.3 0.0 collective-permute-done.11.refs_0_
  27.3 0.0 slice-done
  27.3 0.0 slice-done.1
  27.3 4.7 %shard_map.77.far_ref.refs_7_ = f32[8,128]{1,0:T(8,128)S(1)} custom-call(bf16[32,1152]{1,0:T(8,128)(2,1)S(1)} %collective-permute-done.11.refs_0_, bf16[16,1152]{1,0:T(8,128)(2,1)S(1)} %collective-permute-done.a0.refs_1_, bf16[16,1152]{1,0:T(8,128)(2,1)S(1)} %collective-permute-done.1.a1.refs_2_, bf16[16,1152]{1,0:T(8,128)(2,1)S(1)} %collective-permute-done.2.a2.refs_3_, ...), custom_call_target="tpu_custom_call" | custom-call | flops 3221225472 | bytes 6291456 | tf_op jit(solution)/shard_map/pallas_call | solution.py:335
  32.0 0.0 collective-permute-done.10.y3
  32.0 0.0 collective-permute-done.8.y1
  32.0 0.0 collective-permute-done.9.y2
  32.1 0.0 copy-start
  32.1 0.0 copy-start.1
  32.1 3.5 %collective-permute-start.12 = (f32[24,128]{1,0:T(8,128)S(1)}, f32[24,128]{1,0:T(8,128)S(1)}, u32[]{:S(2)}, u32[]{:S(2)}) collective-permute-start(f32[24,128]{1,0:T(8,128)S(1)} %shard_map.78.refs_8_.sent), channel_id=1, source_target_pairs={{0,4},{1,5},{2,6},{3,7},{4,0},{5,1},{6,2},{7,3},{8,12},{9,13},{10,... | collective-permute-start | bytes 36872 | tf_op jit(solution)/shard_map/ppermute | solution.py:34
  35.6 5.6 %shard_map.79 = (f32[8,128]{1,0:T(8,128)S(1)}, f32[32,1536]{1,0:T(8,128)S(1)}) custom-call(bf16[32,1152]{1,0:T(8,128)(2,1)S(1)} %shard_map.74._.refs_0_, bf16[16,1152]{1,0:T(8,128)(2,1)S(1)} %collective-permute-done.a0.refs_1_, bf16[16,1152]{1,0:T(8,128)(2,1)S(1)} %collective-permute-done.1.a1.refs_2_, ...), custom_call_target="tpu_custom_call" | custom-call | flops 3221225472 | bytes 6291456 | tf_op jit(solution)/shard_map/pallas_call | solution.py:335
  41.2 0.0 collective-permute-done.12.received
  41.2 0.1 collective-permute-start.14
  41.3 0.0 copy-done.2
  41.4 0.8 %collective-permute-start.13 = (f32[24,128]{1,0:T(8,128)S(1)}, f32[24,128]{1,0:T(8,128)S(1)}, u32[]{:S(2)}, u32[]{:S(2)}) collective-permute-start(f32[24,128]{1,0:T(8,128)S(1)} %get-tuple-element.10.sent), channel_id=1, source_target_pairs={{0,2},{1,3},{2,0},{3,1},{4,6},{5,7},{6,4},{7,5},{8,10},{9,11},{10,... | collective-permute-start | bytes 36872 | tf_op jit(solution)/shard_map/ppermute | solution.py:34
  42.1 0.3 collective-permute-done.14
  42.5 5.6 %collective-permute-start.16 = (f32[1,128]{1,0:T(1,128)S(1)}, f32[1,128]{1,0:T(1,128)S(1)}, u32[]{:S(2)}, u32[]{:S(2)}) collective-permute-start(f32[1,128]{1,0:T(1,128)S(1)} %slice.11), channel_id=1, source_target_pairs={{0,200},{1,201},{2,202},{3,203},{4,204},{5,205},{6,206},{7,207},{8... | collective-permute-start | bytes 1544 | tf_op jit(solution)/shard_map/ppermute | solution.py:34
  48.0 0.0 collective-permute-done.13.received._
  48.0 0.8 %collective-permute-start.15 = (f32[1,128]{1,0:T(1,128)S(1)}, f32[1,128]{1,0:T(1,128)S(1)}, u32[]{:S(2)}, u32[]{:S(2)}) collective-permute-start(f32[1,128]{1,0:T(1,128)S(1)} %shard_map.82), channel_id=1, source_target_pairs={{0,192},{1,193},{2,194},{3,195},{4,196},{5,197},{6,198},{7,199},{8... | collective-permute-start | bytes 1544 | tf_op jit(solution)/shard_map/ppermute | solution.py:34
  48.9 1.1 %shard_map.81.exchange_ref = f32[2,16]{1,0:T(2,128)S(1)} custom-call(f32[24,128]{1,0:T(8,128)S(1)} %get-tuple-element.10.sent, f32[24,128]{1,0:T(8,128)S(1)} %collective-permute-done.13.received._, f32[1,1536]{1,0:T(1,128)S(1)} %reshape.19.c_ref, f32[32,1536]{1,0:T(8,128)S(1)} %get-tuple-element.11.rx_ref, bf16[2048,1536]{1,0:T(8,128)(2,1)S(1)} %bitcast.8), custom_call_target="tpu_custom_call" | custom-call | flops 805306368 | bytes 6291456 | tf_op jit(solution)/shard_map/pallas_call | solution.py:406
  49.9 2.2 %collective-permute-done.16.h1 = f32[1,128]{1,0:T(1,128)S(1)} collective-permute-done((f32[1,128]{1,0:T(1,128)S(1)}, f32[1,128]{1,0:T(1,128)S(1)}, u32[]{:S(2)}, u32[]{:S(2)}) %collective-permute-start.16) | collective-permute-done | bytes 544 | tf_op jit(solution)/shard_map/ppermute | solution.py:34
  52.1 0.7 %collective-permute-done.15.h0 = f32[1,128]{1,0:T(1,128)S(1)} collective-permute-done((f32[1,128]{1,0:T(1,128)S(1)}, f32[1,128]{1,0:T(1,128)S(1)}, u32[]{:S(2)}, u32[]{:S(2)}) %collective-permute-start.15) | collective-permute-done | bytes 544 | tf_op jit(solution)/shard_map/ppermute | solution.py:34
  52.8 0.0 copy-done
  52.8 0.6 %shard_map.83 = f32[2,16]{1,0:T(2,128)} custom-call(f32[1,16]{1,0:T(1,128)S(1)} %copy-done.1, f32[2,16]{1,0:T(2,128)S(1)} %bitcast.10, f32[2,16]{1,0:T(2,128)S(1)} %shard_map.81.exchange_ref, f32[24,128]{1,0:T(8,128)S(1)} %get-tuple-element.10.sent, f32[24,128]{1,0:T(8,128)S(1)} %collective-permute-done.13.received._, ...), custom_call_target="tpu_custom_call" | custom-call | tf_op jit(solution)/shard_map/pallas_call | solution.py:354
  (13 shorter events, 0.1 us)
Async XLA Ops:
  0.0 27.3 %slice-start = ((s8[6291456]{0:T(1024)(128)(4,1)}), s8[2097152]{0:T(1024)(128)(4,1)S(1)}, s32[]{:S(2)}) async-start(s8[6291456]{0:T(1024)(128)(4,1)} %bitcast.4), calls=%async_computation | async-start | bytes 4194304
  1.1 26.2 %slice-start.1 = ((s8[6291456]{0:T(1024)(128)(4,1)}), s8[4194304]{0:T(1024)(128)(4,1)S(1)}, s32[]{:S(2)}) async-start(s8[6291456]{0:T(1024)(128)(4,1)} %bitcast.4), calls=%async_computation.1 | async-start | bytes 8388608
  1.1 10.3 %collective-permute-start = (bf16[16,1152]{1,0:T(8,128)(2,1)S(1)}, bf16[16,1152]{1,0:T(8,128)(2,1)S(1)}, u32[]{:S(2)}, u32[]{:S(2)}) collective-permute-start(bf16[16,1152]{1,0:T(8,128)(2,1)S(1)} %shard_map.73.first), channel_id=1, source_target_pairs={{0,64},{1,65},{2,66},{3,67},{4,68},{5,69},{6,70},{7,71},{8,72},{9,... | collective-permute-start | bytes 110600 | tf_op jit(solution)/shard_map/ppermute | solution.py:34
  3.4 8.8 %collective-permute-start.1 = (bf16[16,1152]{1,0:T(8,128)(2,1)S(1)}, bf16[16,1152]{1,0:T(8,128)(2,1)S(1)}, u32[]{:S(2)}, u32[]{:S(2)}) collective-permute-start(bf16[16,1152]{1,0:T(8,128)(2,1)S(1)} %shard_map.73.first), channel_id=1, source_target_pairs={{0,72},{1,73},{2,74},{3,75},{4,76},{5,77},{6,78},{7,79},{8,64},{9,... | collective-permute-start | bytes 110600 | tf_op jit(solution)/shard_map/ppermute | solution.py:34
  9.8 4.1 %collective-permute-start.4 = (bf16[16,1152]{1,0:T(8,128)(2,1)S(1)}, bf16[16,1152]{1,0:T(8,128)(2,1)S(1)}, u32[]{:S(2)}, u32[]{:S(2)}) collective-permute-start(bf16[16,1152]{1,0:T(8,128)(2,1)S(1)} %shard_map.73.first), channel_id=1, source_target_pairs={{0,2},{1,3},{2,0},{3,1},{4,6},{5,7},{6,4},{7,5},{8,10},{9,11},{10,... | collective-permute-start | bytes 110600 | tf_op jit(solution)/shard_map/ppermute | solution.py:34
  11.4 2.6 %collective-permute-start.2 = (bf16[16,1152]{1,0:T(8,128)(2,1)S(1)}, bf16[16,1152]{1,0:T(8,128)(2,1)S(1)}, u32[]{:S(2)}, u32[]{:S(2)}) collective-permute-start(bf16[16,1152]{1,0:T(8,128)(2,1)S(1)} %collective-permute-done.a0.refs_1_), channel_id=1, source_target_pairs={{0,1},{1,0},{2,3},{3,2},{4,5},{5,4},{6,7},{7,6},{8,9},{9,8},{10,11... | collective-permute-start | bytes 110600 | tf_op jit(solution)/shard_map/ppermute | solution.py:34
  12.2 1.8 %collective-permute-start.3 = (bf16[16,1152]{1,0:T(8,128)(2,1)S(1)}, bf16[16,1152]{1,0:T(8,128)(2,1)S(1)}, u32[]{:S(2)}, u32[]{:S(2)}) collective-permute-start(bf16[16,1152]{1,0:T(8,128)(2,1)S(1)} %collective-permute-done.1.a1.refs_2_), channel_id=1, source_target_pairs={{0,1},{1,0},{2,3},{3,2},{4,5},{5,4},{6,7},{7,6},{8,9},{9,8},{10,11... | collective-permute-start | bytes 110600 | tf_op jit(solution)/shard_map/ppermute | solution.py:34
  14.2 7.5 %collective-permute-start.5 = (f32[16,128]{1,0:T(8,128)S(1)}, f32[16,128]{1,0:T(8,128)S(1)}, u32[]{:S(2)}, u32[]{:S(2)}) collective-permute-start(f32[16,128]{1,0:T(8,128)S(1)} %shard_map.76.refs_7_), channel_id=1, source_target_pairs={{0,32},{1,33},{2,34},{3,35},{4,36},{5,37},{6,38},{7,39},{8,40},{9,... | collective-permute-start | bytes 24584 | tf_op jit(solution)/shard_map/ppermute | solution.py:34
  15.8 5.9 %collective-permute-start.6 = (f32[16,128]{1,0:T(8,128)S(1)}, f32[16,128]{1,0:T(8,128)S(1)}, u32[]{:S(2)}, u32[]{:S(2)}) collective-permute-start(f32[16,128]{1,0:T(8,128)S(1)} %shard_map.76.refs_7_), channel_id=1, source_target_pairs={{0,16},{1,17},{2,18},{3,19},{4,20},{5,21},{6,22},{7,23},{8,24},{9,... | collective-permute-start | bytes 24584 | tf_op jit(solution)/shard_map/ppermute | solution.py:34
  17.7 5.4 %collective-permute-start.7 = (f32[16,128]{1,0:T(8,128)S(1)}, f32[16,128]{1,0:T(8,128)S(1)}, u32[]{:S(2)}, u32[]{:S(2)}) collective-permute-start(f32[16,128]{1,0:T(8,128)S(1)} %shard_map.76.refs_7_), channel_id=1, source_target_pairs={{0,48},{1,49},{2,50},{3,51},{4,52},{5,53},{6,54},{7,55},{8,56},{9,... | collective-permute-start | bytes 24584 | tf_op jit(solution)/shard_map/ppermute | solution.py:34
  18.6 8.6 %collective-permute-start.11 = (bf16[32,1152]{1,0:T(8,128)(2,1)S(1)}, bf16[32,1152]{1,0:T(8,128)(2,1)S(1)}, u32[]{:S(2)}, u32[]{:S(2)}) collective-permute-start(bf16[32,1152]{1,0:T(8,128)(2,1)S(1)} %shard_map.74._.refs_0_), channel_id=1, source_target_pairs={{0,4},{1,5},{2,6},{3,7},{4,0},{5,1},{6,2},{7,3},{8,12},{9,13},{10,... | collective-permute-start | bytes 221192 | tf_op jit(solution)/shard_map/ppermute | solution.py:34
  23.2 8.9 %collective-permute-start.10 = (f32[16,128]{1,0:T(8,128)S(1)}, f32[16,128]{1,0:T(8,128)S(1)}, u32[]{:S(2)}, u32[]{:S(2)}) collective-permute-start(f32[16,128]{1,0:T(8,128)S(1)} %add_add_fusion.y0), channel_id=1, source_target_pairs={{0,192},{1,193},{2,194},{3,195},{4,196},{5,197},{6,198},{7,199},{8... | collective-permute-start | bytes 24584 | tf_op jit(solution)/shard_map/ppermute | solution.py:34
  25.9 6.2 %collective-permute-start.8 = (f32[16,128]{1,0:T(8,128)S(1)}, f32[16,128]{1,0:T(8,128)S(1)}, u32[]{:S(2)}, u32[]{:S(2)}) collective-permute-start(f32[16,128]{1,0:T(8,128)S(1)} %add_add_fusion.y0), channel_id=1, source_target_pairs={{0,128},{1,129},{2,130},{3,131},{4,132},{5,133},{6,134},{7,135},{8... | collective-permute-start | bytes 24584 | tf_op jit(solution)/shard_map/ppermute | solution.py:34
  26.8 5.3 %collective-permute-start.9 = (f32[16,128]{1,0:T(8,128)S(1)}, f32[16,128]{1,0:T(8,128)S(1)}, u32[]{:S(2)}, u32[]{:S(2)}) collective-permute-start(f32[16,128]{1,0:T(8,128)S(1)} %add_add_fusion.y0), channel_id=1, source_target_pairs={{0,64},{1,65},{2,66},{3,67},{4,68},{5,69},{6,70},{7,71},{8,72},{9,... | collective-permute-start | bytes 24584 | tf_op jit(solution)/shard_map/ppermute | solution.py:34
  32.0 9.3 %copy-start.2 = (f32[1536]{0:T(1024)S(1)}, f32[1536]{0:T(1024)}, u32[]{:S(2)}) copy-start(f32[1536]{0:T(1024)} %param.12) | copy-start | bytes 18436
  32.1 20.7 %copy-start = (f32[1,2,16]{2,1,0:T(2,128)S(1)}, f32[1,2,16]{2,1,0:T(2,128)}, u32[]{:S(2)}) copy-start(f32[1,2,16]{2,1,0:T(2,128)} %param.8) | copy-start | bytes 388
  32.1 20.7 %copy-start.1 = (f32[1,16]{1,0:T(1,128)S(1)}, f32[1,16]{1,0:T(1,128)}, u32[]{:S(2)}) copy-start(f32[1,16]{1,0:T(1,128)} %energy_ref.1) | copy-start | bytes 196
  32.1 9.1 %collective-permute-start.12 = (f32[24,128]{1,0:T(8,128)S(1)}, f32[24,128]{1,0:T(8,128)S(1)}, u32[]{:S(2)}, u32[]{:S(2)}) collective-permute-start(f32[24,128]{1,0:T(8,128)S(1)} %shard_map.78.refs_8_.sent), channel_id=1, source_target_pairs={{0,4},{1,5},{2,6},{3,7},{4,0},{5,1},{6,2},{7,3},{8,12},{9,13},{10,... | collective-permute-start | bytes 36872 | tf_op jit(solution)/shard_map/ppermute | solution.py:34
  41.2 1.2 %collective-permute-start.14 = (f32[2,128]{1,0:T(2,128)S(1)}, f32[2,128]{1,0:T(2,128)S(1)}, u32[]{:S(2)}, u32[]{:S(2)}) collective-permute-start(f32[2,128]{1,0:T(2,128)S(1)} %slice.10), channel_id=1, source_target_pairs={{0,1},{1,0},{2,3},{3,2},{4,5},{5,4},{6,7},{7,6},{8,9},{9,8},{10,11... | collective-permute-start | bytes 3080 | tf_op jit(solution)/shard_map/ppermute | solution.py:34
  41.4 6.7 %collective-permute-start.13 = (f32[24,128]{1,0:T(8,128)S(1)}, f32[24,128]{1,0:T(8,128)S(1)}, u32[]{:S(2)}, u32[]{:S(2)}) collective-permute-start(f32[24,128]{1,0:T(8,128)S(1)} %get-tuple-element.10.sent), channel_id=1, source_target_pairs={{0,2},{1,3},{2,0},{3,1},{4,6},{5,7},{6,4},{7,5},{8,10},{9,11},{10,... | collective-permute-start | bytes 36872 | tf_op jit(solution)/shard_map/ppermute | solution.py:34
  42.5 9.6 %collective-permute-start.16 = (f32[1,128]{1,0:T(1,128)S(1)}, f32[1,128]{1,0:T(1,128)S(1)}, u32[]{:S(2)}, u32[]{:S(2)}) collective-permute-start(f32[1,128]{1,0:T(1,128)S(1)} %slice.11), channel_id=1, source_target_pairs={{0,200},{1,201},{2,202},{3,203},{4,204},{5,205},{6,206},{7,207},{8... | collective-permute-start | bytes 1544 | tf_op jit(solution)/shard_map/ppermute | solution.py:34
  48.0 4.8 %collective-permute-start.15 = (f32[1,128]{1,0:T(1,128)S(1)}, f32[1,128]{1,0:T(1,128)S(1)}, u32[]{:S(2)}, u32[]{:S(2)}) collective-permute-start(f32[1,128]{1,0:T(1,128)S(1)} %shard_map.82), channel_id=1, source_target_pairs={{0,192},{1,193},{2,194},{3,195},{4,196},{5,197},{6,198},{7,199},{8... | collective-permute-start | bytes 1544 | tf_op jit(solution)/shard_map/ppermute | solution.py:34

commit v8 on v6

--- a/solution.py
+++ b/solution.py
@@ -11,7 +11,7 @@
 NMU = 1024
 NG = 1536
 WIDTH = NMU + 128
-CHUNK = 512
+CHUNK = 1536
 ROWS = 128
 F32 = jnp.float32
 BF16 = jnp.bfloat16
@@ -143,25 +143,26 @@
 
 def pair_kernel(near, *refs):
     if near:
-        w_ref, z_ref, far_ref, _, out_ref, rx_ref, lhs, own, xa, xb, acc, ca, cb = refs[6:]
+        w_ref, z_ref, far_ref, _, out_ref, rx_ref, lhs, xa, xb, acc, ca, cb = refs[6:]
     else:
         w_ref, z_ref, _, out_ref, lhs, xa, xb, acc, ca, cb = refs[6:]
     base = 2 * near
     a_pays = refs[0:2]
     b_pays = refs[2:6]
-    half = 2 * ROWS
-
-    def put(to, row, top, left, right, left_at, right_at):
+    val = ROWS + 16 * near
+    half = ROWS + val
+
+    def put(row, left, right, left_at, right_at):
         real, imag = conj_product(
             left[left_at : left_at + 16],
             left[left_at + 16 : left_at + 32],
             right[right_at : right_at + 16],
             right[right_at + 16 : right_at + 32],
         )
-        to[row : row + 16, 0:NMU] = real
-        to[row : row + 16, NMU : 2 * NMU] = -imag
-        to[top + row : top + row + 16, 0:NMU] = imag
-        to[top + row : top + row + 16, NMU : 2 * NMU] = real
+        lhs[row : row + 16, 0:NMU] = real
+        lhs[row : row + 16, NMU : 2 * NMU] = -imag
+        lhs[half + row : half + row + 16, 0:NMU] = imag
+        lhs[half + row : half + row + 16, NMU : 2 * NMU] = real
 
     rep = spread(True)
     til = spread(False)
@@ -172,30 +173,25 @@
     for m in range(2):
         for n in range(4):
             row = (m * 4 + n) * 16
-            put(lhs, row, half, xa[m], xb[n], 0, 0)
-            put(lhs, ROWS + row, half, xa[m], xb[n], 32, 32)
+            put(row, xa[m], xb[n], 0, 0)
+            put(ROWS + row, xa[m], xb[n], 32, 32)
     if near:
-        put(own, 0, 16, xa[0], dot(til, a_pays[0][:, 0:NMU]), 32, 0)
+        put(2 * ROWS, xa[0], dot(til, a_pays[0][:, 0:NMU]), 32, 0)
     acc[...] = jnp.zeros_like(acc)
     for at in range(0, NG, CHUNK):
-        z = z_ref[:, at : at + CHUNK]
-        con_re = dot(lhs[0:ROWS], z)
-        for p in range(8):
-            weight = w_ref[4 * base + p : 4 * base + p + 1, at : at + CHUNK]
-            ca[p * 16 : p * 16 + 16, 0:CHUNK] = (con_re[p * 16 : p * 16 + 16] * weight).astype(BF16)
-        con_im = dot(lhs[half : half + ROWS], z)
-        for p in range(8):
-            weight = w_ref[4 * base + p : 4 * base + p + 1, at : at + CHUNK]
-            ca[p * 16 : p * 16 + 16, CHUNK : 2 * CHUNK] = (con_im[p * 16 : p * 16 + 16] * weight).astype(BF16)
-        val_re = dot(lhs[ROWS:half], z).astype(BF16)
-        cb[0:ROWS, 0:CHUNK] = val_re
-        cb[ROWS:half, CHUNK : 2 * CHUNK] = -val_re
-        val_im = dot(lhs[half + ROWS : 2 * half], z).astype(BF16)
-        cb[0:ROWS, CHUNK : 2 * CHUNK] = val_im
-        cb[ROWS:half, 0:CHUNK] = val_im
+        part = pl.ds(at, CHUNK)
+        z = z_ref[:, part]
+        for side in range(2):
+            con = dot(lhs[side * half : side * half + ROWS], z)
+            for p in range(8):
+                weight = w_ref[4 * base + p : 4 * base + p + 1, part]
+                row = side * ROWS + p * 16
+                ca[row : row + 16] = (con[p * 16 : p * 16 + 16] * weight).astype(BF16)
+            dens = dot(lhs[side * half + ROWS : side * half + half], z)
+            cb[side * ROWS : side * ROWS + ROWS] = dens[0:ROWS].astype(BF16)
+            if near:
+                rx_ref[side * 16 : side * 16 + 16, part] = dens[ROWS:val]
         acc[...] += dot_t(ca[...], cb[...])
-        if near:
-            rx_ref[:, at : at + CHUNK] = dot(own[...], z)
 
     pick_row = iota((8, 16), 0)
     pick_col = iota((8, 16), 1)
@@ -222,8 +218,8 @@
     first = lane >> 4 == 1
     second = lane >> 4 == 2
     pair = iota((ROWS, ROWS), 0) >> 4 == iota((ROWS, ROWS), 1) >> 4
-    k_re = jnp.where(pair, acc[:, 0:ROWS], 0.0)
-    k_im = jnp.where(pair, acc[:, ROWS:half], 0.0)
+    k_re = jnp.where(pair, acc[0:ROWS, 0:ROWS] + acc[ROWS:, ROWS:], 0.0)
+    k_im = jnp.where(pair, acc[0:ROWS, ROWS:] - acc[ROWS:, 0:ROWS], 0.0)
     xd_re = dot(spread_b, onehot(by_w & first))
     xd_im = dot(spread_b, onehot(by_w & second))
     xh_re = dot(spread_a, onehot(by_v & first))
@@ -272,8 +268,8 @@
             lhs[:, at + j * 128 : at + j * 128 + 128] = rows.astype(BF16)
     acc_re = jnp.zeros((16, 128), F32)
     acc_im = jnp.zeros((16, 128), F32)
-    for start in range(0, NG, CHUNK):
-        part = pl.ds(start, CHUNK)
+    for start in range(0, NG, 512):
+        part = pl.ds(start, 512)
         total = dot(lhs[...], z_ref[:, part])
         pot_re = (total[0:1] + total[2:3]) * c_ref[:, part]
         pot_im = (total[1:2] + total[3:4]) * c_ref[:, part]
@@ -281,7 +277,7 @@
         rx_im = rx_ref[16:32, part]
         real = rx_re * pot_re + rx_im * pot_im
         imag = rx_re * pot_im - rx_im * pot_re
-        for at in range(0, CHUNK, 128):
+        for at in range(0, 512, 128):
             acc_re += real[:, at : at + 128]
             acc_im += imag[:, at : at + 128]
     ones = jnp.ones((8, 128), BF16)
@@ -313,23 +309,21 @@
 
 
 def pair_call(near, operands):
-    scratch = [pltpu.VMEM((4 * ROWS, 2 * NMU), BF16)]
     out_shape = [jax.ShapeDtypeStruct((8, 128), F32)]
     if near:
-        scratch.append(pltpu.VMEM((32, 2 * NMU), BF16))
         out_shape.append(pltpu.VMEM((32, NG), F32))
     return pl.pallas_call(
         functools.partial(pair_kernel, near),
         in_specs=[VMEM] * 8 + [VMEM] * near + [ANY],
         out_specs=[VMEM] * len(out_shape),
         out_shape=out_shape,
-        scratch_shapes=scratch
-        + [
+        scratch_shapes=[
+            pltpu.VMEM((4 * ROWS + 32 * near, 2 * NMU), BF16),
             pltpu.VMEM((2, 64, NMU), F32),
             pltpu.VMEM((4, 64, NMU), F32),
-            pltpu.VMEM((ROWS, 2 * ROWS), F32),
-            pltpu.VMEM((ROWS, 2 * CHUNK), BF16),
-            pltpu.VMEM((2 * ROWS, 2 * CHUNK), BF16),
+            pltpu.VMEM((2 * ROWS, 2 * ROWS), F32),
+            pltpu.VMEM((2 * ROWS, CHUNK), BF16),
+            pltpu.VMEM((2 * ROWS, CHUNK), BF16),
         ],
         compiler_params=params(24),
         cost_estimate=cost(4 * ROWS),

time: 49.5 us -> 48.4 us (0.978)
  Pallas kernels: 15.1 us -> 14.2 us
    pallas_call x2, Pallas kernels: 10.4 us -> 9.43 us  [pair_call(): pl.pallas_call(functools.partial(pair_kernel, near), in_specs=[VMEM] * 8...]
  transfers between devices with their start and end apart: 20 -> 20, of which waited for: 3 -> 3; matrix products, arithmetic and copies ran while one was open for 0% -> 0% of each run, Pallas kernels for 27% -> 26%
where the time goes in v8:
time: 48.4 us; the launch traced here: 48.3 us
  starting transfers between devices  30.3 us (63%)
  Pallas kernels  14.2 us (29%)
  waiting for transfers between devices  3.62 us (7%)
    ppermute x20, starting transfers between devices, move(): return lax.ppermute(value, ('grp', 'kin'), pairs)  30.3 us
    pallas_call x2, Pallas kernels, pair_call(): pl.pallas_call(functools.partial(pair_kernel, near), in_specs=[VMEM] * 8...  9.43 us
    ppermute x20, waiting for transfers between devices, move(): return lax.ppermute(value, ('grp', 'kin'), pairs)  3.62 us
    pallas_call x1, Pallas kernels, on_device(): pl.pallas_call(weights_kernel, in_specs=[SMEM, ANY], out_specs=VMEM, out_...  1.74 us
    pallas_call x1, Pallas kernels, on_device(): pl.pallas_call(pack_kernel, in_specs=[ANY] * 2, out_specs=VMEM, out_shape...  1.1 us
    pallas_call x1, Pallas kernels, on_device(): pl.pallas_call(exchange_kernel, in_specs=[VMEM] * 4, out_specs=VMEM, out_...  1.06 us
  transfers between devices with their start and end apart: 20, of which 3 were waited for; matrix products, arithmetic and copies ran while one was open for 0% of the time, Pallas kernels for 26%

profile of v8, /device:TPU:6, one launch (start us, length us, event | category | flops | bytes accessed | tf_op | source)
XLA Modules:
  0.0 48.3 jit_solution(1784390186526964457)
XLA Ops:
  0.0 1.1 %shard_map.73.a0.refs_0_ = bf16[16,1152]{1,0:T(8,128)(2,1)S(1)} custom-call(bf16[16,1024]{1,0:T(8,128)(2,1)} %bitcast.11, f32[2,16]{1,0:T(2,128)} %bitcast.9), custom_call_target="tpu_custom_call" | custom-call | tf_op jit(solution)/shard_map/pallas_call | solution.py:334
  1.1 0.0 copy-start.2
  1.1 0.0 slice-start.1
  1.1 2.3 %collective-permute-start.9 = (bf16[16,1152]{1,0:T(8,128)(2,1)S(1)}, bf16[16,1152]{1,0:T(8,128)(2,1)S(1)}, u32[]{:S(2)}, u32[]{:S(2)}) collective-permute-start(bf16[16,1152]{1,0:T(8,128)(2,1)S(1)} %shard_map.73.a0.refs_0_), channel_id=1, source_target_pairs={{0,64},{1,65},{2,66},{3,67},{4,68},{5,69},{6,70},{7,71},{8,72},{9,... | collective-permute-start | bytes 110600 | tf_op jit(solution)/shard_map/ppermute | solution.py:34
  3.4 5.5 %collective-permute-start = (bf16[16,1152]{1,0:T(8,128)(2,1)S(1)}, bf16[16,1152]{1,0:T(8,128)(2,1)S(1)}, u32[]{:S(2)}, u32[]{:S(2)}) collective-permute-start(bf16[16,1152]{1,0:T(8,128)(2,1)S(1)} %shard_map.73.a0.refs_0_), channel_id=1, source_target_pairs={{0,8},{1,9},{2,10},{3,11},{4,12},{5,13},{6,14},{7,15},{8,0},{9,1},... | collective-permute-start | bytes 110600 | tf_op jit(solution)/shard_map/ppermute | solution.py:34
  8.9 0.0 collective-permute-start.1
  8.9 0.0 collective-permute-done.9.refs_2_
  8.9 1.6 %collective-permute-start.10 = (bf16[16,1152]{1,0:T(8,128)(2,1)S(1)}, bf16[16,1152]{1,0:T(8,128)(2,1)S(1)}, u32[]{:S(2)}, u32[]{:S(2)}) collective-permute-start(bf16[16,1152]{1,0:T(8,128)(2,1)S(1)} %collective-permute-done.9.refs_2_), channel_id=1, source_target_pairs={{0,2},{1,3},{2,0},{3,1},{4,6},{5,7},{6,4},{7,5},{8,10},{9,11},{10,... | collective-permute-start | bytes 110600 | tf_op jit(solution)/shard_map/ppermute | solution.py:34
  10.5 2.9 %collective-permute-start.11 = (bf16[16,1152]{1,0:T(8,128)(2,1)S(1)}, bf16[16,1152]{1,0:T(8,128)(2,1)S(1)}, u32[]{:S(2)}, u32[]{:S(2)}) collective-permute-start(bf16[16,1152]{1,0:T(8,128)(2,1)S(1)} %collective-permute-done.9.refs_2_), channel_id=1, source_target_pairs={{0,4},{1,5},{2,6},{3,7},{4,0},{5,1},{6,2},{7,3},{8,12},{9,13},{10,... | collective-permute-start | bytes 110600 | tf_op jit(solution)/shard_map/ppermute | solution.py:34
  13.4 0.2 collective-permute-start.12
  13.6 0.0 collective-permute-done.a1.refs_0_
  13.6 0.0 collective-permute-start.2
  13.6 1.7 %shard_map.75.refs_6_ = f32[16,1536]{1,0:T(8,128)S(1)} custom-call(s32[1,256]{1,0:T(1,128)} %qmap_ref.1, f32[256,1536]{1,0:T(8,128)} %screening.1), custom_call_target="tpu_custom_call" | custom-call | flops 4000000000 | bytes 1024 | tf_op jit(solution)/shard_map/pallas_call | solution.py:346
  15.4 0.0 collective-permute-done.1.a2.refs_1_
  15.4 0.0 collective-permute-done.2.a3.refs_1_
  15.4 0.2 shard_map.74.refs_8_
  15.6 1.6 %collective-permute-start.3 = (f32[16,128]{1,0:T(8,128)S(1)}, f32[16,128]{1,0:T(8,128)S(1)}, u32[]{:S(2)}, u32[]{:S(2)}) collective-permute-start(f32[16,128]{1,0:T(8,128)S(1)} %shard_map.74.refs_8_), channel_id=1, source_target_pairs={{0,32},{1,33},{2,34},{3,35},{4,36},{5,37},{6,38},{7,39},{8,40},{9,... | collective-permute-start | bytes 24584 | tf_op jit(solution)/shard_map/ppermute | solution.py:34
  17.1 1.0 %collective-permute-start.4 = (f32[16,128]{1,0:T(8,128)S(1)}, f32[16,128]{1,0:T(8,128)S(1)}, u32[]{:S(2)}, u32[]{:S(2)}) collective-permute-start(f32[16,128]{1,0:T(8,128)S(1)} %shard_map.74.refs_8_), channel_id=1, source_target_pairs={{0,16},{1,17},{2,18},{3,19},{4,20},{5,21},{6,22},{7,23},{8,24},{9,... | collective-permute-start | bytes 24584 | tf_op jit(solution)/shard_map/ppermute | solution.py:34
  18.2 0.0 collective-permute-done.10.refs_3_
  18.2 1.9 %collective-permute-start.5 = (f32[16,128]{1,0:T(8,128)S(1)}, f32[16,128]{1,0:T(8,128)S(1)}, u32[]{:S(2)}, u32[]{:S(2)}) collective-permute-start(f32[16,128]{1,0:T(8,128)S(1)} %shard_map.74.refs_8_), channel_id=1, source_target_pairs={{0,48},{1,49},{2,50},{3,51},{4,52},{5,53},{6,54},{7,55},{8,56},{9,... | collective-permute-start | bytes 24584 | tf_op jit(solution)/shard_map/ppermute | solution.py:34
  20.1 0.0 collective-permute-done.11.refs_4_
  20.1 0.0 collective-permute-done.12.refs_5_
  20.1 4.6 %shard_map.76.refs_8_ = f32[8,128]{1,0:T(8,128)S(1)} custom-call(bf16[16,1152]{1,0:T(8,128)(2,1)S(1)} %collective-permute-done.a1.refs_0_, bf16[16,1152]{1,0:T(8,128)(2,1)S(1)} %collective-permute-done.2.a3.refs_1_, bf16[16,1152]{1,0:T(8,128)(2,1)S(1)} %collective-permute-done.9.refs_2_, bf16[16,1152]{1,0:T(8,128)(2,1)S(1)} %collective-permute-done.10.refs_3_, ...), custom_call_target="tpu_custom_call" | custom-call | flops 3221225472 | bytes 6291456 | tf_op jit(solution)/shard_map/pallas_call | solution.py:315
  24.7 0.0 collective-permute-start.17
  24.7 0.0 collective-permute-done.3
  24.7 0.0 collective-permute-done.4
  24.7 0.0 collective-permute-done.5
  24.8 2.5 %collective-permute-start.6 = (f32[16,128]{1,0:T(8,128)S(1)}, f32[16,128]{1,0:T(8,128)S(1)}, u32[]{:S(2)}, u32[]{:S(2)}) collective-permute-start(f32[16,128]{1,0:T(8,128)S(1)} %add_add_fusion.1.refs_9_.y0), channel_id=1, source_target_pairs={{0,128},{1,129},{2,130},{3,131},{4,132},{5,133},{6,134},{7,135},{8... | collective-permute-start | bytes 24584 | tf_op jit(solution)/shard_map/ppermute | solution.py:34
  27.3 0.0 collective-permute-start.7
  27.3 1.8 %collective-permute-start.8 = (f32[16,128]{1,0:T(8,128)S(1)}, f32[16,128]{1,0:T(8,128)S(1)}, u32[]{:S(2)}, u32[]{:S(2)}) collective-permute-start(f32[16,128]{1,0:T(8,128)S(1)} %add_add_fusion.1.refs_9_.y0), channel_id=1, source_target_pairs={{0,192},{1,193},{2,194},{3,195},{4,196},{5,197},{6,198},{7,199},{8... | collective-permute-start | bytes 24584 | tf_op jit(solution)/shard_map/ppermute | solution.py:34
  29.1 4.8 %shard_map.77 = (f32[8,128]{1,0:T(8,128)S(1)}, f32[32,1536]{1,0:T(8,128)S(1)}) custom-call(bf16[16,1152]{1,0:T(8,128)(2,1)S(1)} %shard_map.73.a0.refs_0_, bf16[16,1152]{1,0:T(8,128)(2,1)S(1)} %collective-permute-done.1.a2.refs_1_, bf16[16,1152]{1,0:T(8,128)(2,1)S(1)} %collective-permute-done.9.refs_2_, bf16[16,1152]{1,0:T(8,128)(2,1)S(1)} %collective-permute-done.10.refs_3_, ...), custom_call_target="tpu_custom_call" | custom-call | flops 3221225472 | bytes 6291456 | tf_op jit(solution)/shard_map/pallas_call | solution.py:315
  33.9 0.0 collective-permute-done.6.y1
  33.9 0.0 collective-permute-done.7.y2
  33.9 0.0 collective-permute-done.8.y3
  34.0 2.1 %collective-permute-start.13 = (f32[24,128]{1,0:T(8,128)S(1)}, f32[24,128]{1,0:T(8,128)S(1)}, u32[]{:S(2)}, u32[]{:S(2)}) collective-permute-start(f32[24,128]{1,0:T(8,128)S(1)} %get-tuple-element.13), channel_id=1, source_target_pairs={{0,4},{1,5},{2,6},{3,7},{4,0},{5,1},{6,2},{7,3},{8,12},{9,13},{10,... | collective-permute-start | bytes 36872 | tf_op jit(solution)/shard_map/ppermute | solution.py:34
  36.0 1.9 %collective-permute-start.14 = (f32[24,128]{1,0:T(8,128)S(1)}, f32[24,128]{1,0:T(8,128)S(1)}, u32[]{:S(2)}, u32[]{:S(2)}) collective-permute-start(f32[24,128]{1,0:T(8,128)S(1)} %get-tuple-element.14), channel_id=1, source_target_pairs={{0,2},{1,3},{2,0},{3,1},{4,6},{5,7},{6,4},{7,5},{8,10},{9,11},{10,... | collective-permute-start | bytes 36872 | tf_op jit(solution)/shard_map/ppermute | solution.py:34
  37.9 0.2 collective-permute-start.15
  38.1 0.0 collective-permute-done.17
  38.2 3.3 %collective-permute-start.18 = (f32[1,128]{1,0:T(1,128)S(1)}, f32[1,128]{1,0:T(1,128)S(1)}, u32[]{:S(2)}, u32[]{:S(2)}) collective-permute-start(f32[1,128]{1,0:T(1,128)S(1)} %slice_add_fusion), channel_id=1, source_target_pairs={{0,8},{1,9},{2,10},{3,11},{4,12},{5,13},{6,14},{7,15},{8,0},{9,1},... | collective-permute-start | bytes 1544 | tf_op jit(solution)/shard_map/ppermute | solution.py:34
  41.5 0.0 collective-permute-start.16
  41.5 0.0 collective-permute-done.13
  41.5 0.0 collective-permute-done.14
  41.5 1.3 %collective-permute-done.15 = f32[24,128]{1,0:T(8,128)S(1)} collective-permute-done((f32[24,128]{1,0:T(8,128)S(1)}, f32[24,128]{1,0:T(8,128)S(1)}, u32[]{:S(2)}, u32[]{:S(2)}) %collective-permute-start.15) | collective-permute-done | bytes 12320 | tf_op jit(solution)/shard_map/ppermute | solution.py:34
  42.8 1.5 %collective-permute-start.19 = (f32[1,128]{1,0:T(1,128)S(1)}, f32[1,128]{1,0:T(1,128)S(1)}, u32[]{:S(2)}, u32[]{:S(2)}) collective-permute-start(f32[1,128]{1,0:T(1,128)S(1)} %slice.16), channel_id=1, source_target_pairs={{0,192},{1,193},{2,194},{3,195},{4,196},{5,197},{6,198},{7,199},{8... | collective-permute-start | bytes 1544 | tf_op jit(solution)/shard_map/ppermute | solution.py:34
  44.3 1.1 %shard_map.79.exchange_ref = f32[2,16]{1,0:T(2,128)S(1)} custom-call(f32[24,128]{1,0:T(8,128)S(1)} %add_add_fusion.y_ref, f32[1,1536]{1,0:T(1,128)S(1)} %reshape.19.c_ref, f32[32,1536]{1,0:T(8,128)S(1)} %get-tuple-element.16.rx_ref, bf16[2048,1536]{1,0:T(8,128)(2,1)S(1)} %bitcast.8), custom_call_target="tpu_custom_call" | custom-call | flops 805306368 | bytes 6291456 | tf_op jit(solution)/shard_map/pallas_call | solution.py:377
  45.4 0.2 collective-permute-done.18.d1
  45.6 2.0 %collective-permute-done.19.d2 = f32[1,128]{1,0:T(1,128)S(1)} collective-permute-done((f32[1,128]{1,0:T(1,128)S(1)}, f32[1,128]{1,0:T(1,128)S(1)}, u32[]{:S(2)}, u32[]{:S(2)}) %collective-permute-start.19) | collective-permute-done | bytes 544 | tf_op jit(solution)/shard_map/ppermute | solution.py:34
  47.7 0.6 %shard_map.80 = f32[2,16]{1,0:T(2,128)} custom-call(f32[1,16]{1,0:T(1,128)S(1)} %copy-done.1, f32[2,16]{1,0:T(2,128)S(1)} %bitcast.10, f32[2,16]{1,0:T(2,128)S(1)} %shard_map.79.exchange_ref, f32[8,128]{1,0:T(8,128)S(1)} %get-tuple-element.11.out_ref.near_ref, f32[1,128]{1,0:T(1,128)S(1)} %collective-permute-done.16.d0, ...), custom_call_target="tpu_custom_call" | custom-call | tf_op jit(solution)/shard_map/pallas_call | solution.py:387
  (18 shorter events, 0.1 us)
Async XLA Ops:
  0.0 20.1 %slice-start = ((s8[6291456]{0:T(1024)(128)(4,1)}), s8[2097152]{0:T(1024)(128)(4,1)S(1)}, s32[]{:S(2)}) async-start(s8[6291456]{0:T(1024)(128)(4,1)} %bitcast.4), calls=%async_computation | async-start | bytes 4194304
  1.1 14.2 %copy-start.2 = (f32[1536]{0:T(1024)S(1)}, f32[1536]{0:T(1024)}, u32[]{:S(2)}) copy-start(f32[1536]{0:T(1024)} %param.12) | copy-start | bytes 18436
  1.1 19.0 %slice-start.1 = ((s8[6291456]{0:T(1024)(128)(4,1)}), s8[4194304]{0:T(1024)(128)(4,1)S(1)}, s32[]{:S(2)}) async-start(s8[6291456]{0:T(1024)(128)(4,1)} %bitcast.4), calls=%async_computation.1 | async-start | bytes 8388608
  1.1 7.8 %collective-permute-start.9 = (bf16[16,1152]{1,0:T(8,128)(2,1)S(1)}, bf16[16,1152]{1,0:T(8,128)(2,1)S(1)}, u32[]{:S(2)}, u32[]{:S(2)}) collective-permute-start(bf16[16,1152]{1,0:T(8,128)(2,1)S(1)} %shard_map.73.a0.refs_0_), channel_id=1, source_target_pairs={{0,64},{1,65},{2,66},{3,67},{4,68},{5,69},{6,70},{7,71},{8,72},{9,... | collective-permute-start | bytes 110600 | tf_op jit(solution)/shard_map/ppermute | solution.py:34
  3.4 10.2 %collective-permute-start = (bf16[16,1152]{1,0:T(8,128)(2,1)S(1)}, bf16[16,1152]{1,0:T(8,128)(2,1)S(1)}, u32[]{:S(2)}, u32[]{:S(2)}) collective-permute-start(bf16[16,1152]{1,0:T(8,128)(2,1)S(1)} %shard_map.73.a0.refs_0_), channel_id=1, source_target_pairs={{0,8},{1,9},{2,10},{3,11},{4,12},{5,13},{6,14},{7,15},{8,0},{9,1},... | collective-permute-start | bytes 110600 | tf_op jit(solution)/shard_map/ppermute | solution.py:34
  8.9 6.5 %collective-permute-start.1 = (bf16[16,1152]{1,0:T(8,128)(2,1)S(1)}, bf16[16,1152]{1,0:T(8,128)(2,1)S(1)}, u32[]{:S(2)}, u32[]{:S(2)}) collective-permute-start(bf16[16,1152]{1,0:T(8,128)(2,1)S(1)} %shard_map.73.a0.refs_0_), channel_id=1, source_target_pairs={{0,1},{1,0},{2,3},{3,2},{4,5},{5,4},{6,7},{7,6},{8,9},{9,8},{10,11... | collective-permute-start | bytes 110600 | tf_op jit(solution)/shard_map/ppermute | solution.py:34
  8.9 9.3 %collective-permute-start.10 = (bf16[16,1152]{1,0:T(8,128)(2,1)S(1)}, bf16[16,1152]{1,0:T(8,128)(2,1)S(1)}, u32[]{:S(2)}, u32[]{:S(2)}) collective-permute-start(bf16[16,1152]{1,0:T(8,128)(2,1)S(1)} %collective-permute-done.9.refs_2_), channel_id=1, source_target_pairs={{0,2},{1,3},{2,0},{3,1},{4,6},{5,7},{6,4},{7,5},{8,10},{9,11},{10,... | collective-permute-start | bytes 110600 | tf_op jit(solution)/shard_map/ppermute | solution.py:34
  10.5 9.6 %collective-permute-start.11 = (bf16[16,1152]{1,0:T(8,128)(2,1)S(1)}, bf16[16,1152]{1,0:T(8,128)(2,1)S(1)}, u32[]{:S(2)}, u32[]{:S(2)}) collective-permute-start(bf16[16,1152]{1,0:T(8,128)(2,1)S(1)} %collective-permute-done.9.refs_2_), channel_id=1, source_target_pairs={{0,4},{1,5},{2,6},{3,7},{4,0},{5,1},{6,2},{7,3},{8,12},{9,13},{10,... | collective-permute-start | bytes 110600 | tf_op jit(solution)/shard_map/ppermute | solution.py:34
  13.4 6.7 %collective-permute-start.12 = (bf16[16,1152]{1,0:T(8,128)(2,1)S(1)}, bf16[16,1152]{1,0:T(8,128)(2,1)S(1)}, u32[]{:S(2)}, u32[]{:S(2)}) collective-permute-start(bf16[16,1152]{1,0:T(8,128)(2,1)S(1)} %collective-permute-done.9.refs_2_), channel_id=1, source_target_pairs={{0,6},{1,7},{2,4},{3,5},{4,2},{5,3},{6,0},{7,1},{8,14},{9,15},{10,... | collective-permute-start | bytes 110600 | tf_op jit(solution)/shard_map/ppermute | solution.py:34
  13.6 1.8 %collective-permute-start.2 = (bf16[16,1152]{1,0:T(8,128)(2,1)S(1)}, bf16[16,1152]{1,0:T(8,128)(2,1)S(1)}, u32[]{:S(2)}, u32[]{:S(2)}) collective-permute-start(bf16[16,1152]{1,0:T(8,128)(2,1)S(1)} %collective-permute-done.a1.refs_0_), channel_id=1, source_target_pairs={{0,1},{1,0},{2,3},{3,2},{4,5},{5,4},{6,7},{7,6},{8,9},{9,8},{10,11... | collective-permute-start | bytes 110600 | tf_op jit(solution)/shard_map/ppermute | solution.py:34
  15.6 9.1 %collective-permute-start.3 = (f32[16,128]{1,0:T(8,128)S(1)}, f32[16,128]{1,0:T(8,128)S(1)}, u32[]{:S(2)}, u32[]{:S(2)}) collective-permute-start(f32[16,128]{1,0:T(8,128)S(1)} %shard_map.74.refs_8_), channel_id=1, source_target_pairs={{0,32},{1,33},{2,34},{3,35},{4,36},{5,37},{6,38},{7,39},{8,40},{9,... | collective-permute-start | bytes 24584 | tf_op jit(solution)/shard_map/ppermute | solution.py:34
  17.1 7.6 %collective-permute-start.4 = (f32[16,128]{1,0:T(8,128)S(1)}, f32[16,128]{1,0:T(8,128)S(1)}, u32[]{:S(2)}, u32[]{:S(2)}) collective-permute-start(f32[16,128]{1,0:T(8,128)S(1)} %shard_map.74.refs_8_), channel_id=1, source_target_pairs={{0,16},{1,17},{2,18},{3,19},{4,20},{5,21},{6,22},{7,23},{8,24},{9,... | collective-permute-start | bytes 24584 | tf_op jit(solution)/shard_map/ppermute | solution.py:34
  18.2 6.6 %collective-permute-start.5 = (f32[16,128]{1,0:T(8,128)S(1)}, f32[16,128]{1,0:T(8,128)S(1)}, u32[]{:S(2)}, u32[]{:S(2)}) collective-permute-start(f32[16,128]{1,0:T(8,128)S(1)} %shard_map.74.refs_8_), channel_id=1, source_target_pairs={{0,48},{1,49},{2,50},{3,51},{4,52},{5,53},{6,54},{7,55},{8,56},{9,... | collective-permute-start | bytes 24584 | tf_op jit(solution)/shard_map/ppermute | solution.py:34
  24.7 13.4 %collective-permute-start.17 = (f32[1,128]{1,0:T(1,128)S(1)}, f32[1,128]{1,0:T(1,128)S(1)}, u32[]{:S(2)}, u32[]{:S(2)}) collective-permute-start(f32[1,128]{1,0:T(1,128)S(1)} %slice.14), channel_id=1, source_target_pairs={{0,1},{1,0},{2,3},{3,2},{4,5},{5,4},{6,7},{7,6},{8,9},{9,8},{10,11... | collective-permute-start | bytes 1544 | tf_op jit(solution)/shard_map/ppermute | solution.py:34
  24.8 9.2 %collective-permute-start.6 = (f32[16,128]{1,0:T(8,128)S(1)}, f32[16,128]{1,0:T(8,128)S(1)}, u32[]{:S(2)}, u32[]{:S(2)}) collective-permute-start(f32[16,128]{1,0:T(8,128)S(1)} %add_add_fusion.1.refs_9_.y0), channel_id=1, source_target_pairs={{0,128},{1,129},{2,130},{3,131},{4,132},{5,133},{6,134},{7,135},{8... | collective-permute-start | bytes 24584 | tf_op jit(solution)/shard_map/ppermute | solution.py:34
  27.3 6.7 %collective-permute-start.7 = (f32[16,128]{1,0:T(8,128)S(1)}, f32[16,128]{1,0:T(8,128)S(1)}, u32[]{:S(2)}, u32[]{:S(2)}) collective-permute-start(f32[16,128]{1,0:T(8,128)S(1)} %add_add_fusion.1.refs_9_.y0), channel_id=1, source_target_pairs={{0,64},{1,65},{2,66},{3,67},{4,68},{5,69},{6,70},{7,71},{8,72},{9,... | collective-permute-start | bytes 24584 | tf_op jit(solution)/shard_map/ppermute | solution.py:34
  27.3 6.7 %collective-permute-start.8 = (f32[16,128]{1,0:T(8,128)S(1)}, f32[16,128]{1,0:T(8,128)S(1)}, u32[]{:S(2)}, u32[]{:S(2)}) collective-permute-start(f32[16,128]{1,0:T(8,128)S(1)} %add_add_fusion.1.refs_9_.y0), channel_id=1, source_target_pairs={{0,192},{1,193},{2,194},{3,195},{4,196},{5,197},{6,198},{7,199},{8... | collective-permute-start | bytes 24584 | tf_op jit(solution)/shard_map/ppermute | solution.py:34
  33.9 13.8 %copy-start = (f32[1,2,16]{2,1,0:T(2,128)S(1)}, f32[1,2,16]{2,1,0:T(2,128)}, u32[]{:S(2)}) copy-start(f32[1,2,16]{2,1,0:T(2,128)} %param.8) | copy-start | bytes 388
  33.9 13.8 %copy-start.1 = (f32[1,16]{1,0:T(1,128)S(1)}, f32[1,16]{1,0:T(1,128)}, u32[]{:S(2)}) copy-start(f32[1,16]{1,0:T(1,128)} %energy_ref.1) | copy-start | bytes 196
  34.0 7.5 %collective-permute-start.13 = (f32[24,128]{1,0:T(8,128)S(1)}, f32[24,128]{1,0:T(8,128)S(1)}, u32[]{:S(2)}, u32[]{:S(2)}) collective-permute-start(f32[24,128]{1,0:T(8,128)S(1)} %get-tuple-element.13), channel_id=1, source_target_pairs={{0,4},{1,5},{2,6},{3,7},{4,0},{5,1},{6,2},{7,3},{8,12},{9,13},{10,... | collective-permute-start | bytes 36872 | tf_op jit(solution)/shard_map/ppermute | solution.py:34
  36.0 5.5 %collective-permute-start.14 = (f32[24,128]{1,0:T(8,128)S(1)}, f32[24,128]{1,0:T(8,128)S(1)}, u32[]{:S(2)}, u32[]{:S(2)}) collective-permute-start(f32[24,128]{1,0:T(8,128)S(1)} %get-tuple-element.14), channel_id=1, source_target_pairs={{0,2},{1,3},{2,0},{3,1},{4,6},{5,7},{6,4},{7,5},{8,10},{9,11},{10,... | collective-permute-start | bytes 36872 | tf_op jit(solution)/shard_map/ppermute | solution.py:34
  37.9 4.9 %collective-permute-start.15 = (f32[24,128]{1,0:T(8,128)S(1)}, f32[24,128]{1,0:T(8,128)S(1)}, u32[]{:S(2)}, u32[]{:S(2)}) collective-permute-start(f32[24,128]{1,0:T(8,128)S(1)} %get-tuple-element.15), channel_id=1, source_target_pairs={{0,6},{1,7},{2,4},{3,5},{4,2},{5,3},{6,0},{7,1},{8,14},{9,15},{10,... | collective-permute-start | bytes 36872 | tf_op jit(solution)/shard_map/ppermute | solution.py:34
  38.2 7.4 %collective-permute-start.18 = (f32[1,128]{1,0:T(1,128)S(1)}, f32[1,128]{1,0:T(1,128)S(1)}, u32[]{:S(2)}, u32[]{:S(2)}) collective-permute-start(f32[1,128]{1,0:T(1,128)S(1)} %slice_add_fusion), channel_id=1, source_target_pairs={{0,8},{1,9},{2,10},{3,11},{4,12},{5,13},{6,14},{7,15},{8,0},{9,1},... | collective-permute-start | bytes 1544 | tf_op jit(solution)/shard_map/ppermute | solution.py:34
  41.5 4.1 %collective-permute-start.16 = (f32[1,128]{1,0:T(1,128)S(1)}, f32[1,128]{1,0:T(1,128)S(1)}, u32[]{:S(2)}, u32[]{:S(2)}) collective-permute-start(f32[1,128]{1,0:T(1,128)S(1)} %slice.12), channel_id=1, source_target_pairs={{0,1},{1,0},{2,3},{3,2},{4,5},{5,4},{6,7},{7,6},{8,9},{9,8},{10,11... | collective-permute-start | bytes 1544 | tf_op jit(solution)/shard_map/ppermute | solution.py:34
  42.8 4.8 %collective-permute-start.19 = (f32[1,128]{1,0:T(1,128)S(1)}, f32[1,128]{1,0:T(1,128)S(1)}, u32[]{:S(2)}, u32[]{:S(2)}) collective-permute-start(f32[1,128]{1,0:T(1,128)S(1)} %slice.16), channel_id=1, source_target_pairs={{0,192},{1,193},{2,194},{3,195},{4,196},{5,197},{6,198},{7,199},{8... | collective-permute-start | bytes 1544 | tf_op jit(solution)/shard_map/ppermute | solution.py:34

commit v9 on v8

--- a/solution.py
+++ b/solution.py
@@ -20,7 +20,7 @@
 ANY = pl.BlockSpec(memory_space=pl.ANY)
 
 
-def move(value, x=0, z=0, far=0, y=0, core=0, step=0):
+def move(value, x=0, z=0, far=0, y=0, core=0, step=0, z_other=None):
     pairs = []
     for a in range(4):
         for b in range(4):
@@ -28,7 +28,8 @@
                 for d in range(4):
                     for e in range(2):
                         source = (a * 4 + b) * 16 + c * 8 + d * 2 + e
-                        group = (((a + step) % 4) ^ x) * 4 + (b ^ z)
+                        turn = z_other if e and z_other is not None else z
+                        group = (((a + step) % 4) ^ x) * 4 + (b ^ turn)
                         member = (c ^ far) * 8 + (d ^ y) * 2 + (e ^ core)
                         pairs.append((source, group * 16 + member))
     return lax.ppermute(value, ("grp", "kin"), pairs)
@@ -143,9 +144,9 @@
 
 def pair_kernel(near, *refs):
     if near:
-        w_ref, z_ref, far_ref, _, out_ref, rx_ref, lhs, xa, xb, acc, ca, cb = refs[6:]
+        w_ref, z_ref, _, __, acc_ref, rx_ref, lhs, xa, xb, ca, cb = refs[6:]
     else:
-        w_ref, z_ref, _, out_ref, lhs, xa, xb, acc, ca, cb = refs[6:]
+        w_ref, z_ref, _, acc_ref, lhs, xa, xb, ca, cb = refs[6:]
     base = 2 * near
     a_pays = refs[0:2]
     b_pays = refs[2:6]
@@ -177,7 +178,6 @@
             put(ROWS + row, xa[m], xb[n], 32, 32)
     if near:
         put(2 * ROWS, xa[0], dot(til, a_pays[0][:, 0:NMU]), 32, 0)
-    acc[...] = jnp.zeros_like(acc)
     for at in range(0, NG, CHUNK):
         part = pl.ds(at, CHUNK)
         z = z_ref[:, part]
@@ -191,16 +191,21 @@
             cb[side * ROWS : side * ROWS + ROWS] = dens[0:ROWS].astype(BF16)
             if near:
                 rx_ref[side * 16 : side * 16 + 16, part] = dens[ROWS:val]
-        acc[...] += dot_t(ca[...], cb[...])
-
+        acc_ref[...] = dot_t(ca[...], cb[...])
+
+
+def rows_kernel(far_ref, near_ref, *refs):
+    a_pays, b_pays, out_ref = refs[0:4], refs[4:8], refs[8]
+    half = 2 * ROWS
     pick_row = iota((8, 16), 0)
     pick_col = iota((8, 16), 1)
-    xv_a = jnp.zeros((8, 128), F32)
-    xv_b = jnp.zeros((8, 128), F32)
-    for m in range(2):
-        xv_a += dot(onehot((pick_row == m) & (pick_col == 12)), a_pays[m][:, NMU:WIDTH])
-    for n in range(4):
-        xv_b += dot(onehot((pick_row == n) & (pick_col == 12)), b_pays[n][:, NMU:WIDTH])
+
+    def lines(pays):
+        total = jnp.zeros((8, 128), F32)
+        for n, pay in enumerate(pays):
+            total += dot(onehot((pick_row == n) & (pick_col == 12)), pay[:, NMU:WIDTH])
+        return total.astype(BF16)
+
     row = iota((ROWS, 8), 0)
     col = iota((ROWS, 8), 1)
     of_a = onehot(row >> 6 == col)
@@ -209,52 +214,55 @@
     lane = iota((ROWS, 128), 1)
     same_c = lane & 3 == (row >> 2) & 3
     same_d = lane & 3 == row & 3
-    spread_a = jnp.where(same_c, dot(of_a, xv_a.astype(BF16)), 0.0).astype(BF16)
-    spread_b = jnp.where(same_d, dot(of_b, xv_b.astype(BF16)), 0.0).astype(BF16)
     lane = iota((128, ROWS), 0)
     col = iota((128, ROWS), 1)
     by_w = (lane >> 2) & 3 == col & 3
     by_v = (lane >> 2) & 3 == (col >> 2) & 3
     first = lane >> 4 == 1
     second = lane >> 4 == 2
-    pair = iota((ROWS, ROWS), 0) >> 4 == iota((ROWS, ROWS), 1) >> 4
-    k_re = jnp.where(pair, acc[0:ROWS, 0:ROWS] + acc[ROWS:, ROWS:], 0.0)
-    k_im = jnp.where(pair, acc[0:ROWS, ROWS:] - acc[ROWS:, 0:ROWS], 0.0)
+    spread_b = jnp.where(same_d, dot(of_b, lines(b_pays)), 0.0).astype(BF16)
     xd_re = dot(spread_b, onehot(by_w & first))
     xd_im = dot(spread_b, onehot(by_w & second))
-    xh_re = dot(spread_a, onehot(by_v & first))
-    xh_im = dot(spread_a, onehot(by_v & second))
+    to_re = onehot(by_v & first)
+    to_im = onehot(by_v & second)
+    pair = iota((ROWS, ROWS), 0) >> 4 == iota((ROWS, ROWS), 1) >> 4
     lane = iota((ROWS, 128), 1)
     col = iota((ROWS, 128), 0)
     by_w = (lane >> 2) & 3 == col & 3
     by_v = (lane >> 2) & 3 == (col >> 2) & 3
     first = lane >> 4 == 0
     second = lane >> 4 == 1
-    sum_d = dot_split(k_re * xd_re - k_im * xd_im, onehot(by_v & first)) + dot_split(
-        k_re * xd_im + k_im * xd_re, onehot(by_v & second)
-    )
-    sum_h = dot_split(k_re * xh_re + k_im * xh_im, onehot(by_w & first)) + dot_split(
-        k_re * xh_im - k_im * xh_re, onehot(by_w & second)
-    )
-    sum_d = jnp.where(same_c, sum_d, 0.0)
-    sum_h = jnp.where(same_d, sum_h, 0.0)
-    row = iota((8, ROWS), 0)
-    col = iota((8, ROWS), 1)
-    to_a = onehot(row == col >> 6)
-    to_b = onehot(row == 4 + ((col >> 4) & 3))
-    high_d, low_d = split(sum_d)
-    high_h, low_h = split(sum_h)
-    total = dot(to_a, high_d) + dot(to_a, low_d) + dot(to_b, high_h) + dot(to_b, low_h)
-    if near:
-        total += jnp.where(iota((8, 128), 0) >= 4, far_ref[...], 0.0)
+    d_re, d_im = onehot(by_v & first), onehot(by_v & second)
+    h_re, h_im = onehot(by_w & first), onehot(by_w & second)
+    row = iota((16, ROWS), 0)
+    col = iota((16, ROWS), 1)
+    to_b = onehot(row == 8 + ((col >> 4) & 3))
+    total = jnp.zeros((16, 128), F32)
+    for side, acc in enumerate((far_ref, near_ref)):
+        spread_a = dot(of_a, lines(a_pays[2 * side : 2 * side + 2]))
+        spread_a = jnp.where(same_c, spread_a, 0.0).astype(BF16)
+        xh_re = dot(spread_a, to_re)
+        xh_im = dot(spread_a, to_im)
+        k_re = jnp.where(pair, acc[0:ROWS, 0:ROWS] + acc[ROWS:half, ROWS:half], 0.0)
+        k_im = jnp.where(pair, acc[0:ROWS, ROWS:half] - acc[ROWS:half, 0:ROWS], 0.0)
+        sum_d = dot_split(k_re * xd_re - k_im * xd_im, d_re) + dot_split(k_re * xd_im + k_im * xd_re, d_im)
+        sum_h = dot_split(k_re * xh_re + k_im * xh_im, h_re) + dot_split(k_re * xh_im - k_im * xh_re, h_im)
+        high_d, low_d = split(jnp.where(same_c, sum_d, 0.0))
+        high_h, low_h = split(jnp.where(same_d, sum_h, 0.0))
+        to_a = onehot(row == side + 2 * (col >> 6))
+        total += dot(to_a, high_d) + dot(to_a, low_d) + dot(to_b, high_h) + dot(to_b, low_h)
     out_ref[...] = total
 
 
-def mail_kernel(y0, y1, y2, y3, out_ref, *mails):
-    total = y0[...] + y1[...] + y2[...] + y3[...]
+def sum_kernel(y0, y1, y2, y3, _, out_ref):
+    out_ref[...] = y0[...] + y1[...] + y2[...] + y3[...]
+
+
+def mail_kernel(y0, y1, rows_ref, *mails):
+    total = y0[...] + y1[...]
     for n, mail in enumerate(mails):
         mail[0:16] = total
-        mail[16:24] = jnp.broadcast_to(out_ref[4 + n : 5 + n], (8, 128))
+        mail[16:24] = jnp.broadcast_to(rows_ref[8 + n : 9 + n], (8, 128))
 
 
 def exchange_kernel(y_ref, c_ref, rx_ref, z_ref, out_ref, lhs):
@@ -288,9 +296,9 @@
     out_ref[...] = jnp.concatenate(out, 0)
 
 
-def final_kernel(energy_ref, vector_ref, exchange_ref, near_ref, d0, d1, d2, out_ref):
+def final_kernel(energy_ref, vector_ref, exchange_ref, near_ref, d_ref, h_ref, out_ref):
     scale = 1.0 / 256
-    terms = near_ref[0:1] + d0[...] + d1[...] + d2[...]
+    terms = near_ref[1:2] + d_ref[...] + h_ref[...]
     for part in range(2):
         term = terms[:, part * NT : part * NT + NT]
         out_ref[part : part + 1] = (
@@ -309,25 +317,34 @@
 
 
 def pair_call(near, operands):
-    out_shape = [jax.ShapeDtypeStruct((8, 128), F32)]
+    out_shape = [pltpu.VMEM((2 * ROWS, 2 * ROWS), F32)]
     if near:
         out_shape.append(pltpu.VMEM((32, NG), F32))
     return pl.pallas_call(
         functools.partial(pair_kernel, near),
-        in_specs=[VMEM] * 8 + [VMEM] * near + [ANY],
+        in_specs=[VMEM] * 8 + [ANY] * (1 + near),
         out_specs=[VMEM] * len(out_shape),
         out_shape=out_shape,
         scratch_shapes=[
             pltpu.VMEM((4 * ROWS + 32 * near, 2 * NMU), BF16),
             pltpu.VMEM((2, 64, NMU), F32),
             pltpu.VMEM((4, 64, NMU), F32),
-            pltpu.VMEM((2 * ROWS, 2 * ROWS), F32),
             pltpu.VMEM((2 * ROWS, CHUNK), BF16),
             pltpu.VMEM((2 * ROWS, CHUNK), BF16),
         ],
         compiler_params=params(24),
         cost_estimate=cost(4 * ROWS),
     )(*operands)
+
+
+def small_call(kernel, shapes, *operands, after=()):
+    return pl.pallas_call(
+        kernel,
+        in_specs=[VMEM] * len(operands) + [ANY] * len(after),
+        out_specs=[VMEM] * len(shapes),
+        out_shape=[jax.ShapeDtypeStruct(shape, F32) for shape in shapes],
+        compiler_params=params(8),
+    )(*operands, *after)
 
 
 def on_device(waves, vector, energies, basis, screening, coulomb, qmap):
@@ -362,18 +379,15 @@
         compiler_params=params(8),
     )(pay, a1, a2, a3)
     b_pays = (b0, b1, b2, b3)
-    (far_out,) = pair_call(0, (a1, a3, *b_pays, weights, z, y))
-    far_sum = far_out[0:1] + move(far_out[1:2], core=1)
-    y = y + move(y, z=2) + move(y, z=1) + move(y, z=3)
-    near_out, rx = pair_call(1, (pay, a2, *b_pays, weights, z, far_out, y))
-    mail = pl.pallas_call(
-        mail_kernel,
-        in_specs=[VMEM] * 5,
-        out_specs=[VMEM] * 4,
-        out_shape=[jax.ShapeDtypeStruct((24, 128), F32)] * 4,
-        compiler_params=params(4),
-    )(y, *(move(y, x=n) for n in (2, 1, 3)), near_out)
-    mail = mail[0] + move(mail[2], y=2) + move(mail[1], y=1) + move(mail[3], y=3)
+    (far_acc,) = pair_call(0, (a1, a3, *b_pays, weights, z, y))
+    y = 0.5 * (y + move(y, z=1)) + move(y, z=3, z_other=2)
+    near_acc, rx = pair_call(1, (pay, a2, *b_pays, weights, z, far_acc, y))
+    (y,) = small_call(sum_kernel, [(16, 128)], y, *(move(y, x=n) for n in (2, 1, 3)), after=(near_acc,))
+    other = move(y, core=1)
+    (rows,) = small_call(rows_kernel, [(16, 128)], far_acc, near_acc, a1, a3, pay, a2, *b_pays)
+    mails = small_call(mail_kernel, [(24, 128)] * 4, y, other, rows)
+    mail = mails[0] + move(mails[2], y=2) + move(mails[1], y=1) + move(mails[3], y=3)
+    rows = rows[0:2] + move(rows[2:4], core=1)
     exchange = pl.pallas_call(
         exchange_kernel,
         in_specs=[VMEM] * 4,
@@ -384,19 +398,14 @@
         cost_estimate=cost(128),
     )(mail, coulomb.reshape(1, NG), rx, z)
 
-    out = pl.pallas_call(
+    (out,) = small_call(
         final_kernel,
-        in_specs=[VMEM] * 7,
-        out_specs=VMEM,
-        out_shape=jax.ShapeDtypeStruct((2, NT), F32),
-        compiler_params=params(4),
-    )(
+        [(2, NT)],
         energies,
         vector.reshape(2, NT),
         exchange,
-        near_out,
-        move(near_out[1:2], core=1),
-        move(far_sum, far=1),
+        rows,
+        move(rows[0:1], far=1),
         move(mail[16:17], step=3),
     )
     return out.reshape(1, 2, NT)

time: 48.4 us -> 47.3 us (0.977)
  waiting for transfers between devices: 3.62 us -> 2.71 us
  starting transfers between devices: 30.3 us -> 29.6 us
    pallas_call x2 -> x4, Pallas kernels: 0.65 us -> 2.1 us  [small_call(): pl.pallas_call(kernel, in_specs=[VMEM] * len(operands) + [ANY] * len(afte...]
    pallas_call x2, Pallas kernels: 9.43 us -> 8.28 us  [pair_call(): pl.pallas_call(functools.partial(pair_kernel, near), in_specs=[VMEM] * 8...]
    ppermute x20 -> x19, waiting for transfers between devices: 3.62 us -> 2.71 us  [move(): return lax.ppermute(value, ('grp', 'kin'), pairs)]
    ppermute x20 -> x19, starting transfers between devices: 30.3 us -> 29.6 us  [move(): return lax.ppermute(value, ('grp', 'kin'), pairs)]
  transfers between devices with their start and end apart: 20 -> 19, of which waited for: 3 -> 3; matrix products, arithmetic and copies ran while one was open for 0% -> 0% of each run, Pallas kernels for 26% -> 27%
where the time goes in v9:
time: 47.3 us; the launch traced here: 47.1 us
  starting transfers between devices  29.6 us (63%)
  Pallas kernels  14.5 us (31%)
  waiting for transfers between devices  2.71 us (6%)
    ppermute x19, starting transfers between devices, move(): return lax.ppermute(value, ('grp', 'kin'), pairs)  29.6 us
    pallas_call x2, Pallas kernels, pair_call(): pl.pallas_call(functools.partial(pair_kernel, near), in_specs=[VMEM] * 8...  8.28 us
    ppermute x19, waiting for transfers between devices, move(): return lax.ppermute(value, ('grp', 'kin'), pairs)  2.71 us
    pallas_call x4, Pallas kernels, small_call(): pl.pallas_call(kernel, in_specs=[VMEM] * len(operands) + [ANY] * len(afte...  2.1 us
    pallas_call x1, Pallas kernels, on_device(): pl.pallas_call(weights_kernel, in_specs=[SMEM, ANY], out_specs=VMEM, out_...  1.74 us
    pallas_call x1, Pallas kernels, on_device(): pl.pallas_call(pack_kernel, in_specs=[ANY] * 2, out_specs=VMEM, out_shape...  1.1 us
    pallas_call x1, Pallas kernels, on_device(): pl.pallas_call(exchange_kernel, in_specs=[VMEM] * 4, out_specs=VMEM, out_...  1.06 us
  transfers between devices with their start and end apart: 19, of which 3 were waited for; matrix products, arithmetic and copies ran while one was open for 0% of the time, Pallas kernels for 27%

profile of v9, /device:TPU:6, one launch (start us, length us, event | category | flops | bytes accessed | tf_op | source)
XLA Modules:
  0.0 47.1 jit_solution(9650836608581161195)
XLA Ops:
  0.0 1.1 %shard_map.73.a0.refs_0_.refs_2_ = bf16[16,1152]{1,0:T(8,128)(2,1)S(1)} custom-call(bf16[16,1024]{1,0:T(8,128)(2,1)} %bitcast.11, f32[2,16]{1,0:T(2,128)} %bitcast.9), custom_call_target="tpu_custom_call" | custom-call | tf_op jit(solution)/shard_map/pallas_call | solution.py:351
  1.1 0.0 slice-start.1
  1.1 2.3 %collective-permute-start.8 = (bf16[16,1152]{1,0:T(8,128)(2,1)S(1)}, bf16[16,1152]{1,0:T(8,128)(2,1)S(1)}, u32[]{:S(2)}, u32[]{:S(2)}) collective-permute-start(bf16[16,1152]{1,0:T(8,128)(2,1)S(1)} %shard_map.73.a0.refs_0_.refs_2_), channel_id=1, source_target_pairs={{0,64},{1,65},{2,66},{3,67},{4,68},{5,69},{6,70},{7,71},{8,72},{9,... | collective-permute-start | bytes 110600 | tf_op jit(solution)/shard_map/ppermute | solution.py:35
  3.4 5.5 %collective-permute-start = (bf16[16,1152]{1,0:T(8,128)(2,1)S(1)}, bf16[16,1152]{1,0:T(8,128)(2,1)S(1)}, u32[]{:S(2)}, u32[]{:S(2)}) collective-permute-start(bf16[16,1152]{1,0:T(8,128)(2,1)S(1)} %shard_map.73.a0.refs_0_.refs_2_), channel_id=1, source_target_pairs={{0,8},{1,9},{2,10},{3,11},{4,12},{5,13},{6,14},{7,15},{8,0},{9,1},... | collective-permute-start | bytes 110600 | tf_op jit(solution)/shard_map/ppermute | solution.py:35
  8.9 0.0 collective-permute-start.1
  8.9 0.0 collective-permute-done.8.refs_2_.refs_4_
  8.9 3.2 %collective-permute-start.10 = (bf16[16,1152]{1,0:T(8,128)(2,1)S(1)}, bf16[16,1152]{1,0:T(8,128)(2,1)S(1)}, u32[]{:S(2)}, u32[]{:S(2)}) collective-permute-start(bf16[16,1152]{1,0:T(8,128)(2,1)S(1)} %collective-permute-done.8.refs_2_.refs_4_), channel_id=1, source_target_pairs={{0,4},{1,5},{2,6},{3,7},{4,0},{5,1},{6,2},{7,3},{8,12},{9,13},{10,... | collective-permute-start | bytes 110600 | tf_op jit(solution)/shard_map/ppermute | solution.py:35
  12.1 1.1 %collective-permute-start.11 = (bf16[16,1152]{1,0:T(8,128)(2,1)S(1)}, bf16[16,1152]{1,0:T(8,128)(2,1)S(1)}, u32[]{:S(2)}, u32[]{:S(2)}) collective-permute-start(bf16[16,1152]{1,0:T(8,128)(2,1)S(1)} %collective-permute-done.8.refs_2_.refs_4_), channel_id=1, source_target_pairs={{0,6},{1,7},{2,4},{3,5},{4,2},{5,3},{6,0},{7,1},{8,14},{9,15},{10,... | collective-permute-start | bytes 110600 | tf_op jit(solution)/shard_map/ppermute | solution.py:35
  13.1 0.0 collective-permute-start.9
  13.1 0.0 collective-permute-done.a1.refs_0_
  13.1 0.0 collective-permute-start.2
  13.1 1.7 %shard_map.75.refs_6_ = f32[16,1536]{1,0:T(8,128)S(1)} custom-call(s32[1,256]{1,0:T(1,128)} %qmap_ref.1, f32[256,1536]{1,0:T(8,128)} %screening.1), custom_call_target="tpu_custom_call" | custom-call | flops 4000000000 | bytes 1024 | tf_op jit(solution)/shard_map/pallas_call | solution.py:363
  14.9 0.0 collective-permute-done.1.a2.refs_1_.refs_3_
  14.9 0.0 collective-permute-done.2.a3.refs_1_
  14.9 0.2 shard_map.74.refs_8_
  15.1 1.1 %collective-permute-start.3 = (f32[16,128]{1,0:T(8,128)S(1)}, f32[16,128]{1,0:T(8,128)S(1)}, u32[]{:S(2)}, u32[]{:S(2)}) collective-permute-start(f32[16,128]{1,0:T(8,128)S(1)} %shard_map.74.refs_8_), channel_id=1, source_target_pairs={{0,16},{1,17},{2,18},{3,19},{4,20},{5,21},{6,22},{7,23},{8,24},{9,... | collective-permute-start | bytes 24584 | tf_op jit(solution)/shard_map/ppermute | solution.py:35
  16.2 1.9 %collective-permute-start.4 = (f32[16,128]{1,0:T(8,128)S(1)}, f32[16,128]{1,0:T(8,128)S(1)}, u32[]{:S(2)}, u32[]{:S(2)}) collective-permute-start(f32[16,128]{1,0:T(8,128)S(1)} %shard_map.74.refs_8_), channel_id=1, source_target_pairs={{0,48},{1,33},{2,50},{3,35},{4,52},{5,37},{6,54},{7,39},{8,56},{9,... | collective-permute-start | bytes 24584 | tf_op jit(solution)/shard_map/ppermute | solution.py:35
  18.1 0.0 collective-permute-done.10.refs_4_.refs_6_
  18.1 0.0 collective-permute-done.11.refs_5_.refs_7_
  18.1 0.0 collective-permute-done.9.refs_3_.refs_5_
  18.2 4.0 %shard_map.76.refs_8_.far_ref = f32[256,256]{1,0:T(8,128)S(1)} custom-call(bf16[16,1152]{1,0:T(8,128)(2,1)S(1)} %collective-permute-done.a1.refs_0_, bf16[16,1152]{1,0:T(8,128)(2,1)S(1)} %collective-permute-done.2.a3.refs_1_, bf16[16,1152]{1,0:T(8,128)(2,1)S(1)} %collective-permute-done.8.refs_2_.refs_4_, ...), custom_call_target="tpu_custom_call" | custom-call | flops 3221225472 | bytes 6291456 | tf_op jit(solution)/shard_map/pallas_call | solution.py:323
  22.2 0.0 collective-permute-done.3
  22.2 0.0 collective-permute-done.4
  22.2 0.0 copy-start.2
  22.2 2.5 %collective-permute-start.5 = (f32[16,128]{1,0:T(8,128)S(1)}, f32[16,128]{1,0:T(8,128)S(1)}, u32[]{:S(2)}, u32[]{:S(2)}) collective-permute-start(f32[16,128]{1,0:T(8,128)S(1)} %multiply_add_fusion.refs_9_.y0), channel_id=1, source_target_pairs={{0,128},{1,129},{2,130},{3,131},{4,132},{5,133},{6,134},{7,135},{8... | collective-permute-start | bytes 24584 | tf_op jit(solution)/shard_map/ppermute | solution.py:35
  24.8 0.0 collective-permute-start.6
  24.8 1.8 %collective-permute-start.7 = (f32[16,128]{1,0:T(8,128)S(1)}, f32[16,128]{1,0:T(8,128)S(1)}, u32[]{:S(2)}, u32[]{:S(2)}) collective-permute-start(f32[16,128]{1,0:T(8,128)S(1)} %multiply_add_fusion.refs_9_.y0), channel_id=1, source_target_pairs={{0,192},{1,193},{2,194},{3,195},{4,196},{5,197},{6,198},{7,199},{8... | collective-permute-start | bytes 24584 | tf_op jit(solution)/shard_map/ppermute | solution.py:35
  26.6 4.3 %shard_map.77 = (f32[256,256]{1,0:T(8,128)S(1)}, f32[32,1536]{1,0:T(8,128)S(1)}) custom-call(bf16[16,1152]{1,0:T(8,128)(2,1)S(1)} %shard_map.73.a0.refs_0_.refs_2_, bf16[16,1152]{1,0:T(8,128)(2,1)S(1)} %collective-permute-done.1.a2.refs_1_.refs_3_, bf16[16,1152]{1,0:T(8,128)(2,1)S(1)} %collective-permute-done.8.refs_2_.refs_4_, ...), custom_call_target="tpu_custom_call" | custom-call | flops 3221225472 | bytes 6291456 | tf_op jit(solution)/shard_map/pallas_call | solution.py:323
  30.8 0.0 copy-start
  30.8 0.0 copy-start.1
  30.8 0.0 collective-permute-done.5.y1
  30.9 0.0 collective-permute-done.6.y2
  30.9 0.1 collective-permute-start.12
  31.0 1.4 %shard_map.79.rows_ref = f32[16,128]{1,0:T(8,128)S(1)} custom-call(f32[256,256]{1,0:T(8,128)S(1)} %shard_map.76.refs_8_.far_ref, f32[256,256]{1,0:T(8,128)S(1)} %get-tuple-element.11._.near_ref, bf16[16,1152]{1,0:T(8,128)(2,1)S(1)} %collective-permute-done.a1.refs_0_, bf16[16,1152]{1,0:T(8,128)(2,1)S(1)} %collective-permute-done.2.a3.refs_1_, ...), custom_call_target="tpu_custom_call" | custom-call | tf_op jit(solution)/shard_map/pallas_call | solution.py:341
  32.4 0.5 %collective-permute-start.16 = (f32[2,128]{1,0:T(2,128)S(1)}, f32[2,128]{1,0:T(2,128)S(1)}, u32[]{:S(2)}, u32[]{:S(2)}) collective-permute-start(f32[2,128]{1,0:T(2,128)S(1)} %slice.17), channel_id=1, source_target_pairs={{0,1},{1,0},{2,3},{3,2},{4,5},{5,4},{6,7},{7,6},{8,9},{9,8},{10,11... | collective-permute-start | bytes 3080 | tf_op jit(solution)/shard_map/ppermute | solution.py:35
  33.0 0.0 collective-permute-done.12.y1
  33.0 3.7 %collective-permute-start.13 = (f32[24,128]{1,0:T(8,128)S(1)}, f32[24,128]{1,0:T(8,128)S(1)}, u32[]{:S(2)}, u32[]{:S(2)}) collective-permute-start(f32[24,128]{1,0:T(8,128)S(1)} %get-tuple-element.13), channel_id=1, source_target_pairs={{0,4},{1,5},{2,6},{3,7},{4,0},{5,1},{6,2},{7,3},{8,12},{9,13},{10,... | collective-permute-start | bytes 36872 | tf_op jit(solution)/shard_map/ppermute | solution.py:35
  36.7 1.0 %collective-permute-start.15 = (f32[24,128]{1,0:T(8,128)S(1)}, f32[24,128]{1,0:T(8,128)S(1)}, u32[]{:S(2)}, u32[]{:S(2)}) collective-permute-start(f32[24,128]{1,0:T(8,128)S(1)} %get-tuple-element.15), channel_id=1, source_target_pairs={{0,6},{1,7},{2,4},{3,5},{4,2},{5,3},{6,0},{7,1},{8,14},{9,15},{10,... | collective-permute-start | bytes 36872 | tf_op jit(solution)/shard_map/ppermute | solution.py:35
  37.8 0.0 collective-permute-done.16
  37.8 3.4 %collective-permute-start.17 = (f32[1,128]{1,0:T(1,128)S(1)}, f32[1,128]{1,0:T(1,128)S(1)}, u32[]{:S(2)}, u32[]{:S(2)}) collective-permute-start(f32[1,128]{1,0:T(1,128)S(1)} %slice.14), channel_id=1, source_target_pairs={{0,8},{1,9},{2,10},{3,11},{4,12},{5,13},{6,14},{7,15},{8,0},{9,1},... | collective-permute-start | bytes 1544 | tf_op jit(solution)/shard_map/ppermute | solution.py:35
  41.2 0.0 collective-permute-done.13
  41.2 0.0 collective-permute-done.14
  41.2 0.4 collective-permute-done.15
  41.6 1.5 %collective-permute-start.18 = (f32[1,128]{1,0:T(1,128)S(1)}, f32[1,128]{1,0:T(1,128)S(1)}, u32[]{:S(2)}, u32[]{:S(2)}) collective-permute-start(f32[1,128]{1,0:T(1,128)S(1)} %slice.18), channel_id=1, source_target_pairs={{0,192},{1,193},{2,194},{3,195},{4,196},{5,197},{6,198},{7,199},{8... | collective-permute-start | bytes 1544 | tf_op jit(solution)/shard_map/ppermute | solution.py:35
  43.1 1.1 %shard_map.81.exchange_ref = f32[2,16]{1,0:T(2,128)S(1)} custom-call(f32[24,128]{1,0:T(8,128)S(1)} %add_add_fusion.y_ref, f32[1,1536]{1,0:T(1,128)S(1)} %reshape.19.c_ref, f32[32,1536]{1,0:T(8,128)S(1)} %get-tuple-element.16.rx_ref, bf16[2048,1536]{1,0:T(8,128)(2,1)S(1)} %bitcast.8), custom_call_target="tpu_custom_call" | custom-call | flops 805306368 | bytes 6291456 | tf_op jit(solution)/shard_map/pallas_call | solution.py:391
  44.2 1.1 %collective-permute-done.17.d_ref = f32[1,128]{1,0:T(1,128)S(1)} collective-permute-done((f32[1,128]{1,0:T(1,128)S(1)}, f32[1,128]{1,0:T(1,128)S(1)}, u32[]{:S(2)}, u32[]{:S(2)}) %collective-permute-start.17) | collective-permute-done | bytes 544 | tf_op jit(solution)/shard_map/ppermute | solution.py:35
  45.3 1.1 %collective-permute-done.18.h_ref = f32[1,128]{1,0:T(1,128)S(1)} collective-permute-done((f32[1,128]{1,0:T(1,128)S(1)}, f32[1,128]{1,0:T(1,128)S(1)}, u32[]{:S(2)}, u32[]{:S(2)}) %collective-permute-start.18) | collective-permute-done | bytes 544 | tf_op jit(solution)/shard_map/ppermute | solution.py:35
  46.5 0.6 %shard_map.82 = f32[2,16]{1,0:T(2,128)} custom-call(f32[1,16]{1,0:T(1,128)S(1)} %copy-done.1, f32[2,16]{1,0:T(2,128)S(1)} %bitcast.10, f32[2,16]{1,0:T(2,128)S(1)} %shard_map.81.exchange_ref, f32[2,128]{1,0:T(2,128)S(1)} %slice_add_fusion.near_ref, f32[1,128]{1,0:T(1,128)S(1)} %collective-permute-done.17.d_ref, f32[1,128]{1,0:T(1,128)S(1)} %collective-permute-done.18.h_ref), custom_call_target="tpu_custom_call" | custom-call | tf_op jit(solution)/shard_map/pallas_call | solution.py:341
  (18 shorter events, 0.1 us)
Async XLA Ops:
  0.0 18.1 %slice-start = ((s8[6291456]{0:T(1024)(128)(4,1)}), s8[2097152]{0:T(1024)(128)(4,1)S(1)}, s32[]{:S(2)}) async-start(s8[6291456]{0:T(1024)(128)(4,1)} %bitcast.4), calls=%async_computation | async-start | bytes 4194304
  1.1 17.0 %slice-start.1 = ((s8[6291456]{0:T(1024)(128)(4,1)}), s8[4194304]{0:T(1024)(128)(4,1)S(1)}, s32[]{:S(2)}) async-start(s8[6291456]{0:T(1024)(128)(4,1)} %bitcast.4), calls=%async_computation.1 | async-start | bytes 8388608
  1.1 7.8 %collective-permute-start.8 = (bf16[16,1152]{1,0:T(8,128)(2,1)S(1)}, bf16[16,1152]{1,0:T(8,128)(2,1)S(1)}, u32[]{:S(2)}, u32[]{:S(2)}) collective-permute-start(bf16[16,1152]{1,0:T(8,128)(2,1)S(1)} %shard_map.73.a0.refs_0_.refs_2_), channel_id=1, source_target_pairs={{0,64},{1,65},{2,66},{3,67},{4,68},{5,69},{6,70},{7,71},{8,72},{9,... | collective-permute-start | bytes 110600 | tf_op jit(solution)/shard_map/ppermute | solution.py:35
  3.4 9.7 %collective-permute-start = (bf16[16,1152]{1,0:T(8,128)(2,1)S(1)}, bf16[16,1152]{1,0:T(8,128)(2,1)S(1)}, u32[]{:S(2)}, u32[]{:S(2)}) collective-permute-start(bf16[16,1152]{1,0:T(8,128)(2,1)S(1)} %shard_map.73.a0.refs_0_.refs_2_), channel_id=1, source_target_pairs={{0,8},{1,9},{2,10},{3,11},{4,12},{5,13},{6,14},{7,15},{8,0},{9,1},... | collective-permute-start | bytes 110600 | tf_op jit(solution)/shard_map/ppermute | solution.py:35
  8.9 6.0 %collective-permute-start.1 = (bf16[16,1152]{1,0:T(8,128)(2,1)S(1)}, bf16[16,1152]{1,0:T(8,128)(2,1)S(1)}, u32[]{:S(2)}, u32[]{:S(2)}) collective-permute-start(bf16[16,1152]{1,0:T(8,128)(2,1)S(1)} %shard_map.73.a0.refs_0_.refs_2_), channel_id=1, source_target_pairs={{0,1},{1,0},{2,3},{3,2},{4,5},{5,4},{6,7},{7,6},{8,9},{9,8},{10,11... | collective-permute-start | bytes 110600 | tf_op jit(solution)/shard_map/ppermute | solution.py:35
  8.9 9.3 %collective-permute-start.10 = (bf16[16,1152]{1,0:T(8,128)(2,1)S(1)}, bf16[16,1152]{1,0:T(8,128)(2,1)S(1)}, u32[]{:S(2)}, u32[]{:S(2)}) collective-permute-start(bf16[16,1152]{1,0:T(8,128)(2,1)S(1)} %collective-permute-done.8.refs_2_.refs_4_), channel_id=1, source_target_pairs={{0,4},{1,5},{2,6},{3,7},{4,0},{5,1},{6,2},{7,3},{8,12},{9,13},{10,... | collective-permute-start | bytes 110600 | tf_op jit(solution)/shard_map/ppermute | solution.py:35
  12.1 6.1 %collective-permute-start.11 = (bf16[16,1152]{1,0:T(8,128)(2,1)S(1)}, bf16[16,1152]{1,0:T(8,128)(2,1)S(1)}, u32[]{:S(2)}, u32[]{:S(2)}) collective-permute-start(bf16[16,1152]{1,0:T(8,128)(2,1)S(1)} %collective-permute-done.8.refs_2_.refs_4_), channel_id=1, source_target_pairs={{0,6},{1,7},{2,4},{3,5},{4,2},{5,3},{6,0},{7,1},{8,14},{9,15},{10,... | collective-permute-start | bytes 110600 | tf_op jit(solution)/shard_map/ppermute | solution.py:35
  13.1 5.0 %collective-permute-start.9 = (bf16[16,1152]{1,0:T(8,128)(2,1)S(1)}, bf16[16,1152]{1,0:T(8,128)(2,1)S(1)}, u32[]{:S(2)}, u32[]{:S(2)}) collective-permute-start(bf16[16,1152]{1,0:T(8,128)(2,1)S(1)} %collective-permute-done.8.refs_2_.refs_4_), channel_id=1, source_target_pairs={{0,2},{1,3},{2,0},{3,1},{4,6},{5,7},{6,4},{7,5},{8,10},{9,11},{10,... | collective-permute-start | bytes 110600 | tf_op jit(solution)/shard_map/ppermute | solution.py:35
  13.1 1.8 %collective-permute-start.2 = (bf16[16,1152]{1,0:T(8,128)(2,1)S(1)}, bf16[16,1152]{1,0:T(8,128)(2,1)S(1)}, u32[]{:S(2)}, u32[]{:S(2)}) collective-permute-start(bf16[16,1152]{1,0:T(8,128)(2,1)S(1)} %collective-permute-done.a1.refs_0_), channel_id=1, source_target_pairs={{0,1},{1,0},{2,3},{3,2},{4,5},{5,4},{6,7},{7,6},{8,9},{9,8},{10,11... | collective-permute-start | bytes 110600 | tf_op jit(solution)/shard_map/ppermute | solution.py:35
  15.1 7.1 %collective-permute-start.3 = (f32[16,128]{1,0:T(8,128)S(1)}, f32[16,128]{1,0:T(8,128)S(1)}, u32[]{:S(2)}, u32[]{:S(2)}) collective-permute-start(f32[16,128]{1,0:T(8,128)S(1)} %shard_map.74.refs_8_), channel_id=1, source_target_pairs={{0,16},{1,17},{2,18},{3,19},{4,20},{5,21},{6,22},{7,23},{8,24},{9,... | collective-permute-start | bytes 24584 | tf_op jit(solution)/shard_map/ppermute | solution.py:35
  16.2 6.0 %collective-permute-start.4 = (f32[16,128]{1,0:T(8,128)S(1)}, f32[16,128]{1,0:T(8,128)S(1)}, u32[]{:S(2)}, u32[]{:S(2)}) collective-permute-start(f32[16,128]{1,0:T(8,128)S(1)} %shard_map.74.refs_8_), channel_id=1, source_target_pairs={{0,48},{1,33},{2,50},{3,35},{4,52},{5,37},{6,54},{7,39},{8,56},{9,... | collective-permute-start | bytes 24584 | tf_op jit(solution)/shard_map/ppermute | solution.py:35
  22.2 10.7 %copy-start.2 = (f32[1536]{0:T(1024)S(1)}, f32[1536]{0:T(1024)}, u32[]{:S(2)}) copy-start(f32[1536]{0:T(1024)} %param.12) | copy-start | bytes 18436
  22.2 8.6 %collective-permute-start.5 = (f32[16,128]{1,0:T(8,128)S(1)}, f32[16,128]{1,0:T(8,128)S(1)}, u32[]{:S(2)}, u32[]{:S(2)}) collective-permute-start(f32[16,128]{1,0:T(8,128)S(1)} %multiply_add_fusion.refs_9_.y0), channel_id=1, source_target_pairs={{0,128},{1,129},{2,130},{3,131},{4,132},{5,133},{6,134},{7,135},{8... | collective-permute-start | bytes 24584 | tf_op jit(solution)/shard_map/ppermute | solution.py:35
  24.8 6.1 %collective-permute-start.6 = (f32[16,128]{1,0:T(8,128)S(1)}, f32[16,128]{1,0:T(8,128)S(1)}, u32[]{:S(2)}, u32[]{:S(2)}) collective-permute-start(f32[16,128]{1,0:T(8,128)S(1)} %multiply_add_fusion.refs_9_.y0), channel_id=1, source_target_pairs={{0,64},{1,65},{2,66},{3,67},{4,68},{5,69},{6,70},{7,71},{8,72},{9,... | collective-permute-start | bytes 24584 | tf_op jit(solution)/shard_map/ppermute | solution.py:35
  24.8 6.1 %collective-permute-start.7 = (f32[16,128]{1,0:T(8,128)S(1)}, f32[16,128]{1,0:T(8,128)S(1)}, u32[]{:S(2)}, u32[]{:S(2)}) collective-permute-start(f32[16,128]{1,0:T(8,128)S(1)} %multiply_add_fusion.refs_9_.y0), channel_id=1, source_target_pairs={{0,192},{1,193},{2,194},{3,195},{4,196},{5,197},{6,198},{7,199},{8... | collective-permute-start | bytes 24584 | tf_op jit(solution)/shard_map/ppermute | solution.py:35
  30.8 15.6 %copy-start = (f32[1,2,16]{2,1,0:T(2,128)S(1)}, f32[1,2,16]{2,1,0:T(2,128)}, u32[]{:S(2)}) copy-start(f32[1,2,16]{2,1,0:T(2,128)} %param.8) | copy-start | bytes 388
  30.8 15.6 %copy-start.1 = (f32[1,16]{1,0:T(1,128)S(1)}, f32[1,16]{1,0:T(1,128)}, u32[]{:S(2)}) copy-start(f32[1,16]{1,0:T(1,128)} %energy_ref.1) | copy-start | bytes 196
  30.9 2.1 %collective-permute-start.12 = (f32[16,128]{1,0:T(8,128)S(1)}, f32[16,128]{1,0:T(8,128)S(1)}, u32[]{:S(2)}, u32[]{:S(2)}) collective-permute-start(f32[16,128]{1,0:T(8,128)S(1)} %shard_map.78.y0), channel_id=1, source_target_pairs={{0,1},{1,0},{2,3},{3,2},{4,5},{5,4},{6,7},{7,6},{8,9},{9,8},{10,11... | collective-permute-start | bytes 24584 | tf_op jit(solution)/shard_map/ppermute | solution.py:35
  32.4 5.3 %collective-permute-start.16 = (f32[2,128]{1,0:T(2,128)S(1)}, f32[2,128]{1,0:T(2,128)S(1)}, u32[]{:S(2)}, u32[]{:S(2)}) collective-permute-start(f32[2,128]{1,0:T(2,128)S(1)} %slice.17), channel_id=1, source_target_pairs={{0,1},{1,0},{2,3},{3,2},{4,5},{5,4},{6,7},{7,6},{8,9},{9,8},{10,11... | collective-permute-start | bytes 3080 | tf_op jit(solution)/shard_map/ppermute | solution.py:35
  33.0 8.2 %collective-permute-start.13 = (f32[24,128]{1,0:T(8,128)S(1)}, f32[24,128]{1,0:T(8,128)S(1)}, u32[]{:S(2)}, u32[]{:S(2)}) collective-permute-start(f32[24,128]{1,0:T(8,128)S(1)} %get-tuple-element.13), channel_id=1, source_target_pairs={{0,4},{1,5},{2,6},{3,7},{4,0},{5,1},{6,2},{7,3},{8,12},{9,13},{10,... | collective-permute-start | bytes 36872 | tf_op jit(solution)/shard_map/ppermute | solution.py:35
  36.7 4.5 %collective-permute-start.14 = (f32[24,128]{1,0:T(8,128)S(1)}, f32[24,128]{1,0:T(8,128)S(1)}, u32[]{:S(2)}, u32[]{:S(2)}) collective-permute-start(f32[24,128]{1,0:T(8,128)S(1)} %get-tuple-element.14), channel_id=1, source_target_pairs={{0,2},{1,3},{2,0},{3,1},{4,6},{5,7},{6,4},{7,5},{8,10},{9,11},{10,... | collective-permute-start | bytes 36872 | tf_op jit(solution)/shard_map/ppermute | solution.py:35
  36.7 4.9 %collective-permute-start.15 = (f32[24,128]{1,0:T(8,128)S(1)}, f32[24,128]{1,0:T(8,128)S(1)}, u32[]{:S(2)}, u32[]{:S(2)}) collective-permute-start(f32[24,128]{1,0:T(8,128)S(1)} %get-tuple-element.15), channel_id=1, source_target_pairs={{0,6},{1,7},{2,4},{3,5},{4,2},{5,3},{6,0},{7,1},{8,14},{9,15},{10,... | collective-permute-start | bytes 36872 | tf_op jit(solution)/shard_map/ppermute | solution.py:35
  37.8 7.5 %collective-permute-start.17 = (f32[1,128]{1,0:T(1,128)S(1)}, f32[1,128]{1,0:T(1,128)S(1)}, u32[]{:S(2)}, u32[]{:S(2)}) collective-permute-start(f32[1,128]{1,0:T(1,128)S(1)} %slice.14), channel_id=1, source_target_pairs={{0,8},{1,9},{2,10},{3,11},{4,12},{5,13},{6,14},{7,15},{8,0},{9,1},... | collective-permute-start | bytes 1544 | tf_op jit(solution)/shard_map/ppermute | solution.py:35
  41.6 4.8 %collective-permute-start.18 = (f32[1,128]{1,0:T(1,128)S(1)}, f32[1,128]{1,0:T(1,128)S(1)}, u32[]{:S(2)}, u32[]{:S(2)}) collective-permute-start(f32[1,128]{1,0:T(1,128)S(1)} %slice.18), channel_id=1, source_target_pairs={{0,192},{1,193},{2,194},{3,195},{4,196},{5,197},{6,198},{7,199},{8... | collective-permute-start | bytes 1544 | tf_op jit(solution)/shard_map/ppermute | solution.py:35

commit v10 on v9

--- a/solution.py
+++ b/solution.py
@@ -20,7 +20,7 @@
 ANY = pl.BlockSpec(memory_space=pl.ANY)
 
 
-def move(value, x=0, z=0, far=0, y=0, core=0, step=0, z_other=None):
+def move(value, x=0, z=0, far=0, y=0, core=0, step=0, other=(0, 0)):
     pairs = []
     for a in range(4):
         for b in range(4):
@@ -28,8 +28,8 @@
                 for d in range(4):
                     for e in range(2):
                         source = (a * 4 + b) * 16 + c * 8 + d * 2 + e
-                        turn = z_other if e and z_other is not None else z
-                        group = (((a + step) % 4) ^ x) * 4 + (b ^ turn)
+                        to_x, to_z = other if e and any(other) else (x, z)
+                        group = (((a + step) % 4) ^ to_x) * 4 + (b ^ to_z)
                         member = (c ^ far) * 8 + (d ^ y) * 2 + (e ^ core)
                         pairs.append((source, group * 16 + member))
     return lax.ppermute(value, ("grp", "kin"), pairs)
@@ -194,68 +194,58 @@
         acc_ref[...] = dot_t(ca[...], cb[...])
 
 
-def rows_kernel(far_ref, near_ref, *refs):
-    a_pays, b_pays, out_ref = refs[0:4], refs[4:8], refs[8]
+def rows_kernel(side, acc, *refs):
+    a_pays, b_pays, out_ref = refs[0:2], refs[2:6], refs[-1]
     half = 2 * ROWS
-    pick_row = iota((8, 16), 0)
-    pick_col = iota((8, 16), 1)
-
-    def lines(pays):
-        total = jnp.zeros((8, 128), F32)
-        for n, pay in enumerate(pays):
-            total += dot(onehot((pick_row == n) & (pick_col == 12)), pay[:, NMU:WIDTH])
-        return total.astype(BF16)
-
-    row = iota((ROWS, 8), 0)
-    col = iota((ROWS, 8), 1)
-    of_a = onehot(row >> 6 == col)
-    of_b = onehot((row >> 4) & 3 == col)
+
+    def line(pay):
+        return pay[:, NMU:WIDTH].astype(F32)[12:13]
+
+    from_a = jnp.concatenate([jnp.broadcast_to(line(pay), (64, 128)) for pay in a_pays], 0)
+    from_b = jnp.concatenate([jnp.broadcast_to(line(pay), (16, 128)) for pay in b_pays] * 2, 0)
     row = iota((ROWS, 128), 0)
     lane = iota((ROWS, 128), 1)
     same_c = lane & 3 == (row >> 2) & 3
     same_d = lane & 3 == row & 3
-    lane = iota((128, ROWS), 0)
-    col = iota((128, ROWS), 1)
-    by_w = (lane >> 2) & 3 == col & 3
-    by_v = (lane >> 2) & 3 == (col >> 2) & 3
-    first = lane >> 4 == 1
-    second = lane >> 4 == 2
-    spread_b = jnp.where(same_d, dot(of_b, lines(b_pays)), 0.0).astype(BF16)
-    xd_re = dot(spread_b, onehot(by_w & first))
-    xd_im = dot(spread_b, onehot(by_w & second))
-    to_re = onehot(by_v & first)
-    to_im = onehot(by_v & second)
+    from_a = jnp.where(same_c, from_a, 0.0).astype(BF16)
+    from_b = jnp.where(same_d, from_b, 0.0).astype(BF16)
+    lane = iota((128, half), 0)
+    col = iota((128, half), 1)
+    part = lane >> 4 == 1 + (col >> 7)
+    x_d = dot(from_b, onehot(part & ((lane >> 2) & 3 == col & 3)))
+    x_h = dot(from_a, onehot(part & ((lane >> 2) & 3 == (col >> 2) & 3)))
     pair = iota((ROWS, ROWS), 0) >> 4 == iota((ROWS, ROWS), 1) >> 4
-    lane = iota((ROWS, 128), 1)
-    col = iota((ROWS, 128), 0)
-    by_w = (lane >> 2) & 3 == col & 3
-    by_v = (lane >> 2) & 3 == (col >> 2) & 3
-    first = lane >> 4 == 0
-    second = lane >> 4 == 1
-    d_re, d_im = onehot(by_v & first), onehot(by_v & second)
-    h_re, h_im = onehot(by_w & first), onehot(by_w & second)
-    row = iota((16, ROWS), 0)
-    col = iota((16, ROWS), 1)
-    to_b = onehot(row == 8 + ((col >> 4) & 3))
-    total = jnp.zeros((16, 128), F32)
-    for side, acc in enumerate((far_ref, near_ref)):
-        spread_a = dot(of_a, lines(a_pays[2 * side : 2 * side + 2]))
-        spread_a = jnp.where(same_c, spread_a, 0.0).astype(BF16)
-        xh_re = dot(spread_a, to_re)
-        xh_im = dot(spread_a, to_im)
-        k_re = jnp.where(pair, acc[0:ROWS, 0:ROWS] + acc[ROWS:half, ROWS:half], 0.0)
-        k_im = jnp.where(pair, acc[0:ROWS, ROWS:half] - acc[ROWS:half, 0:ROWS], 0.0)
-        sum_d = dot_split(k_re * xd_re - k_im * xd_im, d_re) + dot_split(k_re * xd_im + k_im * xd_re, d_im)
-        sum_h = dot_split(k_re * xh_re + k_im * xh_im, h_re) + dot_split(k_re * xh_im - k_im * xh_re, h_im)
-        high_d, low_d = split(jnp.where(same_c, sum_d, 0.0))
-        high_h, low_h = split(jnp.where(same_d, sum_h, 0.0))
-        to_a = onehot(row == side + 2 * (col >> 6))
-        total += dot(to_a, high_d) + dot(to_a, low_d) + dot(to_b, high_h) + dot(to_b, low_h)
+    k_re = jnp.where(pair, acc[0:ROWS, 0:ROWS] + acc[ROWS:half, ROWS:half], 0.0)
+    k_im = jnp.where(pair, acc[0:ROWS, ROWS:half] - acc[ROWS:half, 0:ROWS], 0.0)
+    row = iota((half, 128), 0)
+    lane = iota((half, 128), 1)
+    part = lane >> 4 == row >> 7
+
+    def fold(real, imag, picked, kept):
+        high, low = split(jnp.concatenate([real, imag], 1))
+        both = dot(jnp.concatenate([high, low], 0), onehot(part & picked))
+        return split(jnp.where(kept, both[0:ROWS] + both[ROWS:half], 0.0))
+
+    re, im = x_d[:, 0:ROWS], x_d[:, ROWS:half]
+    terms = fold(k_re * re - k_im * im, k_re * im + k_im * re, (lane >> 2) & 3 == (row >> 2) & 3, same_c)
+    re, im = x_h[:, 0:ROWS], x_h[:, ROWS:half]
+    terms += fold(k_re * re + k_im * im, k_re * im - k_im * re, (lane >> 2) & 3 == row & 3, same_d)
+    row = iota((16, 4 * ROWS), 0)
+    col = iota((16, 4 * ROWS), 1)
+    to_a = (col < half) & (row == side + 2 * ((col >> 6) & 1))
+    to_b = (col >= half) & (row == 8 + ((col >> 4) & 3))
+    total = dot(onehot(to_a | to_b), jnp.concatenate(terms, 0))
+    if side:
+        total += refs[6][...]
     out_ref[...] = total
 
 
-def sum_kernel(y0, y1, y2, y3, _, out_ref):
-    out_ref[...] = y0[...] + y1[...] + y2[...] + y3[...]
+def join_kernel(y0, y1, _, out_ref):
+    out_ref[...] = y0[...] + y1[...]
+
+
+def half_kernel(y0, y1, y2, _, out_ref):
+    out_ref[...] = 0.5 * (y0[...] + y1[...]) + y2[...]
 
 
 def mail_kernel(y0, y1, rows_ref, *mails):
@@ -380,12 +370,15 @@
     )(pay, a1, a2, a3)
     b_pays = (b0, b1, b2, b3)
     (far_acc,) = pair_call(0, (a1, a3, *b_pays, weights, z, y))
-    y = 0.5 * (y + move(y, z=1)) + move(y, z=3, z_other=2)
-    near_acc, rx = pair_call(1, (pay, a2, *b_pays, weights, z, far_acc, y))
-    (y,) = small_call(sum_kernel, [(16, 128)], y, *(move(y, x=n) for n in (2, 1, 3)), after=(near_acc,))
-    other = move(y, core=1)
-    (rows,) = small_call(rows_kernel, [(16, 128)], far_acc, near_acc, a1, a3, pay, a2, *b_pays)
-    mails = small_call(mail_kernel, [(24, 128)] * 4, y, other, rows)
+    (y,) = small_call(half_kernel, [(16, 128)], y, move(y, z=1), move(y, z=3, other=(0, 2)), after=(far_acc,))
+    swapped = move(y, core=1)
+    (far_rows,) = small_call(functools.partial(rows_kernel, 0), [(16, 128)], far_acc, a1, a3, *b_pays)
+    (y,) = small_call(join_kernel, [(16, 128)], y, swapped, after=(far_rows,))
+    near_acc, rx = pair_call(1, (pay, a2, *b_pays, weights, z, far_rows, y))
+    (y,) = small_call(half_kernel, [(16, 128)], y, move(y, x=1), move(y, x=3, other=(2, 0)), after=(near_acc,))
+    swapped = move(y, core=1)
+    (rows,) = small_call(functools.partial(rows_kernel, 1), [(16, 128)], near_acc, pay, a2, *b_pays, far_rows)
+    mails = small_call(mail_kernel, [(24, 128)] * 4, y, swapped, rows)
     mail = mails[0] + move(mails[2], y=2) + move(mails[1], y=1) + move(mails[3], y=3)
     rows = rows[0:2] + move(rows[2:4], core=1)
     exchange = pl.pallas_call(

time: 47.3 us -> 46.9 us (level)
  waiting for transfers between devices: 2.71 us -> 5.67 us
  starting transfers between devices: 29.6 us -> 26.8 us
  Pallas kernels: 14.5 us -> 14 us
    ppermute x19, waiting for transfers between devices: 2.71 us -> 5.67 us  [move(): return lax.ppermute(value, ('grp', 'kin'), pairs)]
    ppermute x19, starting transfers between devices: 29.6 us -> 26.8 us  [move(): return lax.ppermute(value, ('grp', 'kin'), pairs)]
    pallas_call x4 -> x7, Pallas kernels: 2.1 us -> 1.66 us  [small_call(): pl.pallas_call(kernel, in_specs=[VMEM] * len(operands) + [ANY] * len(afte...]
  transfers between devices with their start and end apart: 19 -> 19, of which waited for: 3 -> 5; matrix products, arithmetic and copies ran while one was open for 0% -> 0% of each run, Pallas kernels for 27% -> 26%
where the time goes in v10:
time: 46.9 us; the launch traced here: 46.8 us
  starting transfers between devices  26.8 us (57%)
  Pallas kernels  14 us (30%)
  waiting for transfers between devices  5.67 us (12%)
    ppermute x19, starting transfers between devices, move(): return lax.ppermute(value, ('grp', 'kin'), pairs)  26.8 us
    pallas_call x2, Pallas kernels, pair_call(): pl.pallas_call(functools.partial(pair_kernel, near), in_specs=[VMEM] * 8...  8.29 us
    ppermute x19, waiting for transfers between devices, move(): return lax.ppermute(value, ('grp', 'kin'), pairs)  5.67 us
    pallas_call x1, Pallas kernels, on_device(): pl.pallas_call(weights_kernel, in_specs=[SMEM, ANY], out_specs=VMEM, out_...  1.74 us
    pallas_call x7, Pallas kernels, small_call(): pl.pallas_call(kernel, in_specs=[VMEM] * len(operands) + [ANY] * len(afte...  1.66 us
    pallas_call x1, Pallas kernels, on_device(): pl.pallas_call(pack_kernel, in_specs=[ANY] * 2, out_specs=VMEM, out_shape...  1.1 us
    pallas_call x1, Pallas kernels, on_device(): pl.pallas_call(exchange_kernel, in_specs=[VMEM] * 4, out_specs=VMEM, out_...  1.06 us
  transfers between devices with their start and end apart: 19, of which 5 were waited for; matrix products, arithmetic and copies ran while one was open for 0% of the time, Pallas kernels for 26%

profile of v10, /device:TPU:6, one launch (start us, length us, event | category | flops | bytes accessed | tf_op | source)
XLA Modules:
  0.0 46.8 jit_solution(15592027116292951514)
XLA Ops:
  0.0 1.1 %shard_map.73.a0.refs_0_ = bf16[16,1152]{1,0:T(8,128)(2,1)S(1)} custom-call(bf16[16,1024]{1,0:T(8,128)(2,1)} %bitcast.11, f32[2,16]{1,0:T(2,128)} %bitcast.9), custom_call_target="tpu_custom_call" | custom-call | tf_op jit(solution)/shard_map/pallas_call | solution.py:341
  1.1 0.0 slice-start.1
  1.1 2.3 %collective-permute-start.5 = (bf16[16,1152]{1,0:T(8,128)(2,1)S(1)}, bf16[16,1152]{1,0:T(8,128)(2,1)S(1)}, u32[]{:S(2)}, u32[]{:S(2)}) collective-permute-start(bf16[16,1152]{1,0:T(8,128)(2,1)S(1)} %shard_map.73.a0.refs_0_), channel_id=1, source_target_pairs={{0,64},{1,65},{2,66},{3,67},{4,68},{5,69},{6,70},{7,71},{8,72},{9,... | collective-permute-start | bytes 110600 | tf_op jit(solution)/shard_map/ppermute | solution.py:35
  3.4 5.5 %collective-permute-start = (bf16[16,1152]{1,0:T(8,128)(2,1)S(1)}, bf16[16,1152]{1,0:T(8,128)(2,1)S(1)}, u32[]{:S(2)}, u32[]{:S(2)}) collective-permute-start(bf16[16,1152]{1,0:T(8,128)(2,1)S(1)} %shard_map.73.a0.refs_0_), channel_id=1, source_target_pairs={{0,8},{1,9},{2,10},{3,11},{4,12},{5,13},{6,14},{7,15},{8,0},{9,1},... | collective-permute-start | bytes 110600 | tf_op jit(solution)/shard_map/ppermute | solution.py:35
  8.9 0.0 collective-permute-start.1
  8.9 0.0 collective-permute-done.5.refs_2_
  8.9 1.6 %collective-permute-start.6 = (bf16[16,1152]{1,0:T(8,128)(2,1)S(1)}, bf16[16,1152]{1,0:T(8,128)(2,1)S(1)}, u32[]{:S(2)}, u32[]{:S(2)}) collective-permute-start(bf16[16,1152]{1,0:T(8,128)(2,1)S(1)} %collective-permute-done.5.refs_2_), channel_id=1, source_target_pairs={{0,2},{1,3},{2,0},{3,1},{4,6},{5,7},{6,4},{7,5},{8,10},{9,11},{10,... | collective-permute-start | bytes 110600 | tf_op jit(solution)/shard_map/ppermute | solution.py:35
  10.4 2.9 %collective-permute-start.7 = (bf16[16,1152]{1,0:T(8,128)(2,1)S(1)}, bf16[16,1152]{1,0:T(8,128)(2,1)S(1)}, u32[]{:S(2)}, u32[]{:S(2)}) collective-permute-start(bf16[16,1152]{1,0:T(8,128)(2,1)S(1)} %collective-permute-done.5.refs_2_), channel_id=1, source_target_pairs={{0,4},{1,5},{2,6},{3,7},{4,0},{5,1},{6,2},{7,3},{8,12},{9,13},{10,... | collective-permute-start | bytes 110600 | tf_op jit(solution)/shard_map/ppermute | solution.py:35
  13.3 0.2 collective-permute-start.8
  13.6 0.0 collective-permute-done.a1.refs_0_
  13.6 0.0 collective-permute-start.2
  13.6 1.7 %shard_map.75.refs_6_ = f32[16,1536]{1,0:T(8,128)S(1)} custom-call(s32[1,256]{1,0:T(1,128)} %qmap_ref.1, f32[256,1536]{1,0:T(8,128)} %screening.1), custom_call_target="tpu_custom_call" | custom-call | flops 4000000000 | bytes 1024 | tf_op jit(solution)/shard_map/pallas_call | solution.py:353
  15.3 0.0 collective-permute-done.1.a2.refs_1_
  15.3 0.0 collective-permute-done.2.a3.refs_1_
  15.3 0.2 shard_map.74.refs_8_.y0
  15.5 1.1 %collective-permute-start.3 = (f32[16,128]{1,0:T(8,128)S(1)}, f32[16,128]{1,0:T(8,128)S(1)}, u32[]{:S(2)}, u32[]{:S(2)}) collective-permute-start(f32[16,128]{1,0:T(8,128)S(1)} %shard_map.74.refs_8_.y0), channel_id=1, source_target_pairs={{0,16},{1,17},{2,18},{3,19},{4,20},{5,21},{6,22},{7,23},{8,24},{9,... | collective-permute-start | bytes 24584 | tf_op jit(solution)/shard_map/ppermute | solution.py:35
  16.6 1.9 %collective-permute-start.4 = (f32[16,128]{1,0:T(8,128)S(1)}, f32[16,128]{1,0:T(8,128)S(1)}, u32[]{:S(2)}, u32[]{:S(2)}) collective-permute-start(f32[16,128]{1,0:T(8,128)S(1)} %shard_map.74.refs_8_.y0), channel_id=1, source_target_pairs={{0,48},{1,33},{2,50},{3,35},{4,52},{5,37},{6,54},{7,39},{8,56},{9,... | collective-permute-start | bytes 24584 | tf_op jit(solution)/shard_map/ppermute | solution.py:35
  18.6 0.0 collective-permute-done.6.refs_3_
  18.6 0.0 collective-permute-done.7.refs_4_
  18.6 0.0 collective-permute-done.8.refs_5_
  18.6 4.0 %shard_map.76._.acc = f32[256,256]{1,0:T(8,128)S(1)} custom-call(bf16[16,1152]{1,0:T(8,128)(2,1)S(1)} %collective-permute-done.a1.refs_0_, bf16[16,1152]{1,0:T(8,128)(2,1)S(1)} %collective-permute-done.2.a3.refs_1_, bf16[16,1152]{1,0:T(8,128)(2,1)S(1)} %collective-permute-done.5.refs_2_, bf16[16,1152]{1,0:T(8,128)(2,1)S(1)} %collective-permute-done.6.refs_3_, ...), custom_call_target="tpu_custom_call" | custom-call | flops 3221225472 | bytes 6291456 | tf_op jit(solution)/shard_map/pallas_call | solution.py:313
  22.6 0.0 collective-permute-done.3.y1
  22.6 0.0 collective-permute-done.4.y2
  22.7 0.1 collective-permute-start.9
  22.8 0.5 %shard_map.78._.refs_8_.refs_6_ = f32[16,128]{1,0:T(8,128)S(1)} custom-call(f32[256,256]{1,0:T(8,128)S(1)} %shard_map.76._.acc, bf16[16,1152]{1,0:T(8,128)(2,1)S(1)} %collective-permute-done.a1.refs_0_, bf16[16,1152]{1,0:T(8,128)(2,1)S(1)} %collective-permute-done.2.a3.refs_1_, bf16[16,1152]{1,0:T(8,128)(2,1)S(1)} %collective-permute-done.5.refs_2_, ...), custom_call_target="tpu_custom_call" | custom-call | tf_op jit(solution)/shard_map/pallas_call | solution.py:331
  23.3 0.7 %collective-permute-done.9.y1 = f32[16,128]{1,0:T(8,128)S(1)} collective-permute-done((f32[16,128]{1,0:T(8,128)S(1)}, f32[16,128]{1,0:T(8,128)S(1)}, u32[]{:S(2)}, u32[]{:S(2)}) %collective-permute-start.9) | collective-permute-done | bytes 8224 | tf_op jit(solution)/shard_map/ppermute | solution.py:35
  23.9 1.6 %collective-permute-start.10 = (f32[16,128]{1,0:T(8,128)S(1)}, f32[16,128]{1,0:T(8,128)S(1)}, u32[]{:S(2)}, u32[]{:S(2)}) collective-permute-start(f32[16,128]{1,0:T(8,128)S(1)} %shard_map.79.refs_9_.y0), channel_id=1, source_target_pairs={{0,64},{1,65},{2,66},{3,67},{4,68},{5,69},{6,70},{7,71},{8,72},{9,... | collective-permute-start | bytes 24584 | tf_op jit(solution)/shard_map/ppermute | solution.py:35
  25.5 1.4 %collective-permute-start.11 = (f32[16,128]{1,0:T(8,128)S(1)}, f32[16,128]{1,0:T(8,128)S(1)}, u32[]{:S(2)}, u32[]{:S(2)}) collective-permute-start(f32[16,128]{1,0:T(8,128)S(1)} %shard_map.79.refs_9_.y0), channel_id=1, source_target_pairs={{0,192},{1,129},{2,194},{3,131},{4,196},{5,133},{6,198},{7,135},{8... | collective-permute-start | bytes 24584 | tf_op jit(solution)/shard_map/ppermute | solution.py:35
  26.9 4.3 %shard_map.80 = (f32[256,256]{1,0:T(8,128)S(1)}, f32[32,1536]{1,0:T(8,128)S(1)}) custom-call(bf16[16,1152]{1,0:T(8,128)(2,1)S(1)} %shard_map.73.a0.refs_0_, bf16[16,1152]{1,0:T(8,128)(2,1)S(1)} %collective-permute-done.1.a2.refs_1_, bf16[16,1152]{1,0:T(8,128)(2,1)S(1)} %collective-permute-done.5.refs_2_, ...), custom_call_target="tpu_custom_call" | custom-call | flops 3221225472 | bytes 6291456 | tf_op jit(solution)/shard_map/pallas_call | solution.py:313
  31.2 0.0 copy-start
  31.2 0.0 copy-start.1
  31.2 0.0 collective-permute-done.11.y2
  31.3 0.1 collective-permute-start.12
  31.4 0.5 %shard_map.82.rows_ref = f32[16,128]{1,0:T(8,128)S(1)} custom-call(f32[256,256]{1,0:T(8,128)S(1)} %get-tuple-element.11._.acc, bf16[16,1152]{1,0:T(8,128)(2,1)S(1)} %shard_map.73.a0.refs_0_, bf16[16,1152]{1,0:T(8,128)(2,1)S(1)} %collective-permute-done.1.a2.refs_1_, bf16[16,1152]{1,0:T(8,128)(2,1)S(1)} %collective-permute-done.5.refs_2_, ...), custom_call_target="tpu_custom_call" | custom-call | tf_op jit(solution)/shard_map/pallas_call | solution.py:331
  31.9 0.5 %collective-permute-start.16 = (f32[2,128]{1,0:T(2,128)S(1)}, f32[2,128]{1,0:T(2,128)S(1)}, u32[]{:S(2)}, u32[]{:S(2)}) collective-permute-start(f32[2,128]{1,0:T(2,128)S(1)} %slice.17), channel_id=1, source_target_pairs={{0,1},{1,0},{2,3},{3,2},{4,5},{5,4},{6,7},{7,6},{8,9},{9,8},{10,11... | collective-permute-start | bytes 3080 | tf_op jit(solution)/shard_map/ppermute | solution.py:35
  32.4 0.1 collective-permute-done.12.y1
  32.5 2.0 %collective-permute-start.13 = (f32[24,128]{1,0:T(8,128)S(1)}, f32[24,128]{1,0:T(8,128)S(1)}, u32[]{:S(2)}, u32[]{:S(2)}) collective-permute-start(f32[24,128]{1,0:T(8,128)S(1)} %get-tuple-element.13), channel_id=1, source_target_pairs={{0,4},{1,5},{2,6},{3,7},{4,0},{5,1},{6,2},{7,3},{8,12},{9,13},{10,... | collective-permute-start | bytes 36872 | tf_op jit(solution)/shard_map/ppermute | solution.py:35
  34.5 1.9 %collective-permute-start.14 = (f32[24,128]{1,0:T(8,128)S(1)}, f32[24,128]{1,0:T(8,128)S(1)}, u32[]{:S(2)}, u32[]{:S(2)}) collective-permute-start(f32[24,128]{1,0:T(8,128)S(1)} %get-tuple-element.14), channel_id=1, source_target_pairs={{0,2},{1,3},{2,0},{3,1},{4,6},{5,7},{6,4},{7,5},{8,10},{9,11},{10,... | collective-permute-start | bytes 36872 | tf_op jit(solution)/shard_map/ppermute | solution.py:35
  36.4 0.2 collective-permute-start.15
  36.6 3.4 %collective-permute-start.17 = (f32[1,128]{1,0:T(1,128)S(1)}, f32[1,128]{1,0:T(1,128)S(1)}, u32[]{:S(2)}, u32[]{:S(2)}) collective-permute-start(f32[1,128]{1,0:T(1,128)S(1)} %slice.14), channel_id=1, source_target_pairs={{0,8},{1,9},{2,10},{3,11},{4,12},{5,13},{6,14},{7,15},{8,0},{9,1},... | collective-permute-start | bytes 1544 | tf_op jit(solution)/shard_map/ppermute | solution.py:35
  40.0 0.0 collective-permute-done.13
  40.1 0.0 collective-permute-done.14
  40.1 1.3 %collective-permute-done.15 = f32[24,128]{1,0:T(8,128)S(1)} collective-permute-done((f32[24,128]{1,0:T(8,128)S(1)}, f32[24,128]{1,0:T(8,128)S(1)}, u32[]{:S(2)}, u32[]{:S(2)}) %collective-permute-start.15) | collective-permute-done | bytes 12320 | tf_op jit(solution)/shard_map/ppermute | solution.py:35
  41.3 0.2 collective-permute-start.18
  41.5 1.1 %shard_map.84.exchange_ref = f32[2,16]{1,0:T(2,128)S(1)} custom-call(f32[24,128]{1,0:T(8,128)S(1)} %add_add_fusion.y_ref, f32[1,1536]{1,0:T(1,128)S(1)} %reshape.19.c_ref, f32[32,1536]{1,0:T(8,128)S(1)} %get-tuple-element.16.rx_ref, bf16[2048,1536]{1,0:T(8,128)(2,1)S(1)} %bitcast.8), custom_call_target="tpu_custom_call" | custom-call | flops 805306368 | bytes 6291456 | tf_op jit(solution)/shard_map/pallas_call | solution.py:384
  42.5 1.6 %collective-permute-done.17.d_ref = f32[1,128]{1,0:T(1,128)S(1)} collective-permute-done((f32[1,128]{1,0:T(1,128)S(1)}, f32[1,128]{1,0:T(1,128)S(1)}, u32[]{:S(2)}, u32[]{:S(2)}) %collective-permute-start.17) | collective-permute-done | bytes 544 | tf_op jit(solution)/shard_map/ppermute | solution.py:35
  44.2 2.0 %collective-permute-done.18.h_ref = f32[1,128]{1,0:T(1,128)S(1)} collective-permute-done((f32[1,128]{1,0:T(1,128)S(1)}, f32[1,128]{1,0:T(1,128)S(1)}, u32[]{:S(2)}, u32[]{:S(2)}) %collective-permute-start.18) | collective-permute-done | bytes 544 | tf_op jit(solution)/shard_map/ppermute | solution.py:35
  46.2 0.6 %shard_map.85 = f32[2,16]{1,0:T(2,128)} custom-call(f32[1,16]{1,0:T(1,128)S(1)} %copy-done.1, f32[2,16]{1,0:T(2,128)S(1)} %bitcast.10, f32[2,16]{1,0:T(2,128)S(1)} %shard_map.84.exchange_ref, f32[2,128]{1,0:T(2,128)S(1)} %slice_add_fusion.near_ref, f32[1,128]{1,0:T(1,128)S(1)} %collective-permute-done.17.d_ref, f32[1,128]{1,0:T(1,128)S(1)} %collective-permute-done.18.h_ref), custom_call_target="tpu_custom_call" | custom-call | tf_op jit(solution)/shard_map/pallas_call | solution.py:331
  (20 shorter events, 0.1 us)
Async XLA Ops:
  0.0 18.6 %slice-start = ((s8[6291456]{0:T(1024)(128)(4,1)}), s8[2097152]{0:T(1024)(128)(4,1)S(1)}, s32[]{:S(2)}) async-start(s8[6291456]{0:T(1024)(128)(4,1)} %bitcast.4), calls=%async_computation | async-start | bytes 4194304
  1.1 17.5 %slice-start.1 = ((s8[6291456]{0:T(1024)(128)(4,1)}), s8[4194304]{0:T(1024)(128)(4,1)S(1)}, s32[]{:S(2)}) async-start(s8[6291456]{0:T(1024)(128)(4,1)} %bitcast.4), calls=%async_computation.1 | async-start | bytes 8388608
  1.1 7.8 %collective-permute-start.5 = (bf16[16,1152]{1,0:T(8,128)(2,1)S(1)}, bf16[16,1152]{1,0:T(8,128)(2,1)S(1)}, u32[]{:S(2)}, u32[]{:S(2)}) collective-permute-start(bf16[16,1152]{1,0:T(8,128)(2,1)S(1)} %shard_map.73.a0.refs_0_), channel_id=1, source_target_pairs={{0,64},{1,65},{2,66},{3,67},{4,68},{5,69},{6,70},{7,71},{8,72},{9,... | collective-permute-start | bytes 110600 | tf_op jit(solution)/shard_map/ppermute | solution.py:35
  3.4 10.2 %collective-permute-start = (bf16[16,1152]{1,0:T(8,128)(2,1)S(1)}, bf16[16,1152]{1,0:T(8,128)(2,1)S(1)}, u32[]{:S(2)}, u32[]{:S(2)}) collective-permute-start(bf16[16,1152]{1,0:T(8,128)(2,1)S(1)} %shard_map.73.a0.refs_0_), channel_id=1, source_target_pairs={{0,8},{1,9},{2,10},{3,11},{4,12},{5,13},{6,14},{7,15},{8,0},{9,1},... | collective-permute-start | bytes 110600 | tf_op jit(solution)/shard_map/ppermute | solution.py:35
  8.9 6.5 %collective-permute-start.1 = (bf16[16,1152]{1,0:T(8,128)(2,1)S(1)}, bf16[16,1152]{1,0:T(8,128)(2,1)S(1)}, u32[]{:S(2)}, u32[]{:S(2)}) collective-permute-start(bf16[16,1152]{1,0:T(8,128)(2,1)S(1)} %shard_map.73.a0.refs_0_), channel_id=1, source_target_pairs={{0,1},{1,0},{2,3},{3,2},{4,5},{5,4},{6,7},{7,6},{8,9},{9,8},{10,11... | collective-permute-start | bytes 110600 | tf_op jit(solution)/shard_map/ppermute | solution.py:35
  8.9 9.7 %collective-permute-start.6 = (bf16[16,1152]{1,0:T(8,128)(2,1)S(1)}, bf16[16,1152]{1,0:T(8,128)(2,1)S(1)}, u32[]{:S(2)}, u32[]{:S(2)}) collective-permute-start(bf16[16,1152]{1,0:T(8,128)(2,1)S(1)} %collective-permute-done.5.refs_2_), channel_id=1, source_target_pairs={{0,2},{1,3},{2,0},{3,1},{4,6},{5,7},{6,4},{7,5},{8,10},{9,11},{10,... | collective-permute-start | bytes 110600 | tf_op jit(solution)/shard_map/ppermute | solution.py:35
  10.4 8.1 %collective-permute-start.7 = (bf16[16,1152]{1,0:T(8,128)(2,1)S(1)}, bf16[16,1152]{1,0:T(8,128)(2,1)S(1)}, u32[]{:S(2)}, u32[]{:S(2)}) collective-permute-start(bf16[16,1152]{1,0:T(8,128)(2,1)S(1)} %collective-permute-done.5.refs_2_), channel_id=1, source_target_pairs={{0,4},{1,5},{2,6},{3,7},{4,0},{5,1},{6,2},{7,3},{8,12},{9,13},{10,... | collective-permute-start | bytes 110600 | tf_op jit(solution)/shard_map/ppermute | solution.py:35
  13.3 5.2 %collective-permute-start.8 = (bf16[16,1152]{1,0:T(8,128)(2,1)S(1)}, bf16[16,1152]{1,0:T(8,128)(2,1)S(1)}, u32[]{:S(2)}, u32[]{:S(2)}) collective-permute-start(bf16[16,1152]{1,0:T(8,128)(2,1)S(1)} %collective-permute-done.5.refs_2_), channel_id=1, source_target_pairs={{0,6},{1,7},{2,4},{3,5},{4,2},{5,3},{6,0},{7,1},{8,14},{9,15},{10,... | collective-permute-start | bytes 110600 | tf_op jit(solution)/shard_map/ppermute | solution.py:35
  13.6 1.8 %collective-permute-start.2 = (bf16[16,1152]{1,0:T(8,128)(2,1)S(1)}, bf16[16,1152]{1,0:T(8,128)(2,1)S(1)}, u32[]{:S(2)}, u32[]{:S(2)}) collective-permute-start(bf16[16,1152]{1,0:T(8,128)(2,1)S(1)} %collective-permute-done.a1.refs_0_), channel_id=1, source_target_pairs={{0,1},{1,0},{2,3},{3,2},{4,5},{5,4},{6,7},{7,6},{8,9},{9,8},{10,11... | collective-permute-start | bytes 110600 | tf_op jit(solution)/shard_map/ppermute | solution.py:35
  15.5 7.1 %collective-permute-start.3 = (f32[16,128]{1,0:T(8,128)S(1)}, f32[16,128]{1,0:T(8,128)S(1)}, u32[]{:S(2)}, u32[]{:S(2)}) collective-permute-start(f32[16,128]{1,0:T(8,128)S(1)} %shard_map.74.refs_8_.y0), channel_id=1, source_target_pairs={{0,16},{1,17},{2,18},{3,19},{4,20},{5,21},{6,22},{7,23},{8,24},{9,... | collective-permute-start | bytes 24584 | tf_op jit(solution)/shard_map/ppermute | solution.py:35
  16.6 6.0 %collective-permute-start.4 = (f32[16,128]{1,0:T(8,128)S(1)}, f32[16,128]{1,0:T(8,128)S(1)}, u32[]{:S(2)}, u32[]{:S(2)}) collective-permute-start(f32[16,128]{1,0:T(8,128)S(1)} %shard_map.74.refs_8_.y0), channel_id=1, source_target_pairs={{0,48},{1,33},{2,50},{3,35},{4,52},{5,37},{6,54},{7,39},{8,56},{9,... | collective-permute-start | bytes 24584 | tf_op jit(solution)/shard_map/ppermute | solution.py:35
  22.7 1.3 %collective-permute-start.9 = (f32[16,128]{1,0:T(8,128)S(1)}, f32[16,128]{1,0:T(8,128)S(1)}, u32[]{:S(2)}, u32[]{:S(2)}) collective-permute-start(f32[16,128]{1,0:T(8,128)S(1)} %shard_map.77.y0), channel_id=1, source_target_pairs={{0,1},{1,0},{2,3},{3,2},{4,5},{5,4},{6,7},{7,6},{8,9},{9,8},{10,11... | collective-permute-start | bytes 24584 | tf_op jit(solution)/shard_map/ppermute | solution.py:35
  23.9 8.5 %copy-start.2 = (f32[1536]{0:T(1024)S(1)}, f32[1536]{0:T(1024)}, u32[]{:S(2)}) copy-start(f32[1536]{0:T(1024)} %param.12) | copy-start | bytes 18436
  23.9 7.3 %collective-permute-start.10 = (f32[16,128]{1,0:T(8,128)S(1)}, f32[16,128]{1,0:T(8,128)S(1)}, u32[]{:S(2)}, u32[]{:S(2)}) collective-permute-start(f32[16,128]{1,0:T(8,128)S(1)} %shard_map.79.refs_9_.y0), channel_id=1, source_target_pairs={{0,64},{1,65},{2,66},{3,67},{4,68},{5,69},{6,70},{7,71},{8,72},{9,... | collective-permute-start | bytes 24584 | tf_op jit(solution)/shard_map/ppermute | solution.py:35
  25.5 5.7 %collective-permute-start.11 = (f32[16,128]{1,0:T(8,128)S(1)}, f32[16,128]{1,0:T(8,128)S(1)}, u32[]{:S(2)}, u32[]{:S(2)}) collective-permute-start(f32[16,128]{1,0:T(8,128)S(1)} %shard_map.79.refs_9_.y0), channel_id=1, source_target_pairs={{0,192},{1,129},{2,194},{3,131},{4,196},{5,133},{6,198},{7,135},{8... | collective-permute-start | bytes 24584 | tf_op jit(solution)/shard_map/ppermute | solution.py:35
  31.2 15.0 %copy-start = (f32[1,2,16]{2,1,0:T(2,128)S(1)}, f32[1,2,16]{2,1,0:T(2,128)}, u32[]{:S(2)}) copy-start(f32[1,2,16]{2,1,0:T(2,128)} %param.8) | copy-start | bytes 388
  31.2 14.9 %copy-start.1 = (f32[1,16]{1,0:T(1,128)S(1)}, f32[1,16]{1,0:T(1,128)}, u32[]{:S(2)}) copy-start(f32[1,16]{1,0:T(1,128)} %energy_ref.1) | copy-start | bytes 196
  31.3 1.3 %collective-permute-start.12 = (f32[16,128]{1,0:T(8,128)S(1)}, f32[16,128]{1,0:T(8,128)S(1)}, u32[]{:S(2)}, u32[]{:S(2)}) collective-permute-start(f32[16,128]{1,0:T(8,128)S(1)} %shard_map.81.y0), channel_id=1, source_target_pairs={{0,1},{1,0},{2,3},{3,2},{4,5},{5,4},{6,7},{7,6},{8,9},{9,8},{10,11... | collective-permute-start | bytes 24584 | tf_op jit(solution)/shard_map/ppermute | solution.py:35
  31.9 4.8 %collective-permute-start.16 = (f32[2,128]{1,0:T(2,128)S(1)}, f32[2,128]{1,0:T(2,128)S(1)}, u32[]{:S(2)}, u32[]{:S(2)}) collective-permute-start(f32[2,128]{1,0:T(2,128)S(1)} %slice.17), channel_id=1, source_target_pairs={{0,1},{1,0},{2,3},{3,2},{4,5},{5,4},{6,7},{7,6},{8,9},{9,8},{10,11... | collective-permute-start | bytes 3080 | tf_op jit(solution)/shard_map/ppermute | solution.py:35
  32.5 7.5 %collective-permute-start.13 = (f32[24,128]{1,0:T(8,128)S(1)}, f32[24,128]{1,0:T(8,128)S(1)}, u32[]{:S(2)}, u32[]{:S(2)}) collective-permute-start(f32[24,128]{1,0:T(8,128)S(1)} %get-tuple-element.13), channel_id=1, source_target_pairs={{0,4},{1,5},{2,6},{3,7},{4,0},{5,1},{6,2},{7,3},{8,12},{9,13},{10,... | collective-permute-start | bytes 36872 | tf_op jit(solution)/shard_map/ppermute | solution.py:35
  34.5 5.5 %collective-permute-start.14 = (f32[24,128]{1,0:T(8,128)S(1)}, f32[24,128]{1,0:T(8,128)S(1)}, u32[]{:S(2)}, u32[]{:S(2)}) collective-permute-start(f32[24,128]{1,0:T(8,128)S(1)} %get-tuple-element.14), channel_id=1, source_target_pairs={{0,2},{1,3},{2,0},{3,1},{4,6},{5,7},{6,4},{7,5},{8,10},{9,11},{10,... | collective-permute-start | bytes 36872 | tf_op jit(solution)/shard_map/ppermute | solution.py:35
  36.4 4.9 %collective-permute-start.15 = (f32[24,128]{1,0:T(8,128)S(1)}, f32[24,128]{1,0:T(8,128)S(1)}, u32[]{:S(2)}, u32[]{:S(2)}) collective-permute-start(f32[24,128]{1,0:T(8,128)S(1)} %get-tuple-element.15), channel_id=1, source_target_pairs={{0,6},{1,7},{2,4},{3,5},{4,2},{5,3},{6,0},{7,1},{8,14},{9,15},{10,... | collective-permute-start | bytes 36872 | tf_op jit(solution)/shard_map/ppermute | solution.py:35
  36.6 7.5 %collective-permute-start.17 = (f32[1,128]{1,0:T(1,128)S(1)}, f32[1,128]{1,0:T(1,128)S(1)}, u32[]{:S(2)}, u32[]{:S(2)}) collective-permute-start(f32[1,128]{1,0:T(1,128)S(1)} %slice.14), channel_id=1, source_target_pairs={{0,8},{1,9},{2,10},{3,11},{4,12},{5,13},{6,14},{7,15},{8,0},{9,1},... | collective-permute-start | bytes 1544 | tf_op jit(solution)/shard_map/ppermute | solution.py:35
  41.3 4.8 %collective-permute-start.18 = (f32[1,128]{1,0:T(1,128)S(1)}, f32[1,128]{1,0:T(1,128)S(1)}, u32[]{:S(2)}, u32[]{:S(2)}) collective-permute-start(f32[1,128]{1,0:T(1,128)S(1)} %slice.18), channel_id=1, source_target_pairs={{0,192},{1,193},{2,194},{3,195},{4,196},{5,197},{6,198},{7,199},{8... | collective-permute-start | bytes 1544 | tf_op jit(solution)/shard_map/ppermute | solution.py:35

commit v11 on v10

--- a/solution.py
+++ b/solution.py
@@ -11,7 +11,6 @@
 NMU = 1024
 NG = 1536
 WIDTH = NMU + 128
-CHUNK = 1536
 ROWS = 128
 F32 = jnp.float32
 BF16 = jnp.bfloat16
@@ -142,16 +141,10 @@
         y_ref[8 + j : 9 + j] = total_im[:, j * 128 : j * 128 + 128]
 
 
-def pair_kernel(near, *refs):
-    if near:
-        w_ref, z_ref, _, __, acc_ref, rx_ref, lhs, xa, xb, ca, cb = refs[6:]
-    else:
-        w_ref, z_ref, _, acc_ref, lhs, xa, xb, ca, cb = refs[6:]
-    base = 2 * near
-    a_pays = refs[0:2]
-    b_pays = refs[2:6]
-    val = ROWS + 16 * near
-    half = ROWS + val
+def build_kernel(near, a_near, a_pair, b0, b1, b2, b3, *refs):
+    lhs, xa, xb = refs[-3:]
+    a_pays = (a_near, a_pair)
+    half = lhs.shape[0] // 2
 
     def put(row, left, right, left_at, right_at):
         real, imag = conj_product(
@@ -169,8 +162,8 @@
     til = spread(False)
     for m in range(2):
         xa[m] = dot(rep, a_pays[m][:, 0:NMU])
-    for n in range(4):
-        xb[n] = dot(til, b_pays[n][:, 0:NMU])
+    for n, pay in enumerate((b0, b1, b2, b3)):
+        xb[n] = dot(til, pay[:, 0:NMU])
     for m in range(2):
         for n in range(4):
             row = (m * 4 + n) * 16
@@ -178,20 +171,31 @@
             put(ROWS + row, xa[m], xb[n], 32, 32)
     if near:
         put(2 * ROWS, xa[0], dot(til, a_pays[0][:, 0:NMU]), 32, 0)
-    for at in range(0, NG, CHUNK):
-        part = pl.ds(at, CHUNK)
-        z = z_ref[:, part]
-        for side in range(2):
-            con = dot(lhs[side * half : side * half + ROWS], z)
-            for p in range(8):
-                weight = w_ref[4 * base + p : 4 * base + p + 1, part]
-                row = side * ROWS + p * 16
-                ca[row : row + 16] = (con[p * 16 : p * 16 + 16] * weight).astype(BF16)
-            dens = dot(lhs[side * half + ROWS : side * half + half], z)
-            cb[side * ROWS : side * ROWS + ROWS] = dens[0:ROWS].astype(BF16)
-            if near:
-                rx_ref[side * 16 : side * 16 + 16, part] = dens[ROWS:val]
-        acc_ref[...] = dot_t(ca[...], cb[...])
+
+
+def product_kernel(near, lhs, w_ref, z_ref, acc_ref, rx_ref, ca, cb):
+    half = lhs.shape[0] // 2
+    z = z_ref[...]
+    for side in range(2):
+        con = dot(lhs[side * half : side * half + ROWS], z)
+        for p in range(8):
+            weight = w_ref[8 * near + p : 8 * near + p + 1]
+            row = side * ROWS + p * 16
+            ca[row : row + 16] = (con[p * 16 : p * 16 + 16] * weight).astype(BF16)
+        dens = dot(lhs[side * half + ROWS : side * half + half], z)
+        cb[side * ROWS : side * ROWS + ROWS] = dens[0:ROWS].astype(BF16)
+        if near:
+            rx_ref[side * 16 : side * 16 + 16] = dens[ROWS : ROWS + 16]
+    acc_ref[...] = dot_t(ca[...], cb[...])
+
+
+def far_kernel(a_near, a_pair, b0, b1, b2, b3, w_ref, z_ref, _, acc_ref, lhs, xa, xb, ca, cb):
+    build_kernel(0, a_near, a_pair, b0, b1, b2, b3, lhs, xa, xb)
+    product_kernel(0, lhs, w_ref, z_ref, acc_ref, None, ca, cb)
+
+
+def near_kernel(lhs, w_ref, z_ref, _, acc_ref, rx_ref, ca, cb):
+    product_kernel(1, lhs, w_ref, z_ref, acc_ref, rx_ref, ca, cb)
 
 
 def rows_kernel(side, acc, *refs):
@@ -240,7 +244,7 @@
     out_ref[...] = total
 
 
-def join_kernel(y0, y1, _, out_ref):
+def join_kernel(y0, y1, _, __, out_ref):
     out_ref[...] = y0[...] + y1[...]
 
 
@@ -306,22 +310,40 @@
     return pl.CostEstimate(flops=2 * rows * 2 * NMU * NG, bytes_accessed=4 * NMU * NG, transcendentals=0)
 
 
-def pair_call(near, operands):
-    out_shape = [pltpu.VMEM((2 * ROWS, 2 * ROWS), F32)]
-    if near:
-        out_shape.append(pltpu.VMEM((32, NG), F32))
+def spreads():
+    return [pltpu.VMEM((2, 64, NMU), F32), pltpu.VMEM((4, 64, NMU), F32)]
+
+
+def far_call(*operands):
     return pl.pallas_call(
-        functools.partial(pair_kernel, near),
-        in_specs=[VMEM] * 8 + [ANY] * (1 + near),
-        out_specs=[VMEM] * len(out_shape),
-        out_shape=out_shape,
-        scratch_shapes=[
-            pltpu.VMEM((4 * ROWS + 32 * near, 2 * NMU), BF16),
-            pltpu.VMEM((2, 64, NMU), F32),
-            pltpu.VMEM((4, 64, NMU), F32),
-            pltpu.VMEM((2 * ROWS, CHUNK), BF16),
-            pltpu.VMEM((2 * ROWS, CHUNK), BF16),
-        ],
+        far_kernel,
+        in_specs=[VMEM] * 8 + [ANY],
+        out_specs=VMEM,
+        out_shape=pltpu.VMEM((2 * ROWS, 2 * ROWS), F32),
+        scratch_shapes=[pltpu.VMEM((4 * ROWS, 2 * NMU), BF16)] + spreads() + [pltpu.VMEM((2 * ROWS, NG), BF16)] * 2,
+        compiler_params=params(24),
+        cost_estimate=cost(4 * ROWS),
+    )(*operands)
+
+
+def build_call(*operands):
+    return pl.pallas_call(
+        functools.partial(build_kernel, 1),
+        in_specs=[VMEM] * 6 + [ANY],
+        out_specs=VMEM,
+        out_shape=pltpu.VMEM((4 * ROWS + 32, 2 * NMU), BF16),
+        scratch_shapes=spreads(),
+        compiler_params=params(12),
+    )(*operands)
+
+
+def near_call(*operands):
+    return pl.pallas_call(
+        near_kernel,
+        in_specs=[VMEM] * 3 + [ANY],
+        out_specs=[VMEM] * 2,
+        out_shape=[pltpu.VMEM((2 * ROWS, 2 * ROWS), F32), pltpu.VMEM((32, NG), F32)],
+        scratch_shapes=[pltpu.VMEM((2 * ROWS, NG), BF16)] * 2,
         compiler_params=params(24),
         cost_estimate=cost(4 * ROWS),
     )(*operands)
@@ -369,12 +391,13 @@
         compiler_params=params(8),
     )(pay, a1, a2, a3)
     b_pays = (b0, b1, b2, b3)
-    (far_acc,) = pair_call(0, (a1, a3, *b_pays, weights, z, y))
+    far_acc = far_call(a1, a3, *b_pays, weights, z, y)
     (y,) = small_call(half_kernel, [(16, 128)], y, move(y, z=1), move(y, z=3, other=(0, 2)), after=(far_acc,))
     swapped = move(y, core=1)
     (far_rows,) = small_call(functools.partial(rows_kernel, 0), [(16, 128)], far_acc, a1, a3, *b_pays)
-    (y,) = small_call(join_kernel, [(16, 128)], y, swapped, after=(far_rows,))
-    near_acc, rx = pair_call(1, (pay, a2, *b_pays, weights, z, far_rows, y))
+    lhs = build_call(pay, a2, *b_pays, far_acc)
+    (y,) = small_call(join_kernel, [(16, 128)], y, swapped, after=(far_rows, lhs))
+    near_acc, rx = near_call(lhs, weights, z, y)
     (y,) = small_call(half_kernel, [(16, 128)], y, move(y, x=1), move(y, x=3, other=(2, 0)), after=(near_acc,))
     swapped = move(y, core=1)
     (rows,) = small_call(functools.partial(rows_kernel, 1), [(16, 128)], near_acc, pay, a2, *b_pays, far_rows)

time: 46.9 us -> 46.6 us (level)
  waiting for transfers between devices: 5.67 us -> 4.71 us
    ppermute x19, waiting for transfers between devices: 5.67 us -> 4.71 us  [move(): return lax.ppermute(value, ('grp', 'kin'), pairs)]
    pallas_call x2 -> x3, Pallas kernels: 8.29 us -> 8.52 us  [the longest x1 4.03 us: far_call(): pl.pallas_call(far_kernel, in_specs=[VMEM] * 8 + [ANY], out_specs=VMEM, o...]
  transfers between devices with their start and end apart: 19 -> 19, of which waited for: 5 -> 5; matrix products, arithmetic and copies ran while one was open for 0% -> 0% of each run, Pallas kernels for 26% -> 27%
where the time goes in v11:
time: 46.6 us; the launch traced here: 46.4 us
  starting transfers between devices  27.2 us (58%)
  Pallas kernels  14.3 us (31%)
  waiting for transfers between devices  4.71 us (10%)
    ppermute x19, starting transfers between devices, move(): return lax.ppermute(value, ('grp', 'kin'), pairs)  27.2 us
    ppermute x19, waiting for transfers between devices, move(): return lax.ppermute(value, ('grp', 'kin'), pairs)  4.71 us
    pallas_call x1, Pallas kernels, far_call(): pl.pallas_call(far_kernel, in_specs=[VMEM] * 8 + [ANY], out_specs=VMEM, o...  4.03 us
    pallas_call x1, Pallas kernels, near_call(): pl.pallas_call(near_kernel, in_specs=[VMEM] * 3 + [ANY], out_specs=[VMEM]...  3.9 us
    pallas_call x1, Pallas kernels, on_device(): pl.pallas_call(weights_kernel, in_specs=[SMEM, ANY], out_specs=VMEM, out_...  1.74 us
    pallas_call x7, Pallas kernels, small_call(): pl.pallas_call(kernel, in_specs=[VMEM] * len(operands) + [ANY] * len(afte...  1.65 us
    pallas_call x1, Pallas kernels, on_device(): pl.pallas_call(pack_kernel, in_specs=[ANY] * 2, out_specs=VMEM, out_shape...  1.1 us
    pallas_call x1, Pallas kernels, on_device(): pl.pallas_call(exchange_kernel, in_specs=[VMEM] * 4, out_specs=VMEM, out_...  1.06 us
  transfers between devices with their start and end apart: 19, of which 5 were waited for; matrix products, arithmetic and copies ran while one was open for 0% of the time, Pallas kernels for 27%

profile of v11, /device:TPU:6, one launch (start us, length us, event | category | flops | bytes accessed | tf_op | source)
XLA Modules:
  0.0 46.4 jit_solution(2302005225078761295)
XLA Ops:
  0.0 1.1 %shard_map.73.a0.a_near.refs_0_ = bf16[16,1152]{1,0:T(8,128)(2,1)S(1)} custom-call(bf16[16,1024]{1,0:T(8,128)(2,1)} %bitcast.11, f32[2,16]{1,0:T(2,128)} %bitcast.9), custom_call_target="tpu_custom_call" | custom-call | tf_op jit(solution)/shard_map/pallas_call | solution.py:363
  1.1 0.0 slice-start.1
  1.1 2.3 %collective-permute-start.5 = (bf16[16,1152]{1,0:T(8,128)(2,1)S(1)}, bf16[16,1152]{1,0:T(8,128)(2,1)S(1)}, u32[]{:S(2)}, u32[]{:S(2)}) collective-permute-start(bf16[16,1152]{1,0:T(8,128)(2,1)S(1)} %shard_map.73.a0.a_near.refs_0_), channel_id=1, source_target_pairs={{0,64},{1,65},{2,66},{3,67},{4,68},{5,69},{6,70},{7,71},{8,72},{9,... | collective-permute-start | bytes 110600 | tf_op jit(solution)/shard_map/ppermute | solution.py:34
  3.4 5.5 %collective-permute-start = (bf16[16,1152]{1,0:T(8,128)(2,1)S(1)}, bf16[16,1152]{1,0:T(8,128)(2,1)S(1)}, u32[]{:S(2)}, u32[]{:S(2)}) collective-permute-start(bf16[16,1152]{1,0:T(8,128)(2,1)S(1)} %shard_map.73.a0.a_near.refs_0_), channel_id=1, source_target_pairs={{0,8},{1,9},{2,10},{3,11},{4,12},{5,13},{6,14},{7,15},{8,0},{9,1},... | collective-permute-start | bytes 110600 | tf_op jit(solution)/shard_map/ppermute | solution.py:34
  8.9 0.0 collective-permute-start.1
  8.9 0.0 collective-permute-done.5.b0.refs_2_
  8.9 1.6 %collective-permute-start.6 = (bf16[16,1152]{1,0:T(8,128)(2,1)S(1)}, bf16[16,1152]{1,0:T(8,128)(2,1)S(1)}, u32[]{:S(2)}, u32[]{:S(2)}) collective-permute-start(bf16[16,1152]{1,0:T(8,128)(2,1)S(1)} %collective-permute-done.5.b0.refs_2_), channel_id=1, source_target_pairs={{0,2},{1,3},{2,0},{3,1},{4,6},{5,7},{6,4},{7,5},{8,10},{9,11},{10,... | collective-permute-start | bytes 110600 | tf_op jit(solution)/shard_map/ppermute | solution.py:34
  10.4 2.9 %collective-permute-start.7 = (bf16[16,1152]{1,0:T(8,128)(2,1)S(1)}, bf16[16,1152]{1,0:T(8,128)(2,1)S(1)}, u32[]{:S(2)}, u32[]{:S(2)}) collective-permute-start(bf16[16,1152]{1,0:T(8,128)(2,1)S(1)} %collective-permute-done.5.b0.refs_2_), channel_id=1, source_target_pairs={{0,4},{1,5},{2,6},{3,7},{4,0},{5,1},{6,2},{7,3},{8,12},{9,13},{10,... | collective-permute-start | bytes 110600 | tf_op jit(solution)/shard_map/ppermute | solution.py:34
  13.3 0.2 collective-permute-start.8
  13.6 0.0 collective-permute-done.a1.a_near.refs_0_
  13.6 0.0 collective-permute-start.2
  13.6 1.7 %shard_map.75.w_ref = f32[16,1536]{1,0:T(8,128)S(1)} custom-call(s32[1,256]{1,0:T(1,128)} %qmap_ref.1, f32[256,1536]{1,0:T(8,128)} %screening.1), custom_call_target="tpu_custom_call" | custom-call | flops 4000000000 | bytes 1024 | tf_op jit(solution)/shard_map/pallas_call | solution.py:375
  15.3 0.0 collective-permute-done.1.a2.a_pair.refs_1_
  15.3 0.0 collective-permute-done.2.a3.a_pair.refs_1_
  15.3 0.2 shard_map.74._.y0
  15.5 1.1 %collective-permute-start.3 = (f32[16,128]{1,0:T(8,128)S(1)}, f32[16,128]{1,0:T(8,128)S(1)}, u32[]{:S(2)}, u32[]{:S(2)}) collective-permute-start(f32[16,128]{1,0:T(8,128)S(1)} %shard_map.74._.y0), channel_id=1, source_target_pairs={{0,16},{1,17},{2,18},{3,19},{4,20},{5,21},{6,22},{7,23},{8,24},{9,... | collective-permute-start | bytes 24584 | tf_op jit(solution)/shard_map/ppermute | solution.py:34
  16.6 1.9 %collective-permute-start.4 = (f32[16,128]{1,0:T(8,128)S(1)}, f32[16,128]{1,0:T(8,128)S(1)}, u32[]{:S(2)}, u32[]{:S(2)}) collective-permute-start(f32[16,128]{1,0:T(8,128)S(1)} %shard_map.74._.y0), channel_id=1, source_target_pairs={{0,48},{1,33},{2,50},{3,35},{4,52},{5,37},{6,54},{7,39},{8,56},{9,... | collective-permute-start | bytes 24584 | tf_op jit(solution)/shard_map/ppermute | solution.py:34
  18.6 0.0 collective-permute-done.6.b1.refs_3_
  18.6 0.0 collective-permute-done.7.b2.refs_4_
  18.6 0.0 collective-permute-done.8.b3.refs_5_
  18.6 4.0 %shard_map.76._.acc.refs_0_ = f32[256,256]{1,0:T(8,128)S(1)} custom-call(bf16[16,1152]{1,0:T(8,128)(2,1)S(1)} %collective-permute-done.a1.a_near.refs_0_, bf16[16,1152]{1,0:T(8,128)(2,1)S(1)} %collective-permute-done.2.a3.a_pair.refs_1_, bf16[16,1152]{1,0:T(8,128)(2,1)S(1)} %collective-permute-done.5.b0.refs_2_, ...), custom_call_target="tpu_custom_call" | custom-call | flops 3221225472 | bytes 6291456 | tf_op jit(solution)/shard_map/pallas_call | solution.py:318
  22.6 0.0 collective-permute-done.3.y1
  22.6 0.0 collective-permute-done.4.y2
  22.7 0.1 collective-permute-start.9
  22.8 0.6 %shard_map.79.__.lhs = bf16[544,2048]{1,0:T(8,128)(2,1)S(1)} custom-call(bf16[16,1152]{1,0:T(8,128)(2,1)S(1)} %shard_map.73.a0.a_near.refs_0_, bf16[16,1152]{1,0:T(8,128)(2,1)S(1)} %collective-permute-done.1.a2.a_pair.refs_1_, bf16[16,1152]{1,0:T(8,128)(2,1)S(1)} %collective-permute-done.5.b0.refs_2_, ...), custom_call_target="tpu_custom_call" | custom-call | tf_op jit(solution)/shard_map/pallas_call | solution.py:330
  23.4 0.5 %shard_map.78._.refs_6_ = f32[16,128]{1,0:T(8,128)S(1)} custom-call(f32[256,256]{1,0:T(8,128)S(1)} %shard_map.76._.acc.refs_0_, bf16[16,1152]{1,0:T(8,128)(2,1)S(1)} %collective-permute-done.a1.a_near.refs_0_, bf16[16,1152]{1,0:T(8,128)(2,1)S(1)} %collective-permute-done.2.a3.a_pair.refs_1_, bf16[16,1152]{1,0:T(8,128)(2,1)S(1)} %collective-permute-done.5.b0.refs_2_, ...), custom_call_target="tpu_custom_call" | custom-call | tf_op jit(solution)/shard_map/pallas_call | solution.py:353
  23.9 0.1 collective-permute-done.9.y1
  23.9 1.6 %collective-permute-start.10 = (f32[16,128]{1,0:T(8,128)S(1)}, f32[16,128]{1,0:T(8,128)S(1)}, u32[]{:S(2)}, u32[]{:S(2)}) collective-permute-start(f32[16,128]{1,0:T(8,128)S(1)} %shard_map.80._.y0), channel_id=1, source_target_pairs={{0,64},{1,65},{2,66},{3,67},{4,68},{5,69},{6,70},{7,71},{8,72},{9,... | collective-permute-start | bytes 24584 | tf_op jit(solution)/shard_map/ppermute | solution.py:34
  25.5 1.4 %collective-permute-start.11 = (f32[16,128]{1,0:T(8,128)S(1)}, f32[16,128]{1,0:T(8,128)S(1)}, u32[]{:S(2)}, u32[]{:S(2)}) collective-permute-start(f32[16,128]{1,0:T(8,128)S(1)} %shard_map.80._.y0), channel_id=1, source_target_pairs={{0,192},{1,129},{2,194},{3,131},{4,196},{5,133},{6,198},{7,135},{8... | collective-permute-start | bytes 24584 | tf_op jit(solution)/shard_map/ppermute | solution.py:34
  27.0 3.9 %shard_map.81 = (f32[256,256]{1,0:T(8,128)S(1)}, f32[32,1536]{1,0:T(8,128)S(1)}) custom-call(bf16[544,2048]{1,0:T(8,128)(2,1)S(1)} %shard_map.79.__.lhs, f32[16,1536]{1,0:T(8,128)S(1)} %shard_map.75.w_ref, bf16[2048,1536]{1,0:T(8,128)(2,1)S(1)} %bitcast.7, f32[16,128]{1,0:T(8,128)S(1)} %shard_map.80._.y0), custom_call_target="tpu_custom_call" | custom-call | flops 3221225472 | bytes 6291456 | tf_op jit(solution)/shard_map/pallas_call | solution.py:341
  30.9 0.0 collective-permute-done.10.y1
  30.9 0.0 collective-permute-done.11.y2
  30.9 0.1 collective-permute-start.12
  31.0 0.5 %shard_map.83.rows_ref = f32[16,128]{1,0:T(8,128)S(1)} custom-call(f32[256,256]{1,0:T(8,128)S(1)} %get-tuple-element.11._.acc, bf16[16,1152]{1,0:T(8,128)(2,1)S(1)} %shard_map.73.a0.a_near.refs_0_, bf16[16,1152]{1,0:T(8,128)(2,1)S(1)} %collective-permute-done.1.a2.a_pair.refs_1_, bf16[16,1152]{1,0:T(8,128)(2,1)S(1)} %collective-permute-done.5.b0.refs_2_, ...), custom_call_target="tpu_custom_call" | custom-call | tf_op jit(solution)/shard_map/pallas_call | solution.py:353
  31.5 0.5 %collective-permute-start.16 = (f32[2,128]{1,0:T(2,128)S(1)}, f32[2,128]{1,0:T(2,128)S(1)}, u32[]{:S(2)}, u32[]{:S(2)}) collective-permute-start(f32[2,128]{1,0:T(2,128)S(1)} %slice.17), channel_id=1, source_target_pairs={{0,1},{1,0},{2,3},{3,2},{4,5},{5,4},{6,7},{7,6},{8,9},{9,8},{10,11... | collective-permute-start | bytes 3080 | tf_op jit(solution)/shard_map/ppermute | solution.py:34
  32.1 0.1 collective-permute-done.12.y1
  32.2 2.0 %collective-permute-start.13 = (f32[24,128]{1,0:T(8,128)S(1)}, f32[24,128]{1,0:T(8,128)S(1)}, u32[]{:S(2)}, u32[]{:S(2)}) collective-permute-start(f32[24,128]{1,0:T(8,128)S(1)} %get-tuple-element.13), channel_id=1, source_target_pairs={{0,4},{1,5},{2,6},{3,7},{4,0},{5,1},{6,2},{7,3},{8,12},{9,13},{10,... | collective-permute-start | bytes 36872 | tf_op jit(solution)/shard_map/ppermute | solution.py:34
  34.2 1.9 %collective-permute-start.14 = (f32[24,128]{1,0:T(8,128)S(1)}, f32[24,128]{1,0:T(8,128)S(1)}, u32[]{:S(2)}, u32[]{:S(2)}) collective-permute-start(f32[24,128]{1,0:T(8,128)S(1)} %get-tuple-element.14), channel_id=1, source_target_pairs={{0,2},{1,3},{2,0},{3,1},{4,6},{5,7},{6,4},{7,5},{8,10},{9,11},{10,... | collective-permute-start | bytes 36872 | tf_op jit(solution)/shard_map/ppermute | solution.py:34
  36.1 0.2 collective-permute-start.15
  36.3 3.4 %collective-permute-start.17 = (f32[1,128]{1,0:T(1,128)S(1)}, f32[1,128]{1,0:T(1,128)S(1)}, u32[]{:S(2)}, u32[]{:S(2)}) collective-permute-start(f32[1,128]{1,0:T(1,128)S(1)} %slice.14), channel_id=1, source_target_pairs={{0,8},{1,9},{2,10},{3,11},{4,12},{5,13},{6,14},{7,15},{8,0},{9,1},... | collective-permute-start | bytes 1544 | tf_op jit(solution)/shard_map/ppermute | solution.py:34
  39.7 0.0 collective-permute-done.13
  39.7 0.0 collective-permute-done.14
  39.7 1.3 %collective-permute-done.15 = f32[24,128]{1,0:T(8,128)S(1)} collective-permute-done((f32[24,128]{1,0:T(8,128)S(1)}, f32[24,128]{1,0:T(8,128)S(1)}, u32[]{:S(2)}, u32[]{:S(2)}) %collective-permute-start.15) | collective-permute-done | bytes 12320 | tf_op jit(solution)/shard_map/ppermute | solution.py:34
  41.0 0.5 %collective-permute-start.18 = (f32[1,128]{1,0:T(1,128)S(1)}, f32[1,128]{1,0:T(1,128)S(1)}, u32[]{:S(2)}, u32[]{:S(2)}) collective-permute-start(f32[1,128]{1,0:T(1,128)S(1)} %slice.18), channel_id=1, source_target_pairs={{0,192},{1,193},{2,194},{3,195},{4,196},{5,197},{6,198},{7,199},{8... | collective-permute-start | bytes 1544 | tf_op jit(solution)/shard_map/ppermute | solution.py:34
  41.5 1.1 %shard_map.85.exchange_ref = f32[2,16]{1,0:T(2,128)S(1)} custom-call(f32[24,128]{1,0:T(8,128)S(1)} %add_add_fusion.y_ref, f32[1,1536]{1,0:T(1,128)S(1)} %reshape.19.c_ref, f32[32,1536]{1,0:T(8,128)S(1)} %get-tuple-element.16.rx_ref, bf16[2048,1536]{1,0:T(8,128)(2,1)S(1)} %bitcast.8), custom_call_target="tpu_custom_call" | custom-call | flops 805306368 | bytes 6291456 | tf_op jit(solution)/shard_map/pallas_call | solution.py:407
  42.6 1.3 %collective-permute-done.17.d_ref = f32[1,128]{1,0:T(1,128)S(1)} collective-permute-done((f32[1,128]{1,0:T(1,128)S(1)}, f32[1,128]{1,0:T(1,128)S(1)}, u32[]{:S(2)}, u32[]{:S(2)}) %collective-permute-start.17) | collective-permute-done | bytes 544 | tf_op jit(solution)/shard_map/ppermute | solution.py:34
  43.8 2.0 %collective-permute-done.18.h_ref = f32[1,128]{1,0:T(1,128)S(1)} collective-permute-done((f32[1,128]{1,0:T(1,128)S(1)}, f32[1,128]{1,0:T(1,128)S(1)}, u32[]{:S(2)}, u32[]{:S(2)}) %collective-permute-start.18) | collective-permute-done | bytes 544 | tf_op jit(solution)/shard_map/ppermute | solution.py:34
  45.8 0.6 %shard_map.86 = f32[2,16]{1,0:T(2,128)} custom-call(f32[1,16]{1,0:T(1,128)S(1)} %copy-done.1, f32[2,16]{1,0:T(2,128)S(1)} %bitcast.10, f32[2,16]{1,0:T(2,128)S(1)} %shard_map.85.exchange_ref, f32[2,128]{1,0:T(2,128)S(1)} %slice_add_fusion.near_ref, f32[1,128]{1,0:T(1,128)S(1)} %collective-permute-done.17.d_ref, f32[1,128]{1,0:T(1,128)S(1)} %collective-permute-done.18.h_ref), custom_call_target="tpu_custom_call" | custom-call | tf_op jit(solution)/shard_map/pallas_call | solution.py:353
  (21 shorter events, 0.1 us)
Async XLA Ops:
  0.0 18.6 %slice-start = ((s8[6291456]{0:T(1024)(128)(4,1)}), s8[2097152]{0:T(1024)(128)(4,1)S(1)}, s32[]{:S(2)}) async-start(s8[6291456]{0:T(1024)(128)(4,1)} %bitcast.4), calls=%async_computation | async-start | bytes 4194304
  1.1 17.5 %slice-start.1 = ((s8[6291456]{0:T(1024)(128)(4,1)}), s8[4194304]{0:T(1024)(128)(4,1)S(1)}, s32[]{:S(2)}) async-start(s8[6291456]{0:T(1024)(128)(4,1)} %bitcast.4), calls=%async_computation.1 | async-start | bytes 8388608
  1.1 7.8 %collective-permute-start.5 = (bf16[16,1152]{1,0:T(8,128)(2,1)S(1)}, bf16[16,1152]{1,0:T(8,128)(2,1)S(1)}, u32[]{:S(2)}, u32[]{:S(2)}) collective-permute-start(bf16[16,1152]{1,0:T(8,128)(2,1)S(1)} %shard_map.73.a0.a_near.refs_0_), channel_id=1, source_target_pairs={{0,64},{1,65},{2,66},{3,67},{4,68},{5,69},{6,70},{7,71},{8,72},{9,... | collective-permute-start | bytes 110600 | tf_op jit(solution)/shard_map/ppermute | solution.py:34
  3.4 10.2 %collective-permute-start = (bf16[16,1152]{1,0:T(8,128)(2,1)S(1)}, bf16[16,1152]{1,0:T(8,128)(2,1)S(1)}, u32[]{:S(2)}, u32[]{:S(2)}) collective-permute-start(bf16[16,1152]{1,0:T(8,128)(2,1)S(1)} %shard_map.73.a0.a_near.refs_0_), channel_id=1, source_target_pairs={{0,8},{1,9},{2,10},{3,11},{4,12},{5,13},{6,14},{7,15},{8,0},{9,1},... | collective-permute-start | bytes 110600 | tf_op jit(solution)/shard_map/ppermute | solution.py:34
  8.9 6.5 %collective-permute-start.1 = (bf16[16,1152]{1,0:T(8,128)(2,1)S(1)}, bf16[16,1152]{1,0:T(8,128)(2,1)S(1)}, u32[]{:S(2)}, u32[]{:S(2)}) collective-permute-start(bf16[16,1152]{1,0:T(8,128)(2,1)S(1)} %shard_map.73.a0.a_near.refs_0_), channel_id=1, source_target_pairs={{0,1},{1,0},{2,3},{3,2},{4,5},{5,4},{6,7},{7,6},{8,9},{9,8},{10,11... | collective-permute-start | bytes 110600 | tf_op jit(solution)/shard_map/ppermute | solution.py:34
  8.9 9.7 %collective-permute-start.6 = (bf16[16,1152]{1,0:T(8,128)(2,1)S(1)}, bf16[16,1152]{1,0:T(8,128)(2,1)S(1)}, u32[]{:S(2)}, u32[]{:S(2)}) collective-permute-start(bf16[16,1152]{1,0:T(8,128)(2,1)S(1)} %collective-permute-done.5.b0.refs_2_), channel_id=1, source_target_pairs={{0,2},{1,3},{2,0},{3,1},{4,6},{5,7},{6,4},{7,5},{8,10},{9,11},{10,... | collective-permute-start | bytes 110600 | tf_op jit(solution)/shard_map/ppermute | solution.py:34
  10.4 8.1 %collective-permute-start.7 = (bf16[16,1152]{1,0:T(8,128)(2,1)S(1)}, bf16[16,1152]{1,0:T(8,128)(2,1)S(1)}, u32[]{:S(2)}, u32[]{:S(2)}) collective-permute-start(bf16[16,1152]{1,0:T(8,128)(2,1)S(1)} %collective-permute-done.5.b0.refs_2_), channel_id=1, source_target_pairs={{0,4},{1,5},{2,6},{3,7},{4,0},{5,1},{6,2},{7,3},{8,12},{9,13},{10,... | collective-permute-start | bytes 110600 | tf_op jit(solution)/shard_map/ppermute | solution.py:34
  13.3 5.2 %collective-permute-start.8 = (bf16[16,1152]{1,0:T(8,128)(2,1)S(1)}, bf16[16,1152]{1,0:T(8,128)(2,1)S(1)}, u32[]{:S(2)}, u32[]{:S(2)}) collective-permute-start(bf16[16,1152]{1,0:T(8,128)(2,1)S(1)} %collective-permute-done.5.b0.refs_2_), channel_id=1, source_target_pairs={{0,6},{1,7},{2,4},{3,5},{4,2},{5,3},{6,0},{7,1},{8,14},{9,15},{10,... | collective-permute-start | bytes 110600 | tf_op jit(solution)/shard_map/ppermute | solution.py:34
  13.6 1.8 %collective-permute-start.2 = (bf16[16,1152]{1,0:T(8,128)(2,1)S(1)}, bf16[16,1152]{1,0:T(8,128)(2,1)S(1)}, u32[]{:S(2)}, u32[]{:S(2)}) collective-permute-start(bf16[16,1152]{1,0:T(8,128)(2,1)S(1)} %collective-permute-done.a1.a_near.refs_0_), channel_id=1, source_target_pairs={{0,1},{1,0},{2,3},{3,2},{4,5},{5,4},{6,7},{7,6},{8,9},{9,8},{10,11... | collective-permute-start | bytes 110600 | tf_op jit(solution)/shard_map/ppermute | solution.py:34
  15.5 7.1 %collective-permute-start.3 = (f32[16,128]{1,0:T(8,128)S(1)}, f32[16,128]{1,0:T(8,128)S(1)}, u32[]{:S(2)}, u32[]{:S(2)}) collective-permute-start(f32[16,128]{1,0:T(8,128)S(1)} %shard_map.74._.y0), channel_id=1, source_target_pairs={{0,16},{1,17},{2,18},{3,19},{4,20},{5,21},{6,22},{7,23},{8,24},{9,... | collective-permute-start | bytes 24584 | tf_op jit(solution)/shard_map/ppermute | solution.py:34
  16.6 6.0 %collective-permute-start.4 = (f32[16,128]{1,0:T(8,128)S(1)}, f32[16,128]{1,0:T(8,128)S(1)}, u32[]{:S(2)}, u32[]{:S(2)}) collective-permute-start(f32[16,128]{1,0:T(8,128)S(1)} %shard_map.74._.y0), channel_id=1, source_target_pairs={{0,48},{1,33},{2,50},{3,35},{4,52},{5,37},{6,54},{7,39},{8,56},{9,... | collective-permute-start | bytes 24584 | tf_op jit(solution)/shard_map/ppermute | solution.py:34
  22.7 1.3 %collective-permute-start.9 = (f32[16,128]{1,0:T(8,128)S(1)}, f32[16,128]{1,0:T(8,128)S(1)}, u32[]{:S(2)}, u32[]{:S(2)}) collective-permute-start(f32[16,128]{1,0:T(8,128)S(1)} %shard_map.77.y0), channel_id=1, source_target_pairs={{0,1},{1,0},{2,3},{3,2},{4,5},{5,4},{6,7},{7,6},{8,9},{9,8},{10,11... | collective-permute-start | bytes 24584 | tf_op jit(solution)/shard_map/ppermute | solution.py:34
  23.9 8.1 %copy-start.2 = (f32[1536]{0:T(1024)S(1)}, f32[1536]{0:T(1024)}, u32[]{:S(2)}) copy-start(f32[1536]{0:T(1024)} %param.12) | copy-start | bytes 18436
  23.9 7.0 %collective-permute-start.10 = (f32[16,128]{1,0:T(8,128)S(1)}, f32[16,128]{1,0:T(8,128)S(1)}, u32[]{:S(2)}, u32[]{:S(2)}) collective-permute-start(f32[16,128]{1,0:T(8,128)S(1)} %shard_map.80._.y0), channel_id=1, source_target_pairs={{0,64},{1,65},{2,66},{3,67},{4,68},{5,69},{6,70},{7,71},{8,72},{9,... | collective-permute-start | bytes 24584 | tf_op jit(solution)/shard_map/ppermute | solution.py:34
  25.5 5.4 %collective-permute-start.11 = (f32[16,128]{1,0:T(8,128)S(1)}, f32[16,128]{1,0:T(8,128)S(1)}, u32[]{:S(2)}, u32[]{:S(2)}) collective-permute-start(f32[16,128]{1,0:T(8,128)S(1)} %shard_map.80._.y0), channel_id=1, source_target_pairs={{0,192},{1,129},{2,194},{3,131},{4,196},{5,133},{6,198},{7,135},{8... | collective-permute-start | bytes 24584 | tf_op jit(solution)/shard_map/ppermute | solution.py:34
  30.9 1.3 %collective-permute-start.12 = (f32[16,128]{1,0:T(8,128)S(1)}, f32[16,128]{1,0:T(8,128)S(1)}, u32[]{:S(2)}, u32[]{:S(2)}) collective-permute-start(f32[16,128]{1,0:T(8,128)S(1)} %shard_map.82.y0), channel_id=1, source_target_pairs={{0,1},{1,0},{2,3},{3,2},{4,5},{5,4},{6,7},{7,6},{8,9},{9,8},{10,11... | collective-permute-start | bytes 24584 | tf_op jit(solution)/shard_map/ppermute | solution.py:34
  31.5 4.8 %collective-permute-start.16 = (f32[2,128]{1,0:T(2,128)S(1)}, f32[2,128]{1,0:T(2,128)S(1)}, u32[]{:S(2)}, u32[]{:S(2)}) collective-permute-start(f32[2,128]{1,0:T(2,128)S(1)} %slice.17), channel_id=1, source_target_pairs={{0,1},{1,0},{2,3},{3,2},{4,5},{5,4},{6,7},{7,6},{8,9},{9,8},{10,11... | collective-permute-start | bytes 3080 | tf_op jit(solution)/shard_map/ppermute | solution.py:34
  32.2 7.5 %collective-permute-start.13 = (f32[24,128]{1,0:T(8,128)S(1)}, f32[24,128]{1,0:T(8,128)S(1)}, u32[]{:S(2)}, u32[]{:S(2)}) collective-permute-start(f32[24,128]{1,0:T(8,128)S(1)} %get-tuple-element.13), channel_id=1, source_target_pairs={{0,4},{1,5},{2,6},{3,7},{4,0},{5,1},{6,2},{7,3},{8,12},{9,13},{10,... | collective-permute-start | bytes 36872 | tf_op jit(solution)/shard_map/ppermute | solution.py:34
  34.2 5.5 %collective-permute-start.14 = (f32[24,128]{1,0:T(8,128)S(1)}, f32[24,128]{1,0:T(8,128)S(1)}, u32[]{:S(2)}, u32[]{:S(2)}) collective-permute-start(f32[24,128]{1,0:T(8,128)S(1)} %get-tuple-element.14), channel_id=1, source_target_pairs={{0,2},{1,3},{2,0},{3,1},{4,6},{5,7},{6,4},{7,5},{8,10},{9,11},{10,... | collective-permute-start | bytes 36872 | tf_op jit(solution)/shard_map/ppermute | solution.py:34
  36.1 4.9 %collective-permute-start.15 = (f32[24,128]{1,0:T(8,128)S(1)}, f32[24,128]{1,0:T(8,128)S(1)}, u32[]{:S(2)}, u32[]{:S(2)}) collective-permute-start(f32[24,128]{1,0:T(8,128)S(1)} %get-tuple-element.15), channel_id=1, source_target_pairs={{0,6},{1,7},{2,4},{3,5},{4,2},{5,3},{6,0},{7,1},{8,14},{9,15},{10,... | collective-permute-start | bytes 36872 | tf_op jit(solution)/shard_map/ppermute | solution.py:34
  36.3 7.5 %collective-permute-start.17 = (f32[1,128]{1,0:T(1,128)S(1)}, f32[1,128]{1,0:T(1,128)S(1)}, u32[]{:S(2)}, u32[]{:S(2)}) collective-permute-start(f32[1,128]{1,0:T(1,128)S(1)} %slice.14), channel_id=1, source_target_pairs={{0,8},{1,9},{2,10},{3,11},{4,12},{5,13},{6,14},{7,15},{8,0},{9,1},... | collective-permute-start | bytes 1544 | tf_op jit(solution)/shard_map/ppermute | solution.py:34
  41.0 4.8 %collective-permute-start.18 = (f32[1,128]{1,0:T(1,128)S(1)}, f32[1,128]{1,0:T(1,128)S(1)}, u32[]{:S(2)}, u32[]{:S(2)}) collective-permute-start(f32[1,128]{1,0:T(1,128)S(1)} %slice.18), channel_id=1, source_target_pairs={{0,192},{1,193},{2,194},{3,195},{4,196},{5,197},{6,198},{7,199},{8... | collective-permute-start | bytes 1544 | tf_op jit(solution)/shard_map/ppermute | solution.py:34
  41.5 4.3 %copy-start = (f32[1,2,16]{2,1,0:T(2,128)S(1)}, f32[1,2,16]{2,1,0:T(2,128)}, u32[]{:S(2)}) copy-start(f32[1,2,16]{2,1,0:T(2,128)} %param.8) | copy-start | bytes 388
  41.5 4.3 %copy-start.1 = (f32[1,16]{1,0:T(1,128)S(1)}, f32[1,16]{1,0:T(1,128)}, u32[]{:S(2)}) copy-start(f32[1,16]{1,0:T(1,128)} %energy_ref.1) | copy-start | bytes 196

commit v12 on v11

--- a/solution.py
+++ b/solution.py
@@ -105,11 +105,11 @@
     copies[1].wait()
 
 
-def weights_kernel(qmap_ref, screening, w_ref, sems):
+def fetch_rows(qmap_ref, screening, w_ref, sems):
     own = lax.axis_index("grp")
     member = lax.axis_index("kin")
     partner = (own + 12) & 15
-    steps = []
+    copies = []
     for m, flip in enumerate((8, 9, 0, 1)):
         from_a = qmap_ref[0, own * 16 + (member ^ flip)]
         for n in range(4):
@@ -118,9 +118,12 @@
             at = m * 4 + n
             copy = pltpu.make_async_copy(screening.at[pl.ds(index, 1)], w_ref.at[pl.ds(at, 1)], sems.at[at])
             copy.start()
-            steps.append(copy)
-    for copy in steps:
-        copy.wait()
+            copies.append(copy)
+    return copies
+
+
+def place_kernel(source, out_ref):
+    out_ref[...] = jnp.broadcast_to(source[:, 0:128], (8, 128))
 
 
 def transitions_kernel(a0, a1, a2, a3, y_ref):
@@ -173,11 +176,14 @@
         put(2 * ROWS, xa[0], dot(til, a_pays[0][:, 0:NMU]), 32, 0)
 
 
-def product_kernel(near, lhs, w_ref, z_ref, acc_ref, rx_ref, ca, cb):
+def product_kernel(near, lhs, w_ref, z_ref, acc_ref, rx_ref, ca, cb, copies=()):
     half = lhs.shape[0] // 2
     z = z_ref[...]
     for side in range(2):
         con = dot(lhs[side * half : side * half + ROWS], z)
+        if side == 0:
+            for copy in copies:
+                copy.wait()
         for p in range(8):
             weight = w_ref[8 * near + p : 8 * near + p + 1]
             row = side * ROWS + p * 16
@@ -189,9 +195,13 @@
     acc_ref[...] = dot_t(ca[...], cb[...])
 
 
-def far_kernel(a_near, a_pair, b0, b1, b2, b3, w_ref, z_ref, _, acc_ref, lhs, xa, xb, ca, cb):
+def far_kernel(a_near, a_pair, b0, b1, b2, b3, z_ref, qmap, screening, _, __, acc_ref, w_ref, lhs, xa, xb, ca, cb, qmap_ref, sems):
+    table = pltpu.make_async_copy(qmap, qmap_ref, sems.at[16])
+    table.start()
     build_kernel(0, a_near, a_pair, b0, b1, b2, b3, lhs, xa, xb)
-    product_kernel(0, lhs, w_ref, z_ref, acc_ref, None, ca, cb)
+    table.wait()
+    copies = fetch_rows(qmap_ref, screening, w_ref, sems)
+    product_kernel(0, lhs, w_ref, z_ref, acc_ref, None, ca, cb, copies)
 
 
 def near_kernel(lhs, w_ref, z_ref, _, acc_ref, rx_ref, ca, cb):
@@ -317,11 +327,14 @@
 def far_call(*operands):
     return pl.pallas_call(
         far_kernel,
-        in_specs=[VMEM] * 8 + [ANY],
-        out_specs=VMEM,
-        out_shape=pltpu.VMEM((2 * ROWS, 2 * ROWS), F32),
-        scratch_shapes=[pltpu.VMEM((4 * ROWS, 2 * NMU), BF16)] + spreads() + [pltpu.VMEM((2 * ROWS, NG), BF16)] * 2,
-        compiler_params=params(24),
+        in_specs=[VMEM] * 7 + [ANY] * 4,
+        out_specs=[VMEM] * 2,
+        out_shape=[pltpu.VMEM((2 * ROWS, 2 * ROWS), F32), pltpu.VMEM((16, NG), F32)],
+        scratch_shapes=[pltpu.VMEM((4 * ROWS, 2 * NMU), BF16)]
+        + spreads()
+        + [pltpu.VMEM((2 * ROWS, NG), BF16)] * 2
+        + [pltpu.SMEM((1, 256), jnp.int32), pltpu.SemaphoreType.DMA((17,))],
+        compiler_params=params(30),
         cost_estimate=cost(4 * ROWS),
     )(*operands)
 
@@ -372,15 +385,15 @@
     b0 = move(pay, step=1)
     a2 = move(pay, core=1)
     z = basis.reshape(2 * NMU, NG)
-    weights = pl.pallas_call(
-        weights_kernel,
-        in_specs=[SMEM, ANY],
+    coulomb = coulomb.reshape(1, NG)
+    place = pl.pallas_call(
+        place_kernel,
+        in_specs=[VMEM],
         out_specs=VMEM,
-        out_shape=pltpu.VMEM((16, NG), F32),
-        scratch_shapes=[pltpu.SemaphoreType.DMA((16,))],
-        compiler_params=params(54),
+        out_shape=jax.ShapeDtypeStruct((8, 128), F32),
+        compiler_params=params(24),
         cost_estimate=pl.CostEstimate(flops=4000000000, bytes_accessed=1024, transcendentals=0),
-    )(qmap, screening)
+    )(coulomb)
     b1, b2, b3 = (move(b0, y=n) for n in (1, 2, 3))
     a3 = move(a1, core=1)
     y = pl.pallas_call(
@@ -391,7 +404,7 @@
         compiler_params=params(8),
     )(pay, a1, a2, a3)
     b_pays = (b0, b1, b2, b3)
-    far_acc = far_call(a1, a3, *b_pays, weights, z, y)
+    far_acc, weights = far_call(a1, a3, *b_pays, z, qmap, screening, place, y)
     (y,) = small_call(half_kernel, [(16, 128)], y, move(y, z=1), move(y, z=3, other=(0, 2)), after=(far_acc,))
     swapped = move(y, core=1)
     (far_rows,) = small_call(functools.partial(rows_kernel, 0), [(16, 128)], far_acc, a1, a3, *b_pays)
@@ -412,7 +425,7 @@
         scratch_shapes=[pltpu.VMEM((16, 2 * NMU), BF16)],
         compiler_params=params(24),
         cost_estimate=cost(128),
-    )(mail, coulomb.reshape(1, NG), rx, z)
+    )(mail, coulomb, rx, z)
 
     (out,) = small_call(
         final_kernel,

time: 46.6 us -> 46 us (0.987)
  starting transfers between devices: 27.2 us -> 25.2 us
  waiting for transfers between devices: 4.71 us -> 5.93 us
  Pallas kernels: 14.3 us -> 13.2 us
  local copies, waits for them, and re-layouts: 0.04 us -> 0.89 us
    ppermute x19, starting transfers between devices: 27.2 us -> 25.2 us  [move(): return lax.ppermute(value, ('grp', 'kin'), pairs)]
    ppermute x19, waiting for transfers between devices: 4.71 us -> 5.93 us  [move(): return lax.ppermute(value, ('grp', 'kin'), pairs)]
    pallas_call x2, Pallas kernels: 5.77 us -> 4.84 us  [the longest x1 4.84 us: far_call(): pl.pallas_call(far_kernel, in_specs=[VMEM] * 7 + [ANY] * 4, out_specs=[VM...]
    reshape x1, local copies, waits for them, and re-layouts: 0.01 us -> 0.85 us  [on_device(): coulomb = coulomb.reshape(1, NG)]
  transfers between devices with their start and end apart: 19 -> 19, of which waited for: 5 -> 6; matrix products, arithmetic and copies ran while one was open for 0% -> 2% of each run, Pallas kernels for 27% -> 26%
where the time goes in v12:
time: 46 us; the launch traced here: 45.5 us
  starting transfers between devices  25.2 us (55%)
  Pallas kernels  13.2 us (29%)
  waiting for transfers between devices  5.93 us (13%)
  local copies, waits for them, and re-layouts  0.89 us (2%)
    ppermute x19, starting transfers between devices, move(): return lax.ppermute(value, ('grp', 'kin'), pairs)  25.2 us
    ppermute x19, waiting for transfers between devices, move(): return lax.ppermute(value, ('grp', 'kin'), pairs)  5.93 us
    pallas_call x1, Pallas kernels, far_call(): pl.pallas_call(far_kernel, in_specs=[VMEM] * 7 + [ANY] * 4, out_specs=[VM...  4.84 us
    pallas_call x1, Pallas kernels, near_call(): pl.pallas_call(near_kernel, in_specs=[VMEM] * 3 + [ANY], out_specs=[VMEM]...  3.9 us
    pallas_call x7, Pallas kernels, small_call(): pl.pallas_call(kernel, in_specs=[VMEM] * len(operands) + [ANY] * len(afte...  1.66 us
    pallas_call x1, Pallas kernels, on_device(): pl.pallas_call(exchange_kernel, in_specs=[VMEM] * 4, out_specs=VMEM, out_...  1.07 us
    pallas_call x1, Pallas kernels, on_device(): pl.pallas_call(pack_kernel, in_specs=[ANY] * 2, out_specs=VMEM, out_shape...  0.95 us
  transfers between devices with their start and end apart: 19, of which 6 were waited for; matrix products, arithmetic and copies ran while one was open for 2% of the time, Pallas kernels for 26%

profile of v12, /device:TPU:6, one launch (start us, length us, event | category | flops | bytes accessed | tf_op | source)
XLA Modules:
  0.0 45.5 jit_solution(7746085908761952000)
XLA Ops:
  0.0 0.9 %shard_map.73.a0.a_near.refs_0_ = bf16[16,1152]{1,0:T(8,128)(2,1)S(1)} custom-call(bf16[16,1024]{1,0:T(8,128)(2,1)} %bitcast.11, f32[2,16]{1,0:T(2,128)} %bitcast.9), custom_call_target="tpu_custom_call" | custom-call | tf_op jit(solution)/shard_map/pallas_call | solution.py:376
  1.0 2.3 %collective-permute-start.5 = (bf16[16,1152]{1,0:T(8,128)(2,1)S(1)}, bf16[16,1152]{1,0:T(8,128)(2,1)S(1)}, u32[]{:S(2)}, u32[]{:S(2)}) collective-permute-start(bf16[16,1152]{1,0:T(8,128)(2,1)S(1)} %shard_map.73.a0.a_near.refs_0_), channel_id=1, source_target_pairs={{0,64},{1,65},{2,66},{3,67},{4,68},{5,69},{6,70},{7,71},{8,72},{9,... | collective-permute-start | bytes 110600 | tf_op jit(solution)/shard_map/ppermute | solution.py:34
  3.2 5.5 %collective-permute-start = (bf16[16,1152]{1,0:T(8,128)(2,1)S(1)}, bf16[16,1152]{1,0:T(8,128)(2,1)S(1)}, u32[]{:S(2)}, u32[]{:S(2)}) collective-permute-start(bf16[16,1152]{1,0:T(8,128)(2,1)S(1)} %shard_map.73.a0.a_near.refs_0_), channel_id=1, source_target_pairs={{0,8},{1,9},{2,10},{3,11},{4,12},{5,13},{6,14},{7,15},{8,0},{9,1},... | collective-permute-start | bytes 110600 | tf_op jit(solution)/shard_map/ppermute | solution.py:34
  8.7 0.0 collective-permute-start.1
  8.7 0.9 %reshape.19.source.c_ref = f32[1,1536]{1,0:T(1,128)S(1)} reshape(f32[1536]{0:T(1024)} %param.12) | data formatting | bytes 12288 | tf_op jit(solution)/shard_map/reshape | solution.py:388
  9.6 0.0 copy-start.3
  9.6 0.0 collective-permute-done.5.b0.refs_2_
  9.6 3.1 %collective-permute-start.8 = (bf16[16,1152]{1,0:T(8,128)(2,1)S(1)}, bf16[16,1152]{1,0:T(8,128)(2,1)S(1)}, u32[]{:S(2)}, u32[]{:S(2)}) collective-permute-start(bf16[16,1152]{1,0:T(8,128)(2,1)S(1)} %collective-permute-done.5.b0.refs_2_), channel_id=1, source_target_pairs={{0,6},{1,7},{2,4},{3,5},{4,2},{5,3},{6,0},{7,1},{8,14},{9,15},{10,... | collective-permute-start | bytes 110600 | tf_op jit(solution)/shard_map/ppermute | solution.py:34
  12.7 0.6 %collective-permute-start.7 = (bf16[16,1152]{1,0:T(8,128)(2,1)S(1)}, bf16[16,1152]{1,0:T(8,128)(2,1)S(1)}, u32[]{:S(2)}, u32[]{:S(2)}) collective-permute-start(bf16[16,1152]{1,0:T(8,128)(2,1)S(1)} %collective-permute-done.5.b0.refs_2_), channel_id=1, source_target_pairs={{0,4},{1,5},{2,6},{3,7},{4,0},{5,1},{6,2},{7,3},{8,12},{9,13},{10,... | collective-permute-start | bytes 110600 | tf_op jit(solution)/shard_map/ppermute | solution.py:34
  13.3 0.5 %collective-permute-start.6 = (bf16[16,1152]{1,0:T(8,128)(2,1)S(1)}, bf16[16,1152]{1,0:T(8,128)(2,1)S(1)}, u32[]{:S(2)}, u32[]{:S(2)}) collective-permute-start(bf16[16,1152]{1,0:T(8,128)(2,1)S(1)} %collective-permute-done.5.b0.refs_2_), channel_id=1, source_target_pairs={{0,2},{1,3},{2,0},{3,1},{4,6},{5,7},{6,4},{7,5},{8,10},{9,11},{10,... | collective-permute-start | bytes 110600 | tf_op jit(solution)/shard_map/ppermute | solution.py:34
  13.8 0.0 collective-permute-done.a1.a_near.refs_0_
  13.8 0.0 collective-permute-start.2
  13.8 0.0 collective-permute-done.1.a2.a_pair.refs_1_
  13.8 1.2 %collective-permute-done.2.a3.a_pair.refs_1_ = bf16[16,1152]{1,0:T(8,128)(2,1)S(1)} collective-permute-done((bf16[16,1152]{1,0:T(8,128)(2,1)S(1)}, bf16[16,1152]{1,0:T(8,128)(2,1)S(1)}, u32[]{:S(2)}, u32[]{:S(2)}) %collective-permute-start.2) | collective-permute-done | bytes 36896 | tf_op jit(solution)/shard_map/ppermute | solution.py:34
  15.0 0.2 shard_map.74.__.y0
  15.2 2.0 %collective-permute-start.4 = (f32[16,128]{1,0:T(8,128)S(1)}, f32[16,128]{1,0:T(8,128)S(1)}, u32[]{:S(2)}, u32[]{:S(2)}) collective-permute-start(f32[16,128]{1,0:T(8,128)S(1)} %shard_map.74.__.y0), channel_id=1, source_target_pairs={{0,48},{1,33},{2,50},{3,35},{4,52},{5,37},{6,54},{7,39},{8,56},{9,... | collective-permute-start | bytes 24584 | tf_op jit(solution)/shard_map/ppermute | solution.py:34
  17.2 0.1 collective-permute-start.3
  17.3 0.0 collective-permute-done.8.b3.refs_5_
  17.3 0.9 %collective-permute-done.7.b2.refs_4_ = bf16[16,1152]{1,0:T(8,128)(2,1)S(1)} collective-permute-done((bf16[16,1152]{1,0:T(8,128)(2,1)S(1)}, bf16[16,1152]{1,0:T(8,128)(2,1)S(1)}, u32[]{:S(2)}, u32[]{:S(2)}) %collective-permute-start.7) | collective-permute-done | bytes 36896 | tf_op jit(solution)/shard_map/ppermute | solution.py:34
  18.3 0.0 collective-permute-done.6.b1.refs_3_
  18.3 4.8 %shard_map.76 = (f32[256,256]{1,0:T(8,128)S(1)}, f32[16,1536]{1,0:T(8,128)S(1)}) custom-call(bf16[16,1152]{1,0:T(8,128)(2,1)S(1)} %collective-permute-done.a1.a_near.refs_0_, bf16[16,1152]{1,0:T(8,128)(2,1)S(1)} %collective-permute-done.2.a3.a_pair.refs_1_, bf16[16,1152]{1,0:T(8,128)(2,1)S(1)} %collective-permute-done.5.b0.refs_2_, ...), custom_call_target="tpu_custom_call" | custom-call | flops 3221225472 | bytes 6291456 | tf_op jit(solution)/shard_map/pallas_call | solution.py:328
  23.2 0.0 collective-permute-done.4.y2
  23.2 0.0 collective-permute-done.3.y1
  23.2 0.1 collective-permute-start.9
  23.3 0.5 %shard_map.78._.refs_6_ = f32[16,128]{1,0:T(8,128)S(1)} custom-call(f32[256,256]{1,0:T(8,128)S(1)} %get-tuple-element.13._.acc.refs_0_, bf16[16,1152]{1,0:T(8,128)(2,1)S(1)} %collective-permute-done.a1.a_near.refs_0_, bf16[16,1152]{1,0:T(8,128)(2,1)S(1)} %collective-permute-done.2.a3.a_pair.refs_1_, bf16[16,1152]{1,0:T(8,128)(2,1)S(1)} %collective-permute-done.5.b0.refs_2_, ...), custom_call_target="tpu_custom_call" | custom-call | tf_op jit(solution)/shard_map/pallas_call | solution.py:366
  23.8 0.6 %shard_map.79.__.lhs = bf16[544,2048]{1,0:T(8,128)(2,1)S(1)} custom-call(bf16[16,1152]{1,0:T(8,128)(2,1)S(1)} %shard_map.73.a0.a_near.refs_0_, bf16[16,1152]{1,0:T(8,128)(2,1)S(1)} %collective-permute-done.1.a2.a_pair.refs_1_, bf16[16,1152]{1,0:T(8,128)(2,1)S(1)} %collective-permute-done.5.b0.refs_2_, ...), custom_call_target="tpu_custom_call" | custom-call | tf_op jit(solution)/shard_map/pallas_call | solution.py:343
  24.4 0.0 collective-permute-done.9.y1
  24.5 1.5 %collective-permute-start.11 = (f32[16,128]{1,0:T(8,128)S(1)}, f32[16,128]{1,0:T(8,128)S(1)}, u32[]{:S(2)}, u32[]{:S(2)}) collective-permute-start(f32[16,128]{1,0:T(8,128)S(1)} %shard_map.80._.y0), channel_id=1, source_target_pairs={{0,192},{1,129},{2,194},{3,131},{4,196},{5,133},{6,198},{7,135},{8... | collective-permute-start | bytes 24584 | tf_op jit(solution)/shard_map/ppermute | solution.py:34
  26.0 0.9 %collective-permute-start.10 = (f32[16,128]{1,0:T(8,128)S(1)}, f32[16,128]{1,0:T(8,128)S(1)}, u32[]{:S(2)}, u32[]{:S(2)}) collective-permute-start(f32[16,128]{1,0:T(8,128)S(1)} %shard_map.80._.y0), channel_id=1, source_target_pairs={{0,64},{1,65},{2,66},{3,67},{4,68},{5,69},{6,70},{7,71},{8,72},{9,... | collective-permute-start | bytes 24584 | tf_op jit(solution)/shard_map/ppermute | solution.py:34
  26.9 3.9 %shard_map.81 = (f32[256,256]{1,0:T(8,128)S(1)}, f32[32,1536]{1,0:T(8,128)S(1)}) custom-call(bf16[544,2048]{1,0:T(8,128)(2,1)S(1)} %shard_map.79.__.lhs, f32[16,1536]{1,0:T(8,128)S(1)} %get-tuple-element.14.w_ref, bf16[2048,1536]{1,0:T(8,128)(2,1)S(1)} %bitcast.7, f32[16,128]{1,0:T(8,128)S(1)} %shard_map.80._.y0), custom_call_target="tpu_custom_call" | custom-call | flops 3221225472 | bytes 6291456 | tf_op jit(solution)/shard_map/pallas_call | solution.py:354
  30.8 0.0 collective-permute-done.11.y2
  30.8 0.0 collective-permute-done.10.y1
  30.8 0.3 collective-permute-start.12
  31.2 0.5 %shard_map.83.rows_ref = f32[16,128]{1,0:T(8,128)S(1)} custom-call(f32[256,256]{1,0:T(8,128)S(1)} %get-tuple-element.15._.acc, bf16[16,1152]{1,0:T(8,128)(2,1)S(1)} %shard_map.73.a0.a_near.refs_0_, bf16[16,1152]{1,0:T(8,128)(2,1)S(1)} %collective-permute-done.1.a2.a_pair.refs_1_, bf16[16,1152]{1,0:T(8,128)(2,1)S(1)} %collective-permute-done.5.b0.refs_2_, ...), custom_call_target="tpu_custom_call" | custom-call | tf_op jit(solution)/shard_map/pallas_call | solution.py:366
  31.7 0.3 collective-permute-start.16
  32.0 0.1 collective-permute-done.12.y1
  32.1 2.3 %collective-permute-start.13 = (f32[24,128]{1,0:T(8,128)S(1)}, f32[24,128]{1,0:T(8,128)S(1)}, u32[]{:S(2)}, u32[]{:S(2)}) collective-permute-start(f32[24,128]{1,0:T(8,128)S(1)} %get-tuple-element.17), channel_id=1, source_target_pairs={{0,4},{1,5},{2,6},{3,7},{4,0},{5,1},{6,2},{7,3},{8,12},{9,13},{10,... | collective-permute-start | bytes 36872 | tf_op jit(solution)/shard_map/ppermute | solution.py:34
  34.4 0.7 %collective-permute-start.14 = (f32[24,128]{1,0:T(8,128)S(1)}, f32[24,128]{1,0:T(8,128)S(1)}, u32[]{:S(2)}, u32[]{:S(2)}) collective-permute-start(f32[24,128]{1,0:T(8,128)S(1)} %get-tuple-element.18), channel_id=1, source_target_pairs={{0,2},{1,3},{2,0},{3,1},{4,6},{5,7},{6,4},{7,5},{8,10},{9,11},{10,... | collective-permute-start | bytes 36872 | tf_op jit(solution)/shard_map/ppermute | solution.py:34
  35.1 1.1 %collective-permute-start.15 = (f32[24,128]{1,0:T(8,128)S(1)}, f32[24,128]{1,0:T(8,128)S(1)}, u32[]{:S(2)}, u32[]{:S(2)}) collective-permute-start(f32[24,128]{1,0:T(8,128)S(1)} %get-tuple-element.19), channel_id=1, source_target_pairs={{0,6},{1,7},{2,4},{3,5},{4,2},{5,3},{6,0},{7,1},{8,14},{9,15},{10,... | collective-permute-start | bytes 36872 | tf_op jit(solution)/shard_map/ppermute | solution.py:34
  36.2 2.2 %collective-permute-start.17 = (f32[1,128]{1,0:T(1,128)S(1)}, f32[1,128]{1,0:T(1,128)S(1)}, u32[]{:S(2)}, u32[]{:S(2)}) collective-permute-start(f32[1,128]{1,0:T(1,128)S(1)} %slice.14), channel_id=1, source_target_pairs={{0,8},{1,9},{2,10},{3,11},{4,12},{5,13},{6,14},{7,15},{8,0},{9,1},... | collective-permute-start | bytes 1544 | tf_op jit(solution)/shard_map/ppermute | solution.py:34
  38.4 0.0 collective-permute-done.13
  38.4 0.0 collective-permute-done.14
  38.4 1.5 %collective-permute-done.15 = f32[24,128]{1,0:T(8,128)S(1)} collective-permute-done((f32[24,128]{1,0:T(8,128)S(1)}, f32[24,128]{1,0:T(8,128)S(1)}, u32[]{:S(2)}, u32[]{:S(2)}) %collective-permute-start.15) | collective-permute-done | bytes 12320 | tf_op jit(solution)/shard_map/ppermute | solution.py:34
  40.0 1.7 %collective-permute-start.18 = (f32[1,128]{1,0:T(1,128)S(1)}, f32[1,128]{1,0:T(1,128)S(1)}, u32[]{:S(2)}, u32[]{:S(2)}) collective-permute-start(f32[1,128]{1,0:T(1,128)S(1)} %slice.18), channel_id=1, source_target_pairs={{0,192},{1,193},{2,194},{3,195},{4,196},{5,197},{6,198},{7,199},{8... | collective-permute-start | bytes 1544 | tf_op jit(solution)/shard_map/ppermute | solution.py:34
  41.7 1.1 %shard_map.85.exchange_ref = f32[2,16]{1,0:T(2,128)S(1)} custom-call(f32[24,128]{1,0:T(8,128)S(1)} %add_add_fusion.y_ref, f32[1,1536]{1,0:T(1,128)S(1)} %reshape.19.source.c_ref, f32[32,1536]{1,0:T(8,128)S(1)} %get-tuple-element.20.rx_ref, bf16[2048,1536]{1,0:T(8,128)(2,1)S(1)} %bitcast.8), custom_call_target="tpu_custom_call" | custom-call | flops 805306368 | bytes 6291456 | tf_op jit(solution)/shard_map/pallas_call | solution.py:420
  42.7 1.0 %collective-permute-done.17.d_ref = f32[1,128]{1,0:T(1,128)S(1)} collective-permute-done((f32[1,128]{1,0:T(1,128)S(1)}, f32[1,128]{1,0:T(1,128)S(1)}, u32[]{:S(2)}, u32[]{:S(2)}) %collective-permute-start.17) | collective-permute-done | bytes 544 | tf_op jit(solution)/shard_map/ppermute | solution.py:34
  43.7 1.1 %collective-permute-done.18.h_ref = f32[1,128]{1,0:T(1,128)S(1)} collective-permute-done((f32[1,128]{1,0:T(1,128)S(1)}, f32[1,128]{1,0:T(1,128)S(1)}, u32[]{:S(2)}, u32[]{:S(2)}) %collective-permute-start.18) | collective-permute-done | bytes 544 | tf_op jit(solution)/shard_map/ppermute | solution.py:34
  44.8 0.6 %shard_map.86 = f32[2,16]{1,0:T(2,128)} custom-call(f32[1,16]{1,0:T(1,128)S(1)} %copy-done.1, f32[2,16]{1,0:T(2,128)S(1)} %bitcast.10, f32[2,16]{1,0:T(2,128)S(1)} %shard_map.85.exchange_ref, f32[2,128]{1,0:T(2,128)S(1)} %slice_add_fusion.near_ref, f32[1,128]{1,0:T(1,128)S(1)} %collective-permute-done.17.d_ref, f32[1,128]{1,0:T(1,128)S(1)} %collective-permute-done.18.h_ref), custom_call_target="tpu_custom_call" | custom-call | tf_op jit(solution)/shard_map/pallas_call | solution.py:366
  (23 shorter events, 0.1 us)
Async XLA Ops:
  1.0 8.6 %collective-permute-start.5 = (bf16[16,1152]{1,0:T(8,128)(2,1)S(1)}, bf16[16,1152]{1,0:T(8,128)(2,1)S(1)}, u32[]{:S(2)}, u32[]{:S(2)}) collective-permute-start(bf16[16,1152]{1,0:T(8,128)(2,1)S(1)} %shard_map.73.a0.a_near.refs_0_), channel_id=1, source_target_pairs={{0,64},{1,65},{2,66},{3,67},{4,68},{5,69},{6,70},{7,71},{8,72},{9,... | collective-permute-start | bytes 110600 | tf_op jit(solution)/shard_map/ppermute | solution.py:34
  3.2 10.5 %collective-permute-start = (bf16[16,1152]{1,0:T(8,128)(2,1)S(1)}, bf16[16,1152]{1,0:T(8,128)(2,1)S(1)}, u32[]{:S(2)}, u32[]{:S(2)}) collective-permute-start(bf16[16,1152]{1,0:T(8,128)(2,1)S(1)} %shard_map.73.a0.a_near.refs_0_), channel_id=1, source_target_pairs={{0,8},{1,9},{2,10},{3,11},{4,12},{5,13},{6,14},{7,15},{8,0},{9,1},... | collective-permute-start | bytes 110600 | tf_op jit(solution)/shard_map/ppermute | solution.py:34
  8.7 5.1 %collective-permute-start.1 = (bf16[16,1152]{1,0:T(8,128)(2,1)S(1)}, bf16[16,1152]{1,0:T(8,128)(2,1)S(1)}, u32[]{:S(2)}, u32[]{:S(2)}) collective-permute-start(bf16[16,1152]{1,0:T(8,128)(2,1)S(1)} %shard_map.73.a0.a_near.refs_0_), channel_id=1, source_target_pairs={{0,1},{1,0},{2,3},{3,2},{4,5},{5,4},{6,7},{7,6},{8,9},{9,8},{10,11... | collective-permute-start | bytes 110600 | tf_op jit(solution)/shard_map/ppermute | solution.py:34
  8.7 9.6 %slice-start = ((s8[6291456]{0:T(1024)(128)(4,1)}), s8[4194304]{0:T(1024)(128)(4,1)S(1)}, s32[]{:S(2)}) async-start(s8[6291456]{0:T(1024)(128)(4,1)} %bitcast.4), calls=%async_computation | async-start | bytes 8388608
  9.6 8.7 %slice-start.1 = ((s8[6291456]{0:T(1024)(128)(4,1)}), s8[2097152]{0:T(1024)(128)(4,1)S(1)}, s32[]{:S(2)}) async-start(s8[6291456]{0:T(1024)(128)(4,1)} %bitcast.4), calls=%async_computation.1 | async-start | bytes 4194304
  9.6 8.7 %copy-start.2 = (f32[256,1536]{1,0:T(8,128)S(1)}, f32[256,1536]{1,0:T(8,128)}, u32[]{:S(2)}) copy-start(f32[256,1536]{1,0:T(8,128)} %screening.1) | copy-start | bytes 4718596
  9.6 8.7 %copy-start.3 = (s32[1,256]{1,0:T(1,128)S(1)}, s32[1,256]{1,0:T(1,128)}, u32[]{:S(2)}) copy-start(s32[1,256]{1,0:T(1,128)} %qmap.1) | copy-start | bytes 3076
  9.6 7.7 %collective-permute-start.8 = (bf16[16,1152]{1,0:T(8,128)(2,1)S(1)}, bf16[16,1152]{1,0:T(8,128)(2,1)S(1)}, u32[]{:S(2)}, u32[]{:S(2)}) collective-permute-start(bf16[16,1152]{1,0:T(8,128)(2,1)S(1)} %collective-permute-done.5.b0.refs_2_), channel_id=1, source_target_pairs={{0,6},{1,7},{2,4},{3,5},{4,2},{5,3},{6,0},{7,1},{8,14},{9,15},{10,... | collective-permute-start | bytes 110600 | tf_op jit(solution)/shard_map/ppermute | solution.py:34
  12.7 5.6 %collective-permute-start.7 = (bf16[16,1152]{1,0:T(8,128)(2,1)S(1)}, bf16[16,1152]{1,0:T(8,128)(2,1)S(1)}, u32[]{:S(2)}, u32[]{:S(2)}) collective-permute-start(bf16[16,1152]{1,0:T(8,128)(2,1)S(1)} %collective-permute-done.5.b0.refs_2_), channel_id=1, source_target_pairs={{0,4},{1,5},{2,6},{3,7},{4,0},{5,1},{6,2},{7,3},{8,12},{9,13},{10,... | collective-permute-start | bytes 110600 | tf_op jit(solution)/shard_map/ppermute | solution.py:34
  13.3 5.0 %collective-permute-start.6 = (bf16[16,1152]{1,0:T(8,128)(2,1)S(1)}, bf16[16,1152]{1,0:T(8,128)(2,1)S(1)}, u32[]{:S(2)}, u32[]{:S(2)}) collective-permute-start(bf16[16,1152]{1,0:T(8,128)(2,1)S(1)} %collective-permute-done.5.b0.refs_2_), channel_id=1, source_target_pairs={{0,2},{1,3},{2,0},{3,1},{4,6},{5,7},{6,4},{7,5},{8,10},{9,11},{10,... | collective-permute-start | bytes 110600 | tf_op jit(solution)/shard_map/ppermute | solution.py:34
  13.8 1.2 %collective-permute-start.2 = (bf16[16,1152]{1,0:T(8,128)(2,1)S(1)}, bf16[16,1152]{1,0:T(8,128)(2,1)S(1)}, u32[]{:S(2)}, u32[]{:S(2)}) collective-permute-start(bf16[16,1152]{1,0:T(8,128)(2,1)S(1)} %collective-permute-done.a1.a_near.refs_0_), channel_id=1, source_target_pairs={{0,1},{1,0},{2,3},{3,2},{4,5},{5,4},{6,7},{7,6},{8,9},{9,8},{10,11... | collective-permute-start | bytes 110600 | tf_op jit(solution)/shard_map/ppermute | solution.py:34
  15.2 8.0 %collective-permute-start.4 = (f32[16,128]{1,0:T(8,128)S(1)}, f32[16,128]{1,0:T(8,128)S(1)}, u32[]{:S(2)}, u32[]{:S(2)}) collective-permute-start(f32[16,128]{1,0:T(8,128)S(1)} %shard_map.74.__.y0), channel_id=1, source_target_pairs={{0,48},{1,33},{2,50},{3,35},{4,52},{5,37},{6,54},{7,39},{8,56},{9,... | collective-permute-start | bytes 24584 | tf_op jit(solution)/shard_map/ppermute | solution.py:34
  17.2 6.0 %collective-permute-start.3 = (f32[16,128]{1,0:T(8,128)S(1)}, f32[16,128]{1,0:T(8,128)S(1)}, u32[]{:S(2)}, u32[]{:S(2)}) collective-permute-start(f32[16,128]{1,0:T(8,128)S(1)} %shard_map.74.__.y0), channel_id=1, source_target_pairs={{0,16},{1,17},{2,18},{3,19},{4,20},{5,21},{6,22},{7,23},{8,24},{9,... | collective-permute-start | bytes 24584 | tf_op jit(solution)/shard_map/ppermute | solution.py:34
  23.2 1.3 %collective-permute-start.9 = (f32[16,128]{1,0:T(8,128)S(1)}, f32[16,128]{1,0:T(8,128)S(1)}, u32[]{:S(2)}, u32[]{:S(2)}) collective-permute-start(f32[16,128]{1,0:T(8,128)S(1)} %shard_map.77.y0), channel_id=1, source_target_pairs={{0,1},{1,0},{2,3},{3,2},{4,5},{5,4},{6,7},{7,6},{8,9},{9,8},{10,11... | collective-permute-start | bytes 24584 | tf_op jit(solution)/shard_map/ppermute | solution.py:34
  24.5 6.4 %collective-permute-start.11 = (f32[16,128]{1,0:T(8,128)S(1)}, f32[16,128]{1,0:T(8,128)S(1)}, u32[]{:S(2)}, u32[]{:S(2)}) collective-permute-start(f32[16,128]{1,0:T(8,128)S(1)} %shard_map.80._.y0), channel_id=1, source_target_pairs={{0,192},{1,129},{2,194},{3,131},{4,196},{5,133},{6,198},{7,135},{8... | collective-permute-start | bytes 24584 | tf_op jit(solution)/shard_map/ppermute | solution.py:34
  26.0 4.8 %collective-permute-start.10 = (f32[16,128]{1,0:T(8,128)S(1)}, f32[16,128]{1,0:T(8,128)S(1)}, u32[]{:S(2)}, u32[]{:S(2)}) collective-permute-start(f32[16,128]{1,0:T(8,128)S(1)} %shard_map.80._.y0), channel_id=1, source_target_pairs={{0,64},{1,65},{2,66},{3,67},{4,68},{5,69},{6,70},{7,71},{8,72},{9,... | collective-permute-start | bytes 24584 | tf_op jit(solution)/shard_map/ppermute | solution.py:34
  30.8 1.3 %collective-permute-start.12 = (f32[16,128]{1,0:T(8,128)S(1)}, f32[16,128]{1,0:T(8,128)S(1)}, u32[]{:S(2)}, u32[]{:S(2)}) collective-permute-start(f32[16,128]{1,0:T(8,128)S(1)} %shard_map.82.y0), channel_id=1, source_target_pairs={{0,1},{1,0},{2,3},{3,2},{4,5},{5,4},{6,7},{7,6},{8,9},{9,8},{10,11... | collective-permute-start | bytes 24584 | tf_op jit(solution)/shard_map/ppermute | solution.py:34
  31.7 4.5 %collective-permute-start.16 = (f32[2,128]{1,0:T(2,128)S(1)}, f32[2,128]{1,0:T(2,128)S(1)}, u32[]{:S(2)}, u32[]{:S(2)}) collective-permute-start(f32[2,128]{1,0:T(2,128)S(1)} %slice.17), channel_id=1, source_target_pairs={{0,1},{1,0},{2,3},{3,2},{4,5},{5,4},{6,7},{7,6},{8,9},{9,8},{10,11... | collective-permute-start | bytes 3080 | tf_op jit(solution)/shard_map/ppermute | solution.py:34
  32.1 6.3 %collective-permute-start.13 = (f32[24,128]{1,0:T(8,128)S(1)}, f32[24,128]{1,0:T(8,128)S(1)}, u32[]{:S(2)}, u32[]{:S(2)}) collective-permute-start(f32[24,128]{1,0:T(8,128)S(1)} %get-tuple-element.17), channel_id=1, source_target_pairs={{0,4},{1,5},{2,6},{3,7},{4,0},{5,1},{6,2},{7,3},{8,12},{9,13},{10,... | collective-permute-start | bytes 36872 | tf_op jit(solution)/shard_map/ppermute | solution.py:34
  34.4 4.0 %collective-permute-start.14 = (f32[24,128]{1,0:T(8,128)S(1)}, f32[24,128]{1,0:T(8,128)S(1)}, u32[]{:S(2)}, u32[]{:S(2)}) collective-permute-start(f32[24,128]{1,0:T(8,128)S(1)} %get-tuple-element.18), channel_id=1, source_target_pairs={{0,2},{1,3},{2,0},{3,1},{4,6},{5,7},{6,4},{7,5},{8,10},{9,11},{10,... | collective-permute-start | bytes 36872 | tf_op jit(solution)/shard_map/ppermute | solution.py:34
  35.1 4.9 %collective-permute-start.15 = (f32[24,128]{1,0:T(8,128)S(1)}, f32[24,128]{1,0:T(8,128)S(1)}, u32[]{:S(2)}, u32[]{:S(2)}) collective-permute-start(f32[24,128]{1,0:T(8,128)S(1)} %get-tuple-element.19), channel_id=1, source_target_pairs={{0,6},{1,7},{2,4},{3,5},{4,2},{5,3},{6,0},{7,1},{8,14},{9,15},{10,... | collective-permute-start | bytes 36872 | tf_op jit(solution)/shard_map/ppermute | solution.py:34
  36.2 7.5 %collective-permute-start.17 = (f32[1,128]{1,0:T(1,128)S(1)}, f32[1,128]{1,0:T(1,128)S(1)}, u32[]{:S(2)}, u32[]{:S(2)}) collective-permute-start(f32[1,128]{1,0:T(1,128)S(1)} %slice.14), channel_id=1, source_target_pairs={{0,8},{1,9},{2,10},{3,11},{4,12},{5,13},{6,14},{7,15},{8,0},{9,1},... | collective-permute-start | bytes 1544 | tf_op jit(solution)/shard_map/ppermute | solution.py:34
  40.0 4.8 %collective-permute-start.18 = (f32[1,128]{1,0:T(1,128)S(1)}, f32[1,128]{1,0:T(1,128)S(1)}, u32[]{:S(2)}, u32[]{:S(2)}) collective-permute-start(f32[1,128]{1,0:T(1,128)S(1)} %slice.18), channel_id=1, source_target_pairs={{0,192},{1,193},{2,194},{3,195},{4,196},{5,197},{6,198},{7,199},{8... | collective-permute-start | bytes 1544 | tf_op jit(solution)/shard_map/ppermute | solution.py:34
  41.7 3.1 %copy-start = (f32[1,2,16]{2,1,0:T(2,128)S(1)}, f32[1,2,16]{2,1,0:T(2,128)}, u32[]{:S(2)}) copy-start(f32[1,2,16]{2,1,0:T(2,128)} %param.8) | copy-start | bytes 388
  41.7 3.1 %copy-start.1 = (f32[1,16]{1,0:T(1,128)S(1)}, f32[1,16]{1,0:T(1,128)}, u32[]{:S(2)}) copy-start(f32[1,16]{1,0:T(1,128)} %energy_ref.1) | copy-start | bytes 196

commit v13 on v11

--- a/solution.py
+++ b/solution.py
@@ -105,7 +105,11 @@
     copies[1].wait()
 
 
-def weights_kernel(qmap_ref, screening, w_ref, sems):
+def place_kernel(_, out_ref):
+    out_ref[...] = jnp.zeros((8, 128), F32)
+
+
+def weights_kernel(qmap_ref, screening, _, w_ref, sems):
     own = lax.axis_index("grp")
     member = lax.axis_index("kin")
     partner = (own + 12) & 15
@@ -372,15 +376,23 @@
     b0 = move(pay, step=1)
     a2 = move(pay, core=1)
     z = basis.reshape(2 * NMU, NG)
+    place = pl.pallas_call(
+        place_kernel,
+        in_specs=[ANY],
+        out_specs=VMEM,
+        out_shape=jax.ShapeDtypeStruct((8, 128), F32),
+        compiler_params=params(8),
+        cost_estimate=pl.CostEstimate(flops=4000000000, bytes_accessed=1024, transcendentals=0),
+    )(b0)
     weights = pl.pallas_call(
         weights_kernel,
-        in_specs=[SMEM, ANY],
+        in_specs=[SMEM, ANY, ANY],
         out_specs=VMEM,
         out_shape=pltpu.VMEM((16, NG), F32),
         scratch_shapes=[pltpu.SemaphoreType.DMA((16,))],
-        compiler_params=params(54),
+        compiler_params=params(16),
         cost_estimate=pl.CostEstimate(flops=4000000000, bytes_accessed=1024, transcendentals=0),
-    )(qmap, screening)
+    )(qmap, screening, place)
     b1, b2, b3 = (move(b0, y=n) for n in (1, 2, 3))
     a3 = move(a1, core=1)
     y = pl.pallas_call(

time: 46.6 us -> 46 us (0.987)
  Pallas kernels: 14.3 us -> 13.3 us
    pallas_call x1 -> x2, Pallas kernels: 1.74 us -> 0.96 us  [the longest x1 0.96 us: on_device(): pl.pallas_call(weights_kernel, in_specs=[SMEM, ANY, ANY], out_specs=VMEM,...]
  transfers between devices with their start and end apart: 19 -> 19, of which waited for: 5 -> 7; matrix products, arithmetic and copies ran while one was open for 0% -> 0% of each run, Pallas kernels for 27% -> 26%
where the time goes in v13:
time: 46 us; the launch traced here: 45.9 us
  starting transfers between devices  27.2 us (59%)
  Pallas kernels  13.3 us (29%)
  waiting for transfers between devices  5.03 us (11%)
    ppermute x19, starting transfers between devices, move(): return lax.ppermute(value, ('grp', 'kin'), pairs)  27.2 us
    ppermute x19, waiting for transfers between devices, move(): return lax.ppermute(value, ('grp', 'kin'), pairs)  5.03 us
    pallas_call x1, Pallas kernels, far_call(): pl.pallas_call(far_kernel, in_specs=[VMEM] * 8 + [ANY], out_specs=VMEM, o...  4.03 us
    pallas_call x1, Pallas kernels, near_call(): pl.pallas_call(near_kernel, in_specs=[VMEM] * 3 + [ANY], out_specs=[VMEM]...  3.91 us
    pallas_call x7, Pallas kernels, small_call(): pl.pallas_call(kernel, in_specs=[VMEM] * len(operands) + [ANY] * len(afte...  1.66 us
    pallas_call x1, Pallas kernels, on_device(): pl.pallas_call(exchange_kernel, in_specs=[VMEM] * 4, out_specs=VMEM, out_...  1.07 us
    pallas_call x1, Pallas kernels, on_device(): pl.pallas_call(weights_kernel, in_specs=[SMEM, ANY, ANY], out_specs=VMEM,...  0.96 us
    pallas_call x1, Pallas kernels, on_device(): pl.pallas_call(pack_kernel, in_specs=[ANY] * 2, out_specs=VMEM, out_shape...  0.95 us
  transfers between devices with their start and end apart: 19, of which 7 were waited for; matrix products, arithmetic and copies ran while one was open for 0% of the time, Pallas kernels for 26%

profile of v13, /device:TPU:6, one launch (start us, length us, event | category | flops | bytes accessed | tf_op | source)
XLA Modules:
  0.0 45.9 jit_solution(4972408892785291274)
XLA Ops:
  0.0 0.9 %shard_map.73.a0.a_near.refs_0_ = bf16[16,1152]{1,0:T(8,128)(2,1)S(1)} custom-call(bf16[16,1024]{1,0:T(8,128)(2,1)} %bitcast.11, f32[2,16]{1,0:T(2,128)} %bitcast.9), custom_call_target="tpu_custom_call" | custom-call | tf_op jit(solution)/shard_map/pallas_call | solution.py:367
  1.0 0.0 copy-start.2
  1.0 0.0 copy-start.3
  1.0 2.3 %collective-permute-start.5 = (bf16[16,1152]{1,0:T(8,128)(2,1)S(1)}, bf16[16,1152]{1,0:T(8,128)(2,1)S(1)}, u32[]{:S(2)}, u32[]{:S(2)}) collective-permute-start(bf16[16,1152]{1,0:T(8,128)(2,1)S(1)} %shard_map.73.a0.a_near.refs_0_), channel_id=1, source_target_pairs={{0,64},{1,65},{2,66},{3,67},{4,68},{5,69},{6,70},{7,71},{8,72},{9,... | collective-permute-start | bytes 110600 | tf_op jit(solution)/shard_map/ppermute | solution.py:34
  3.3 5.5 %collective-permute-start = (bf16[16,1152]{1,0:T(8,128)(2,1)S(1)}, bf16[16,1152]{1,0:T(8,128)(2,1)S(1)}, u32[]{:S(2)}, u32[]{:S(2)}) collective-permute-start(bf16[16,1152]{1,0:T(8,128)(2,1)S(1)} %shard_map.73.a0.a_near.refs_0_), channel_id=1, source_target_pairs={{0,8},{1,9},{2,10},{3,11},{4,12},{5,13},{6,14},{7,15},{8,0},{9,1},... | collective-permute-start | bytes 110600 | tf_op jit(solution)/shard_map/ppermute | solution.py:34
  8.7 0.0 collective-permute-start.1
  8.7 0.0 collective-permute-done.5._.b0.refs_2_
  8.7 1.6 %collective-permute-start.6 = (bf16[16,1152]{1,0:T(8,128)(2,1)S(1)}, bf16[16,1152]{1,0:T(8,128)(2,1)S(1)}, u32[]{:S(2)}, u32[]{:S(2)}) collective-permute-start(bf16[16,1152]{1,0:T(8,128)(2,1)S(1)} %collective-permute-done.5._.b0.refs_2_), channel_id=1, source_target_pairs={{0,2},{1,3},{2,0},{3,1},{4,6},{5,7},{6,4},{7,5},{8,10},{9,11},{10,... | collective-permute-start | bytes 110600 | tf_op jit(solution)/shard_map/ppermute | solution.py:34
  10.3 2.9 %collective-permute-start.7 = (bf16[16,1152]{1,0:T(8,128)(2,1)S(1)}, bf16[16,1152]{1,0:T(8,128)(2,1)S(1)}, u32[]{:S(2)}, u32[]{:S(2)}) collective-permute-start(bf16[16,1152]{1,0:T(8,128)(2,1)S(1)} %collective-permute-done.5._.b0.refs_2_), channel_id=1, source_target_pairs={{0,4},{1,5},{2,6},{3,7},{4,0},{5,1},{6,2},{7,3},{8,12},{9,13},{10,... | collective-permute-start | bytes 110600 | tf_op jit(solution)/shard_map/ppermute | solution.py:34
  13.2 0.2 collective-permute-start.8
  13.4 0.0 collective-permute-done.a1.a_near.refs_0_
  13.4 0.1 collective-permute-start.2
  13.6 1.0 %shard_map.76.w_ref = f32[16,1536]{1,0:T(8,128)S(1)} custom-call(s32[1,256]{1,0:T(1,128)S(1)} %copy-done.3, f32[256,1536]{1,0:T(8,128)S(1)} %copy-done.2, f32[8,128]{1,0:T(8,128)S(1)} %shard_map.75._), custom_call_target="tpu_custom_call" | custom-call | flops 4000000000 | bytes 1024 | tf_op jit(solution)/shard_map/pallas_call | solution.py:387
  14.5 0.0 collective-permute-done.1.a2.a_pair.refs_1_
  14.5 0.2 collective-permute-done.2.a3.a_pair.refs_1_
  14.7 0.2 shard_map.74._.y0
  14.9 1.1 %collective-permute-start.3 = (f32[16,128]{1,0:T(8,128)S(1)}, f32[16,128]{1,0:T(8,128)S(1)}, u32[]{:S(2)}, u32[]{:S(2)}) collective-permute-start(f32[16,128]{1,0:T(8,128)S(1)} %shard_map.74._.y0), channel_id=1, source_target_pairs={{0,16},{1,17},{2,18},{3,19},{4,20},{5,21},{6,22},{7,23},{8,24},{9,... | collective-permute-start | bytes 24584 | tf_op jit(solution)/shard_map/ppermute | solution.py:34
  16.0 1.9 %collective-permute-start.4 = (f32[16,128]{1,0:T(8,128)S(1)}, f32[16,128]{1,0:T(8,128)S(1)}, u32[]{:S(2)}, u32[]{:S(2)}) collective-permute-start(f32[16,128]{1,0:T(8,128)S(1)} %shard_map.74._.y0), channel_id=1, source_target_pairs={{0,48},{1,33},{2,50},{3,35},{4,52},{5,37},{6,54},{7,39},{8,56},{9,... | collective-permute-start | bytes 24584 | tf_op jit(solution)/shard_map/ppermute | solution.py:34
  18.0 0.0 collective-permute-done.6.b1.refs_3_
  18.0 0.0 collective-permute-done.7.b2.refs_4_
  18.0 0.4 collective-permute-done.8.b3.refs_5_
  18.4 4.0 %shard_map.77._.acc.refs_0_ = f32[256,256]{1,0:T(8,128)S(1)} custom-call(bf16[16,1152]{1,0:T(8,128)(2,1)S(1)} %collective-permute-done.a1.a_near.refs_0_, bf16[16,1152]{1,0:T(8,128)(2,1)S(1)} %collective-permute-done.2.a3.a_pair.refs_1_, bf16[16,1152]{1,0:T(8,128)(2,1)S(1)} %collective-permute-done.5._.b0.refs_2_, ...), custom_call_target="tpu_custom_call" | custom-call | flops 3221225472 | bytes 6291456 | tf_op jit(solution)/shard_map/pallas_call | solution.py:322
  22.4 0.0 collective-permute-done.3.y1
  22.4 0.0 collective-permute-done.4.y2
  22.5 0.1 collective-permute-start.9
  22.6 0.6 %shard_map.80.__.lhs = bf16[544,2048]{1,0:T(8,128)(2,1)S(1)} custom-call(bf16[16,1152]{1,0:T(8,128)(2,1)S(1)} %shard_map.73.a0.a_near.refs_0_, bf16[16,1152]{1,0:T(8,128)(2,1)S(1)} %collective-permute-done.1.a2.a_pair.refs_1_, bf16[16,1152]{1,0:T(8,128)(2,1)S(1)} %collective-permute-done.5._.b0.refs_2_, ...), custom_call_target="tpu_custom_call" | custom-call | tf_op jit(solution)/shard_map/pallas_call | solution.py:334
  23.2 0.5 %shard_map.79._.refs_6_ = f32[16,128]{1,0:T(8,128)S(1)} custom-call(f32[256,256]{1,0:T(8,128)S(1)} %shard_map.77._.acc.refs_0_, bf16[16,1152]{1,0:T(8,128)(2,1)S(1)} %collective-permute-done.a1.a_near.refs_0_, bf16[16,1152]{1,0:T(8,128)(2,1)S(1)} %collective-permute-done.2.a3.a_pair.refs_1_, bf16[16,1152]{1,0:T(8,128)(2,1)S(1)} %collective-permute-done.5._.b0.refs_2_, ...), custom_call_target="tpu_custom_call" | custom-call | tf_op jit(solution)/shard_map/pallas_call | solution.py:357
  23.7 0.1 collective-permute-done.9.y1
  23.7 1.6 %collective-permute-start.10 = (f32[16,128]{1,0:T(8,128)S(1)}, f32[16,128]{1,0:T(8,128)S(1)}, u32[]{:S(2)}, u32[]{:S(2)}) collective-permute-start(f32[16,128]{1,0:T(8,128)S(1)} %shard_map.81._.y0), channel_id=1, source_target_pairs={{0,64},{1,65},{2,66},{3,67},{4,68},{5,69},{6,70},{7,71},{8,72},{9,... | collective-permute-start | bytes 24584 | tf_op jit(solution)/shard_map/ppermute | solution.py:34
  25.3 1.4 %collective-permute-start.11 = (f32[16,128]{1,0:T(8,128)S(1)}, f32[16,128]{1,0:T(8,128)S(1)}, u32[]{:S(2)}, u32[]{:S(2)}) collective-permute-start(f32[16,128]{1,0:T(8,128)S(1)} %shard_map.81._.y0), channel_id=1, source_target_pairs={{0,192},{1,129},{2,194},{3,131},{4,196},{5,133},{6,198},{7,135},{8... | collective-permute-start | bytes 24584 | tf_op jit(solution)/shard_map/ppermute | solution.py:34
  26.8 3.9 %shard_map.82 = (f32[256,256]{1,0:T(8,128)S(1)}, f32[32,1536]{1,0:T(8,128)S(1)}) custom-call(bf16[544,2048]{1,0:T(8,128)(2,1)S(1)} %shard_map.80.__.lhs, f32[16,1536]{1,0:T(8,128)S(1)} %shard_map.76.w_ref, bf16[2048,1536]{1,0:T(8,128)(2,1)S(1)} %bitcast.7, f32[16,128]{1,0:T(8,128)S(1)} %shard_map.81._.y0), custom_call_target="tpu_custom_call" | custom-call | flops 3221225472 | bytes 6291456 | tf_op jit(solution)/shard_map/pallas_call | solution.py:345
  30.7 0.0 collective-permute-done.11.y2
  30.7 0.1 collective-permute-start.12
  30.8 0.5 %shard_map.84.rows_ref = f32[16,128]{1,0:T(8,128)S(1)} custom-call(f32[256,256]{1,0:T(8,128)S(1)} %get-tuple-element.11._.acc, bf16[16,1152]{1,0:T(8,128)(2,1)S(1)} %shard_map.73.a0.a_near.refs_0_, bf16[16,1152]{1,0:T(8,128)(2,1)S(1)} %collective-permute-done.1.a2.a_pair.refs_1_, bf16[16,1152]{1,0:T(8,128)(2,1)S(1)} %collective-permute-done.5._.b0.refs_2_, ...), custom_call_target="tpu_custom_call" | custom-call | tf_op jit(solution)/shard_map/pallas_call | solution.py:357
  31.3 0.5 %collective-permute-start.16 = (f32[2,128]{1,0:T(2,128)S(1)}, f32[2,128]{1,0:T(2,128)S(1)}, u32[]{:S(2)}, u32[]{:S(2)}) collective-permute-start(f32[2,128]{1,0:T(2,128)S(1)} %slice.17), channel_id=1, source_target_pairs={{0,1},{1,0},{2,3},{3,2},{4,5},{5,4},{6,7},{7,6},{8,9},{9,8},{10,11... | collective-permute-start | bytes 3080 | tf_op jit(solution)/shard_map/ppermute | solution.py:34
  31.9 0.1 collective-permute-done.12.y1
  32.0 1.6 %collective-permute-start.13 = (f32[24,128]{1,0:T(8,128)S(1)}, f32[24,128]{1,0:T(8,128)S(1)}, u32[]{:S(2)}, u32[]{:S(2)}) collective-permute-start(f32[24,128]{1,0:T(8,128)S(1)} %get-tuple-element.13), channel_id=1, source_target_pairs={{0,4},{1,5},{2,6},{3,7},{4,0},{5,1},{6,2},{7,3},{8,12},{9,13},{10,... | collective-permute-start | bytes 36872 | tf_op jit(solution)/shard_map/ppermute | solution.py:34
  33.6 1.9 %collective-permute-start.14 = (f32[24,128]{1,0:T(8,128)S(1)}, f32[24,128]{1,0:T(8,128)S(1)}, u32[]{:S(2)}, u32[]{:S(2)}) collective-permute-start(f32[24,128]{1,0:T(8,128)S(1)} %get-tuple-element.14), channel_id=1, source_target_pairs={{0,2},{1,3},{2,0},{3,1},{4,6},{5,7},{6,4},{7,5},{8,10},{9,11},{10,... | collective-permute-start | bytes 36872 | tf_op jit(solution)/shard_map/ppermute | solution.py:34
  35.5 0.6 %collective-permute-start.15 = (f32[24,128]{1,0:T(8,128)S(1)}, f32[24,128]{1,0:T(8,128)S(1)}, u32[]{:S(2)}, u32[]{:S(2)}) collective-permute-start(f32[24,128]{1,0:T(8,128)S(1)} %get-tuple-element.15), channel_id=1, source_target_pairs={{0,6},{1,7},{2,4},{3,5},{4,2},{5,3},{6,0},{7,1},{8,14},{9,15},{10,... | collective-permute-start | bytes 36872 | tf_op jit(solution)/shard_map/ppermute | solution.py:34
  36.1 3.3 %collective-permute-start.17 = (f32[1,128]{1,0:T(1,128)S(1)}, f32[1,128]{1,0:T(1,128)S(1)}, u32[]{:S(2)}, u32[]{:S(2)}) collective-permute-start(f32[1,128]{1,0:T(1,128)S(1)} %slice.14), channel_id=1, source_target_pairs={{0,8},{1,9},{2,10},{3,11},{4,12},{5,13},{6,14},{7,15},{8,0},{9,1},... | collective-permute-start | bytes 1544 | tf_op jit(solution)/shard_map/ppermute | solution.py:34
  39.4 0.0 collective-permute-done.13
  39.4 0.0 collective-permute-done.14
  39.4 1.0 %collective-permute-done.15 = f32[24,128]{1,0:T(8,128)S(1)} collective-permute-done((f32[24,128]{1,0:T(8,128)S(1)}, f32[24,128]{1,0:T(8,128)S(1)}, u32[]{:S(2)}, u32[]{:S(2)}) %collective-permute-start.15) | collective-permute-done | bytes 12320 | tf_op jit(solution)/shard_map/ppermute | solution.py:34
  40.4 0.5 %collective-permute-start.18 = (f32[1,128]{1,0:T(1,128)S(1)}, f32[1,128]{1,0:T(1,128)S(1)}, u32[]{:S(2)}, u32[]{:S(2)}) collective-permute-start(f32[1,128]{1,0:T(1,128)S(1)} %slice.18), channel_id=1, source_target_pairs={{0,192},{1,193},{2,194},{3,195},{4,196},{5,197},{6,198},{7,199},{8... | collective-permute-start | bytes 1544 | tf_op jit(solution)/shard_map/ppermute | solution.py:34
  40.9 1.1 %shard_map.86.exchange_ref = f32[2,16]{1,0:T(2,128)S(1)} custom-call(f32[24,128]{1,0:T(8,128)S(1)} %add_add_fusion.y_ref, f32[1,1536]{1,0:T(1,128)S(1)} %reshape.19.c_ref, f32[32,1536]{1,0:T(8,128)S(1)} %get-tuple-element.16.rx_ref, bf16[2048,1536]{1,0:T(8,128)(2,1)S(1)} %bitcast.8), custom_call_target="tpu_custom_call" | custom-call | flops 805306368 | bytes 6291456 | tf_op jit(solution)/shard_map/pallas_call | solution.py:419
  42.0 1.7 %collective-permute-done.17.d_ref = f32[1,128]{1,0:T(1,128)S(1)} collective-permute-done((f32[1,128]{1,0:T(1,128)S(1)}, f32[1,128]{1,0:T(1,128)S(1)}, u32[]{:S(2)}, u32[]{:S(2)}) %collective-permute-start.17) | collective-permute-done | bytes 544 | tf_op jit(solution)/shard_map/ppermute | solution.py:34
  43.6 1.6 %collective-permute-done.18.h_ref = f32[1,128]{1,0:T(1,128)S(1)} collective-permute-done((f32[1,128]{1,0:T(1,128)S(1)}, f32[1,128]{1,0:T(1,128)S(1)}, u32[]{:S(2)}, u32[]{:S(2)}) %collective-permute-start.18) | collective-permute-done | bytes 544 | tf_op jit(solution)/shard_map/ppermute | solution.py:34
  45.2 0.6 %shard_map.87 = f32[2,16]{1,0:T(2,128)} custom-call(f32[1,16]{1,0:T(1,128)S(1)} %copy-done.1, f32[2,16]{1,0:T(2,128)S(1)} %bitcast.10, f32[2,16]{1,0:T(2,128)S(1)} %shard_map.86.exchange_ref, f32[2,128]{1,0:T(2,128)S(1)} %slice_add_fusion.near_ref, f32[1,128]{1,0:T(1,128)S(1)} %collective-permute-done.17.d_ref, f32[1,128]{1,0:T(1,128)S(1)} %collective-permute-done.18.h_ref), custom_call_target="tpu_custom_call" | custom-call | tf_op jit(solution)/shard_map/pallas_call | solution.py:357
  (26 shorter events, 0.1 us)
Async XLA Ops:
  1.0 12.6 %copy-start.2 = (f32[256,1536]{1,0:T(8,128)S(1)}, f32[256,1536]{1,0:T(8,128)}, u32[]{:S(2)}) copy-start(f32[256,1536]{1,0:T(8,128)} %screening.1) | copy-start | bytes 4718596
  1.0 12.6 %copy-start.3 = (s32[1,256]{1,0:T(1,128)S(1)}, s32[1,256]{1,0:T(1,128)}, u32[]{:S(2)}) copy-start(s32[1,256]{1,0:T(1,128)} %qmap_ref.1) | copy-start | bytes 3076
  1.0 7.8 %collective-permute-start.5 = (bf16[16,1152]{1,0:T(8,128)(2,1)S(1)}, bf16[16,1152]{1,0:T(8,128)(2,1)S(1)}, u32[]{:S(2)}, u32[]{:S(2)}) collective-permute-start(bf16[16,1152]{1,0:T(8,128)(2,1)S(1)} %shard_map.73.a0.a_near.refs_0_), channel_id=1, source_target_pairs={{0,64},{1,65},{2,66},{3,67},{4,68},{5,69},{6,70},{7,71},{8,72},{9,... | collective-permute-start | bytes 110600 | tf_op jit(solution)/shard_map/ppermute | solution.py:34
  3.3 10.2 %collective-permute-start = (bf16[16,1152]{1,0:T(8,128)(2,1)S(1)}, bf16[16,1152]{1,0:T(8,128)(2,1)S(1)}, u32[]{:S(2)}, u32[]{:S(2)}) collective-permute-start(bf16[16,1152]{1,0:T(8,128)(2,1)S(1)} %shard_map.73.a0.a_near.refs_0_), channel_id=1, source_target_pairs={{0,8},{1,9},{2,10},{3,11},{4,12},{5,13},{6,14},{7,15},{8,0},{9,1},... | collective-permute-start | bytes 110600 | tf_op jit(solution)/shard_map/ppermute | solution.py:34
  8.7 5.8 %collective-permute-start.1 = (bf16[16,1152]{1,0:T(8,128)(2,1)S(1)}, bf16[16,1152]{1,0:T(8,128)(2,1)S(1)}, u32[]{:S(2)}, u32[]{:S(2)}) collective-permute-start(bf16[16,1152]{1,0:T(8,128)(2,1)S(1)} %shard_map.73.a0.a_near.refs_0_), channel_id=1, source_target_pairs={{0,1},{1,0},{2,3},{3,2},{4,5},{5,4},{6,7},{7,6},{8,9},{9,8},{10,11... | collective-permute-start | bytes 110600 | tf_op jit(solution)/shard_map/ppermute | solution.py:34
  8.7 9.2 %collective-permute-start.6 = (bf16[16,1152]{1,0:T(8,128)(2,1)S(1)}, bf16[16,1152]{1,0:T(8,128)(2,1)S(1)}, u32[]{:S(2)}, u32[]{:S(2)}) collective-permute-start(bf16[16,1152]{1,0:T(8,128)(2,1)S(1)} %collective-permute-done.5._.b0.refs_2_), channel_id=1, source_target_pairs={{0,2},{1,3},{2,0},{3,1},{4,6},{5,7},{6,4},{7,5},{8,10},{9,11},{10,... | collective-permute-start | bytes 110600 | tf_op jit(solution)/shard_map/ppermute | solution.py:34
  10.3 7.7 %collective-permute-start.7 = (bf16[16,1152]{1,0:T(8,128)(2,1)S(1)}, bf16[16,1152]{1,0:T(8,128)(2,1)S(1)}, u32[]{:S(2)}, u32[]{:S(2)}) collective-permute-start(bf16[16,1152]{1,0:T(8,128)(2,1)S(1)} %collective-permute-done.5._.b0.refs_2_), channel_id=1, source_target_pairs={{0,4},{1,5},{2,6},{3,7},{4,0},{5,1},{6,2},{7,3},{8,12},{9,13},{10,... | collective-permute-start | bytes 110600 | tf_op jit(solution)/shard_map/ppermute | solution.py:34
  13.2 5.2 %collective-permute-start.8 = (bf16[16,1152]{1,0:T(8,128)(2,1)S(1)}, bf16[16,1152]{1,0:T(8,128)(2,1)S(1)}, u32[]{:S(2)}, u32[]{:S(2)}) collective-permute-start(bf16[16,1152]{1,0:T(8,128)(2,1)S(1)} %collective-permute-done.5._.b0.refs_2_), channel_id=1, source_target_pairs={{0,6},{1,7},{2,4},{3,5},{4,2},{5,3},{6,0},{7,1},{8,14},{9,15},{10,... | collective-permute-start | bytes 110600 | tf_op jit(solution)/shard_map/ppermute | solution.py:34
  13.4 4.9 %slice-start = ((s8[6291456]{0:T(1024)(128)(4,1)}), s8[4194304]{0:T(1024)(128)(4,1)S(1)}, s32[]{:S(2)}) async-start(s8[6291456]{0:T(1024)(128)(4,1)} %bitcast.4), calls=%async_computation | async-start | bytes 8388608
  13.4 4.9 %slice-start.1 = ((s8[6291456]{0:T(1024)(128)(4,1)}), s8[2097152]{0:T(1024)(128)(4,1)S(1)}, s32[]{:S(2)}) async-start(s8[6291456]{0:T(1024)(128)(4,1)} %bitcast.4), calls=%async_computation.1 | async-start | bytes 4194304
  13.4 1.3 %collective-permute-start.2 = (bf16[16,1152]{1,0:T(8,128)(2,1)S(1)}, bf16[16,1152]{1,0:T(8,128)(2,1)S(1)}, u32[]{:S(2)}, u32[]{:S(2)}) collective-permute-start(bf16[16,1152]{1,0:T(8,128)(2,1)S(1)} %collective-permute-done.a1.a_near.refs_0_), channel_id=1, source_target_pairs={{0,1},{1,0},{2,3},{3,2},{4,5},{5,4},{6,7},{7,6},{8,9},{9,8},{10,11... | collective-permute-start | bytes 110600 | tf_op jit(solution)/shard_map/ppermute | solution.py:34
  14.9 7.5 %collective-permute-start.3 = (f32[16,128]{1,0:T(8,128)S(1)}, f32[16,128]{1,0:T(8,128)S(1)}, u32[]{:S(2)}, u32[]{:S(2)}) collective-permute-start(f32[16,128]{1,0:T(8,128)S(1)} %shard_map.74._.y0), channel_id=1, source_target_pairs={{0,16},{1,17},{2,18},{3,19},{4,20},{5,21},{6,22},{7,23},{8,24},{9,... | collective-permute-start | bytes 24584 | tf_op jit(solution)/shard_map/ppermute | solution.py:34
  16.0 6.4 %collective-permute-start.4 = (f32[16,128]{1,0:T(8,128)S(1)}, f32[16,128]{1,0:T(8,128)S(1)}, u32[]{:S(2)}, u32[]{:S(2)}) collective-permute-start(f32[16,128]{1,0:T(8,128)S(1)} %shard_map.74._.y0), channel_id=1, source_target_pairs={{0,48},{1,33},{2,50},{3,35},{4,52},{5,37},{6,54},{7,39},{8,56},{9,... | collective-permute-start | bytes 24584 | tf_op jit(solution)/shard_map/ppermute | solution.py:34
  22.5 1.3 %collective-permute-start.9 = (f32[16,128]{1,0:T(8,128)S(1)}, f32[16,128]{1,0:T(8,128)S(1)}, u32[]{:S(2)}, u32[]{:S(2)}) collective-permute-start(f32[16,128]{1,0:T(8,128)S(1)} %shard_map.78.y0), channel_id=1, source_target_pairs={{0,1},{1,0},{2,3},{3,2},{4,5},{5,4},{6,7},{7,6},{8,9},{9,8},{10,11... | collective-permute-start | bytes 24584 | tf_op jit(solution)/shard_map/ppermute | solution.py:34
  23.7 8.1 %copy-start.4 = (f32[1536]{0:T(1024)S(1)}, f32[1536]{0:T(1024)}, u32[]{:S(2)}) copy-start(f32[1536]{0:T(1024)} %param.12) | copy-start | bytes 18436
  23.7 7.0 %collective-permute-start.10 = (f32[16,128]{1,0:T(8,128)S(1)}, f32[16,128]{1,0:T(8,128)S(1)}, u32[]{:S(2)}, u32[]{:S(2)}) collective-permute-start(f32[16,128]{1,0:T(8,128)S(1)} %shard_map.81._.y0), channel_id=1, source_target_pairs={{0,64},{1,65},{2,66},{3,67},{4,68},{5,69},{6,70},{7,71},{8,72},{9,... | collective-permute-start | bytes 24584 | tf_op jit(solution)/shard_map/ppermute | solution.py:34
  25.3 5.4 %collective-permute-start.11 = (f32[16,128]{1,0:T(8,128)S(1)}, f32[16,128]{1,0:T(8,128)S(1)}, u32[]{:S(2)}, u32[]{:S(2)}) collective-permute-start(f32[16,128]{1,0:T(8,128)S(1)} %shard_map.81._.y0), channel_id=1, source_target_pairs={{0,192},{1,129},{2,194},{3,131},{4,196},{5,133},{6,198},{7,135},{8... | collective-permute-start | bytes 24584 | tf_op jit(solution)/shard_map/ppermute | solution.py:34
  30.7 1.3 %collective-permute-start.12 = (f32[16,128]{1,0:T(8,128)S(1)}, f32[16,128]{1,0:T(8,128)S(1)}, u32[]{:S(2)}, u32[]{:S(2)}) collective-permute-start(f32[16,128]{1,0:T(8,128)S(1)} %shard_map.83.y0), channel_id=1, source_target_pairs={{0,1},{1,0},{2,3},{3,2},{4,5},{5,4},{6,7},{7,6},{8,9},{9,8},{10,11... | collective-permute-start | bytes 24584 | tf_op jit(solution)/shard_map/ppermute | solution.py:34
  31.3 4.8 %collective-permute-start.16 = (f32[2,128]{1,0:T(2,128)S(1)}, f32[2,128]{1,0:T(2,128)S(1)}, u32[]{:S(2)}, u32[]{:S(2)}) collective-permute-start(f32[2,128]{1,0:T(2,128)S(1)} %slice.17), channel_id=1, source_target_pairs={{0,1},{1,0},{2,3},{3,2},{4,5},{5,4},{6,7},{7,6},{8,9},{9,8},{10,11... | collective-permute-start | bytes 3080 | tf_op jit(solution)/shard_map/ppermute | solution.py:34
  32.0 7.4 %collective-permute-start.13 = (f32[24,128]{1,0:T(8,128)S(1)}, f32[24,128]{1,0:T(8,128)S(1)}, u32[]{:S(2)}, u32[]{:S(2)}) collective-permute-start(f32[24,128]{1,0:T(8,128)S(1)} %get-tuple-element.13), channel_id=1, source_target_pairs={{0,4},{1,5},{2,6},{3,7},{4,0},{5,1},{6,2},{7,3},{8,12},{9,13},{10,... | collective-permute-start | bytes 36872 | tf_op jit(solution)/shard_map/ppermute | solution.py:34
  33.6 5.8 %collective-permute-start.14 = (f32[24,128]{1,0:T(8,128)S(1)}, f32[24,128]{1,0:T(8,128)S(1)}, u32[]{:S(2)}, u32[]{:S(2)}) collective-permute-start(f32[24,128]{1,0:T(8,128)S(1)} %get-tuple-element.14), channel_id=1, source_target_pairs={{0,2},{1,3},{2,0},{3,1},{4,6},{5,7},{6,4},{7,5},{8,10},{9,11},{10,... | collective-permute-start | bytes 36872 | tf_op jit(solution)/shard_map/ppermute | solution.py:34
  35.5 4.9 %collective-permute-start.15 = (f32[24,128]{1,0:T(8,128)S(1)}, f32[24,128]{1,0:T(8,128)S(1)}, u32[]{:S(2)}, u32[]{:S(2)}) collective-permute-start(f32[24,128]{1,0:T(8,128)S(1)} %get-tuple-element.15), channel_id=1, source_target_pairs={{0,6},{1,7},{2,4},{3,5},{4,2},{5,3},{6,0},{7,1},{8,14},{9,15},{10,... | collective-permute-start | bytes 36872 | tf_op jit(solution)/shard_map/ppermute | solution.py:34
  36.1 7.5 %collective-permute-start.17 = (f32[1,128]{1,0:T(1,128)S(1)}, f32[1,128]{1,0:T(1,128)S(1)}, u32[]{:S(2)}, u32[]{:S(2)}) collective-permute-start(f32[1,128]{1,0:T(1,128)S(1)} %slice.14), channel_id=1, source_target_pairs={{0,8},{1,9},{2,10},{3,11},{4,12},{5,13},{6,14},{7,15},{8,0},{9,1},... | collective-permute-start | bytes 1544 | tf_op jit(solution)/shard_map/ppermute | solution.py:34
  40.4 4.8 %collective-permute-start.18 = (f32[1,128]{1,0:T(1,128)S(1)}, f32[1,128]{1,0:T(1,128)S(1)}, u32[]{:S(2)}, u32[]{:S(2)}) collective-permute-start(f32[1,128]{1,0:T(1,128)S(1)} %slice.18), channel_id=1, source_target_pairs={{0,192},{1,193},{2,194},{3,195},{4,196},{5,197},{6,198},{7,199},{8... | collective-permute-start | bytes 1544 | tf_op jit(solution)/shard_map/ppermute | solution.py:34
  40.9 4.3 %copy-start = (f32[1,2,16]{2,1,0:T(2,128)S(1)}, f32[1,2,16]{2,1,0:T(2,128)}, u32[]{:S(2)}) copy-start(f32[1,2,16]{2,1,0:T(2,128)} %param.8) | copy-start | bytes 388
  40.9 4.3 %copy-start.1 = (f32[1,16]{1,0:T(1,128)S(1)}, f32[1,16]{1,0:T(1,128)}, u32[]{:S(2)}) copy-start(f32[1,16]{1,0:T(1,128)} %energy_ref.1) | copy-start | bytes 196

commit v14 on v13

--- a/solution.py
+++ b/solution.py
@@ -248,6 +248,10 @@
     out_ref[...] = total
 
 
+def relay_kernel(source, _, __, target):
+    target[...] = source[...]
+
+
 def join_kernel(y0, y1, _, __, out_ref):
     out_ref[...] = y0[...] + y1[...]
 
@@ -393,7 +397,15 @@
         compiler_params=params(16),
         cost_estimate=pl.CostEstimate(flops=4000000000, bytes_accessed=1024, transcendentals=0),
     )(qmap, screening, place)
-    b1, b2, b3 = (move(b0, y=n) for n in (1, 2, 3))
+    b1, b2 = (move(b0, y=n) for n in (1, 2))
+    later = pl.pallas_call(
+        relay_kernel,
+        in_specs=[VMEM, ANY, ANY],
+        out_specs=VMEM,
+        out_shape=jax.ShapeDtypeStruct((16, WIDTH), BF16),
+        compiler_params=params(8),
+    )(b0, a1, b1)
+    b3 = move(later, y=3)
     a3 = move(a1, core=1)
     y = pl.pallas_call(
         transitions_kernel,

time: 46 us -> 47.4 us (1.030)
  starting transfers between devices: 27.2 us -> 30.2 us
  waiting for transfers between devices: 5.03 us -> 3.44 us
    ppermute x19, starting transfers between devices: 27.2 us -> 30.2 us  [move(): return lax.ppermute(value, ('grp', 'kin'), pairs)]
    ppermute x19, waiting for transfers between devices: 5.03 us -> 3.44 us  [move(): return lax.ppermute(value, ('grp', 'kin'), pairs)]
  transfers between devices with their start and end apart: 19 -> 19, of which waited for: 7 -> 4; matrix products, arithmetic and copies ran while one was open for 0% -> 0% of each run, Pallas kernels for 26% -> 25%
where the time goes in v14:
time: 47.4 us; the launch traced here: 47.3 us
  starting transfers between devices  30.2 us (64%)
  Pallas kernels  13.4 us (28%)
  waiting for transfers between devices  3.44 us (7%)
    ppermute x19, starting transfers between devices, move(): return lax.ppermute(value, ('grp', 'kin'), pairs)  30.2 us
    pallas_call x1, Pallas kernels, far_call(): pl.pallas_call(far_kernel, in_specs=[VMEM] * 8 + [ANY], out_specs=VMEM, o...  4.04 us
    pallas_call x1, Pallas kernels, near_call(): pl.pallas_call(near_kernel, in_specs=[VMEM] * 3 + [ANY], out_specs=[VMEM]...  3.91 us
    ppermute x19, waiting for transfers between devices, move(): return lax.ppermute(value, ('grp', 'kin'), pairs)  3.44 us
    pallas_call x7, Pallas kernels, small_call(): pl.pallas_call(kernel, in_specs=[VMEM] * len(operands) + [ANY] * len(afte...  1.66 us
    pallas_call x1, Pallas kernels, on_device(): pl.pallas_call(exchange_kernel, in_specs=[VMEM] * 4, out_specs=VMEM, out_...  1.07 us
    pallas_call x1, Pallas kernels, on_device(): pl.pallas_call(weights_kernel, in_specs=[SMEM, ANY, ANY], out_specs=VMEM,...  0.95 us
  transfers between devices with their start and end apart: 19, of which 4 were waited for; matrix products, arithmetic and copies ran while one was open for 0% of the time, Pallas kernels for 25%

profile of v14, /device:TPU:6, one launch (start us, length us, event | category | flops | bytes accessed | tf_op | source)
XLA Modules:
  0.0 47.3 jit_solution(12219389054906965715)
XLA Ops:
  0.0 0.9 %shard_map.73.a0.a_near.refs_0_ = bf16[16,1152]{1,0:T(8,128)(2,1)S(1)} custom-call(bf16[16,1024]{1,0:T(8,128)(2,1)} %bitcast.11, f32[2,16]{1,0:T(2,128)} %bitcast.9), custom_call_target="tpu_custom_call" | custom-call | tf_op jit(solution)/shard_map/pallas_call | solution.py:371
  1.0 0.0 copy-start.2
  1.0 0.0 copy-start.3
  1.0 2.3 %collective-permute-start.5 = (bf16[16,1152]{1,0:T(8,128)(2,1)S(1)}, bf16[16,1152]{1,0:T(8,128)(2,1)S(1)}, u32[]{:S(2)}, u32[]{:S(2)}) collective-permute-start(bf16[16,1152]{1,0:T(8,128)(2,1)S(1)} %shard_map.73.a0.a_near.refs_0_), channel_id=1, source_target_pairs={{0,64},{1,65},{2,66},{3,67},{4,68},{5,69},{6,70},{7,71},{8,72},{9,... | collective-permute-start | bytes 110600 | tf_op jit(solution)/shard_map/ppermute | solution.py:34
  3.3 5.5 %collective-permute-start = (bf16[16,1152]{1,0:T(8,128)(2,1)S(1)}, bf16[16,1152]{1,0:T(8,128)(2,1)S(1)}, u32[]{:S(2)}, u32[]{:S(2)}) collective-permute-start(bf16[16,1152]{1,0:T(8,128)(2,1)S(1)} %shard_map.73.a0.a_near.refs_0_), channel_id=1, source_target_pairs={{0,8},{1,9},{2,10},{3,11},{4,12},{5,13},{6,14},{7,15},{8,0},{9,1},... | collective-permute-start | bytes 110600 | tf_op jit(solution)/shard_map/ppermute | solution.py:34
  8.7 0.0 collective-permute-start.1
  8.7 0.0 collective-permute-done.5.source._.b0.refs_2_
  8.7 1.6 %collective-permute-start.6 = (bf16[16,1152]{1,0:T(8,128)(2,1)S(1)}, bf16[16,1152]{1,0:T(8,128)(2,1)S(1)}, u32[]{:S(2)}, u32[]{:S(2)}) collective-permute-start(bf16[16,1152]{1,0:T(8,128)(2,1)S(1)} %collective-permute-done.5.source._.b0.refs_2_), channel_id=1, source_target_pairs={{0,2},{1,3},{2,0},{3,1},{4,6},{5,7},{6,4},{7,5},{8,10},{9,11},{10,... | collective-permute-start | bytes 110600 | tf_op jit(solution)/shard_map/ppermute | solution.py:34
  10.3 2.9 %collective-permute-start.7 = (bf16[16,1152]{1,0:T(8,128)(2,1)S(1)}, bf16[16,1152]{1,0:T(8,128)(2,1)S(1)}, u32[]{:S(2)}, u32[]{:S(2)}) collective-permute-start(bf16[16,1152]{1,0:T(8,128)(2,1)S(1)} %collective-permute-done.5.source._.b0.refs_2_), channel_id=1, source_target_pairs={{0,4},{1,5},{2,6},{3,7},{4,0},{5,1},{6,2},{7,3},{8,12},{9,13},{10,... | collective-permute-start | bytes 110600 | tf_op jit(solution)/shard_map/ppermute | solution.py:34
  13.2 0.0 collective-permute-done.a1._.a_near.refs_0_
  13.2 0.0 collective-permute-start.2
  13.2 0.0 collective-permute-done.6.__.b1.refs_3_
  13.2 0.0 slice-start
  13.3 0.0 slice-start.1
  13.3 2.8 %collective-permute-start.8 = (bf16[16,1152]{1,0:T(8,128)(2,1)S(1)}, bf16[16,1152]{1,0:T(8,128)(2,1)S(1)}, u32[]{:S(2)}, u32[]{:S(2)}) collective-permute-start(bf16[16,1152]{1,0:T(8,128)(2,1)S(1)} %shard_map.75), channel_id=1, source_target_pairs={{0,6},{1,7},{2,4},{3,5},{4,2},{5,3},{6,0},{7,1},{8,14},{9,15},{10,... | collective-permute-start | bytes 110600 | tf_op jit(solution)/shard_map/ppermute | solution.py:34
  16.1 1.0 %shard_map.77.w_ref = f32[16,1536]{1,0:T(8,128)S(1)} custom-call(s32[1,256]{1,0:T(1,128)S(1)} %copy-done.3, f32[256,1536]{1,0:T(8,128)S(1)} %copy-done.2, f32[8,128]{1,0:T(8,128)S(1)} %shard_map.76._), custom_call_target="tpu_custom_call" | custom-call | flops 4000000000 | bytes 1024 | tf_op jit(solution)/shard_map/pallas_call | solution.py:391
  17.1 0.0 collective-permute-done.1.a2.a_pair.refs_1_
  17.1 0.0 collective-permute-done.2.a3.a_pair.refs_1_
  17.1 0.2 shard_map.74._.y0
  17.3 1.1 %collective-permute-start.3 = (f32[16,128]{1,0:T(8,128)S(1)}, f32[16,128]{1,0:T(8,128)S(1)}, u32[]{:S(2)}, u32[]{:S(2)}) collective-permute-start(f32[16,128]{1,0:T(8,128)S(1)} %shard_map.74._.y0), channel_id=1, source_target_pairs={{0,16},{1,17},{2,18},{3,19},{4,20},{5,21},{6,22},{7,23},{8,24},{9,... | collective-permute-start | bytes 24584 | tf_op jit(solution)/shard_map/ppermute | solution.py:34
  18.4 1.9 %collective-permute-start.4 = (f32[16,128]{1,0:T(8,128)S(1)}, f32[16,128]{1,0:T(8,128)S(1)}, u32[]{:S(2)}, u32[]{:S(2)}) collective-permute-start(f32[16,128]{1,0:T(8,128)S(1)} %shard_map.74._.y0), channel_id=1, source_target_pairs={{0,48},{1,33},{2,50},{3,35},{4,52},{5,37},{6,54},{7,39},{8,56},{9,... | collective-permute-start | bytes 24584 | tf_op jit(solution)/shard_map/ppermute | solution.py:34
  20.3 0.0 collective-permute-done.7.b2.refs_4_
  20.3 0.0 collective-permute-done.8.b3.refs_5_
  20.4 4.0 %shard_map.78._.acc.refs_0_ = f32[256,256]{1,0:T(8,128)S(1)} custom-call(bf16[16,1152]{1,0:T(8,128)(2,1)S(1)} %collective-permute-done.a1._.a_near.refs_0_, bf16[16,1152]{1,0:T(8,128)(2,1)S(1)} %collective-permute-done.2.a3.a_pair.refs_1_, bf16[16,1152]{1,0:T(8,128)(2,1)S(1)} %collective-permute-done.5.source._.b0.refs_2_, ...), custom_call_target="tpu_custom_call" | custom-call | flops 3221225472 | bytes 6291456 | tf_op jit(solution)/shard_map/pallas_call | solution.py:326
  24.4 0.0 collective-permute-done.3.y1
  24.4 0.0 collective-permute-done.4.y2
  24.4 0.1 collective-permute-start.9
  24.5 0.6 %shard_map.81.__.lhs = bf16[544,2048]{1,0:T(8,128)(2,1)S(1)} custom-call(bf16[16,1152]{1,0:T(8,128)(2,1)S(1)} %shard_map.73.a0.a_near.refs_0_, bf16[16,1152]{1,0:T(8,128)(2,1)S(1)} %collective-permute-done.1.a2.a_pair.refs_1_, bf16[16,1152]{1,0:T(8,128)(2,1)S(1)} %collective-permute-done.5.source._.b0.refs_2_, ...), custom_call_target="tpu_custom_call" | custom-call | tf_op jit(solution)/shard_map/pallas_call | solution.py:338
  25.1 0.5 %shard_map.80._.refs_6_ = f32[16,128]{1,0:T(8,128)S(1)} custom-call(f32[256,256]{1,0:T(8,128)S(1)} %shard_map.78._.acc.refs_0_, bf16[16,1152]{1,0:T(8,128)(2,1)S(1)} %collective-permute-done.a1._.a_near.refs_0_, bf16[16,1152]{1,0:T(8,128)(2,1)S(1)} %collective-permute-done.2.a3.a_pair.refs_1_, ...), custom_call_target="tpu_custom_call" | custom-call | tf_op jit(solution)/shard_map/pallas_call | solution.py:361
  25.6 0.1 collective-permute-done.9.y1
  25.7 1.6 %collective-permute-start.10 = (f32[16,128]{1,0:T(8,128)S(1)}, f32[16,128]{1,0:T(8,128)S(1)}, u32[]{:S(2)}, u32[]{:S(2)}) collective-permute-start(f32[16,128]{1,0:T(8,128)S(1)} %shard_map.82._.y0), channel_id=1, source_target_pairs={{0,64},{1,65},{2,66},{3,67},{4,68},{5,69},{6,70},{7,71},{8,72},{9,... | collective-permute-start | bytes 24584 | tf_op jit(solution)/shard_map/ppermute | solution.py:34
  27.3 1.4 %collective-permute-start.11 = (f32[16,128]{1,0:T(8,128)S(1)}, f32[16,128]{1,0:T(8,128)S(1)}, u32[]{:S(2)}, u32[]{:S(2)}) collective-permute-start(f32[16,128]{1,0:T(8,128)S(1)} %shard_map.82._.y0), channel_id=1, source_target_pairs={{0,192},{1,129},{2,194},{3,131},{4,196},{5,133},{6,198},{7,135},{8... | collective-permute-start | bytes 24584 | tf_op jit(solution)/shard_map/ppermute | solution.py:34
  28.7 3.9 %shard_map.83 = (f32[256,256]{1,0:T(8,128)S(1)}, f32[32,1536]{1,0:T(8,128)S(1)}) custom-call(bf16[544,2048]{1,0:T(8,128)(2,1)S(1)} %shard_map.81.__.lhs, f32[16,1536]{1,0:T(8,128)S(1)} %shard_map.77.w_ref, bf16[2048,1536]{1,0:T(8,128)(2,1)S(1)} %bitcast.7, f32[16,128]{1,0:T(8,128)S(1)} %shard_map.82._.y0), custom_call_target="tpu_custom_call" | custom-call | flops 3221225472 | bytes 6291456 | tf_op jit(solution)/shard_map/pallas_call | solution.py:349
  32.6 0.0 collective-permute-done.10.y1
  32.7 0.1 collective-permute-start.12
  32.8 0.5 %shard_map.85.rows_ref = f32[16,128]{1,0:T(8,128)S(1)} custom-call(f32[256,256]{1,0:T(8,128)S(1)} %get-tuple-element.11._.acc, bf16[16,1152]{1,0:T(8,128)(2,1)S(1)} %shard_map.73.a0.a_near.refs_0_, bf16[16,1152]{1,0:T(8,128)(2,1)S(1)} %collective-permute-done.1.a2.a_pair.refs_1_, bf16[16,1152]{1,0:T(8,128)(2,1)S(1)} %collective-permute-done.5.source._.b0.refs_2_, ...), custom_call_target="tpu_custom_call" | custom-call | tf_op jit(solution)/shard_map/pallas_call | solution.py:361
  33.3 0.5 %collective-permute-start.16 = (f32[2,128]{1,0:T(2,128)S(1)}, f32[2,128]{1,0:T(2,128)S(1)}, u32[]{:S(2)}, u32[]{:S(2)}) collective-permute-start(f32[2,128]{1,0:T(2,128)S(1)} %slice.17), channel_id=1, source_target_pairs={{0,1},{1,0},{2,3},{3,2},{4,5},{5,4},{6,7},{7,6},{8,9},{9,8},{10,11... | collective-permute-start | bytes 3080 | tf_op jit(solution)/shard_map/ppermute | solution.py:34
  33.8 0.1 collective-permute-done.12.y1
  33.9 0.3 collective-permute-start.13
  34.3 1.5 %collective-permute-start.14 = (f32[24,128]{1,0:T(8,128)S(1)}, f32[24,128]{1,0:T(8,128)S(1)}, u32[]{:S(2)}, u32[]{:S(2)}) collective-permute-start(f32[24,128]{1,0:T(8,128)S(1)} %get-tuple-element.14), channel_id=1, source_target_pairs={{0,2},{1,3},{2,0},{3,1},{4,6},{5,7},{6,4},{7,5},{8,10},{9,11},{10,... | collective-permute-start | bytes 36872 | tf_op jit(solution)/shard_map/ppermute | solution.py:34
  35.8 2.3 %collective-permute-start.15 = (f32[24,128]{1,0:T(8,128)S(1)}, f32[24,128]{1,0:T(8,128)S(1)}, u32[]{:S(2)}, u32[]{:S(2)}) collective-permute-start(f32[24,128]{1,0:T(8,128)S(1)} %get-tuple-element.15), channel_id=1, source_target_pairs={{0,6},{1,7},{2,4},{3,5},{4,2},{5,3},{6,0},{7,1},{8,14},{9,15},{10,... | collective-permute-start | bytes 36872 | tf_op jit(solution)/shard_map/ppermute | solution.py:34
  38.1 0.0 collective-permute-done.16
  38.1 3.7 %collective-permute-start.17 = (f32[1,128]{1,0:T(1,128)S(1)}, f32[1,128]{1,0:T(1,128)S(1)}, u32[]{:S(2)}, u32[]{:S(2)}) collective-permute-start(f32[1,128]{1,0:T(1,128)S(1)} %slice.14), channel_id=1, source_target_pairs={{0,8},{1,9},{2,10},{3,11},{4,12},{5,13},{6,14},{7,15},{8,0},{9,1},... | collective-permute-start | bytes 1544 | tf_op jit(solution)/shard_map/ppermute | solution.py:34
  41.8 0.5 %collective-permute-start.18 = (f32[1,128]{1,0:T(1,128)S(1)}, f32[1,128]{1,0:T(1,128)S(1)}, u32[]{:S(2)}, u32[]{:S(2)}) collective-permute-start(f32[1,128]{1,0:T(1,128)S(1)} %slice.18), channel_id=1, source_target_pairs={{0,192},{1,193},{2,194},{3,195},{4,196},{5,197},{6,198},{7,199},{8... | collective-permute-start | bytes 1544 | tf_op jit(solution)/shard_map/ppermute | solution.py:34
  42.3 1.1 %shard_map.87.exchange_ref = f32[2,16]{1,0:T(2,128)S(1)} custom-call(f32[24,128]{1,0:T(8,128)S(1)} %add_add_fusion.y_ref, f32[1,1536]{1,0:T(1,128)S(1)} %reshape.19.c_ref, f32[32,1536]{1,0:T(8,128)S(1)} %get-tuple-element.16.rx_ref, bf16[2048,1536]{1,0:T(8,128)(2,1)S(1)} %bitcast.8), custom_call_target="tpu_custom_call" | custom-call | flops 805306368 | bytes 6291456 | tf_op jit(solution)/shard_map/pallas_call | solution.py:431
  43.4 2.2 %collective-permute-done.17.d_ref = f32[1,128]{1,0:T(1,128)S(1)} collective-permute-done((f32[1,128]{1,0:T(1,128)S(1)}, f32[1,128]{1,0:T(1,128)S(1)}, u32[]{:S(2)}, u32[]{:S(2)}) %collective-permute-start.17) | collective-permute-done | bytes 544 | tf_op jit(solution)/shard_map/ppermute | solution.py:34
  45.6 1.0 %collective-permute-done.18.h_ref = f32[1,128]{1,0:T(1,128)S(1)} collective-permute-done((f32[1,128]{1,0:T(1,128)S(1)}, f32[1,128]{1,0:T(1,128)S(1)}, u32[]{:S(2)}, u32[]{:S(2)}) %collective-permute-start.18) | collective-permute-done | bytes 544 | tf_op jit(solution)/shard_map/ppermute | solution.py:34
  46.6 0.6 %shard_map.88 = f32[2,16]{1,0:T(2,128)} custom-call(f32[1,16]{1,0:T(1,128)S(1)} %copy-done.1, f32[2,16]{1,0:T(2,128)S(1)} %bitcast.10, f32[2,16]{1,0:T(2,128)S(1)} %shard_map.87.exchange_ref, f32[2,128]{1,0:T(2,128)S(1)} %slice_add_fusion.near_ref, f32[1,128]{1,0:T(1,128)S(1)} %collective-permute-done.17.d_ref, f32[1,128]{1,0:T(1,128)S(1)} %collective-permute-done.18.h_ref), custom_call_target="tpu_custom_call" | custom-call | tf_op jit(solution)/shard_map/pallas_call | solution.py:361
  (27 shorter events, 0.1 us)
Async XLA Ops:
  1.0 15.2 %copy-start.2 = (f32[256,1536]{1,0:T(8,128)S(1)}, f32[256,1536]{1,0:T(8,128)}, u32[]{:S(2)}) copy-start(f32[256,1536]{1,0:T(8,128)} %screening.1) | copy-start | bytes 4718596
  1.0 15.2 %copy-start.3 = (s32[1,256]{1,0:T(1,128)S(1)}, s32[1,256]{1,0:T(1,128)}, u32[]{:S(2)}) copy-start(s32[1,256]{1,0:T(1,128)} %qmap_ref.1) | copy-start | bytes 3076
  1.0 7.8 %collective-permute-start.5 = (bf16[16,1152]{1,0:T(8,128)(2,1)S(1)}, bf16[16,1152]{1,0:T(8,128)(2,1)S(1)}, u32[]{:S(2)}, u32[]{:S(2)}) collective-permute-start(bf16[16,1152]{1,0:T(8,128)(2,1)S(1)} %shard_map.73.a0.a_near.refs_0_), channel_id=1, source_target_pairs={{0,64},{1,65},{2,66},{3,67},{4,68},{5,69},{6,70},{7,71},{8,72},{9,... | collective-permute-start | bytes 110600 | tf_op jit(solution)/shard_map/ppermute | solution.py:34
  3.3 9.9 %collective-permute-start = (bf16[16,1152]{1,0:T(8,128)(2,1)S(1)}, bf16[16,1152]{1,0:T(8,128)(2,1)S(1)}, u32[]{:S(2)}, u32[]{:S(2)}) collective-permute-start(bf16[16,1152]{1,0:T(8,128)(2,1)S(1)} %shard_map.73.a0.a_near.refs_0_), channel_id=1, source_target_pairs={{0,8},{1,9},{2,10},{3,11},{4,12},{5,13},{6,14},{7,15},{8,0},{9,1},... | collective-permute-start | bytes 110600 | tf_op jit(solution)/shard_map/ppermute | solution.py:34
  8.7 8.4 %collective-permute-start.1 = (bf16[16,1152]{1,0:T(8,128)(2,1)S(1)}, bf16[16,1152]{1,0:T(8,128)(2,1)S(1)}, u32[]{:S(2)}, u32[]{:S(2)}) collective-permute-start(bf16[16,1152]{1,0:T(8,128)(2,1)S(1)} %shard_map.73.a0.a_near.refs_0_), channel_id=1, source_target_pairs={{0,1},{1,0},{2,3},{3,2},{4,5},{5,4},{6,7},{7,6},{8,9},{9,8},{10,11... | collective-permute-start | bytes 110600 | tf_op jit(solution)/shard_map/ppermute | solution.py:34
  8.7 4.5 %collective-permute-start.6 = (bf16[16,1152]{1,0:T(8,128)(2,1)S(1)}, bf16[16,1152]{1,0:T(8,128)(2,1)S(1)}, u32[]{:S(2)}, u32[]{:S(2)}) collective-permute-start(bf16[16,1152]{1,0:T(8,128)(2,1)S(1)} %collective-permute-done.5.source._.b0.refs_2_), channel_id=1, source_target_pairs={{0,2},{1,3},{2,0},{3,1},{4,6},{5,7},{6,4},{7,5},{8,10},{9,11},{10,... | collective-permute-start | bytes 110600 | tf_op jit(solution)/shard_map/ppermute | solution.py:34
  10.3 10.0 %collective-permute-start.7 = (bf16[16,1152]{1,0:T(8,128)(2,1)S(1)}, bf16[16,1152]{1,0:T(8,128)(2,1)S(1)}, u32[]{:S(2)}, u32[]{:S(2)}) collective-permute-start(bf16[16,1152]{1,0:T(8,128)(2,1)S(1)} %collective-permute-done.5.source._.b0.refs_2_), channel_id=1, source_target_pairs={{0,4},{1,5},{2,6},{3,7},{4,0},{5,1},{6,2},{7,3},{8,12},{9,13},{10,... | collective-permute-start | bytes 110600 | tf_op jit(solution)/shard_map/ppermute | solution.py:34
  13.2 3.9 %collective-permute-start.2 = (bf16[16,1152]{1,0:T(8,128)(2,1)S(1)}, bf16[16,1152]{1,0:T(8,128)(2,1)S(1)}, u32[]{:S(2)}, u32[]{:S(2)}) collective-permute-start(bf16[16,1152]{1,0:T(8,128)(2,1)S(1)} %collective-permute-done.a1._.a_near.refs_0_), channel_id=1, source_target_pairs={{0,1},{1,0},{2,3},{3,2},{4,5},{5,4},{6,7},{7,6},{8,9},{9,8},{10,11... | collective-permute-start | bytes 110600 | tf_op jit(solution)/shard_map/ppermute | solution.py:34
  13.2 7.1 %slice-start = ((s8[6291456]{0:T(1024)(128)(4,1)}), s8[4194304]{0:T(1024)(128)(4,1)S(1)}, s32[]{:S(2)}) async-start(s8[6291456]{0:T(1024)(128)(4,1)} %bitcast.4), calls=%async_computation | async-start | bytes 8388608
  13.3 7.1 %slice-start.1 = ((s8[6291456]{0:T(1024)(128)(4,1)}), s8[2097152]{0:T(1024)(128)(4,1)S(1)}, s32[]{:S(2)}) async-start(s8[6291456]{0:T(1024)(128)(4,1)} %bitcast.4), calls=%async_computation.1 | async-start | bytes 4194304
  13.3 7.1 %collective-permute-start.8 = (bf16[16,1152]{1,0:T(8,128)(2,1)S(1)}, bf16[16,1152]{1,0:T(8,128)(2,1)S(1)}, u32[]{:S(2)}, u32[]{:S(2)}) collective-permute-start(bf16[16,1152]{1,0:T(8,128)(2,1)S(1)} %shard_map.75), channel_id=1, source_target_pairs={{0,6},{1,7},{2,4},{3,5},{4,2},{5,3},{6,0},{7,1},{8,14},{9,15},{10,... | collective-permute-start | bytes 110600 | tf_op jit(solution)/shard_map/ppermute | solution.py:34
  17.3 7.1 %collective-permute-start.3 = (f32[16,128]{1,0:T(8,128)S(1)}, f32[16,128]{1,0:T(8,128)S(1)}, u32[]{:S(2)}, u32[]{:S(2)}) collective-permute-start(f32[16,128]{1,0:T(8,128)S(1)} %shard_map.74._.y0), channel_id=1, source_target_pairs={{0,16},{1,17},{2,18},{3,19},{4,20},{5,21},{6,22},{7,23},{8,24},{9,... | collective-permute-start | bytes 24584 | tf_op jit(solution)/shard_map/ppermute | solution.py:34
  18.4 6.0 %collective-permute-start.4 = (f32[16,128]{1,0:T(8,128)S(1)}, f32[16,128]{1,0:T(8,128)S(1)}, u32[]{:S(2)}, u32[]{:S(2)}) collective-permute-start(f32[16,128]{1,0:T(8,128)S(1)} %shard_map.74._.y0), channel_id=1, source_target_pairs={{0,48},{1,33},{2,50},{3,35},{4,52},{5,37},{6,54},{7,39},{8,56},{9,... | collective-permute-start | bytes 24584 | tf_op jit(solution)/shard_map/ppermute | solution.py:34
  24.4 1.3 %collective-permute-start.9 = (f32[16,128]{1,0:T(8,128)S(1)}, f32[16,128]{1,0:T(8,128)S(1)}, u32[]{:S(2)}, u32[]{:S(2)}) collective-permute-start(f32[16,128]{1,0:T(8,128)S(1)} %shard_map.79.y0), channel_id=1, source_target_pairs={{0,1},{1,0},{2,3},{3,2},{4,5},{5,4},{6,7},{7,6},{8,9},{9,8},{10,11... | collective-permute-start | bytes 24584 | tf_op jit(solution)/shard_map/ppermute | solution.py:34
  25.7 8.1 %copy-start.4 = (f32[1536]{0:T(1024)S(1)}, f32[1536]{0:T(1024)}, u32[]{:S(2)}) copy-start(f32[1536]{0:T(1024)} %param.12) | copy-start | bytes 18436
  25.7 6.9 %collective-permute-start.10 = (f32[16,128]{1,0:T(8,128)S(1)}, f32[16,128]{1,0:T(8,128)S(1)}, u32[]{:S(2)}, u32[]{:S(2)}) collective-permute-start(f32[16,128]{1,0:T(8,128)S(1)} %shard_map.82._.y0), channel_id=1, source_target_pairs={{0,64},{1,65},{2,66},{3,67},{4,68},{5,69},{6,70},{7,71},{8,72},{9,... | collective-permute-start | bytes 24584 | tf_op jit(solution)/shard_map/ppermute | solution.py:34
  27.3 5.4 %collective-permute-start.11 = (f32[16,128]{1,0:T(8,128)S(1)}, f32[16,128]{1,0:T(8,128)S(1)}, u32[]{:S(2)}, u32[]{:S(2)}) collective-permute-start(f32[16,128]{1,0:T(8,128)S(1)} %shard_map.82._.y0), channel_id=1, source_target_pairs={{0,192},{1,129},{2,194},{3,131},{4,196},{5,133},{6,198},{7,135},{8... | collective-permute-start | bytes 24584 | tf_op jit(solution)/shard_map/ppermute | solution.py:34
  32.7 1.3 %collective-permute-start.12 = (f32[16,128]{1,0:T(8,128)S(1)}, f32[16,128]{1,0:T(8,128)S(1)}, u32[]{:S(2)}, u32[]{:S(2)}) collective-permute-start(f32[16,128]{1,0:T(8,128)S(1)} %shard_map.84.y0), channel_id=1, source_target_pairs={{0,1},{1,0},{2,3},{3,2},{4,5},{5,4},{6,7},{7,6},{8,9},{9,8},{10,11... | collective-permute-start | bytes 24584 | tf_op jit(solution)/shard_map/ppermute | solution.py:34
  33.3 4.8 %collective-permute-start.16 = (f32[2,128]{1,0:T(2,128)S(1)}, f32[2,128]{1,0:T(2,128)S(1)}, u32[]{:S(2)}, u32[]{:S(2)}) collective-permute-start(f32[2,128]{1,0:T(2,128)S(1)} %slice.17), channel_id=1, source_target_pairs={{0,1},{1,0},{2,3},{3,2},{4,5},{5,4},{6,7},{7,6},{8,9},{9,8},{10,11... | collective-permute-start | bytes 3080 | tf_op jit(solution)/shard_map/ppermute | solution.py:34
  33.9 7.8 %collective-permute-start.13 = (f32[24,128]{1,0:T(8,128)S(1)}, f32[24,128]{1,0:T(8,128)S(1)}, u32[]{:S(2)}, u32[]{:S(2)}) collective-permute-start(f32[24,128]{1,0:T(8,128)S(1)} %get-tuple-element.13), channel_id=1, source_target_pairs={{0,4},{1,5},{2,6},{3,7},{4,0},{5,1},{6,2},{7,3},{8,12},{9,13},{10,... | collective-permute-start | bytes 36872 | tf_op jit(solution)/shard_map/ppermute | solution.py:34
  34.3 7.5 %collective-permute-start.14 = (f32[24,128]{1,0:T(8,128)S(1)}, f32[24,128]{1,0:T(8,128)S(1)}, u32[]{:S(2)}, u32[]{:S(2)}) collective-permute-start(f32[24,128]{1,0:T(8,128)S(1)} %get-tuple-element.14), channel_id=1, source_target_pairs={{0,2},{1,3},{2,0},{3,1},{4,6},{5,7},{6,4},{7,5},{8,10},{9,11},{10,... | collective-permute-start | bytes 36872 | tf_op jit(solution)/shard_map/ppermute | solution.py:34
  35.8 6.0 %collective-permute-start.15 = (f32[24,128]{1,0:T(8,128)S(1)}, f32[24,128]{1,0:T(8,128)S(1)}, u32[]{:S(2)}, u32[]{:S(2)}) collective-permute-start(f32[24,128]{1,0:T(8,128)S(1)} %get-tuple-element.15), channel_id=1, source_target_pairs={{0,6},{1,7},{2,4},{3,5},{4,2},{5,3},{6,0},{7,1},{8,14},{9,15},{10,... | collective-permute-start | bytes 36872 | tf_op jit(solution)/shard_map/ppermute | solution.py:34
  38.1 7.5 %collective-permute-start.17 = (f32[1,128]{1,0:T(1,128)S(1)}, f32[1,128]{1,0:T(1,128)S(1)}, u32[]{:S(2)}, u32[]{:S(2)}) collective-permute-start(f32[1,128]{1,0:T(1,128)S(1)} %slice.14), channel_id=1, source_target_pairs={{0,8},{1,9},{2,10},{3,11},{4,12},{5,13},{6,14},{7,15},{8,0},{9,1},... | collective-permute-start | bytes 1544 | tf_op jit(solution)/shard_map/ppermute | solution.py:34
  41.8 4.8 %collective-permute-start.18 = (f32[1,128]{1,0:T(1,128)S(1)}, f32[1,128]{1,0:T(1,128)S(1)}, u32[]{:S(2)}, u32[]{:S(2)}) collective-permute-start(f32[1,128]{1,0:T(1,128)S(1)} %slice.18), channel_id=1, source_target_pairs={{0,192},{1,193},{2,194},{3,195},{4,196},{5,197},{6,198},{7,199},{8... | collective-permute-start | bytes 1544 | tf_op jit(solution)/shard_map/ppermute | solution.py:34
  42.3 4.3 %copy-start = (f32[1,2,16]{2,1,0:T(2,128)S(1)}, f32[1,2,16]{2,1,0:T(2,128)}, u32[]{:S(2)}) copy-start(f32[1,2,16]{2,1,0:T(2,128)} %param.8) | copy-start | bytes 388
  42.3 4.3 %copy-start.1 = (f32[1,16]{1,0:T(1,128)S(1)}, f32[1,16]{1,0:T(1,128)}, u32[]{:S(2)}) copy-start(f32[1,16]{1,0:T(1,128)} %energy_ref.1) | copy-start | bytes 196

commit v15 on v13

--- a/solution.py
+++ b/solution.py
@@ -296,7 +296,7 @@
 
 def final_kernel(energy_ref, vector_ref, exchange_ref, near_ref, d_ref, h_ref, out_ref):
     scale = 1.0 / 256
-    terms = near_ref[1:2] + d_ref[...] + h_ref[...]
+    terms = near_ref[...] + d_ref[...] + h_ref[...]
     for part in range(2):
         term = terms[:, part * NT : part * NT + NT]
         out_ref[part : part + 1] = (
@@ -415,7 +415,8 @@
     (rows,) = small_call(functools.partial(rows_kernel, 1), [(16, 128)], near_acc, pay, a2, *b_pays, far_rows)
     mails = small_call(mail_kernel, [(24, 128)] * 4, y, swapped, rows)
     mail = mails[0] + move(mails[2], y=2) + move(mails[1], y=1) + move(mails[3], y=3)
-    rows = rows[0:2] + move(rows[2:4], core=1)
+    far_row = far_rows[0:1] + move(far_rows[2:3], core=1)
+    near_row = rows[1:2] + move(rows[3:4], core=1)
     exchange = pl.pallas_call(
         exchange_kernel,
         in_specs=[VMEM] * 4,
@@ -432,8 +433,8 @@
         energies,
         vector.reshape(2, NT),
         exchange,
-        rows,
-        move(rows[0:1], far=1),
+        near_row,
+        move(far_row, far=1),
         move(mail[16:17], step=3),
     )
     return out.reshape(1, 2, NT)

time: 46 us -> 49.5 us (1.076)
  waiting for transfers between devices: 5.03 us -> 8.3 us
    ppermute x19 -> x20, waiting for transfers between devices: 5.03 us -> 8.3 us  [move(): return lax.ppermute(value, ('grp', 'kin'), pairs)]
    ppermute x19 -> x20, starting transfers between devices: 27.2 us -> 27.5 us  [move(): return lax.ppermute(value, ('grp', 'kin'), pairs)]
  transfers between devices with their start and end apart: 19 -> 20, of which waited for: 7 -> 6; matrix products, arithmetic and copies ran while one was open for 0% -> 0% of each run, Pallas kernels for 26% -> 24%
where the time goes in v15:
time: 49.5 us; the launch traced here: 49.4 us
  starting transfers between devices  27.5 us (56%)
  Pallas kernels  13.3 us (27%)
  waiting for transfers between devices  8.3 us (17%)
    ppermute x20, starting transfers between devices, move(): return lax.ppermute(value, ('grp', 'kin'), pairs)  27.5 us
    ppermute x20, waiting for transfers between devices, move(): return lax.ppermute(value, ('grp', 'kin'), pairs)  8.3 us
    pallas_call x1, Pallas kernels, far_call(): pl.pallas_call(far_kernel, in_specs=[VMEM] * 8 + [ANY], out_specs=VMEM, o...  4.04 us
    pallas_call x1, Pallas kernels, near_call(): pl.pallas_call(near_kernel, in_specs=[VMEM] * 3 + [ANY], out_specs=[VMEM]...  3.9 us
    pallas_call x7, Pallas kernels, small_call(): pl.pallas_call(kernel, in_specs=[VMEM] * len(operands) + [ANY] * len(afte...  1.65 us
    pallas_call x1, Pallas kernels, on_device(): pl.pallas_call(exchange_kernel, in_specs=[VMEM] * 4, out_specs=VMEM, out_...  1.07 us
  transfers between devices with their start and end apart: 20, of which 6 were waited for; matrix products, arithmetic and copies ran while one was open for 0% of the time, Pallas kernels for 24%

profile of v15, /device:TPU:6, one launch (start us, length us, event | category | flops | bytes accessed | tf_op | source)
XLA Modules:
  0.0 49.4 jit_solution(16496880517106796112)
XLA Ops:
  0.0 0.9 %shard_map.73.a0.a_near.refs_0_ = bf16[16,1152]{1,0:T(8,128)(2,1)S(1)} custom-call(bf16[16,1024]{1,0:T(8,128)(2,1)} %bitcast.11, f32[2,16]{1,0:T(2,128)} %bitcast.9), custom_call_target="tpu_custom_call" | custom-call | tf_op jit(solution)/shard_map/pallas_call | solution.py:367
  1.0 0.0 copy-start.2
  1.0 0.0 copy-start.3
  1.0 2.3 %collective-permute-start.5 = (bf16[16,1152]{1,0:T(8,128)(2,1)S(1)}, bf16[16,1152]{1,0:T(8,128)(2,1)S(1)}, u32[]{:S(2)}, u32[]{:S(2)}) collective-permute-start(bf16[16,1152]{1,0:T(8,128)(2,1)S(1)} %shard_map.73.a0.a_near.refs_0_), channel_id=1, source_target_pairs={{0,64},{1,65},{2,66},{3,67},{4,68},{5,69},{6,70},{7,71},{8,72},{9,... | collective-permute-start | bytes 110600 | tf_op jit(solution)/shard_map/ppermute | solution.py:34
  3.3 5.5 %collective-permute-start = (bf16[16,1152]{1,0:T(8,128)(2,1)S(1)}, bf16[16,1152]{1,0:T(8,128)(2,1)S(1)}, u32[]{:S(2)}, u32[]{:S(2)}) collective-permute-start(bf16[16,1152]{1,0:T(8,128)(2,1)S(1)} %shard_map.73.a0.a_near.refs_0_), channel_id=1, source_target_pairs={{0,8},{1,9},{2,10},{3,11},{4,12},{5,13},{6,14},{7,15},{8,0},{9,1},... | collective-permute-start | bytes 110600 | tf_op jit(solution)/shard_map/ppermute | solution.py:34
  8.7 0.0 collective-permute-start.1
  8.7 0.0 collective-permute-done.5._.b0.refs_2_
  8.7 1.6 %collective-permute-start.6 = (bf16[16,1152]{1,0:T(8,128)(2,1)S(1)}, bf16[16,1152]{1,0:T(8,128)(2,1)S(1)}, u32[]{:S(2)}, u32[]{:S(2)}) collective-permute-start(bf16[16,1152]{1,0:T(8,128)(2,1)S(1)} %collective-permute-done.5._.b0.refs_2_), channel_id=1, source_target_pairs={{0,2},{1,3},{2,0},{3,1},{4,6},{5,7},{6,4},{7,5},{8,10},{9,11},{10,... | collective-permute-start | bytes 110600 | tf_op jit(solution)/shard_map/ppermute | solution.py:34
  10.3 2.9 %collective-permute-start.7 = (bf16[16,1152]{1,0:T(8,128)(2,1)S(1)}, bf16[16,1152]{1,0:T(8,128)(2,1)S(1)}, u32[]{:S(2)}, u32[]{:S(2)}) collective-permute-start(bf16[16,1152]{1,0:T(8,128)(2,1)S(1)} %collective-permute-done.5._.b0.refs_2_), channel_id=1, source_target_pairs={{0,4},{1,5},{2,6},{3,7},{4,0},{5,1},{6,2},{7,3},{8,12},{9,13},{10,... | collective-permute-start | bytes 110600 | tf_op jit(solution)/shard_map/ppermute | solution.py:34
  13.2 0.2 collective-permute-start.8
  13.4 0.0 collective-permute-done.a1.a_near.refs_0_
  13.4 0.1 collective-permute-start.2
  13.6 1.0 %shard_map.76.w_ref = f32[16,1536]{1,0:T(8,128)S(1)} custom-call(s32[1,256]{1,0:T(1,128)S(1)} %copy-done.3, f32[256,1536]{1,0:T(8,128)S(1)} %copy-done.2, f32[8,128]{1,0:T(8,128)S(1)} %shard_map.75._), custom_call_target="tpu_custom_call" | custom-call | flops 4000000000 | bytes 1024 | tf_op jit(solution)/shard_map/pallas_call | solution.py:387
  14.5 0.0 collective-permute-done.1.a2.a_pair.refs_1_
  14.5 0.2 collective-permute-done.2.a3.a_pair.refs_1_
  14.7 0.2 shard_map.74._.y0
  14.9 1.1 %collective-permute-start.3 = (f32[16,128]{1,0:T(8,128)S(1)}, f32[16,128]{1,0:T(8,128)S(1)}, u32[]{:S(2)}, u32[]{:S(2)}) collective-permute-start(f32[16,128]{1,0:T(8,128)S(1)} %shard_map.74._.y0), channel_id=1, source_target_pairs={{0,16},{1,17},{2,18},{3,19},{4,20},{5,21},{6,22},{7,23},{8,24},{9,... | collective-permute-start | bytes 24584 | tf_op jit(solution)/shard_map/ppermute | solution.py:34
  16.0 1.9 %collective-permute-start.4 = (f32[16,128]{1,0:T(8,128)S(1)}, f32[16,128]{1,0:T(8,128)S(1)}, u32[]{:S(2)}, u32[]{:S(2)}) collective-permute-start(f32[16,128]{1,0:T(8,128)S(1)} %shard_map.74._.y0), channel_id=1, source_target_pairs={{0,48},{1,33},{2,50},{3,35},{4,52},{5,37},{6,54},{7,39},{8,56},{9,... | collective-permute-start | bytes 24584 | tf_op jit(solution)/shard_map/ppermute | solution.py:34
  18.0 0.0 collective-permute-done.6.b1.refs_3_
  18.0 0.0 collective-permute-done.7.b2.refs_4_
  18.0 0.4 collective-permute-done.8.b3.refs_5_
  18.4 4.0 %shard_map.77._.acc.refs_0_ = f32[256,256]{1,0:T(8,128)S(1)} custom-call(bf16[16,1152]{1,0:T(8,128)(2,1)S(1)} %collective-permute-done.a1.a_near.refs_0_, bf16[16,1152]{1,0:T(8,128)(2,1)S(1)} %collective-permute-done.2.a3.a_pair.refs_1_, bf16[16,1152]{1,0:T(8,128)(2,1)S(1)} %collective-permute-done.5._.b0.refs_2_, ...), custom_call_target="tpu_custom_call" | custom-call | flops 3221225472 | bytes 6291456 | tf_op jit(solution)/shard_map/pallas_call | solution.py:322
  22.5 0.1 collective-permute-start.9
  22.6 0.5 %shard_map.79._.refs_6_ = f32[16,128]{1,0:T(8,128)S(1)} custom-call(f32[256,256]{1,0:T(8,128)S(1)} %shard_map.77._.acc.refs_0_, bf16[16,1152]{1,0:T(8,128)(2,1)S(1)} %collective-permute-done.a1.a_near.refs_0_, bf16[16,1152]{1,0:T(8,128)(2,1)S(1)} %collective-permute-done.2.a3.a_pair.refs_1_, bf16[16,1152]{1,0:T(8,128)(2,1)S(1)} %collective-permute-done.5._.b0.refs_2_, ...), custom_call_target="tpu_custom_call" | custom-call | tf_op jit(solution)/shard_map/pallas_call | solution.py:357
  23.1 0.5 collective-permute-start.17
  23.6 0.6 %shard_map.80.__.lhs = bf16[544,2048]{1,0:T(8,128)(2,1)S(1)} custom-call(bf16[16,1152]{1,0:T(8,128)(2,1)S(1)} %shard_map.73.a0.a_near.refs_0_, bf16[16,1152]{1,0:T(8,128)(2,1)S(1)} %collective-permute-done.1.a2.a_pair.refs_1_, bf16[16,1152]{1,0:T(8,128)(2,1)S(1)} %collective-permute-done.5._.b0.refs_2_, ...), custom_call_target="tpu_custom_call" | custom-call | tf_op jit(solution)/shard_map/pallas_call | solution.py:334
  24.2 0.0 collective-permute-done.9.y1
  24.2 1.6 %collective-permute-start.10 = (f32[16,128]{1,0:T(8,128)S(1)}, f32[16,128]{1,0:T(8,128)S(1)}, u32[]{:S(2)}, u32[]{:S(2)}) collective-permute-start(f32[16,128]{1,0:T(8,128)S(1)} %shard_map.81._.y0), channel_id=1, source_target_pairs={{0,64},{1,65},{2,66},{3,67},{4,68},{5,69},{6,70},{7,71},{8,72},{9,... | collective-permute-start | bytes 24584 | tf_op jit(solution)/shard_map/ppermute | solution.py:34
  25.9 1.4 %collective-permute-start.11 = (f32[16,128]{1,0:T(8,128)S(1)}, f32[16,128]{1,0:T(8,128)S(1)}, u32[]{:S(2)}, u32[]{:S(2)}) collective-permute-start(f32[16,128]{1,0:T(8,128)S(1)} %shard_map.81._.y0), channel_id=1, source_target_pairs={{0,192},{1,129},{2,194},{3,131},{4,196},{5,133},{6,198},{7,135},{8... | collective-permute-start | bytes 24584 | tf_op jit(solution)/shard_map/ppermute | solution.py:34
  27.3 3.9 %shard_map.82 = (f32[256,256]{1,0:T(8,128)S(1)}, f32[32,1536]{1,0:T(8,128)S(1)}) custom-call(bf16[544,2048]{1,0:T(8,128)(2,1)S(1)} %shard_map.80.__.lhs, f32[16,1536]{1,0:T(8,128)S(1)} %shard_map.76.w_ref, bf16[2048,1536]{1,0:T(8,128)(2,1)S(1)} %bitcast.7, f32[16,128]{1,0:T(8,128)S(1)} %shard_map.81._.y0), custom_call_target="tpu_custom_call" | custom-call | flops 3221225472 | bytes 6291456 | tf_op jit(solution)/shard_map/pallas_call | solution.py:345
  31.2 0.5 shard_map.84.rows_ref
  31.7 0.0 collective-permute-start.16
  31.8 0.0 collective-permute-done.10.y1
  31.8 0.6 %collective-permute-start.12 = (f32[16,128]{1,0:T(8,128)S(1)}, f32[16,128]{1,0:T(8,128)S(1)}, u32[]{:S(2)}, u32[]{:S(2)}) collective-permute-start(f32[16,128]{1,0:T(8,128)S(1)} %shard_map.83.y0), channel_id=1, source_target_pairs={{0,1},{1,0},{2,3},{3,2},{4,5},{5,4},{6,7},{7,6},{8,9},{9,8},{10,11... | collective-permute-start | bytes 24584 | tf_op jit(solution)/shard_map/ppermute | solution.py:34
  32.4 2.8 %collective-permute-start.18 = (f32[1,128]{1,0:T(1,128)S(1)}, f32[1,128]{1,0:T(1,128)S(1)}, u32[]{:S(2)}, u32[]{:S(2)}) collective-permute-start(f32[1,128]{1,0:T(1,128)S(1)} %slice_add_fusion), channel_id=1, source_target_pairs={{0,8},{1,9},{2,10},{3,11},{4,12},{5,13},{6,14},{7,15},{8,0},{9,1},... | collective-permute-start | bytes 1544 | tf_op jit(solution)/shard_map/ppermute | solution.py:34
  35.1 0.0 collective-permute-done.12.y1
  35.1 3.2 %collective-permute-start.13 = (f32[24,128]{1,0:T(8,128)S(1)}, f32[24,128]{1,0:T(8,128)S(1)}, u32[]{:S(2)}, u32[]{:S(2)}) collective-permute-start(f32[24,128]{1,0:T(8,128)S(1)} %get-tuple-element.13), channel_id=1, source_target_pairs={{0,4},{1,5},{2,6},{3,7},{4,0},{5,1},{6,2},{7,3},{8,12},{9,13},{10,... | collective-permute-start | bytes 36872 | tf_op jit(solution)/shard_map/ppermute | solution.py:34
  38.3 0.7 %collective-permute-start.14 = (f32[24,128]{1,0:T(8,128)S(1)}, f32[24,128]{1,0:T(8,128)S(1)}, u32[]{:S(2)}, u32[]{:S(2)}) collective-permute-start(f32[24,128]{1,0:T(8,128)S(1)} %get-tuple-element.14), channel_id=1, source_target_pairs={{0,2},{1,3},{2,0},{3,1},{4,6},{5,7},{6,4},{7,5},{8,10},{9,11},{10,... | collective-permute-start | bytes 36872 | tf_op jit(solution)/shard_map/ppermute | solution.py:34
  39.0 0.4 collective-permute-start.15
  39.4 0.0 collective-permute-done.16
  39.4 1.0 %collective-permute-done.13 = f32[24,128]{1,0:T(8,128)S(1)} collective-permute-done((f32[24,128]{1,0:T(8,128)S(1)}, f32[24,128]{1,0:T(8,128)S(1)}, u32[]{:S(2)}, u32[]{:S(2)}) %collective-permute-start.13) | collective-permute-done | bytes 12320 | tf_op jit(solution)/shard_map/ppermute | solution.py:34
  40.4 1.6 %collective-permute-done.14 = f32[24,128]{1,0:T(8,128)S(1)} collective-permute-done((f32[24,128]{1,0:T(8,128)S(1)}, f32[24,128]{1,0:T(8,128)S(1)}, u32[]{:S(2)}, u32[]{:S(2)}) %collective-permute-start.14) | collective-permute-done | bytes 12320 | tf_op jit(solution)/shard_map/ppermute | solution.py:34
  42.0 1.9 %collective-permute-done.15 = f32[24,128]{1,0:T(8,128)S(1)} collective-permute-done((f32[24,128]{1,0:T(8,128)S(1)}, f32[24,128]{1,0:T(8,128)S(1)}, u32[]{:S(2)}, u32[]{:S(2)}) %collective-permute-start.15) | collective-permute-done | bytes 12320 | tf_op jit(solution)/shard_map/ppermute | solution.py:34
  43.9 0.6 %collective-permute-start.19 = (f32[1,128]{1,0:T(1,128)S(1)}, f32[1,128]{1,0:T(1,128)S(1)}, u32[]{:S(2)}, u32[]{:S(2)}) collective-permute-start(f32[1,128]{1,0:T(1,128)S(1)} %slice.24), channel_id=1, source_target_pairs={{0,192},{1,193},{2,194},{3,195},{4,196},{5,197},{6,198},{7,199},{8... | collective-permute-start | bytes 1544 | tf_op jit(solution)/shard_map/ppermute | solution.py:34
  44.6 1.1 %shard_map.86.exchange_ref = f32[2,16]{1,0:T(2,128)S(1)} custom-call(f32[24,128]{1,0:T(8,128)S(1)} %add_add_fusion.y_ref, f32[1,1536]{1,0:T(1,128)S(1)} %reshape.19.c_ref, f32[32,1536]{1,0:T(8,128)S(1)} %get-tuple-element.16.rx_ref, bf16[2048,1536]{1,0:T(8,128)(2,1)S(1)} %bitcast.8), custom_call_target="tpu_custom_call" | custom-call | flops 805306368 | bytes 6291456 | tf_op jit(solution)/shard_map/pallas_call | solution.py:420
  45.6 0.0 collective-permute-done.18.d_ref
  45.6 3.1 %collective-permute-done.19.h_ref = f32[1,128]{1,0:T(1,128)S(1)} collective-permute-done((f32[1,128]{1,0:T(1,128)S(1)}, f32[1,128]{1,0:T(1,128)S(1)}, u32[]{:S(2)}, u32[]{:S(2)}) %collective-permute-start.19) | collective-permute-done | bytes 544 | tf_op jit(solution)/shard_map/ppermute | solution.py:34
  48.8 0.6 %shard_map.87 = f32[2,16]{1,0:T(2,128)} custom-call(f32[1,16]{1,0:T(1,128)S(1)} %copy-done.1, f32[2,16]{1,0:T(2,128)S(1)} %bitcast.10, f32[2,16]{1,0:T(2,128)S(1)} %shard_map.86.exchange_ref, f32[1,128]{1,0:T(1,128)S(1)} %slice_add_fusion.1.near_ref, f32[1,128]{1,0:T(1,128)S(1)} %collective-permute-done.18.d_ref, f32[1,128]{1,0:T(1,128)S(1)} %collective-permute-done.19.h_ref), custom_call_target="tpu_custom_call" | custom-call | tf_op jit(solution)/shard_map/pallas_call | solution.py:357
  (29 shorter events, 0.1 us)
Async XLA Ops:
  1.0 12.6 %copy-start.2 = (f32[256,1536]{1,0:T(8,128)S(1)}, f32[256,1536]{1,0:T(8,128)}, u32[]{:S(2)}) copy-start(f32[256,1536]{1,0:T(8,128)} %screening.1) | copy-start | bytes 4718596
  1.0 12.6 %copy-start.3 = (s32[1,256]{1,0:T(1,128)S(1)}, s32[1,256]{1,0:T(1,128)}, u32[]{:S(2)}) copy-start(s32[1,256]{1,0:T(1,128)} %qmap_ref.1) | copy-start | bytes 3076
  1.0 7.8 %collective-permute-start.5 = (bf16[16,1152]{1,0:T(8,128)(2,1)S(1)}, bf16[16,1152]{1,0:T(8,128)(2,1)S(1)}, u32[]{:S(2)}, u32[]{:S(2)}) collective-permute-start(bf16[16,1152]{1,0:T(8,128)(2,1)S(1)} %shard_map.73.a0.a_near.refs_0_), channel_id=1, source_target_pairs={{0,64},{1,65},{2,66},{3,67},{4,68},{5,69},{6,70},{7,71},{8,72},{9,... | collective-permute-start | bytes 110600 | tf_op jit(solution)/shard_map/ppermute | solution.py:34
  3.3 10.2 %collective-permute-start = (bf16[16,1152]{1,0:T(8,128)(2,1)S(1)}, bf16[16,1152]{1,0:T(8,128)(2,1)S(1)}, u32[]{:S(2)}, u32[]{:S(2)}) collective-permute-start(bf16[16,1152]{1,0:T(8,128)(2,1)S(1)} %shard_map.73.a0.a_near.refs_0_), channel_id=1, source_target_pairs={{0,8},{1,9},{2,10},{3,11},{4,12},{5,13},{6,14},{7,15},{8,0},{9,1},... | collective-permute-start | bytes 110600 | tf_op jit(solution)/shard_map/ppermute | solution.py:34
  8.7 5.8 %collective-permute-start.1 = (bf16[16,1152]{1,0:T(8,128)(2,1)S(1)}, bf16[16,1152]{1,0:T(8,128)(2,1)S(1)}, u32[]{:S(2)}, u32[]{:S(2)}) collective-permute-start(bf16[16,1152]{1,0:T(8,128)(2,1)S(1)} %shard_map.73.a0.a_near.refs_0_), channel_id=1, source_target_pairs={{0,1},{1,0},{2,3},{3,2},{4,5},{5,4},{6,7},{7,6},{8,9},{9,8},{10,11... | collective-permute-start | bytes 110600 | tf_op jit(solution)/shard_map/ppermute | solution.py:34
  8.7 9.2 %collective-permute-start.6 = (bf16[16,1152]{1,0:T(8,128)(2,1)S(1)}, bf16[16,1152]{1,0:T(8,128)(2,1)S(1)}, u32[]{:S(2)}, u32[]{:S(2)}) collective-permute-start(bf16[16,1152]{1,0:T(8,128)(2,1)S(1)} %collective-permute-done.5._.b0.refs_2_), channel_id=1, source_target_pairs={{0,2},{1,3},{2,0},{3,1},{4,6},{5,7},{6,4},{7,5},{8,10},{9,11},{10,... | collective-permute-start | bytes 110600 | tf_op jit(solution)/shard_map/ppermute | solution.py:34
  10.3 7.7 %collective-permute-start.7 = (bf16[16,1152]{1,0:T(8,128)(2,1)S(1)}, bf16[16,1152]{1,0:T(8,128)(2,1)S(1)}, u32[]{:S(2)}, u32[]{:S(2)}) collective-permute-start(bf16[16,1152]{1,0:T(8,128)(2,1)S(1)} %collective-permute-done.5._.b0.refs_2_), channel_id=1, source_target_pairs={{0,4},{1,5},{2,6},{3,7},{4,0},{5,1},{6,2},{7,3},{8,12},{9,13},{10,... | collective-permute-start | bytes 110600 | tf_op jit(solution)/shard_map/ppermute | solution.py:34
  13.2 5.2 %collective-permute-start.8 = (bf16[16,1152]{1,0:T(8,128)(2,1)S(1)}, bf16[16,1152]{1,0:T(8,128)(2,1)S(1)}, u32[]{:S(2)}, u32[]{:S(2)}) collective-permute-start(bf16[16,1152]{1,0:T(8,128)(2,1)S(1)} %collective-permute-done.5._.b0.refs_2_), channel_id=1, source_target_pairs={{0,6},{1,7},{2,4},{3,5},{4,2},{5,3},{6,0},{7,1},{8,14},{9,15},{10,... | collective-permute-start | bytes 110600 | tf_op jit(solution)/shard_map/ppermute | solution.py:34
  13.4 4.9 %slice-start = ((s8[6291456]{0:T(1024)(128)(4,1)}), s8[4194304]{0:T(1024)(128)(4,1)S(1)}, s32[]{:S(2)}) async-start(s8[6291456]{0:T(1024)(128)(4,1)} %bitcast.4), calls=%async_computation | async-start | bytes 8388608
  13.4 4.9 %slice-start.1 = ((s8[6291456]{0:T(1024)(128)(4,1)}), s8[2097152]{0:T(1024)(128)(4,1)S(1)}, s32[]{:S(2)}) async-start(s8[6291456]{0:T(1024)(128)(4,1)} %bitcast.4), calls=%async_computation.1 | async-start | bytes 4194304
  13.4 1.3 %collective-permute-start.2 = (bf16[16,1152]{1,0:T(8,128)(2,1)S(1)}, bf16[16,1152]{1,0:T(8,128)(2,1)S(1)}, u32[]{:S(2)}, u32[]{:S(2)}) collective-permute-start(bf16[16,1152]{1,0:T(8,128)(2,1)S(1)} %collective-permute-done.a1.a_near.refs_0_), channel_id=1, source_target_pairs={{0,1},{1,0},{2,3},{3,2},{4,5},{5,4},{6,7},{7,6},{8,9},{9,8},{10,11... | collective-permute-start | bytes 110600 | tf_op jit(solution)/shard_map/ppermute | solution.py:34
  14.9 7.5 %collective-permute-start.3 = (f32[16,128]{1,0:T(8,128)S(1)}, f32[16,128]{1,0:T(8,128)S(1)}, u32[]{:S(2)}, u32[]{:S(2)}) collective-permute-start(f32[16,128]{1,0:T(8,128)S(1)} %shard_map.74._.y0), channel_id=1, source_target_pairs={{0,16},{1,17},{2,18},{3,19},{4,20},{5,21},{6,22},{7,23},{8,24},{9,... | collective-permute-start | bytes 24584 | tf_op jit(solution)/shard_map/ppermute | solution.py:34
  16.0 6.4 %collective-permute-start.4 = (f32[16,128]{1,0:T(8,128)S(1)}, f32[16,128]{1,0:T(8,128)S(1)}, u32[]{:S(2)}, u32[]{:S(2)}) collective-permute-start(f32[16,128]{1,0:T(8,128)S(1)} %shard_map.74._.y0), channel_id=1, source_target_pairs={{0,48},{1,33},{2,50},{3,35},{4,52},{5,37},{6,54},{7,39},{8,56},{9,... | collective-permute-start | bytes 24584 | tf_op jit(solution)/shard_map/ppermute | solution.py:34
  18.4 4.2 %copy-start.4 = (f32[1536]{0:T(1024)S(1)}, f32[1536]{0:T(1024)}, u32[]{:S(2)}) copy-start(f32[1536]{0:T(1024)} %param.12) | copy-start | bytes 18436
  22.5 1.7 %collective-permute-start.9 = (f32[16,128]{1,0:T(8,128)S(1)}, f32[16,128]{1,0:T(8,128)S(1)}, u32[]{:S(2)}, u32[]{:S(2)}) collective-permute-start(f32[16,128]{1,0:T(8,128)S(1)} %shard_map.78.y0), channel_id=1, source_target_pairs={{0,1},{1,0},{2,3},{3,2},{4,5},{5,4},{6,7},{7,6},{8,9},{9,8},{10,11... | collective-permute-start | bytes 24584 | tf_op jit(solution)/shard_map/ppermute | solution.py:34
  23.1 9.3 %collective-permute-start.17 = (f32[1,128]{1,0:T(1,128)S(1)}, f32[1,128]{1,0:T(1,128)S(1)}, u32[]{:S(2)}, u32[]{:S(2)}) collective-permute-start(f32[1,128]{1,0:T(1,128)S(1)} %slice.23), channel_id=1, source_target_pairs={{0,1},{1,0},{2,3},{3,2},{4,5},{5,4},{6,7},{7,6},{8,9},{9,8},{10,11... | collective-permute-start | bytes 1544 | tf_op jit(solution)/shard_map/ppermute | solution.py:34
  24.2 7.5 %collective-permute-start.10 = (f32[16,128]{1,0:T(8,128)S(1)}, f32[16,128]{1,0:T(8,128)S(1)}, u32[]{:S(2)}, u32[]{:S(2)}) collective-permute-start(f32[16,128]{1,0:T(8,128)S(1)} %shard_map.81._.y0), channel_id=1, source_target_pairs={{0,64},{1,65},{2,66},{3,67},{4,68},{5,69},{6,70},{7,71},{8,72},{9,... | collective-permute-start | bytes 24584 | tf_op jit(solution)/shard_map/ppermute | solution.py:34
  25.9 5.9 %collective-permute-start.11 = (f32[16,128]{1,0:T(8,128)S(1)}, f32[16,128]{1,0:T(8,128)S(1)}, u32[]{:S(2)}, u32[]{:S(2)}) collective-permute-start(f32[16,128]{1,0:T(8,128)S(1)} %shard_map.81._.y0), channel_id=1, source_target_pairs={{0,192},{1,129},{2,194},{3,131},{4,196},{5,133},{6,198},{7,135},{8... | collective-permute-start | bytes 24584 | tf_op jit(solution)/shard_map/ppermute | solution.py:34
  31.7 7.7 %collective-permute-start.16 = (f32[1,128]{1,0:T(1,128)S(1)}, f32[1,128]{1,0:T(1,128)S(1)}, u32[]{:S(2)}, u32[]{:S(2)}) collective-permute-start(f32[1,128]{1,0:T(1,128)S(1)} %slice.21), channel_id=1, source_target_pairs={{0,1},{1,0},{2,3},{3,2},{4,5},{5,4},{6,7},{7,6},{8,9},{9,8},{10,11... | collective-permute-start | bytes 1544 | tf_op jit(solution)/shard_map/ppermute | solution.py:34
  31.8 3.3 %collective-permute-start.12 = (f32[16,128]{1,0:T(8,128)S(1)}, f32[16,128]{1,0:T(8,128)S(1)}, u32[]{:S(2)}, u32[]{:S(2)}) collective-permute-start(f32[16,128]{1,0:T(8,128)S(1)} %shard_map.83.y0), channel_id=1, source_target_pairs={{0,1},{1,0},{2,3},{3,2},{4,5},{5,4},{6,7},{7,6},{8,9},{9,8},{10,11... | collective-permute-start | bytes 24584 | tf_op jit(solution)/shard_map/ppermute | solution.py:34
  32.4 13.3 %collective-permute-start.18 = (f32[1,128]{1,0:T(1,128)S(1)}, f32[1,128]{1,0:T(1,128)S(1)}, u32[]{:S(2)}, u32[]{:S(2)}) collective-permute-start(f32[1,128]{1,0:T(1,128)S(1)} %slice_add_fusion), channel_id=1, source_target_pairs={{0,8},{1,9},{2,10},{3,11},{4,12},{5,13},{6,14},{7,15},{8,0},{9,1},... | collective-permute-start | bytes 1544 | tf_op jit(solution)/shard_map/ppermute | solution.py:34
  35.1 5.3 %collective-permute-start.13 = (f32[24,128]{1,0:T(8,128)S(1)}, f32[24,128]{1,0:T(8,128)S(1)}, u32[]{:S(2)}, u32[]{:S(2)}) collective-permute-start(f32[24,128]{1,0:T(8,128)S(1)} %get-tuple-element.13), channel_id=1, source_target_pairs={{0,4},{1,5},{2,6},{3,7},{4,0},{5,1},{6,2},{7,3},{8,12},{9,13},{10,... | collective-permute-start | bytes 36872 | tf_op jit(solution)/shard_map/ppermute | solution.py:34
  38.3 3.7 %collective-permute-start.14 = (f32[24,128]{1,0:T(8,128)S(1)}, f32[24,128]{1,0:T(8,128)S(1)}, u32[]{:S(2)}, u32[]{:S(2)}) collective-permute-start(f32[24,128]{1,0:T(8,128)S(1)} %get-tuple-element.14), channel_id=1, source_target_pairs={{0,2},{1,3},{2,0},{3,1},{4,6},{5,7},{6,4},{7,5},{8,10},{9,11},{10,... | collective-permute-start | bytes 36872 | tf_op jit(solution)/shard_map/ppermute | solution.py:34
  39.0 4.9 %collective-permute-start.15 = (f32[24,128]{1,0:T(8,128)S(1)}, f32[24,128]{1,0:T(8,128)S(1)}, u32[]{:S(2)}, u32[]{:S(2)}) collective-permute-start(f32[24,128]{1,0:T(8,128)S(1)} %get-tuple-element.15), channel_id=1, source_target_pairs={{0,6},{1,7},{2,4},{3,5},{4,2},{5,3},{6,0},{7,1},{8,14},{9,15},{10,... | collective-permute-start | bytes 36872 | tf_op jit(solution)/shard_map/ppermute | solution.py:34
  43.9 4.8 %collective-permute-start.19 = (f32[1,128]{1,0:T(1,128)S(1)}, f32[1,128]{1,0:T(1,128)S(1)}, u32[]{:S(2)}, u32[]{:S(2)}) collective-permute-start(f32[1,128]{1,0:T(1,128)S(1)} %slice.24), channel_id=1, source_target_pairs={{0,192},{1,193},{2,194},{3,195},{4,196},{5,197},{6,198},{7,199},{8... | collective-permute-start | bytes 1544 | tf_op jit(solution)/shard_map/ppermute | solution.py:34
  44.6 4.2 %copy-start = (f32[1,2,16]{2,1,0:T(2,128)S(1)}, f32[1,2,16]{2,1,0:T(2,128)}, u32[]{:S(2)}) copy-start(f32[1,2,16]{2,1,0:T(2,128)} %param.8) | copy-start | bytes 388
  44.6 4.2 %copy-start.1 = (f32[1,16]{1,0:T(1,128)S(1)}, f32[1,16]{1,0:T(1,128)}, u32[]{:S(2)}) copy-start(f32[1,16]{1,0:T(1,128)} %energy_ref.1) | copy-start | bytes 196
